TPU v7x, 256 devices: a whole 4x4x8 slice. The times are simulated.
256 devices in a mesh: pb: 4 (over y), ka: 16 (over z, x_lo), ha: 4 (over x_hi, core).
Axes of the slice: x: 4 (x_hi: 2, x_lo: 2; x = x_hi * 2 + x_lo), y: 4, z: 8, core: 2. Of those that a mesh axis runs over, the one named last changes fastest.
Arguments:
- queries: bfloat16 [16384, 512], P(('pb', 'ka'), 'ha'), may hold values from -6 to 6
- key_rows: bfloat16 [16384, 512], P(('pb', 'ka'), 'ha'), may hold values from -6 to 6
- value_rows: bfloat16 [16384, 512], P(('pb', 'ka'), 'ha'), may hold values from -6 to 6
- outputs: bfloat16 [16384, 512], P(('pb', 'ka'), 'ha'), may hold values from -6 to 6
- out_grad: bfloat16 [16384, 512], P(('pb', 'ka'), 'ha'), may hold values from -6 to 6
- saved_lse: bfloat16 [16384, 4], P(('pb', 'ka'), 'ha'), may hold values from -1 to 12, as said below
- fold_map: int32 [128], replicated, may hold values from 0 to 127, as said below
Outputs:
- query_grad: bfloat16 [16384, 512], P(('pb', 'ka'), 'ha')
- key_grad: bfloat16 [16384, 512], P(('pb', 'ka'), 'ha')
- value_grad: bfloat16 [16384, 512], P(('pb', 'ka'), 'ha')
Inputs may be any that keep to these rules, and one draw needn't show every extreme that they name: `fold_map`: stored blocks 2 d and 2 d + 1 hold a mirrored pair of blocks, b and 127 - b, in either order; every block is held once. `saved_lse`: close to the log-sum-exp of the row's visible scores.
All inputs are finite; a program needn't handle non-finite values.
Results may differ from a plain program's by a relative error of at most 0.0055.
Values may be sent and summed in bfloat16 or wider, within the bound.
No kernel may reach another device: no remote copies, remote signals or barrier semaphores. Data moves between devices by JAX's collectives and lax.ppermute only.
A program may use at most 64 MiB of HBM per device.

v0:
```python
import math

import jax
import jax.numpy as jnp
from jax import lax
from jax.sharding import PartitionSpec as P


def block_length(row_total):
    length = row_total
    while length > 512 and length % 2 == 0:
        length = length // 2
    return length


def tile_grads(
    query_blk, grad_blk, lse_blk, delta_blk, query_pos, key_blk, value_blk, key_pos, factor
):
    scores = (
        jnp.einsum("qhd,khd->hqk", query_blk, key_blk, preferred_element_type=jnp.float32) * factor
    )
    visible = key_pos[None, :] <= query_pos[:, None]
    probs = jnp.where(visible[None], jnp.exp(scores - lse_blk.T[:, :, None]), 0.0)
    probs_low = probs.astype(jnp.bfloat16)
    value_part = jnp.einsum("hqk,qhd->khd", probs_low, grad_blk, preferred_element_type=jnp.float32)
    dprobs = jnp.einsum("qhd,khd->hqk", grad_blk, value_blk, preferred_element_type=jnp.float32)
    dscores = (probs * (dprobs - delta_blk.T[:, :, None])).astype(jnp.bfloat16)
    query_part = jnp.einsum("hqk,khd->qhd", dscores, key_blk, preferred_element_type=jnp.float32)
    key_part = jnp.einsum("hqk,qhd->khd", dscores, query_blk, preferred_element_type=jnp.float32)
    return (query_part, key_part, value_part)


def add_rows(target, update, first_row):
    length = update.shape[0]
    current = lax.dynamic_slice_in_dim(target, first_row, length, 0)
    return lax.dynamic_update_slice_in_dim(target, current + update, first_row, 0)


def body(queries, key_rows, value_rows, outputs, out_grad, saved_lse, fold_map):
    row_count, full_width = queries.shape
    head_count = saved_lse.shape[1]
    head_dim = full_width // head_count
    factor = 1.0 / math.sqrt(head_dim)
    fold_rows = row_count // 2
    size_pb = lax.axis_size("pb")
    size_ka = lax.axis_size("ka")
    index_pb = lax.axis_index("pb")
    index_ka = lax.axis_index("ka")
    key_all, value_all = (
        lax.all_gather(key_rows, "pb", axis=0, tiled=True),
        lax.all_gather(value_rows, "pb", axis=0, tiled=True),
    )
    key_len = size_pb * row_count
    key_all = key_all.reshape(key_len, head_count, head_dim)
    value_all = value_all.reshape(key_len, head_count, head_dim)
    key_iota = jnp.arange(key_len, dtype=jnp.int32)
    key_global = (key_iota // row_count * size_ka + index_ka) * row_count + key_iota % row_count
    key_pos = fold_map[key_global // fold_rows] * fold_rows + key_global % fold_rows
    query_len = size_ka * row_count
    query_first = index_pb * query_len
    query_empty = jnp.zeros((query_len, head_count, head_dim), jnp.float32)
    key_empty = jnp.zeros((key_len, head_count, head_dim), jnp.float32)
    init = (query_empty, key_empty, key_empty)
    query_src = lax.all_gather(queries, "ka", axis=0, tiled=True)
    grad_src = lax.all_gather(out_grad, "ka", axis=0, tiled=True)
    saved_src = lax.all_gather(outputs, "ka", axis=0, tiled=True)
    lse_src = lax.all_gather(saved_lse, "ka", axis=0, tiled=True)
    piece_rows = query_src.shape[0]
    step_rows = block_length(piece_rows)

    def one_block(number, state):
        dq_all, dk_all, dv_all = state
        offset = number * step_rows
        query_blk = lax.dynamic_slice_in_dim(query_src, offset, step_rows, 0).reshape(
            step_rows, head_count, head_dim
        )
        grad_blk = lax.dynamic_slice_in_dim(grad_src, offset, step_rows, 0).reshape(
            step_rows, head_count, head_dim
        )
        lse_blk = lax.dynamic_slice_in_dim(lse_src, offset, step_rows, 0).astype(jnp.float32)
        saved_blk = lax.dynamic_slice_in_dim(saved_src, offset, step_rows, 0).reshape(
            step_rows, head_count, head_dim
        )
        delta_low = jnp.einsum(
            "qhd,qhd->qh", grad_blk, saved_blk, preferred_element_type=jnp.float32
        ).astype(jnp.bfloat16)
        delta_blk = lax.optimization_barrier(delta_low).astype(jnp.float32)
        row_global = query_first + offset + jnp.arange(step_rows, dtype=jnp.int32)
        query_pos = fold_map[row_global // fold_rows] * fold_rows + row_global % fold_rows
        dq_blk, dk_part, dv_part = tile_grads(
            query_blk, grad_blk, lse_blk, delta_blk, query_pos, key_all, value_all, key_pos, factor
        )
        dk_all = dk_all + dk_part
        dv_all = dv_all + dv_part
        dq_all = add_rows(dq_all, dq_blk, offset)
        return (dq_all, dk_all, dv_all)

    dq_all, dk_all, dv_all = lax.fori_loop(0, piece_rows // step_rows, one_block, init)
    query_mine = lax.psum_scatter(
        dq_all.reshape(query_len, full_width), "ka", scatter_dimension=0, tiled=True
    )
    query_grad = (query_mine * factor).astype(jnp.bfloat16)
    key_flat = dk_all.reshape(key_len, full_width)
    value_flat = dv_all.reshape(key_len, full_width)
    key_total, value_total = lax.psum((key_flat, value_flat), "pb")
    key_mine = lax.dynamic_slice_in_dim(key_total, index_pb * row_count, row_count, 0)
    value_mine = lax.dynamic_slice_in_dim(value_total, index_pb * row_count, row_count, 0)
    key_grad = (key_mine * factor).astype(jnp.bfloat16)
    value_grad = value_mine.astype(jnp.bfloat16)
    return (query_grad, key_grad, value_grad)


def solution(mesh):
    return jax.shard_map(
        body,
        mesh=mesh,
        in_specs=(
            P(("pb", "ka"), "ha"),
            P(("pb", "ka"), "ha"),
            P(("pb", "ka"), "ha"),
            P(("pb", "ka"), "ha"),
            P(("pb", "ka"), "ha"),
            P(("pb", "ka"), "ha"),
            P(),
        ),
        out_specs=(P(("pb", "ka"), "ha"), P(("pb", "ka"), "ha"), P(("pb", "ka"), "ha")),
        check_vma=False,
    )
```

profile of v0, /device:TPU:4, one launch (start us, length us, event | category | flops | bytes accessed | tf_op | source)
XLA Modules:
  0.0 445.2 jit_solution(9629851402031755443)
XLA Ops:
  9.6 6.6 %gather_fusion.1 = s32[1024]{0:T(1024)S(1)} fusion(s32[128]{0:T(128)S(1)} %copy-done, s32[1024]{0:T(1024)S(1)} %broadcast_clamp_fusion), kind=kCustom, calls=%fused_computation.1 | custom fusion | bytes 12288 | tf_op jit(solution)/shard_map/gather | solution.py:58
  16.2 36.0 %all_gather.20 = bf16[4096,1]{0,1:T(2,128)(2,1)S(1)} all-gather(bf16[256,1]{0,1:T(2,128)(2,1)S(1)} %copy-done.5), channel_id=1, replica_groups=mesh['pb'=4,'ka'=16,'ha'=4] {'ka'}, dimensions={0}, use_global_device_ids=true | all-gather | bytes 8704 | tf_op jit(solution)/shard_map/all_gather | solution.py:67
  52.2 13.6 %all_gather.19 = bf16[1024,128]{1,0:T(8,128)(2,1)} all-gather(bf16[256,128]{1,0:T(8,128)(2,1)S(1)} %copy-done.3), channel_id=1, replica_groups=mesh['pb'=4,'ka'=16,'ha'=4] {'pb'}, dimensions={0}, use_global_device_ids=true | all-gather | bytes 327680 | tf_op jit(solution)/shard_map/all_gather | solution.py:50
  65.8 12.2 %all_gather.22 = bf16[1024,128]{1,0:T(8,128)(2,1)S(1)} all-gather(bf16[256,128]{1,0:T(8,128)(2,1)S(1)} %copy-done.4), channel_id=1, replica_groups=mesh['pb'=4,'ka'=16,'ha'=4] {'pb'}, dimensions={0}, use_global_device_ids=true | all-gather | bytes 327680 | tf_op jit(solution)/shard_map/all_gather | solution.py:51
  78.1 3.2 all-gather.4.cloned.1.call-done
  81.3 71.2 %all-gather.8.cloned.1.call-done = bf16[4096,128]{1,0:T(8,128)(2,1)} async-done(((bf16[256,128]{1,0:T(8,128)(2,1)}), bf16[4096,128]{1,0:T(8,128)(2,1)}) %all-gather.8.cloned.1.call-update) | async-done | bytes 1048592 | tf_op jit(solution)/shard_map/all_gather | solution.py:66
  152.4 71.0 %all-gather.6.cloned.1.call-done = bf16[4096,128]{1,0:T(8,128)(2,1)} async-done(((bf16[256,128]{1,0:T(8,128)(2,1)}), bf16[4096,128]{1,0:T(8,128)(2,1)}) %all-gather.6.cloned.1.call-update) | async-done | bytes 1048592 | tf_op jit(solution)/shard_map/all_gather | solution.py:65
  223.6 85.5 %while.20 = (s32[]{:T(128)}, f32[4096,1,128]{2,0,1:T(8,128)S(1)}, f32[1024,1,128]{0,2,1:T(8,128)S(1)}, f32[1024,1,128]{0,2,1:T(8,128)S(1)}, s32[1024]{0:T(1024)S...) while((s32[]{:T(128)}, f32[4096,1,128]{2,0,1:T(8,128)S(1)}, ...), condition=%wide.region_1.2_spmd.clone, body=%wide.region_0.1_spmd.clone.sunk | while | flops 676153344 | bytes 14718250 | solution.py:98
  224.8 3.3 gather_fusion
  235.5 3.3 gather_fusion
  246.2 3.3 gather_fusion
  249.6 1.6 exponential_select_fusion.2
  256.9 3.3 gather_fusion
  260.2 1.6 exponential_select_fusion.2
  267.6 3.3 gather_fusion
  270.9 1.6 exponential_select_fusion.2
  278.2 3.3 gather_fusion
  281.6 1.6 exponential_select_fusion.2
  288.9 3.3 gather_fusion
  299.6 3.3 gather_fusion
  303.0 1.6 exponential_select_fusion.2
  311.1 22.6 %all-reduce.4 = bf16[1024,128]{1,0:T(8,128)(2,1)S(1)} all-reduce(f32[1024,128]{1,0:T(8,128)S(1)} %bitcast.67), channel_id=1, replica_groups=mesh['pb'=4,'ka'=16,'ha'=4] {'pb'}, use_global_device_ids=true, to_apply=%region_4.5 | all-reduce | flops 131072 | bytes 786432 | tf_op jit(solution)/shard_map/psum | solution.py:105
  334.4 25.4 %all-reduce.3.cloned.1.call-done = f32[1024,128]{1,0:T(8,128)} async-done(((f32[1024,128]{1,0:T(8,128)}), f32[1024,128]{1,0:T(8,128)}) %all-reduce.3.cloned.1.call-update) | async-done | bytes 524304 | tf_op jit(solution)/shard_map/psum | solution.py:105
  361.3 75.8 %reduce-scatter.2.cloned.1.call-done = f32[256,128]{1,0:T(8,128)} async-done(((f32[4096,128]{1,0:T(8,128)}), f32[256,128]{1,0:T(8,128)}) %reduce-scatter.2.cloned.1.call-update) | async-done | bytes 131088 | tf_op jit(solution)/shard_map/reduce_scatter | solution.py:99
  (138 shorter events, 57.7 us)
Async XLA Ops:
  7.2 2.4 copy-start
  7.2 74.1 %all-gather.4.cloned.1.call-start = ((), (), s32[]{:S(2)}) async-start(), calls=%async_computation.1 | async-start | bytes 1114112 | tf_op jit(solution)/shard_map/all_gather | solution.py:64
  7.9 144.5 %all-gather.8.cloned.1.call-start = ((), (), s32[]{:S(2)}) async-start(), calls=%async_computation.3 | async-start | bytes 1114112 | tf_op jit(solution)/shard_map/all_gather | solution.py:66
  8.7 214.8 %all-gather.6.cloned.1.call-start = ((), (), s32[]{:S(2)}) async-start(), calls=%async_computation.2 | async-start | bytes 1114112 | tf_op jit(solution)/shard_map/all_gather | solution.py:65
  9.4 350.4 %all-reduce.3.cloned.1.call-start = ((), (), s32[]{:S(2)}) async-start(), calls=%async_computation.5 | async-start | bytes 1048576 | tf_op jit(solution)/shard_map/psum | solution.py:105
  9.5 6.6 %copy-start.5 = (bf16[256,1]{0,1:T(2,128)(2,1)S(1)}, bf16[256,1]{0,1:T(2,128)(2,1)}, u32[]{:S(2)}) copy-start(bf16[256,1]{0,1:T(2,128)(2,1)} %param.14) | copy-start | bytes 1540
  9.5 42.6 %copy-start.3 = (bf16[256,128]{1,0:T(8,128)(2,1)S(1)}, bf16[256,128]{1,0:T(8,128)(2,1)}, u32[]{:S(2)}) copy-start(bf16[256,128]{1,0:T(8,128)(2,1)} %param.10) | copy-start | bytes 196612
  9.6 56.3 %copy-start.4 = (bf16[256,128]{1,0:T(8,128)(2,1)S(1)}, bf16[256,128]{1,0:T(8,128)(2,1)}, u32[]{:S(2)}) copy-start(bf16[256,128]{1,0:T(8,128)(2,1)} %param.11) | copy-start | bytes 196612
  231.1 2.7 copy-start.2
  241.8 2.7 copy-start.2
  252.5 2.7 copy-start.2
  263.2 2.7 copy-start.2
  273.8 2.7 copy-start.2
  284.5 2.7 copy-start.2
  295.2 2.7 copy-start.2
  305.9 2.7 copy-start.2
  309.1 1.5 copy-start.1
  310.3 126.8 %reduce-scatter.2.cloned.1.call-start = ((), (), s32[]{:S(2)}) async-start(), calls=%async_computation.4 | async-start | bytes 2228224 | tf_op jit(solution)/shard_map/reduce_scatter | solution.py:99
Sparse Core Ops, SparseCore 0:
  9.8 71.4 all-gather.3
  83.0 69.3 all-gather.7
  154.2 69.2 all-gather.5
  310.4 49.2 all-reduce.2
  362.2 74.9 reduce-scatter.1
where the time goes:
time: 447 us; the launch traced here: 445 us
  waiting for transfers between devices  249 us (56%)
  blocking collectives  84.5 us (19%)
  matrix products  48.2 us (11%)
  local copies, waits for them, and re-layouts  35.9 us (8%)
  between operations  13.9 us (3%)
  other arithmetic  12.5 us (3%)
    reduce_scatter x1, waiting for transfers between devices, body(): lax.psum_scatter(dq_all.reshape(query_len, full_width), 'ka', scatter_dim...  75.8 us
    all_gather x1, waiting for transfers between devices, body(): saved_src = lax.all_gather(outputs, 'ka', axis=0, tiled=True)  71.2 us
    all_gather x1, waiting for transfers between devices, body(): grad_src = lax.all_gather(out_grad, 'ka', axis=0, tiled=True)  71 us
    all_gather x1, blocking collectives, body(): lse_src = lax.all_gather(saved_lse, 'ka', axis=0, tiled=True)  36 us
    gather x8, local copies, waits for them, and re-layouts, one_block(): fold_map[row_global // fold_rows] * fold_rows + row_global % fold_rows  26.8 us
    psum x1, waiting for transfers between devices, body(): key_total, value_total = lax.psum((key_flat, value_flat), 'pb')  25.4 us
    psum x1, blocking collectives, body(): key_total, value_total = lax.psum((key_flat, value_flat), 'pb')  22.6 us
    all_gather x1, blocking collectives, body(): lax.all_gather(key_rows, 'pb', axis=0, tiled=True)  13.6 us
  transfers between devices with their start and end apart: 5, of which 5 were waited for; matrix products, arithmetic and copies ran while one was open for 2% of the time, Pallas kernels for 0%

commit v1 on v0

v1 whole, which is shorter than its diff:
```python
import functools
import math

import jax
import jax.numpy as jnp
from jax import lax
from jax.experimental import pallas as pl
from jax.experimental.pallas import tpu as pltpu
from jax.sharding import Mesh, PartitionSpec as P

F32 = jnp.float32
BF16 = jnp.bfloat16
BLK = 128
DIM = 128
NZ = 8
NY = 8
LOG2E = math.log2(math.e)
FACTOR = 1.0 / math.sqrt(DIM)
VMEM_LIMIT = 48 * 1024 * 1024
YX = ("pb", "kx")
NT = (((1,), (1,)), ((), ()))


def dot(a, b):
    return jnp.dot(a, b, preferred_element_type=F32)


def dot_nt(a, b):
    return lax.dot_general(a, b, NT, preferred_element_type=F32)


def low_block(fold_ref, device):
    first = fold_ref[2 * device]
    second = fold_ref[2 * device + 1]
    return jnp.minimum(first, second), second < first


def prep_kernel(fold_ref, where_ref, q_ref, k_ref, v_ref, o_ref, g_ref, lse_ref, zout_ref, kout_ref):
    _, swapped = low_block(fold_ref, where_ref[0])
    low = pl.multiple_of(jnp.where(swapped, BLK, 0), BLK)
    high = pl.multiple_of(jnp.where(swapped, 0, BLK), BLK)
    rows = []
    for start in (low, high):
        prod = g_ref[pl.ds(start, BLK), :].astype(F32) * o_ref[pl.ds(start, BLK), :].astype(F32)
        delta = jnp.sum(prod.T, axis=0, keepdims=True)
        lse = jnp.broadcast_to(lse_ref[pl.ds(start, BLK), :].astype(F32), (BLK, DIM)).T[0:1, :]
        rows.append((lse, delta))
    stats = jnp.concatenate(
        [rows[0][0], rows[1][0], rows[0][1], rows[1][1], jnp.zeros((12, DIM), F32)], axis=0
    ).astype(BF16)
    for c in range(NZ):
        for at, ref in ((0, q_ref), (2 * BLK, g_ref)):
            zout_ref[c, at : at + BLK, :] = ref[pl.ds(low, BLK), :]
            zout_ref[c, at + BLK : at + 2 * BLK, :] = ref[pl.ds(high, BLK), :]
        zout_ref[c, 4 * BLK :, :] = stats
    for c in range(NY):
        for at, ref in ((0, k_ref), (2 * BLK, v_ref)):
            kout_ref[c, at : at + BLK, :] = ref[pl.ds(low, BLK), :]
            kout_ref[c, at + BLK : at + 2 * BLK, :] = ref[pl.ds(high, BLK), :]


def tile(k, v, kt, q, g, lse, delta, limit=None):
    s = dot_nt(k, q)
    p = jnp.exp2(s * (FACTOR * LOG2E) - lse)
    if limit is not None:
        shape = p.shape
        ahead = lax.broadcasted_iota(jnp.int32, shape, 0) - lax.broadcasted_iota(jnp.int32, shape, 1)
        p = jnp.where(ahead <= limit, p, 0.0)
    dp = dot_nt(v, g)
    ds = (p * (dp - delta)).astype(BF16)
    return dot(p.astype(BF16), g), dot(ds, q), dot(kt, ds)


def grad_kernel(
    fold_ref, where_ref, z_ref, y_ref, dq_ref, dkv_ref, dv_acc, dk_acc, dqt_acc, kt_ref, lse_ref, delta_ref
):
    me_z, me_y = where_ref[1], where_ref[2]
    dv_acc[...] = jnp.zeros_like(dv_acc)
    dk_acc[...] = jnp.zeros_like(dk_acc)
    dqt_acc[...] = jnp.zeros_like(dqt_acc)
    for j in range(NY):
        kt = y_ref[j, : 2 * BLK, :].T
        kt_ref[2 * j] = kt[:, :BLK]
        kt_ref[2 * j + 1] = kt[:, BLK:]
    for i in range(NZ):
        stats = z_ref[i, 4 * BLK :, :].astype(F32)
        for b in range(2):
            lse_ref[2 * i + b] = jnp.broadcast_to(stats[b : b + 1, :] * LOG2E, (8, DIM))
            delta_ref[2 * i + b] = jnp.broadcast_to(stats[2 + b : 3 + b, :], (8, DIM))

    def dense(ip, _):
        def two(at):
            return jnp.concatenate([z_ref[2 * ip, at : at + BLK, :], z_ref[2 * ip + 1, at : at + BLK, :]], 0)

        def row(ref):
            return jnp.concatenate([ref[4 * ip + 1, 0:1, :], ref[4 * ip + 3, 0:1, :]], 1)

        q, g = two(BLK), two(3 * BLK)
        lse, delta = row(lse_ref), row(delta_ref)
        total = jnp.zeros((DIM, 2 * BLK), F32)
        for jp in range(NY // 2):
            a, b = 2 * jp, 2 * jp + 1
            k = jnp.concatenate([y_ref[a, :BLK, :], y_ref[b, :BLK, :]], 0)
            v = jnp.concatenate([y_ref[a, 2 * BLK : 3 * BLK, :], y_ref[b, 2 * BLK : 3 * BLK, :]], 0)
            kt = jnp.concatenate([kt_ref[2 * a], kt_ref[2 * b]], 1)
            dv, dk, dqt = tile(k, v, kt, q, g, lse, delta)
            dv_acc[2 * a] += dv[:BLK]
            dv_acc[2 * b] += dv[BLK:]
            dk_acc[2 * a] += dk[:BLK]
            dk_acc[2 * b] += dk[BLK:]
            total += dqt
        dqt_acc[4 * ip + 1] += total[:, :BLK]
        dqt_acc[4 * ip + 3] += total[:, BLK:]
        return 0

    lax.fori_loop(0, NZ // 2, dense, 0)

    def one(i, j, half, limit):
        at = pl.multiple_of(half * BLK, BLK)
        dv, dk, dqt = tile(
            y_ref[j, pl.ds(at, BLK), :],
            y_ref[j, pl.ds(2 * BLK + at, BLK), :],
            kt_ref[2 * j + half],
            z_ref[i, pl.ds(at, BLK), :],
            z_ref[i, pl.ds(2 * BLK + at, BLK), :],
            lse_ref[2 * i + half, 0:1, :],
            delta_ref[2 * i + half, 0:1, :],
            limit,
        )
        dv_acc[2 * j + half] += dv
        dk_acc[2 * j + half] += dk
        dqt_acc[2 * i + half] += dqt

    def sparse(i, _):
        device_i = where_ref[3] + 2 * i
        low_i, _ = low_block(fold_ref, device_i)
        for j in range(NY):
            low_j, _ = low_block(fold_ref, where_ref[4] + (j // 2) * 16 + j % 2)
            half = jnp.where(low_j < low_i, 0, 1)
            own = jnp.logical_and(i == me_z, j == me_y)
            one(i, j, half, jnp.where(own, 0, BLK))
        return 0

    lax.fori_loop(0, NZ, sparse, 0)
    one(me_z, me_y, 0, 0)

    for b in range(2 * NZ):
        dq_ref[b // 2, (b % 2) * BLK : (b % 2 + 1) * BLK, :] = dqt_acc[b].T.astype(BF16)
    for b in range(2 * NY):
        at = (b % 2) * BLK
        dkv_ref[b // 2, at : at + BLK, :] = dk_acc[b].astype(BF16)
        dkv_ref[b // 2, 2 * BLK + at : 3 * BLK + at, :] = dv_acc[b].astype(BF16)


def sum_kernel(fold_ref, where_ref, dq_ref, dkv_ref, q_ref, k_ref, v_ref):
    _, swapped = low_block(fold_ref, where_ref[0])
    for part in range(2):
        to = pl.multiple_of(jnp.where(swapped, (1 - part) * BLK, part * BLK), BLK)
        at = part * BLK

        def total(ref, start):
            out = ref[0, start : start + BLK, :].astype(F32)
            for c in range(1, ref.shape[0]):
                out += ref[c, start : start + BLK, :].astype(F32)
            return out

        q_ref[pl.ds(to, BLK), :] = (total(dq_ref, at) * FACTOR).astype(BF16)
        k_ref[pl.ds(to, BLK), :] = (total(dkv_ref, at) * FACTOR).astype(BF16)
        v_ref[pl.ds(to, BLK), :] = total(dkv_ref, 2 * BLK + at).astype(BF16)


def body(queries, key_rows, value_rows, outputs, out_grad, saved_lse, fold_map):
    pb, kz, kx = lax.axis_index("pb"), lax.axis_index("kz"), lax.axis_index("kx")
    where = jnp.stack([pb * 16 + kz * 2 + kx, kz, pb * 2 + kx, pb * 16 + kx, kz * 2]).astype(jnp.int32)
    smem = pl.BlockSpec(memory_space=pltpu.SMEM)
    vmem = pl.BlockSpec(memory_space=pltpu.VMEM)
    params = pltpu.CompilerParams(vmem_limit_bytes=VMEM_LIMIT)
    z_rows = 4 * BLK + 16

    def call(kernel, shapes, count, scratch=()):
        return pl.pallas_call(
            kernel,
            out_shape=[jax.ShapeDtypeStruct(s, BF16) for s in shapes],
            in_specs=[smem, smem] + [vmem] * count,
            out_specs=[vmem] * len(shapes),
            scratch_shapes=list(scratch),
            compiler_params=params,
        )

    zout, kout = call(prep_kernel, [(NZ, z_rows, DIM), (NY, 4 * BLK, DIM)], 6)(
        fold_map, where, queries, key_rows, value_rows, outputs, out_grad, saved_lse
    )
    y_all = lax.all_to_all(kout, YX, 0, 0)
    z_all = lax.all_to_all(zout, "kz", 0, 0)
    acc = lambda n: pltpu.VMEM((2 * n, BLK, DIM), F32)
    dq, dkv = call(
        grad_kernel,
        [(NZ, 2 * BLK, DIM), (NY, 4 * BLK, DIM)],
        2,
        [
            acc(NY),
            acc(NY),
            acc(NZ),
            pltpu.VMEM((2 * NY, DIM, BLK), BF16),
            pltpu.VMEM((2 * NZ, 8, DIM), F32),
            pltpu.VMEM((2 * NZ, 8, DIM), F32),
        ],
    )(fold_map, where, z_all, y_all)
    dkv = lax.all_to_all(dkv, YX, 0, 0)
    dq = lax.all_to_all(dq, "kz", 0, 0)
    return tuple(call(sum_kernel, [(2 * BLK, DIM)] * 3, 2)(fold_map, where, dq, dkv))


def solution(mesh):
    fine = Mesh(mesh.devices.reshape(4, 8, 2, 2, 2), ("pb", "kz", "kx", "hx", "hc"))
    rows = P(("pb", "kz", "kx"), ("hx", "hc"))
    return jax.shard_map(
        body,
        mesh=fine,
        in_specs=(rows,) * 6 + (P(),),
        out_specs=(rows,) * 3,
        check_vma=False,
    )
```

time: 447 us -> 117 us (0.26)
  waiting for transfers between devices: 249 us -> 0 us
  matrix products: 48.2 us -> 0 us
  local copies, waits for them, and re-layouts: 35.9 us -> 5.75 us
  Pallas kernels: 0 us -> 21 us
  between operations: 13.9 us -> 0.67 us
  other arithmetic: 12.5 us -> 0 us
  blocking collectives: 84.5 us -> 89.2 us
    all_gather x3 -> x0, waiting for transfers between devices: 145 us -> none  [the longest x1 71.2 us: body(): saved_src = lax.all_gather(outputs, 'ka', axis=0, tiled=True)]
    all_to_all x0 -> x4, blocking collectives: none -> 89.2 us  [the longest x1 36.5 us: body(): z_all = lax.all_to_all(zout, 'kz', 0, 0)]
    reduce_scatter x1 -> x0, waiting for transfers between devices: 75.8 us -> none  [body(): lax.psum_scatter(dq_all.reshape(query_len, full_width), 'ka', scatter_dim...]
    all_gather x3 -> x0, blocking collectives: 61.9 us -> none  [the longest x1 36 us: body(): lse_src = lax.all_gather(saved_lse, 'ka', axis=0, tiled=True)]
    dot_general x40 -> x0, matrix products: 48.2 us -> none  [the longest x8 13 us: tile_grads(): jnp.einsum('qhd,khd->hqk', query_blk, key_blk, preferred_element_type=jnp...]
    gather x9 -> x0, local copies, waits for them, and re-layouts: 33.4 us -> none  [the longest x8 26.8 us: one_block(): fold_map[row_global // fold_rows] * fold_rows + row_global % fold_rows]
    psum x1 -> x0, waiting for transfers between devices: 25.4 us -> none  [body(): key_total, value_total = lax.psum((key_flat, value_flat), 'pb')]
    psum x1 -> x0, blocking collectives: 22.6 us -> none  [body(): key_total, value_total = lax.psum((key_flat, value_flat), 'pb')]
  transfers between devices with their start and end apart: 5 -> 0, of which waited for: 5 -> 0; matrix products, arithmetic and copies ran while one was open for 2% -> 0% of each run, Pallas kernels for 0% -> 0%
where the time goes in v1:
time: 117 us
  blocking collectives  89.2 us (76%)
  Pallas kernels  21 us (18%)
  local copies, waits for them, and re-layouts  5.75 us (5%)
    all_to_all x1, blocking collectives, body(): z_all = lax.all_to_all(zout, 'kz', 0, 0)  36.5 us
    all_to_all x1, blocking collectives, body(): y_all = lax.all_to_all(kout, YX, 0, 0)  20.7 us
    pallas_call x1, Pallas kernels, body(): call(grad_kernel, [(NZ, 2 * BLK, DIM), (NY, 4 * BLK, DIM)], 2, [acc(NY),...  18.6 us
    all_to_all x1, blocking collectives, body(): dq = lax.all_to_all(dq, 'kz', 0, 0)  17.8 us
    all_to_all x1, blocking collectives, body(): dkv = lax.all_to_all(dkv, YX, 0, 0)  14.2 us
    unnamed x13, local copies, waits for them, and re-layouts  5.67 us

profile of v1, /device:TPU:4, one launch (start us, length us, event | category | flops | bytes accessed | tf_op | source)
XLA Modules:
  0.0 116.6 jit_solution(5573521004873076832)
XLA Ops:
  0.6 0.8 copy.10.lse_ref
  1.5 0.1 stack.23.where_ref
  1.6 0.0 copy-start
  1.6 0.8 copy-done
  2.4 0.0 copy-start.1
  2.4 0.8 copy-done.1
  3.2 0.0 copy-start.2
  3.2 0.8 copy-done.2
  4.1 0.0 copy-start.3
  4.1 0.8 copy-done.3
  4.9 0.0 copy-start.4
  4.9 0.8 copy-done.4
  5.8 0.0 copy-start.5
  5.8 0.7 copy-done.5
  6.4 1.0 shard_map.94
  7.4 20.7 %all_to_all.20.y_ref = bf16[8,512,128]{2,1,0:T(8,128)(2,1)S(1)} all-to-all(bf16[8,512,128]{2,1,0:T(8,128)(2,1)S(1)} %get-tuple-element.8), channel_id=1, replica_groups=mesh['pb'=4,'kz'=8,'kx'=2,'hx'=2,'hc'=2] {'pb','kx'}, dimensions={0} | all-to-all | bytes 2097152 | tf_op jit(solution)/shard_map/all_to_all | solution.py:193
  28.1 36.5 %all_to_all.21.z_ref = bf16[8,528,128]{2,1,0:T(8,128)(2,1)S(1)} all-to-all(bf16[8,528,128]{2,1,0:T(8,128)(2,1)S(1)} %get-tuple-element.7), channel_id=1, replica_groups=mesh['pb'=4,'kz'=8,'kx'=2,'hx'=2,'hc'=2] {'kz'}, dimensions={0} | all-to-all | bytes 2162688 | tf_op jit(solution)/shard_map/all_to_all | solution.py:194
  64.6 18.6 %shard_map.95 = (bf16[8,256,128]{2,1,0:T(8,128)(2,1)S(1)}, bf16[8,512,128]{2,1,0:T(8,128)(2,1)S(1)}) custom-call(s32[128]{0:T(128)S(1)} %copy-done.5, s32[5]{0:T(128)S(1)} %stack.23.where_ref, bf16[8,528,128]{2,1,0:T(8,128)(2,1)S(1)} %all_to_all.21.z_ref, bf16[8,512,128]{2,1,0:T(8,128)(2,1)S(1)} %all_to_all.20.y_ref), custom_call_target="tpu_custom_call" | custom-call | tf_op jit(solution)/shard_map/pallas_call | solution.py:196
  83.2 17.8 %all_to_all.22.dq_ref = bf16[8,256,128]{2,1,0:T(8,128)(2,1)S(1)} all-to-all(bf16[8,256,128]{2,1,0:T(8,128)(2,1)S(1)} %get-tuple-element.9), channel_id=1, replica_groups=mesh['pb'=4,'kz'=8,'kx'=2,'hx'=2,'hc'=2] {'kz'}, dimensions={0} | all-to-all | bytes 1048576 | tf_op jit(solution)/shard_map/all_to_all | solution.py:210
  101.0 14.2 %all_to_all.23.dkv_ref = bf16[8,512,128]{2,1,0:T(8,128)(2,1)S(1)} all-to-all(bf16[8,512,128]{2,1,0:T(8,128)(2,1)S(1)} %get-tuple-element.10), channel_id=1, replica_groups=mesh['pb'=4,'kz'=8,'kx'=2,'hx'=2,'hc'=2] {'pb','kx'}, dimensions={0} | all-to-all | bytes 2097152 | tf_op jit(solution)/shard_map/all_to_all | solution.py:209
  115.2 1.4 %shard_map.96 = (bf16[256,128]{1,0:T(8,128)(2,1)}, bf16[256,128]{1,0:T(8,128)(2,1)}, bf16[256,128]{1,0:T(8,128)(2,1)}) custom-call(s32[128]{0:T(128)S(1)} %copy-done.5, s32[5]{0:T(128)S(1)} %stack.23.where_ref, bf16[8,256,128]{2,1,0:T(8,128)(2,1)S(1)} %all_to_all.22.dq_ref, bf16[8,512,128]{2,1,0:T(8,128)(2,1)S(1)} %all_to_all.23.dkv_ref), custom_call_target="tpu_custom_call" | custom-call | tf_op jit(solution)/shard_map/pallas_call | solution.py:211
Async XLA Ops:
  1.6 0.8 copy-start
  2.4 0.8 copy-start.1
  3.2 0.8 copy-start.2
  4.1 0.8 copy-start.3
  4.9 0.8 copy-start.4
  5.8 0.7 copy-start.5

commit v2 on v1

v2 whole, which is shorter than its diff:
```python
import functools
import math

import jax
import jax.numpy as jnp
from jax import lax
from jax.experimental import pallas as pl
from jax.experimental.pallas import tpu as pltpu
from jax.sharding import Mesh, PartitionSpec as P

F32 = jnp.float32
BF16 = jnp.bfloat16
BLK = 128
DIM = 128
LOG2E = math.log2(math.e)
FACTOR = 1.0 / math.sqrt(DIM)
VMEM_LIMIT = 48 * 1024 * 1024
NT = (((1,), (1,)), ((), ()))
Q_ROWS = 4 * BLK + 16
K_ROWS = 4 * BLK


def dot(a, b):
    return jnp.dot(a, b, preferred_element_type=F32)


def dot_nt(a, b):
    return lax.dot_general(a, b, NT, preferred_element_type=F32)


def ring(value, size):
    return lax.rem(value + size, size)


def low_block(fold_ref, device):
    first = fold_ref[2 * device]
    second = fold_ref[2 * device + 1]
    return jnp.minimum(first, second), second < first


def device_row(y, z, x):
    return y * 16 + z * 2 + x


def prep_kernel(fold_ref, where_ref, q_ref, k_ref, v_ref, o_ref, g_ref, lse_ref, zout_ref, kout_ref):
    _, swapped = low_block(fold_ref, device_row(where_ref[0], where_ref[1], where_ref[2]))
    low = pl.multiple_of(jnp.where(swapped, BLK, 0), BLK)
    high = pl.multiple_of(jnp.where(swapped, 0, BLK), BLK)
    rows = []
    for start in (low, high):
        prod = g_ref[pl.ds(start, BLK), :].astype(F32) * o_ref[pl.ds(start, BLK), :].astype(F32)
        delta = jnp.sum(prod.T, axis=0, keepdims=True)
        lse = jnp.broadcast_to(lse_ref[pl.ds(start, BLK), :].astype(F32), (BLK, DIM)).T[0:1, :]
        rows.append((lse, delta))
    stats = jnp.concatenate(
        [rows[0][0], rows[1][0], rows[0][1], rows[1][1], jnp.zeros((12, DIM), F32)], axis=0
    ).astype(BF16)
    for out_ref, at, ref in (
        (zout_ref, 0, q_ref),
        (zout_ref, 2 * BLK, g_ref),
        (kout_ref, 0, k_ref),
        (kout_ref, 2 * BLK, v_ref),
    ):
        out_ref[at : at + BLK, :] = ref[pl.ds(low, BLK), :]
        out_ref[at + BLK : at + 2 * BLK, :] = ref[pl.ds(high, BLK), :]
    zout_ref[4 * BLK :, :] = stats


def tile(k, v, kt, q, g, lse, delta, visible=None):
    s = dot_nt(k, q)
    p = jnp.exp2(s * (FACTOR * LOG2E) - lse)
    if visible is not None:
        p = jnp.where(visible, p, 0.0)
    dp = dot_nt(v, g)
    ds = (p * (dp - delta)).astype(BF16)
    return dot(p.astype(BF16), g), dot(ds, q), dot(kt, ds)


def grad_kernel(turn, fold_ref, where_ref, *refs):
    q_refs, y_ref = refs[:4], refs[4]
    refs = refs[5:]
    if turn > 0:
        dqin_ref, refs = refs[0], refs[1:]
    if turn < 3:
        dqt_acc, dkv_ref, dv_acc, dk_acc, kt_ref, lse_ref, delta_ref = refs
    else:
        dq_refs, (dkv_ref, dv_acc, dk_acc, kt_ref, lse_ref, delta_ref, dqt_acc) = refs[:4], refs[4:]
    y, z, x = where_ref[0], where_ref[1], where_ref[2]
    dv_acc[...] = jnp.zeros_like(dv_acc)
    dk_acc[...] = jnp.zeros_like(dk_acc)
    dqt_acc[...] = dqin_ref[...] if turn > 0 else jnp.zeros_like(dqt_acc)
    for j in range(2):
        kt = y_ref[j, : 2 * BLK, :].T
        kt_ref[2 * j] = kt[:, :BLK]
        kt_ref[2 * j + 1] = kt[:, BLK:]
    for i in range(8):
        stats = q_refs[i // 2][i % 2, 4 * BLK :, :].astype(F32)
        for b in range(2):
            lse_ref[2 * i + b] = jnp.broadcast_to(stats[b : b + 1, :] * LOG2E, (8, DIM))
            delta_ref[2 * i + b] = jnp.broadcast_to(stats[2 + b : 3 + b, :], (8, DIM))

    k = jnp.concatenate([y_ref[0, :BLK, :], y_ref[1, :BLK, :]], 0)
    v = jnp.concatenate([y_ref[0, 2 * BLK : 3 * BLK, :], y_ref[1, 2 * BLK : 3 * BLK, :]], 0)
    kt = jnp.concatenate([kt_ref[0], kt_ref[2]], 1)
    for s in range(4):
        ref = q_refs[s]
        q = jnp.concatenate([ref[0, BLK : 2 * BLK, :], ref[1, BLK : 2 * BLK, :]], 0)
        g = jnp.concatenate([ref[0, 3 * BLK : 4 * BLK, :], ref[1, 3 * BLK : 4 * BLK, :]], 0)
        lse = jnp.concatenate([lse_ref[4 * s + 1, 0:1, :], lse_ref[4 * s + 3, 0:1, :]], 1)
        delta = jnp.concatenate([delta_ref[4 * s + 1, 0:1, :], delta_ref[4 * s + 3, 0:1, :]], 1)
        dv, dk, dqt = tile(k, v, kt, q, g, lse, delta)
        dv_acc[0] += dv[:BLK]
        dv_acc[2] += dv[BLK:]
        dk_acc[0] += dk[:BLK]
        dk_acc[2] += dk[BLK:]
        dqt_acc[4 * s + 1] += dqt[:, :BLK]
        dqt_acc[4 * s + 3] += dqt[:, BLK:]

    def one(i, j, half, visible):
        at = half * BLK if isinstance(half, int) else pl.multiple_of(half * BLK, BLK)
        ref = q_refs[i // 2]
        dv, dk, dqt = tile(
            y_ref[j, pl.ds(at, BLK), :],
            y_ref[j, pl.ds(2 * BLK + at, BLK), :],
            kt_ref[2 * j + half],
            ref[i % 2, pl.ds(at, BLK), :],
            ref[i % 2, pl.ds(2 * BLK + at, BLK), :],
            lse_ref[2 * i + half, 0:1, :],
            delta_ref[2 * i + half, 0:1, :],
            visible,
        )
        dv_acc[2 * j + half] += dv
        dk_acc[2 * j + half] += dk
        dqt_acc[2 * i + half] += dqt

    y_at = ring(y + (0, 3, 1, 2)[turn], 4)
    z_at = (z, ring(z + 7, 8), ring(z + 1, 8), ring(z + jnp.where(lax.rem(z, 2) == 0, 2, 6), 8))
    for i in range(8):
        low_i, _ = low_block(fold_ref, device_row(y, z_at[i // 2], x if i % 2 == 0 else 1 - x))
        for j in range(2):
            if turn == 0 and i == 0 and j == 0:
                shape = (BLK, BLK)
                diagonal = lax.broadcasted_iota(jnp.int32, shape, 0) <= lax.broadcasted_iota(jnp.int32, shape, 1)
                one(i, j, 0, diagonal)
                one(i, j, 1, diagonal)
            else:
                low_j, _ = low_block(fold_ref, device_row(y_at, ring(z + 4 * j, 8), x))
                one(i, j, jnp.where(low_j < low_i, 0, 1), None)

    for b in range(4):
        at = (b % 2) * BLK
        dkv_ref[b // 2, at : at + BLK, :] = dk_acc[b].astype(dkv_ref.dtype)
        dkv_ref[b // 2, 2 * BLK + at : 3 * BLK + at, :] = dv_acc[b].astype(dkv_ref.dtype)
    if turn == 3:
        for b in range(16):
            ref = dq_refs[b // 4]
            at = (b % 2) * BLK
            ref[(b // 2) % 2, at : at + BLK, :] = dqt_acc[b].T.astype(ref.dtype)


def meet_kernel(own_ref, a_ref, b_ref, c_ref, keep_ref, send_ref):
    for part, out_ref in ((0, keep_ref), (1, send_ref)):
        total = own_ref[part].astype(F32)
        for ref in (a_ref, b_ref, c_ref):
            total += ref[part].astype(F32)
        out_ref[...] = total.astype(out_ref.dtype)


def last_kernel(fold_ref, where_ref, dq_ref, dqx_ref, dkv_ref, dkvz_ref, q_ref, k_ref, v_ref):
    _, swapped = low_block(fold_ref, device_row(where_ref[0], where_ref[1], where_ref[2]))
    for part in range(2):
        to = pl.multiple_of(jnp.where(swapped, (1 - part) * BLK, part * BLK), BLK)
        at = part * BLK

        def total(ref, other, start):
            return ref[start : start + BLK, :] + other[start : start + BLK, :].astype(F32)

        q_ref[pl.ds(to, BLK), :] = (total(dq_ref, dqx_ref, at) * FACTOR).astype(BF16)
        k_ref[pl.ds(to, BLK), :] = (total(dkv_ref, dkvz_ref, at) * FACTOR).astype(BF16)
        v_ref[pl.ds(to, BLK), :] = total(dkv_ref, dkvz_ref, 2 * BLK + at).astype(BF16)


def z_step(step):
    return [(i, (i + step) % 8) for i in range(8)]


def y_step(step):
    return [(i, (i + step) % 4) for i in range(4)]


Z_PAIRS = [(i, (i - 2) % 8 if i % 2 == 0 else (i + 2) % 8) for i in range(8)]
Z_BACK = [(b, a) for a, b in Z_PAIRS]
X_SWAP = [(0, 1), (1, 0)]


def call(kernel, outs, operands, scalars=(), scratch=(), **options):
    smem = pl.BlockSpec(memory_space=pltpu.SMEM)
    vmem = pl.BlockSpec(memory_space=pltpu.VMEM)
    return pl.pallas_call(
        kernel,
        out_shape=[jax.ShapeDtypeStruct(s, t) for s, t in outs],
        in_specs=[smem] * len(scalars) + [vmem] * len(operands),
        out_specs=[vmem] * len(outs),
        scratch_shapes=list(scratch),
        compiler_params=pltpu.CompilerParams(vmem_limit_bytes=VMEM_LIMIT),
        **options,
    )(*scalars, *operands)


def body(queries, key_rows, value_rows, outputs, out_grad, saved_lse, fold_map):
    where = jnp.stack([lax.axis_index("pb"), lax.axis_index("kz"), lax.axis_index("kx")]).astype(jnp.int32)
    scalars = (fold_map, where)
    mine_q, mine_k = call(
        prep_kernel,
        [((Q_ROWS, DIM), BF16), ((K_ROWS, DIM), BF16)],
        (queries, key_rows, value_rows, outputs, out_grad, saved_lse),
        scalars,
    )
    q0 = jnp.stack([mine_q, lax.ppermute(mine_q, "kx", X_SWAP)])
    k0 = jnp.stack([mine_k, lax.ppermute(mine_k, "kz", z_step(4))])
    q_sets = [q0] + [lax.ppermute(q0, "kz", p) for p in (z_step(1), z_step(-1), Z_PAIRS)]
    k_sets = [k0] + [lax.ppermute(k0, "pb", y_step(s)) for s in (1, -1, 2)]

    acc = pltpu.VMEM((4, BLK, DIM), F32)
    row = pltpu.VMEM((16, 8, DIM), F32)
    scratch = [acc, acc, pltpu.VMEM((4, DIM, BLK), BF16), row, row]
    dq_acc = ((16, DIM, BLK), F32)
    cost = pl.CostEstimate(flops=16 * 2 * 5 * 4 * BLK**3 // 2, bytes_accessed=1 << 20, transcendentals=0)
    dkv = []
    dq = None
    for turn in range(4):
        operands = q_sets + [k_sets[turn]] + ([dq] if turn else [])
        dkv_out = ((2, K_ROWS, DIM), F32 if turn == 0 else BF16)
        if turn < 3:
            dq, part = call(
                functools.partial(grad_kernel, turn),
                [dq_acc, dkv_out],
                operands,
                scalars,
                scratch,
                input_output_aliases={7: 0} if turn else {},
                cost_estimate=cost,
            )
        else:
            *dqs, part = call(
                functools.partial(grad_kernel, turn),
                [((2, 2 * BLK, DIM), F32 if s == 0 else BF16) for s in range(4)] + [dkv_out],
                operands,
                scalars,
                scratch + [pltpu.VMEM(*dq_acc)],
                cost_estimate=cost,
            )
        dkv.append(part)

    dkv_back = [lax.ppermute(dkv[t], "pb", y_step(s)) for t, s in ((1, -1), (2, 1), (3, 2))]
    dq_back = [lax.ppermute(dqs[t], "kz", p) for t, p in ((1, z_step(-1)), (2, z_step(1)), (3, Z_BACK))]

    def meet(own, back):
        shape = own.shape[1:]
        return call(meet_kernel, [(shape, F32), (shape, BF16)], [own] + back)

    dkv_keep, dkv_send = meet(dkv[0], dkv_back)
    dkv_last = lax.ppermute(dkv_send, "kz", z_step(4))
    dq_keep, dq_send = meet(dqs[0], dq_back)
    dq_last = lax.ppermute(dq_send, "kx", X_SWAP)
    grads = [((2 * BLK, DIM), BF16)] * 3
    return tuple(call(last_kernel, grads, (dq_keep, dq_last, dkv_keep, dkv_last), scalars))


def solution(mesh):
    fine = Mesh(mesh.devices.reshape(4, 8, 2, 2, 2), ("pb", "kz", "kx", "hx", "hc"))
    rows = P(("pb", "kz", "kx"), ("hx", "hc"))
    return jax.shard_map(
        body,
        mesh=fine,
        in_specs=(rows,) * 6 + (P(),),
        out_specs=(rows,) * 3,
        check_vma=False,
    )
```

time: 117 us -> 81.2 us (0.69)
  blocking collectives: 89.2 us -> 0 us
  starting transfers between devices: 0 us -> 36.6 us
  waiting for transfers between devices: 0 us -> 16.6 us
    all_to_all x4 -> x0, blocking collectives: 89.2 us -> none  [the longest x1 36.5 us: body(): z_all = lax.all_to_all(zout, 'kz', 0, 0)]
    ppermute x0 -> x16, starting transfers between devices: none -> 36.6 us  [the longest x1 7.19 us: body(): k0 = jnp.stack([mine_k, lax.ppermute(mine_k, 'kz', z_step(4))])]
    ppermute x0 -> x16, waiting for transfers between devices: none -> 16.6 us  [the longest x3 6.43 us: body(): lax.ppermute(q0, 'kz', p)]
    pallas_call x3 -> x8, Pallas kernels: 21 us -> 21.2 us  [call(): pl.pallas_call(kernel, out_shape=[jax.ShapeDtypeStruct(s, t) for s, t in...]
  transfers between devices with their start and end apart: 0 -> 16, of which waited for: 0 -> 7; matrix products, arithmetic and copies ran while one was open for 0% -> 0% of each run, Pallas kernels for 0% -> 18%
where the time goes in v2:
time: 81.2 us; the launch traced here: 80 us
  starting transfers between devices  36.6 us (45%)
  Pallas kernels  21.2 us (26%)
  waiting for transfers between devices  16.6 us (20%)
  local copies, waits for them, and re-layouts  4.78 us (6%)
    pallas_call x8, Pallas kernels, call(): pl.pallas_call(kernel, out_shape=[jax.ShapeDtypeStruct(s, t) for s, t in...  21.2 us
    ppermute x1, starting transfers between devices, body(): k0 = jnp.stack([mine_k, lax.ppermute(mine_k, 'kz', z_step(4))])  7.19 us
    ppermute x3, starting transfers between devices, body(): lax.ppermute(dkv[t], 'pb', y_step(s))  6.52 us
    ppermute x3, starting transfers between devices, body(): k_sets = [k0] + [lax.ppermute(k0, 'pb', y_step(s)) for s in (1, -1, 2)]  6.51 us
    ppermute x3, waiting for transfers between devices, body(): lax.ppermute(q0, 'kz', p)  6.43 us
    ppermute x3, starting transfers between devices, body(): lax.ppermute(q0, 'kz', p)  5.34 us
    ppermute x1, starting transfers between devices, body(): dkv_last = lax.ppermute(dkv_send, 'kz', z_step(4))  4.89 us
    unnamed x13, local copies, waits for them, and re-layouts  4.78 us
  transfers between devices with their start and end apart: 16, of which 7 were waited for; matrix products, arithmetic and copies ran while one was open for 0% of the time, Pallas kernels for 18%

profile of v2, /device:TPU:4, one launch (start us, length us, event | category | flops | bytes accessed | tf_op | source)
XLA Modules:
  0.0 80.0 jit_solution(4056088622427582498)
XLA Ops:
  6.3 1.2 %collective-permute-start = (bf16[528,128]{1,0:T(8,128)(2,1)S(1)}, bf16[528,128]{1,0:T(8,128)(2,1)S(1)}, u32[]{:S(2)}, u32[]{:S(2)}) collective-permute-start(bf16[528,128]{1,0:T(8,128)(2,1)S(1)} %get-tuple-element.20), channel_id=1, source_target_pairs={{0,4},{4,0},{1,5},{5,1},{2,6},{6,2},{3,7},{7,3},{8,12},{12,8},{9,1... | collective-permute-start | bytes 405512 | tf_op jit(solution)/shard_map/ppermute | solution.py:219
  7.5 7.2 %collective-permute-start.4 = (bf16[512,128]{1,0:T(8,128)(2,1)S(1)}, bf16[512,128]{1,0:T(8,128)(2,1)S(1)}, u32[]{:S(2)}, u32[]{:S(2)}) collective-permute-start(bf16[512,128]{1,0:T(8,128)(2,1)S(1)} %get-tuple-element.21), channel_id=1, source_target_pairs={{0,32},{8,40},{16,48},{24,56},{32,0},{40,8},{48,16},{56,24},{1,33}... | collective-permute-start | bytes 393224 | tf_op jit(solution)/shard_map/ppermute | solution.py:220
  14.8 3.3 %collective-permute-start.3 = (bf16[2,528,128]{2,1,0:T(8,128)(2,1)S(1)}, bf16[2,528,128]{2,1,0:T(8,128)(2,1)S(1)}, u32[]{:S(2)}, u32[]{:S(2)}) collective-permute-start(bf16[2,528,128]{2,1,0:T(8,128)(2,1)S(1)} %pad_maximum_fusion.refs_0_), channel_id=1, source_target_pairs={{0,48},{8,24},{16,0},{24,40},{32,16},{40,56},{48,32},{56,8},{1,49}... | collective-permute-start | bytes 811016 | tf_op jit(solution)/shard_map/ppermute | solution.py:221
  18.5 1.6 %collective-permute-start.1 = (bf16[2,528,128]{2,1,0:T(8,128)(2,1)S(1)}, bf16[2,528,128]{2,1,0:T(8,128)(2,1)S(1)}, u32[]{:S(2)}, u32[]{:S(2)}) collective-permute-start(bf16[2,528,128]{2,1,0:T(8,128)(2,1)S(1)} %pad_maximum_fusion.refs_0_), channel_id=1, source_target_pairs={{0,8},{8,16},{16,24},{24,32},{32,40},{40,48},{48,56},{56,0},{1,9},... | collective-permute-start | bytes 811016 | tf_op jit(solution)/shard_map/ppermute | solution.py:221
  20.1 1.7 %collective-permute-start.7 = (bf16[2,512,128]{2,1,0:T(8,128)(2,1)S(1)}, bf16[2,512,128]{2,1,0:T(8,128)(2,1)S(1)}, u32[]{:S(2)}, u32[]{:S(2)}) collective-permute-start(bf16[2,512,128]{2,1,0:T(8,128)(2,1)S(1)} %pad_maximum_fusion.1.refs_4_), channel_id=1, source_target_pairs={{0,64},{64,128},{128,192},{192,0},{1,65},{65,129},{129,193},{193,1... | collective-permute-start | bytes 786440 | tf_op jit(solution)/shard_map/ppermute | solution.py:222
  21.8 1.7 %collective-permute-start.6 = (bf16[2,512,128]{2,1,0:T(8,128)(2,1)S(1)}, bf16[2,512,128]{2,1,0:T(8,128)(2,1)S(1)}, u32[]{:S(2)}, u32[]{:S(2)}) collective-permute-start(bf16[2,512,128]{2,1,0:T(8,128)(2,1)S(1)} %pad_maximum_fusion.1.refs_4_), channel_id=1, source_target_pairs={{0,192},{64,0},{128,64},{192,128},{1,193},{65,1},{129,65},{193,129... | collective-permute-start | bytes 786440 | tf_op jit(solution)/shard_map/ppermute | solution.py:222
  23.5 3.5 %collective-permute-done.3.refs_3_ = bf16[2,528,128]{2,1,0:T(8,128)(2,1)S(1)} collective-permute-done((bf16[2,528,128]{2,1,0:T(8,128)(2,1)S(1)}, bf16[2,528,128]{2,1,0:T(8,128)(2,1)S(1)}, u32[]{:S(2)}, u32[]{:S(2)}) %collective-permute-start.3) | collective-permute-done | bytes 270368 | tf_op jit(solution)/shard_map/ppermute | solution.py:221
  26.9 3.2 %collective-permute-start.5 = (bf16[2,512,128]{2,1,0:T(8,128)(2,1)S(1)}, bf16[2,512,128]{2,1,0:T(8,128)(2,1)S(1)}, u32[]{:S(2)}, u32[]{:S(2)}) collective-permute-start(bf16[2,512,128]{2,1,0:T(8,128)(2,1)S(1)} %pad_maximum_fusion.1.refs_4_), channel_id=1, source_target_pairs={{0,128},{64,192},{128,0},{192,64},{1,129},{65,193},{129,1},{193,65... | collective-permute-start | bytes 786440 | tf_op jit(solution)/shard_map/ppermute | solution.py:222
  30.1 3.0 %collective-permute-done.2.refs_2_ = bf16[2,528,128]{2,1,0:T(8,128)(2,1)S(1)} collective-permute-done((bf16[2,528,128]{2,1,0:T(8,128)(2,1)S(1)}, bf16[2,528,128]{2,1,0:T(8,128)(2,1)S(1)}, u32[]{:S(2)}, u32[]{:S(2)}) %collective-permute-start.2) | collective-permute-done | bytes 270368 | tf_op jit(solution)/shard_map/ppermute | solution.py:221
  33.1 4.8 %shard_map.95 = (f32[16,128,128]{2,1,0:T(8,128)S(1)}, f32[2,512,128]{2,1,0:T(8,128)S(1)}) custom-call(s32[128]{0:T(128)S(1)} %copy-done.5, s32[3]{0:T(128)S(1)} %pad_add_fusion.where_ref, bf16[2,528,128]{2,1,0:T(8,128)(2,1)S(1)} %pad_maximum_fusion.refs_0_, bf16[2,528,128]{2,1,0:T(8,128)(2,1)S(1)} %collective-permute-done.1.refs_1_, ...), custom_call_target="tpu_custom_call" | custom-call | flops 671088640 | bytes 1048576 | tf_op jit(solution)/shard_map/pallas_call | solution.py:199
  37.9 4.6 %shard_map.96 = (f32[16,128,128]{2,1,0:T(8,128)S(1)}, bf16[2,512,128]{2,1,0:T(8,128)(2,1)S(1)}) custom-call(s32[128]{0:T(128)S(1)} %copy-done.5, s32[3]{0:T(128)S(1)} %pad_add_fusion.where_ref, bf16[2,528,128]{2,1,0:T(8,128)(2,1)S(1)} %pad_maximum_fusion.refs_0_, ...), custom_call_target="tpu_custom_call", output_to_operand_aliasing={{0}: (7, {})} | custom-call | flops 671088640 | bytes 1048576 | tf_op jit(solution)/shard_map/pallas_call | solution.py:199
  42.5 4.6 %shard_map.97 = (f32[16,128,128]{2,1,0:T(8,128)S(1)}, bf16[2,512,128]{2,1,0:T(8,128)(2,1)S(1)}) custom-call(s32[128]{0:T(128)S(1)} %copy-done.5, s32[3]{0:T(128)S(1)} %pad_add_fusion.where_ref, bf16[2,528,128]{2,1,0:T(8,128)(2,1)S(1)} %pad_maximum_fusion.refs_0_, ...), custom_call_target="tpu_custom_call", output_to_operand_aliasing={{0}: (7, {})} | custom-call | flops 671088640 | bytes 1048576 | tf_op jit(solution)/shard_map/pallas_call | solution.py:199
  47.2 4.9 %shard_map.98 = (f32[2,256,128]{2,1,0:T(8,128)S(1)}, bf16[2,256,128]{2,1,0:T(8,128)(2,1)S(1)}, bf16[2,256,128]{2,1,0:T(8,128)(2,1)S(1)}, bf16[2,256,128]{2,1,0:T(8,128)(2,1)S(1)}, bf16[2,512,128]{2,1,0:T(8,128)(2,1)S(1)}) custom-call(s32[128]{0:T(128)S(1)} %copy-done.5, s32[3]{0:T(128)S(1)} %pad_add_fusion.where_ref, ...), custom_call_target="tpu_custom_call" | custom-call | flops 671088640 | bytes 1048576 | tf_op jit(solution)/shard_map/pallas_call | solution.py:199
  52.1 3.3 %collective-permute-start.14 = (bf16[2,512,128]{2,1,0:T(8,128)(2,1)S(1)}, bf16[2,512,128]{2,1,0:T(8,128)(2,1)S(1)}, u32[]{:S(2)}, u32[]{:S(2)}) collective-permute-start(bf16[2,512,128]{2,1,0:T(8,128)(2,1)S(1)} %get-tuple-element.34), channel_id=1, source_target_pairs={{0,128},{64,192},{128,0},{192,64},{1,129},{65,193},{129,1},{193,65... | collective-permute-start | bytes 786440 | tf_op jit(solution)/shard_map/ppermute | solution.py:255
  56.1 2.6 %collective-permute-start.12 = (bf16[2,512,128]{2,1,0:T(8,128)(2,1)S(1)}, bf16[2,512,128]{2,1,0:T(8,128)(2,1)S(1)}, u32[]{:S(2)}, u32[]{:S(2)}) collective-permute-start(bf16[2,512,128]{2,1,0:T(8,128)(2,1)S(1)} %get-tuple-element.32), channel_id=1, source_target_pairs={{0,192},{64,0},{128,64},{192,128},{1,193},{65,1},{129,65},{193,129... | collective-permute-start | bytes 786440 | tf_op jit(solution)/shard_map/ppermute | solution.py:255
  58.6 2.7 %collective-permute-start.8 = (bf16[2,256,128]{2,1,0:T(8,128)(2,1)S(1)}, bf16[2,256,128]{2,1,0:T(8,128)(2,1)S(1)}, u32[]{:S(2)}, u32[]{:S(2)}) collective-permute-start(bf16[2,256,128]{2,1,0:T(8,128)(2,1)S(1)} %get-tuple-element.26), channel_id=1, source_target_pairs={{0,56},{8,0},{16,8},{24,16},{32,24},{40,32},{48,40},{56,48},{1,57}... | collective-permute-start | bytes 393224 | tf_op jit(solution)/shard_map/ppermute | solution.py:256
  61.3 1.6 %collective-permute-done.14.c_ref = bf16[2,512,128]{2,1,0:T(8,128)(2,1)S(1)} collective-permute-done((bf16[2,512,128]{2,1,0:T(8,128)(2,1)S(1)}, bf16[2,512,128]{2,1,0:T(8,128)(2,1)S(1)}, u32[]{:S(2)}, u32[]{:S(2)}) %collective-permute-start.14) | collective-permute-done | bytes 262176 | tf_op jit(solution)/shard_map/ppermute | solution.py:255
  62.9 1.2 %collective-permute-start.10 = (bf16[2,256,128]{2,1,0:T(8,128)(2,1)S(1)}, bf16[2,256,128]{2,1,0:T(8,128)(2,1)S(1)}, u32[]{:S(2)}, u32[]{:S(2)}) collective-permute-start(bf16[2,256,128]{2,1,0:T(8,128)(2,1)S(1)} %get-tuple-element.28), channel_id=1, source_target_pairs={{48,0},{24,8},{0,16},{40,24},{16,32},{56,40},{32,48},{8,56},{49,1}... | collective-permute-start | bytes 393224 | tf_op jit(solution)/shard_map/ppermute | solution.py:256
  64.2 2.7 %collective-permute-done.13.b_ref = bf16[2,512,128]{2,1,0:T(8,128)(2,1)S(1)} collective-permute-done((bf16[2,512,128]{2,1,0:T(8,128)(2,1)S(1)}, bf16[2,512,128]{2,1,0:T(8,128)(2,1)S(1)}, u32[]{:S(2)}, u32[]{:S(2)}) %collective-permute-start.13) | collective-permute-done | bytes 262176 | tf_op jit(solution)/shard_map/ppermute | solution.py:255
  67.3 4.9 %collective-permute-start.15 = (bf16[512,128]{1,0:T(8,128)(2,1)S(1)}, bf16[512,128]{1,0:T(8,128)(2,1)S(1)}, u32[]{:S(2)}, u32[]{:S(2)}) collective-permute-start(bf16[512,128]{1,0:T(8,128)(2,1)S(1)} %get-tuple-element.36), channel_id=1, source_target_pairs={{0,32},{8,40},{16,48},{24,56},{32,0},{40,8},{48,16},{56,24},{1,33}... | collective-permute-start | bytes 393224 | tf_op jit(solution)/shard_map/ppermute | solution.py:263
  72.3 1.0 %collective-permute-start.11 = (bf16[256,128]{1,0:T(8,128)(2,1)S(1)}, bf16[256,128]{1,0:T(8,128)(2,1)S(1)}, u32[]{:S(2)}, u32[]{:S(2)}) collective-permute-start(bf16[256,128]{1,0:T(8,128)(2,1)S(1)} %get-tuple-element.30), channel_id=1, source_target_pairs={{0,4},{4,0},{1,5},{5,1},{2,6},{6,2},{3,7},{7,3},{8,12},{12,8},{9,1... | collective-permute-start | bytes 196616 | tf_op jit(solution)/shard_map/ppermute | solution.py:265
  73.3 3.4 %collective-permute-done.11.dqx_ref = bf16[256,128]{1,0:T(8,128)(2,1)S(1)} collective-permute-done((bf16[256,128]{1,0:T(8,128)(2,1)S(1)}, bf16[256,128]{1,0:T(8,128)(2,1)S(1)}, u32[]{:S(2)}, u32[]{:S(2)}) %collective-permute-start.11) | collective-permute-done | bytes 65568 | tf_op jit(solution)/shard_map/ppermute | solution.py:265
  76.7 2.1 %collective-permute-done.15.dkvz_ref = bf16[512,128]{1,0:T(8,128)(2,1)S(1)} collective-permute-done((bf16[512,128]{1,0:T(8,128)(2,1)S(1)}, bf16[512,128]{1,0:T(8,128)(2,1)S(1)}, u32[]{:S(2)}, u32[]{:S(2)}) %collective-permute-start.15) | collective-permute-done | bytes 131104 | tf_op jit(solution)/shard_map/ppermute | solution.py:263
  78.8 1.2 %shard_map.101 = (bf16[256,128]{1,0:T(8,128)(2,1)}, bf16[256,128]{1,0:T(8,128)(2,1)}, bf16[256,128]{1,0:T(8,128)(2,1)}) custom-call(s32[128]{0:T(128)S(1)} %copy-done.5, s32[3]{0:T(128)S(1)} %pad_add_fusion.where_ref, f32[256,128]{1,0:T(8,128)S(1)} %get-tuple-element.29.dq_ref, bf16[256,128]{1,0:T(8,128)(2,1)S(1)} %collective-permute-done.11.dqx_ref, ...), custom_call_target="tpu_custom_call" | custom-call | tf_op jit(solution)/shard_map/pallas_call | solution.py:199
  (32 shorter events, 7.4 us)
Async XLA Ops:
  0.6 1.0 %copy-start = (bf16[256,128]{1,0:T(8,128)(2,1)S(1)}, bf16[256,128]{1,0:T(8,128)(2,1)}, u32[]{:S(2)}) copy-start(bf16[256,128]{1,0:T(8,128)(2,1)} %q_ref.1) | copy-start | bytes 196612
  1.5 0.7 copy-start.5
  2.2 0.8 %copy-start.1 = (bf16[256,128]{1,0:T(8,128)(2,1)S(1)}, bf16[256,128]{1,0:T(8,128)(2,1)}, u32[]{:S(2)}) copy-start(bf16[256,128]{1,0:T(8,128)(2,1)} %k_ref.1) | copy-start | bytes 196612
  3.0 0.8 %copy-start.2 = (bf16[256,128]{1,0:T(8,128)(2,1)S(1)}, bf16[256,128]{1,0:T(8,128)(2,1)}, u32[]{:S(2)}) copy-start(bf16[256,128]{1,0:T(8,128)(2,1)} %v_ref.1) | copy-start | bytes 196612
  3.8 0.8 %copy-start.3 = (bf16[256,128]{1,0:T(8,128)(2,1)S(1)}, bf16[256,128]{1,0:T(8,128)(2,1)}, u32[]{:S(2)}) copy-start(bf16[256,128]{1,0:T(8,128)(2,1)} %o_ref.1) | copy-start | bytes 196612
  4.7 0.8 %copy-start.4 = (bf16[256,128]{1,0:T(8,128)(2,1)S(1)}, bf16[256,128]{1,0:T(8,128)(2,1)}, u32[]{:S(2)}) copy-start(bf16[256,128]{1,0:T(8,128)(2,1)} %g_ref.1) | copy-start | bytes 196612
  6.3 8.4 %collective-permute-start = (bf16[528,128]{1,0:T(8,128)(2,1)S(1)}, bf16[528,128]{1,0:T(8,128)(2,1)S(1)}, u32[]{:S(2)}, u32[]{:S(2)}) collective-permute-start(bf16[528,128]{1,0:T(8,128)(2,1)S(1)} %get-tuple-element.20), channel_id=1, source_target_pairs={{0,4},{4,0},{1,5},{5,1},{2,6},{6,2},{3,7},{7,3},{8,12},{12,8},{9,1... | collective-permute-start | bytes 405512 | tf_op jit(solution)/shard_map/ppermute | solution.py:219
  7.5 12.6 %collective-permute-start.4 = (bf16[512,128]{1,0:T(8,128)(2,1)S(1)}, bf16[512,128]{1,0:T(8,128)(2,1)S(1)}, u32[]{:S(2)}, u32[]{:S(2)}) collective-permute-start(bf16[512,128]{1,0:T(8,128)(2,1)S(1)} %get-tuple-element.21), channel_id=1, source_target_pairs={{0,32},{8,40},{16,48},{24,56},{32,0},{40,8},{48,16},{56,24},{1,33}... | collective-permute-start | bytes 393224 | tf_op jit(solution)/shard_map/ppermute | solution.py:220
  14.8 12.1 %collective-permute-start.3 = (bf16[2,528,128]{2,1,0:T(8,128)(2,1)S(1)}, bf16[2,528,128]{2,1,0:T(8,128)(2,1)S(1)}, u32[]{:S(2)}, u32[]{:S(2)}) collective-permute-start(bf16[2,528,128]{2,1,0:T(8,128)(2,1)S(1)} %pad_maximum_fusion.refs_0_), channel_id=1, source_target_pairs={{0,48},{8,24},{16,0},{24,40},{32,16},{40,56},{48,32},{56,8},{1,49}... | collective-permute-start | bytes 811016 | tf_op jit(solution)/shard_map/ppermute | solution.py:221
  18.1 15.0 %collective-permute-start.2 = (bf16[2,528,128]{2,1,0:T(8,128)(2,1)S(1)}, bf16[2,528,128]{2,1,0:T(8,128)(2,1)S(1)}, u32[]{:S(2)}, u32[]{:S(2)}) collective-permute-start(bf16[2,528,128]{2,1,0:T(8,128)(2,1)S(1)} %pad_maximum_fusion.refs_0_), channel_id=1, source_target_pairs={{0,56},{8,0},{16,8},{24,16},{32,24},{40,32},{48,40},{56,48},{1,57}... | collective-permute-start | bytes 811016 | tf_op jit(solution)/shard_map/ppermute | solution.py:221
  18.5 14.5 %collective-permute-start.1 = (bf16[2,528,128]{2,1,0:T(8,128)(2,1)S(1)}, bf16[2,528,128]{2,1,0:T(8,128)(2,1)S(1)}, u32[]{:S(2)}, u32[]{:S(2)}) collective-permute-start(bf16[2,528,128]{2,1,0:T(8,128)(2,1)S(1)} %pad_maximum_fusion.refs_0_), channel_id=1, source_target_pairs={{0,8},{8,16},{16,24},{24,32},{32,40},{40,48},{48,56},{56,0},{1,9},... | collective-permute-start | bytes 811016 | tf_op jit(solution)/shard_map/ppermute | solution.py:221
  20.1 17.7 %collective-permute-start.7 = (bf16[2,512,128]{2,1,0:T(8,128)(2,1)S(1)}, bf16[2,512,128]{2,1,0:T(8,128)(2,1)S(1)}, u32[]{:S(2)}, u32[]{:S(2)}) collective-permute-start(bf16[2,512,128]{2,1,0:T(8,128)(2,1)S(1)} %pad_maximum_fusion.1.refs_4_), channel_id=1, source_target_pairs={{0,64},{64,128},{128,192},{192,0},{1,65},{65,129},{129,193},{193,1... | collective-permute-start | bytes 786440 | tf_op jit(solution)/shard_map/ppermute | solution.py:222
  21.8 20.7 %collective-permute-start.6 = (bf16[2,512,128]{2,1,0:T(8,128)(2,1)S(1)}, bf16[2,512,128]{2,1,0:T(8,128)(2,1)S(1)}, u32[]{:S(2)}, u32[]{:S(2)}) collective-permute-start(bf16[2,512,128]{2,1,0:T(8,128)(2,1)S(1)} %pad_maximum_fusion.1.refs_4_), channel_id=1, source_target_pairs={{0,192},{64,0},{128,64},{192,128},{1,193},{65,1},{129,65},{193,129... | collective-permute-start | bytes 786440 | tf_op jit(solution)/shard_map/ppermute | solution.py:222
  26.9 20.3 %collective-permute-start.5 = (bf16[2,512,128]{2,1,0:T(8,128)(2,1)S(1)}, bf16[2,512,128]{2,1,0:T(8,128)(2,1)S(1)}, u32[]{:S(2)}, u32[]{:S(2)}) collective-permute-start(bf16[2,512,128]{2,1,0:T(8,128)(2,1)S(1)} %pad_maximum_fusion.1.refs_4_), channel_id=1, source_target_pairs={{0,128},{64,192},{128,0},{192,64},{1,129},{65,193},{129,1},{193,65... | collective-permute-start | bytes 786440 | tf_op jit(solution)/shard_map/ppermute | solution.py:222
  52.1 10.8 %collective-permute-start.14 = (bf16[2,512,128]{2,1,0:T(8,128)(2,1)S(1)}, bf16[2,512,128]{2,1,0:T(8,128)(2,1)S(1)}, u32[]{:S(2)}, u32[]{:S(2)}) collective-permute-start(bf16[2,512,128]{2,1,0:T(8,128)(2,1)S(1)} %get-tuple-element.34), channel_id=1, source_target_pairs={{0,128},{64,192},{128,0},{192,64},{1,129},{65,193},{129,1},{193,65... | collective-permute-start | bytes 786440 | tf_op jit(solution)/shard_map/ppermute | solution.py:255
  55.4 11.5 %collective-permute-start.13 = (bf16[2,512,128]{2,1,0:T(8,128)(2,1)S(1)}, bf16[2,512,128]{2,1,0:T(8,128)(2,1)S(1)}, u32[]{:S(2)}, u32[]{:S(2)}) collective-permute-start(bf16[2,512,128]{2,1,0:T(8,128)(2,1)S(1)} %get-tuple-element.33), channel_id=1, source_target_pairs={{0,64},{64,128},{128,192},{192,0},{1,65},{65,129},{129,193},{193,1... | collective-permute-start | bytes 786440 | tf_op jit(solution)/shard_map/ppermute | solution.py:255
  56.1 11.2 %collective-permute-start.12 = (bf16[2,512,128]{2,1,0:T(8,128)(2,1)S(1)}, bf16[2,512,128]{2,1,0:T(8,128)(2,1)S(1)}, u32[]{:S(2)}, u32[]{:S(2)}) collective-permute-start(bf16[2,512,128]{2,1,0:T(8,128)(2,1)S(1)} %get-tuple-element.32), channel_id=1, source_target_pairs={{0,192},{64,0},{128,64},{192,128},{1,193},{65,1},{129,65},{193,129... | collective-permute-start | bytes 786440 | tf_op jit(solution)/shard_map/ppermute | solution.py:255
  58.6 13.6 %collective-permute-start.8 = (bf16[2,256,128]{2,1,0:T(8,128)(2,1)S(1)}, bf16[2,256,128]{2,1,0:T(8,128)(2,1)S(1)}, u32[]{:S(2)}, u32[]{:S(2)}) collective-permute-start(bf16[2,256,128]{2,1,0:T(8,128)(2,1)S(1)} %get-tuple-element.26), channel_id=1, source_target_pairs={{0,56},{8,0},{16,8},{24,16},{32,24},{40,32},{48,40},{56,48},{1,57}... | collective-permute-start | bytes 393224 | tf_op jit(solution)/shard_map/ppermute | solution.py:256
  61.3 10.9 %collective-permute-start.9 = (bf16[2,256,128]{2,1,0:T(8,128)(2,1)S(1)}, bf16[2,256,128]{2,1,0:T(8,128)(2,1)S(1)}, u32[]{:S(2)}, u32[]{:S(2)}) collective-permute-start(bf16[2,256,128]{2,1,0:T(8,128)(2,1)S(1)} %get-tuple-element.27), channel_id=1, source_target_pairs={{0,8},{8,16},{16,24},{24,32},{32,40},{40,48},{48,56},{56,0},{1,9},... | collective-permute-start | bytes 393224 | tf_op jit(solution)/shard_map/ppermute | solution.py:256
  62.9 9.3 %collective-permute-start.10 = (bf16[2,256,128]{2,1,0:T(8,128)(2,1)S(1)}, bf16[2,256,128]{2,1,0:T(8,128)(2,1)S(1)}, u32[]{:S(2)}, u32[]{:S(2)}) collective-permute-start(bf16[2,256,128]{2,1,0:T(8,128)(2,1)S(1)} %get-tuple-element.28), channel_id=1, source_target_pairs={{48,0},{24,8},{0,16},{40,24},{16,32},{56,40},{32,48},{8,56},{49,1}... | collective-permute-start | bytes 393224 | tf_op jit(solution)/shard_map/ppermute | solution.py:256
  67.3 11.4 %collective-permute-start.15 = (bf16[512,128]{1,0:T(8,128)(2,1)S(1)}, bf16[512,128]{1,0:T(8,128)(2,1)S(1)}, u32[]{:S(2)}, u32[]{:S(2)}) collective-permute-start(bf16[512,128]{1,0:T(8,128)(2,1)S(1)} %get-tuple-element.36), channel_id=1, source_target_pairs={{0,32},{8,40},{16,48},{24,56},{32,0},{40,8},{48,16},{56,24},{1,33}... | collective-permute-start | bytes 393224 | tf_op jit(solution)/shard_map/ppermute | solution.py:263
  72.3 4.4 %collective-permute-start.11 = (bf16[256,128]{1,0:T(8,128)(2,1)S(1)}, bf16[256,128]{1,0:T(8,128)(2,1)S(1)}, u32[]{:S(2)}, u32[]{:S(2)}) collective-permute-start(bf16[256,128]{1,0:T(8,128)(2,1)S(1)} %get-tuple-element.30), channel_id=1, source_target_pairs={{0,4},{4,0},{1,5},{5,1},{2,6},{6,2},{3,7},{7,3},{8,12},{12,8},{9,1... | collective-permute-start | bytes 196616 | tf_op jit(solution)/shard_map/ppermute | solution.py:265

commit v3 on v2

v3 whole, which is shorter than its diff:
```python
import functools
import math

import jax
import jax.numpy as jnp
from jax import lax
from jax.experimental import pallas as pl
from jax.experimental.pallas import tpu as pltpu
from jax.sharding import Mesh, PartitionSpec as P

F32 = jnp.float32
BF16 = jnp.bfloat16
BLK = 128
DIM = 128
LOG2E = math.log2(math.e)
FACTOR = 1.0 / math.sqrt(DIM)
VMEM_LIMIT = 48 * 1024 * 1024
PREP_VMEM = 62 * 1024 * 1024
BLOCKS = 128
HIDE = 1e30
Y_FROM = (0, 2, 3, 1)
NT = (((1,), (1,)), ((), ()))
Q_ROWS = 4 * BLK + 16
K_ROWS = 4 * BLK


def dot(a, b):
    return jnp.dot(a, b, preferred_element_type=F32)


def dot_nt(a, b):
    return lax.dot_general(a, b, NT, preferred_element_type=F32)


def ring(value, size):
    return lax.rem(value + size, size)


def low_block(fold_ref, device):
    first = fold_ref[2 * device]
    second = fold_ref[2 * device + 1]
    return jnp.minimum(first, second), second < first


def place(info_ref):
    return info_ref[BLOCKS], info_ref[BLOCKS + 1], info_ref[BLOCKS + 2]


def device_row(y, z, x):
    return y * 16 + z * 2 + x


def prep_kernel(where_ref, *refs):
    sources, (zout_ref, kout_ref), buffers, sems = refs[:7], refs[7:9], refs[9:16], refs[16]
    copies = [pltpu.make_async_copy(s, b, sems.at[n]) for n, (s, b) in enumerate(zip(sources, buffers))]
    for copy in copies:
        copy.start()
    for copy in copies:
        copy.wait()
    fold_ref, q_ref, k_ref, v_ref, o_ref, g_ref, lse_ref = buffers
    _, swapped = low_block(fold_ref, device_row(where_ref[0], where_ref[1], where_ref[2]))
    low = pl.multiple_of(jnp.where(swapped, BLK, 0), BLK)
    high = pl.multiple_of(jnp.where(swapped, 0, BLK), BLK)
    lse = lse_ref[...].astype(F32)
    halves = (lse[:, :BLK], lse[:, BLK:])
    rows = [jnp.where(swapped, halves[1], halves[0]), jnp.where(swapped, halves[0], halves[1])]
    for start in (low, high):
        prod = g_ref[pl.ds(start, BLK), :].astype(F32) * o_ref[pl.ds(start, BLK), :].astype(F32)
        rows.append(jnp.sum(prod.T, axis=0, keepdims=True))
    zout_ref[4 * BLK :, :] = jnp.concatenate(rows + [jnp.zeros((12, DIM), F32)], axis=0).astype(BF16)
    for out_ref, at, ref in (
        (zout_ref, 0, q_ref),
        (zout_ref, 2 * BLK, g_ref),
        (kout_ref, 0, k_ref),
        (kout_ref, 2 * BLK, v_ref),
    ):
        out_ref[at : at + BLK, :] = ref[pl.ds(low, BLK), :]
        out_ref[at + BLK : at + 2 * BLK, :] = ref[pl.ds(high, BLK), :]


def tile(k, v, kt, q, g, lses, delta, diagonal=False):
    s = dot_nt(k, q)
    probs = []
    for b, lse in enumerate(lses):
        p = jnp.exp2(s[b * BLK : (b + 1) * BLK] * (FACTOR * LOG2E) - lse)
        if diagonal and b == 0:
            shape = (BLK, BLK)
            seen = lax.broadcasted_iota(jnp.int32, shape, 0) <= lax.broadcasted_iota(jnp.int32, shape, 1)
            p = jnp.concatenate([jnp.where(seen, p[:, :BLK], 0.0), p[:, BLK:]], 1)
        probs.append(p)
    p = jnp.concatenate(probs, 0)
    dp = dot_nt(v, g)
    ds = (p * (dp - delta)).astype(BF16)
    return dot(p.astype(BF16), g), dot(ds, q), dot(kt, ds)


def grad_kernel(turn, info_ref, *refs):
    q_refs, y_ref, refs = refs[:4], refs[4], refs[5:]
    if turn > 0:
        dqin_ref, refs = refs[0], refs[1:]
    if turn < 3:
        dq_ref, dkv_ref, dv_acc, dk_acc = refs
    else:
        kept_ref, back_ref, refs = refs[0], refs[1], refs[2:]
        dq_refs, (dkv_ref, sum_ref, dv_acc, dk_acc) = refs[:4], refs[4:]
    y, z, x = place(info_ref)
    y_at = ring(y + Y_FROM[turn], 4)
    z_at = (z, ring(z + 7, 8), ring(z + 1, 8), ring(z + jnp.where(lax.rem(z, 2) == 0, 2, 6), 8))
    low_j = [low_block(info_ref, device_row(y_at, ring(z + 4 * j, 8), x))[0] for j in range(2)]

    def keys(at):
        return jnp.concatenate([y_ref[j, at : at + BLK, :] for j in range(2)], 0)

    k_low, k_high, v_low, v_high = (keys(b * BLK) for b in range(4))
    kt_low, kt_high = k_low.T, k_high.T

    def add(at, dv, dk, fresh):
        rows = slice(at, at + 2 * BLK)
        dv_acc[rows] = dv if fresh else dv_acc[rows] + dv
        dk_acc[rows] = dk if fresh else dk_acc[rows] + dk

    for pair in range(2):
        chunks = [(s, a) for s in (2 * pair, 2 * pair + 1) for a in range(2)]

        def rows(at):
            return jnp.concatenate([q_refs[s][a, at : at + BLK, :] for s, a in chunks], 0)

        stats = [q_refs[s][a, 4 * BLK :, :].astype(F32) for s, a in chunks]
        lse_low, lse_high, delta_low, delta_high = (
            jnp.concatenate([st[r : r + 1, :] for st in stats], 1) * (LOG2E if r < 2 else 1.0) for r in range(4)
        )
        low_i = [low_block(info_ref, device_row(y, z_at[s], 1 - x if a else x))[0] for s, a in chunks]
        own = turn == 0 and pair == 0

        def hide(j, low):
            parts = []
            for n, li in enumerate(low_i):
                seen = low_j[j] < li if low else li < low_j[j]
                hidden = jnp.float32(0.0) if own and n == 0 and j == 0 else jnp.where(seen, 0.0, HIDE)
                parts.append(jnp.full((1, BLK), hidden, F32))
            return jnp.concatenate(parts, 1)

        q_low, q_high, g_low, g_high = (rows(b * BLK) for b in range(4))
        fresh = pair == 0
        dv, dk, dq_high = tile(k_low, v_low, kt_low, q_high, g_high, [lse_high] * 2, delta_high)
        add(0, dv, dk, fresh)
        lses = [lse_high + hide(j, False) for j in range(2)]
        dv, dk, more = tile(k_high, v_high, kt_high, q_high, g_high, lses, delta_high, own)
        add(2 * BLK, dv, dk, fresh)
        dq_high += more
        lses = [lse_low + hide(j, True) for j in range(2)]
        dv, dk, dq_low = tile(k_low, v_low, kt_low, q_low, g_low, lses, delta_low, own)
        add(0, dv, dk, False)
        columns = slice(pair * 4 * BLK, (pair + 1) * 4 * BLK)
        for b, dq in ((0, dq_low), (1, dq_high)):
            if turn > 0:
                dq = dqin_ref[b, :, columns] + dq
            if turn < 3:
                dq_ref[b, :, columns] = dq
            else:
                for n, (s, a) in enumerate(chunks):
                    ref = dq_refs[s]
                    ref[a, b * BLK : (b + 1) * BLK, :] = dq[:, n * BLK : (n + 1) * BLK].T.astype(ref.dtype)

    for j in range(2):
        for b in range(2):
            source = slice((2 * b + j) * BLK, (2 * b + j + 1) * BLK)
            dkv_ref[j, b * BLK : (b + 1) * BLK, :] = dk_acc[source].astype(dkv_ref.dtype)
            dkv_ref[j, (2 + b) * BLK : (3 + b) * BLK, :] = dv_acc[source].astype(dkv_ref.dtype)
    if turn == 3:
        sum_ref[...] = kept_ref[...] + back_ref[...].astype(F32)


def meet_kernel(own_ref, *refs):
    *back_refs, keep_ref, send_ref = refs
    for part, out_ref in ((0, keep_ref), (1, send_ref)):
        total = own_ref[part]
        for ref in back_refs:
            total += ref[part].astype(F32)
        out_ref[...] = total.astype(out_ref.dtype)


def last_kernel(info_ref, dq_ref, dqx_ref, dkv_ref, dkvz_ref, q_ref, k_ref, v_ref):
    _, swapped = low_block(info_ref, device_row(*place(info_ref)))
    for part in range(2):
        to = pl.multiple_of(jnp.where(swapped, (1 - part) * BLK, part * BLK), BLK)
        at = part * BLK

        def total(ref, other, start):
            return ref[start : start + BLK, :] + other[start : start + BLK, :].astype(F32)

        q_ref[pl.ds(to, BLK), :] = (total(dq_ref, dqx_ref, at) * FACTOR).astype(BF16)
        k_ref[pl.ds(to, BLK), :] = (total(dkv_ref, dkvz_ref, at) * FACTOR).astype(BF16)
        v_ref[pl.ds(to, BLK), :] = total(dkv_ref, dkvz_ref, 2 * BLK + at).astype(BF16)


def z_step(step):
    return [(i, (i + step) % 8) for i in range(8)]


def y_step(step):
    return [(i, (i + step) % 4) for i in range(4)]


Z_PAIRS = [(i, (i - 2) % 8 if i % 2 == 0 else (i + 2) % 8) for i in range(8)]
Z_BACK = [(b, a) for a, b in Z_PAIRS]
X_SWAP = [(0, 1), (1, 0)]


def call(kernel, outs, operands, info=None, scratch=(), in_specs=None, vmem_limit=VMEM_LIMIT, **options):
    smem = pl.BlockSpec(memory_space=pltpu.SMEM)
    vmem = pl.BlockSpec(memory_space=pltpu.VMEM)
    scalars = [] if info is None else [info]
    return pl.pallas_call(
        kernel,
        out_shape=[jax.ShapeDtypeStruct(s, t) for s, t in outs],
        in_specs=[smem] * len(scalars) + (in_specs or [vmem] * len(operands)),
        out_specs=[vmem] * len(outs),
        scratch_shapes=list(scratch),
        compiler_params=pltpu.CompilerParams(vmem_limit_bytes=vmem_limit),
        **options,
    )(*scalars, *operands)


def body(queries, key_rows, value_rows, outputs, out_grad, saved_lse, fold_map):
    where = jnp.stack([lax.axis_index(name) for name in ("pb", "kz", "kx")]).astype(jnp.int32)
    info = jnp.concatenate([fold_map, where])
    operands = (fold_map, queries, key_rows, value_rows, outputs, out_grad, saved_lse.T)
    mine_q, mine_k = call(
        prep_kernel,
        [((Q_ROWS, DIM), BF16), ((K_ROWS, DIM), BF16)],
        operands,
        where,
        [pltpu.SMEM(a.shape, a.dtype) if a is fold_map else pltpu.VMEM(a.shape, a.dtype) for a in operands]
        + [pltpu.SemaphoreType.DMA((len(operands),))],
        in_specs=[pl.BlockSpec(memory_space=pltpu.HBM)] * len(operands),
        vmem_limit=PREP_VMEM,
    )
    q0 = jnp.stack([mine_q, lax.ppermute(mine_q, "kx", X_SWAP)])
    k0 = jnp.stack([mine_k, lax.ppermute(mine_k, "kz", z_step(4))])
    q_sets = [q0] + [lax.ppermute(q0, "kz", p) for p in (z_step(1), z_step(-1), Z_PAIRS)]
    k_sets = [k0] + [lax.ppermute(k0, "pb", y_step(-s)) for s in Y_FROM[1:]]

    acc = pltpu.VMEM((4 * BLK, DIM), F32)
    dq_acc = ((2, DIM, 8 * BLK), F32)
    dkv_acc = ((2, K_ROWS, DIM), F32)
    cost = pl.CostEstimate(flops=16 * 2 * 5 * 4 * BLK**3 // 2, bytes_accessed=1 << 20, transcendentals=0)
    back = []
    for turn in range(4):
        operands = q_sets + [k_sets[turn]] + ([dq] if turn else [])
        outs = [dq_acc, dkv_acc if turn == 0 else ((2, K_ROWS, DIM), BF16)]
        options = dict(input_output_aliases={6: 0}) if turn else {}
        if turn == 3:
            operands += [kept, back[0]]
            outs = [((2, 2 * BLK, DIM), F32 if s == 0 else BF16) for s in range(4)] + [outs[1], dkv_acc]
            options = {}
        kernel = functools.partial(grad_kernel, turn)
        *dq, part = call(kernel, outs, operands, info, [acc, acc], cost_estimate=cost, **options)
        if turn == 0:
            (dq,), kept = dq, part
        elif turn < 3:
            (dq,) = dq
            back.append(lax.ppermute(part, "pb", y_step(Y_FROM[turn])))
        else:
            *dq, last = dq
            kept = part
            back.append(lax.ppermute(last, "pb", y_step(Y_FROM[turn])))
    dq_back = [lax.ppermute(dq[t], "kz", p) for t, p in ((1, z_step(-1)), (2, z_step(1)), (3, Z_BACK))]

    def meet(own, partners):
        shape = own.shape[1:]
        return call(meet_kernel, [(shape, F32), (shape, BF16)], [own] + partners)

    dkv_keep, dkv_send = meet(kept, back[1:])
    dkv_last = lax.ppermute(dkv_send, "kz", z_step(4))
    dq_keep, dq_send = meet(dq[0], dq_back)
    dq_last = lax.ppermute(dq_send, "kx", X_SWAP)
    grads = [((2 * BLK, DIM), BF16)] * 3
    return tuple(call(last_kernel, grads, (dq_keep, dq_last, dkv_keep, dkv_last), info))


def solution(mesh):
    fine = Mesh(mesh.devices.reshape(4, 8, 2, 2, 2), ("pb", "kz", "kx", "hx", "hc"))
    rows = P(("pb", "kz", "kx"), ("hx", "hc"))
    return jax.shard_map(
        body,
        mesh=fine,
        in_specs=(rows,) * 6 + (P(),),
        out_specs=(rows,) * 3,
        check_vma=False,
    )
```

time: 81.2 us -> 73.1 us (0.900); the launches traced: 80 us -> 73 us
  Pallas kernels: 21.2 us -> 14.4 us
  local copies, waits for them, and re-layouts: 4.78 us -> 0.01 us
  waiting for transfers between devices: 16.6 us -> 18.9 us
  other arithmetic: 0.13 us -> 1.68 us
    pallas_call x8, Pallas kernels: 21.2 us -> 14.4 us  [call(): pl.pallas_call(kernel, out_shape=[jax.ShapeDtypeStruct(s, t) for s, t in...]
    ppermute x9, waiting for transfers between devices: 4.65 us -> 10.5 us  [the longest x3 5.86 us: body(): lax.ppermute(dq[t], 'kz', p)]
    unnamed x13 -> x4, local copies, waits for them, and re-layouts: 4.78 us -> 0.01 us
    ppermute x1, waiting for transfers between devices: 2.12 us -> 0.01 us  [body(): dkv_last = lax.ppermute(dkv_send, 'kz', z_step(4))]
    ppermute x3, waiting for transfers between devices: 6.43 us -> 4.93 us  [body(): lax.ppermute(q0, 'kz', p)]
    ppermute x9, starting transfers between devices: 17 us -> 18.1 us  [the longest x3 6.99 us: body(): k_sets = [k0] + [lax.ppermute(k0, 'pb', y_step(-s)) for s in Y_FROM[1:]]]
    another operation x1, other arithmetic: 0.03 us -> 0.97 us  [body(): q0 = jnp.stack([mine_q, lax.ppermute(mine_q, 'kx', X_SWAP)])]
  transfers between devices with their start and end apart: 16 -> 16, of which waited for: 7 -> 6; matrix products, arithmetic and copies ran while one was open for 0% -> 1% of each run, Pallas kernels for 18% -> 15%
where the time goes in v3:
time: 73.1 us; the launch traced here: 73 us
  starting transfers between devices  37.3 us (51%)
  waiting for transfers between devices  18.9 us (26%)
  Pallas kernels  14.4 us (20%)
  other arithmetic  1.68 us (2%)
    pallas_call x8, Pallas kernels, call(): pl.pallas_call(kernel, out_shape=[jax.ShapeDtypeStruct(s, t) for s, t in...  14.4 us
    ppermute x1, starting transfers between devices, body(): k0 = jnp.stack([mine_k, lax.ppermute(mine_k, 'kz', z_step(4))])  7.19 us
    ppermute x3, starting transfers between devices, body(): k_sets = [k0] + [lax.ppermute(k0, 'pb', y_step(-s)) for s in Y_FROM[1:]]  6.99 us
    ppermute x3, waiting for transfers between devices, body(): lax.ppermute(dq[t], 'kz', p)  5.86 us
    ppermute x3, starting transfers between devices, body(): lax.ppermute(q0, 'kz', p)  5.55 us
    ppermute x3, waiting for transfers between devices, body(): lax.ppermute(q0, 'kz', p)  4.93 us
    ppermute x2, starting transfers between devices, body(): back.append(lax.ppermute(part, 'pb', y_step(Y_FROM[turn])))  4.6 us
    ppermute x1, starting transfers between devices, body(): dkv_last = lax.ppermute(dkv_send, 'kz', z_step(4))  4.19 us
  transfers between devices with their start and end apart: 16, of which 6 were waited for; matrix products, arithmetic and copies ran while one was open for 1% of the time, Pallas kernels for 15%

profile of v3, /device:TPU:4, one launch (start us, length us, event | category | flops | bytes accessed | tf_op | source)
XLA Modules:
  0.0 73.0 jit_solution(9331156509384455412)
XLA Ops:
  1.3 2.5 %shard_map.94 = (bf16[528,128]{1,0:T(8,128)(2,1)}, bf16[512,128]{1,0:T(8,128)(2,1)}) custom-call(s32[3]{0:T(128)} %pad_add_fusion.1.where_ref, s32[128]{0:T(128)} %refs_0_.1, bf16[256,128]{1,0:T(8,128)(2,1)} %refs_1_.1, bf16[256,128]{1,0:T(8,128)(2,1)} %refs_2_.1, bf16[256,128]{1,0:T(8,128)(2,1)} %refs_3_.1, bf16[256,128]{1,0:T(8,128)(2,1)} %refs_4_.1, ...), custom_call_target="tpu_custom_call" | custom-call | tf_op jit(solution)/shard_map/pallas_call | solution.py:214
  3.7 1.3 %collective-permute-start = (bf16[528,128]{1,0:T(8,128)(2,1)}, bf16[528,128]{1,0:T(8,128)(2,1)S(1)}, u32[]{:S(2)}, u32[]{:S(2)}) collective-permute-start(bf16[528,128]{1,0:T(8,128)(2,1)} %get-tuple-element.21), channel_id=1, source_target_pairs={{0,4},{4,0},{1,5},{5,1},{2,6},{6,2},{3,7},{7,3},{8,12},{12,8},{9,1... | collective-permute-start | bytes 405512 | tf_op jit(solution)/shard_map/ppermute | solution.py:239
  5.0 7.2 %collective-permute-start.4 = (bf16[512,128]{1,0:T(8,128)(2,1)}, bf16[512,128]{1,0:T(8,128)(2,1)S(1)}, u32[]{:S(2)}, u32[]{:S(2)}) collective-permute-start(bf16[512,128]{1,0:T(8,128)(2,1)} %get-tuple-element.22), channel_id=1, source_target_pairs={{0,32},{8,40},{16,48},{24,56},{32,0},{40,8},{48,16},{56,24},{1,33}... | collective-permute-start | bytes 393224 | tf_op jit(solution)/shard_map/ppermute | solution.py:240
  13.2 3.5 %collective-permute-start.3 = (bf16[2,528,128]{2,1,0:T(8,128)(2,1)S(1)}, bf16[2,528,128]{2,1,0:T(8,128)(2,1)S(1)}, u32[]{:S(2)}, u32[]{:S(2)}) collective-permute-start(bf16[2,528,128]{2,1,0:T(8,128)(2,1)S(1)} %pad_maximum_fusion.refs_0_), channel_id=1, source_target_pairs={{0,48},{8,24},{16,0},{24,40},{32,16},{40,56},{48,32},{56,8},{1,49}... | collective-permute-start | bytes 811016 | tf_op jit(solution)/shard_map/ppermute | solution.py:241
  16.9 1.8 %collective-permute-start.1 = (bf16[2,528,128]{2,1,0:T(8,128)(2,1)S(1)}, bf16[2,528,128]{2,1,0:T(8,128)(2,1)S(1)}, u32[]{:S(2)}, u32[]{:S(2)}) collective-permute-start(bf16[2,528,128]{2,1,0:T(8,128)(2,1)S(1)} %pad_maximum_fusion.refs_0_), channel_id=1, source_target_pairs={{0,8},{8,16},{16,24},{24,32},{32,40},{40,48},{48,56},{56,0},{1,9},... | collective-permute-start | bytes 811016 | tf_op jit(solution)/shard_map/ppermute | solution.py:241
  18.8 3.3 %collective-permute-start.7 = (bf16[2,512,128]{2,1,0:T(8,128)(2,1)S(1)}, bf16[2,512,128]{2,1,0:T(8,128)(2,1)S(1)}, u32[]{:S(2)}, u32[]{:S(2)}) collective-permute-start(bf16[2,512,128]{2,1,0:T(8,128)(2,1)S(1)} %pad_maximum_fusion.1.refs_4_), channel_id=1, source_target_pairs={{0,128},{64,192},{128,0},{192,64},{1,129},{65,193},{129,1},{193,65... | collective-permute-start | bytes 786440 | tf_op jit(solution)/shard_map/ppermute | solution.py:242
  22.8 2.0 %collective-permute-done.3.refs_3_ = bf16[2,528,128]{2,1,0:T(8,128)(2,1)S(1)} collective-permute-done((bf16[2,528,128]{2,1,0:T(8,128)(2,1)S(1)}, bf16[2,528,128]{2,1,0:T(8,128)(2,1)S(1)}, u32[]{:S(2)}, u32[]{:S(2)}) %collective-permute-start.3) | collective-permute-done | bytes 270368 | tf_op jit(solution)/shard_map/ppermute | solution.py:241
  24.8 3.0 %collective-permute-start.5 = (bf16[2,512,128]{2,1,0:T(8,128)(2,1)S(1)}, bf16[2,512,128]{2,1,0:T(8,128)(2,1)S(1)}, u32[]{:S(2)}, u32[]{:S(2)}) collective-permute-start(bf16[2,512,128]{2,1,0:T(8,128)(2,1)S(1)} %pad_maximum_fusion.1.refs_4_), channel_id=1, source_target_pairs={{0,192},{64,0},{128,64},{192,128},{1,193},{65,1},{129,65},{193,129... | collective-permute-start | bytes 786440 | tf_op jit(solution)/shard_map/ppermute | solution.py:242
  27.8 2.9 %collective-permute-done.2.refs_2_ = bf16[2,528,128]{2,1,0:T(8,128)(2,1)S(1)} collective-permute-done((bf16[2,528,128]{2,1,0:T(8,128)(2,1)S(1)}, bf16[2,528,128]{2,1,0:T(8,128)(2,1)S(1)}, u32[]{:S(2)}, u32[]{:S(2)}) %collective-permute-start.2) | collective-permute-done | bytes 270368 | tf_op jit(solution)/shard_map/ppermute | solution.py:241
  30.8 2.6 %shard_map.95 = (f32[2,128,1024]{2,1,0:T(8,128)S(1)}, f32[2,512,128]{2,1,0:T(8,128)S(1)}) custom-call(s32[131]{0:T(256)S(1)} %pad_add_fusion.info_ref, bf16[2,528,128]{2,1,0:T(8,128)(2,1)S(1)} %pad_maximum_fusion.refs_0_, bf16[2,528,128]{2,1,0:T(8,128)(2,1)S(1)} %collective-permute-done.1.refs_1_, bf16[2,528,128]{2,1,0:T(8,128)(2,1)S(1)} %collective-permute-done.2.refs_2_, ...), custom_call_target="tpu_custom_call" | custom-call | flops 671088640 | bytes 1048576 | tf_op jit(solution)/shard_map/pallas_call | solution.py:214
  33.4 2.6 %shard_map.96 = (f32[2,128,1024]{2,1,0:T(8,128)S(1)}, bf16[2,512,128]{2,1,0:T(8,128)(2,1)S(1)}) custom-call(s32[131]{0:T(256)S(1)} %pad_add_fusion.info_ref, bf16[2,528,128]{2,1,0:T(8,128)(2,1)S(1)} %pad_maximum_fusion.refs_0_, bf16[2,528,128]{2,1,0:T(8,128)(2,1)S(1)} %collective-permute-done.1.refs_1_, ...), custom_call_target="tpu_custom_call", output_to_operand_aliasing={{0}: (6, {})} | custom-call | flops 671088640 | bytes 1048576 | tf_op jit(solution)/shard_map/pallas_call | solution.py:214
  36.0 3.5 %collective-permute-start.8 = (bf16[2,512,128]{2,1,0:T(8,128)(2,1)S(1)}, bf16[2,512,128]{2,1,0:T(8,128)(2,1)S(1)}, u32[]{:S(2)}, u32[]{:S(2)}) collective-permute-start(bf16[2,512,128]{2,1,0:T(8,128)(2,1)S(1)} %get-tuple-element.27), channel_id=1, source_target_pairs={{0,128},{64,192},{128,0},{192,64},{1,129},{65,193},{129,1},{193,65... | collective-permute-start | bytes 786440 | tf_op jit(solution)/shard_map/ppermute | solution.py:263
  39.4 2.6 %shard_map.97 = (f32[2,128,1024]{2,1,0:T(8,128)S(1)}, bf16[2,512,128]{2,1,0:T(8,128)(2,1)S(1)}) custom-call(s32[131]{0:T(256)S(1)} %pad_add_fusion.info_ref, bf16[2,528,128]{2,1,0:T(8,128)(2,1)S(1)} %pad_maximum_fusion.refs_0_, bf16[2,528,128]{2,1,0:T(8,128)(2,1)S(1)} %collective-permute-done.1.refs_1_, ...), custom_call_target="tpu_custom_call", output_to_operand_aliasing={{0}: (6, {})} | custom-call | flops 671088640 | bytes 1048576 | tf_op jit(solution)/shard_map/pallas_call | solution.py:214
  42.0 1.1 %collective-permute-start.13 = (bf16[2,512,128]{2,1,0:T(8,128)(2,1)S(1)}, bf16[2,512,128]{2,1,0:T(8,128)(2,1)S(1)}, u32[]{:S(2)}, u32[]{:S(2)}) collective-permute-start(bf16[2,512,128]{2,1,0:T(8,128)(2,1)S(1)} %get-tuple-element.35), channel_id=1, source_target_pairs={{0,192},{64,0},{128,64},{192,128},{1,193},{65,1},{129,65},{193,129... | collective-permute-start | bytes 786440 | tf_op jit(solution)/shard_map/ppermute | solution.py:263
  43.2 2.1 %collective-permute-done.8.refs_7_ = bf16[2,512,128]{2,1,0:T(8,128)(2,1)S(1)} collective-permute-done((bf16[2,512,128]{2,1,0:T(8,128)(2,1)S(1)}, bf16[2,512,128]{2,1,0:T(8,128)(2,1)S(1)}, u32[]{:S(2)}, u32[]{:S(2)}) %collective-permute-start.8) | collective-permute-done | bytes 262176 | tf_op jit(solution)/shard_map/ppermute | solution.py:263
  45.3 2.7 %shard_map.98 = (f32[2,256,128]{2,1,0:T(8,128)S(1)}, bf16[2,256,128]{2,1,0:T(8,128)(2,1)S(1)}, bf16[2,256,128]{2,1,0:T(8,128)(2,1)S(1)}, bf16[2,256,128]{2,1,0:T...) custom-call(s32[131]{0:T(256)S(1)} %pad_add_fusion.info_ref, ...), custom_call_target="tpu_custom_call" | custom-call | flops 671088640 | bytes 1048576 | tf_op jit(solution)/shard_map/pallas_call | solution.py:214
  48.0 3.3 %collective-permute-start.14 = (bf16[2,512,128]{2,1,0:T(8,128)(2,1)S(1)}, bf16[2,512,128]{2,1,0:T(8,128)(2,1)S(1)}, u32[]{:S(2)}, u32[]{:S(2)}) collective-permute-start(bf16[2,512,128]{2,1,0:T(8,128)(2,1)S(1)} %get-tuple-element.36), channel_id=1, source_target_pairs={{0,64},{64,128},{128,192},{192,0},{1,65},{65,129},{129,193},{193,1... | collective-permute-start | bytes 786440 | tf_op jit(solution)/shard_map/ppermute | solution.py:267
  51.4 2.7 %collective-permute-start.9 = (bf16[2,256,128]{2,1,0:T(8,128)(2,1)S(1)}, bf16[2,256,128]{2,1,0:T(8,128)(2,1)S(1)}, u32[]{:S(2)}, u32[]{:S(2)}) collective-permute-start(bf16[2,256,128]{2,1,0:T(8,128)(2,1)S(1)} %get-tuple-element.29), channel_id=1, source_target_pairs={{0,56},{8,0},{16,8},{24,16},{32,24},{40,32},{48,40},{56,48},{1,57}... | collective-permute-start | bytes 393224 | tf_op jit(solution)/shard_map/ppermute | solution.py:268
  54.6 2.6 %collective-permute-done.14.refs_1_ = bf16[2,512,128]{2,1,0:T(8,128)(2,1)S(1)} collective-permute-done((bf16[2,512,128]{2,1,0:T(8,128)(2,1)S(1)}, bf16[2,512,128]{2,1,0:T(8,128)(2,1)S(1)}, u32[]{:S(2)}, u32[]{:S(2)}) %collective-permute-start.14) | collective-permute-done | bytes 262176 | tf_op jit(solution)/shard_map/ppermute | solution.py:267
  57.3 4.2 %collective-permute-start.15 = (bf16[512,128]{1,0:T(8,128)(2,1)S(1)}, bf16[512,128]{1,0:T(8,128)(2,1)S(1)}, u32[]{:S(2)}, u32[]{:S(2)}) collective-permute-start(bf16[512,128]{1,0:T(8,128)(2,1)S(1)} %get-tuple-element.38), channel_id=1, source_target_pairs={{0,32},{8,40},{16,48},{24,56},{32,0},{40,8},{48,16},{56,24},{1,33}... | collective-permute-start | bytes 393224 | tf_op jit(solution)/shard_map/ppermute | solution.py:275
  61.4 5.9 %collective-permute-done.10.refs_1_ = bf16[2,256,128]{2,1,0:T(8,128)(2,1)S(1)} collective-permute-done((bf16[2,256,128]{2,1,0:T(8,128)(2,1)S(1)}, bf16[2,256,128]{2,1,0:T(8,128)(2,1)S(1)}, u32[]{:S(2)}, u32[]{:S(2)}) %collective-permute-start.10) | collective-permute-done | bytes 131104 | tf_op jit(solution)/shard_map/ppermute | solution.py:268
  67.4 1.0 %collective-permute-start.12 = (bf16[256,128]{1,0:T(8,128)(2,1)S(1)}, bf16[256,128]{1,0:T(8,128)(2,1)S(1)}, u32[]{:S(2)}, u32[]{:S(2)}) collective-permute-start(bf16[256,128]{1,0:T(8,128)(2,1)S(1)} %get-tuple-element.33), channel_id=1, source_target_pairs={{0,4},{4,0},{1,5},{5,1},{2,6},{6,2},{3,7},{7,3},{8,12},{12,8},{9,1... | collective-permute-start | bytes 196616 | tf_op jit(solution)/shard_map/ppermute | solution.py:277
  68.4 3.4 %collective-permute-done.12.dqx_ref = bf16[256,128]{1,0:T(8,128)(2,1)S(1)} collective-permute-done((bf16[256,128]{1,0:T(8,128)(2,1)S(1)}, bf16[256,128]{1,0:T(8,128)(2,1)S(1)}, u32[]{:S(2)}, u32[]{:S(2)}) %collective-permute-start.12) | collective-permute-done | bytes 65568 | tf_op jit(solution)/shard_map/ppermute | solution.py:277
  71.7 1.3 %shard_map.101 = (bf16[256,128]{1,0:T(8,128)(2,1)}, bf16[256,128]{1,0:T(8,128)(2,1)}, bf16[256,128]{1,0:T(8,128)(2,1)}) custom-call(s32[131]{0:T(256)S(1)} %pad_add_fusion.info_ref, f32[256,128]{1,0:T(8,128)S(1)} %get-tuple-element.32.dq_ref, bf16[256,128]{1,0:T(8,128)(2,1)S(1)} %collective-permute-done.12.dqx_ref, ...), custom_call_target="tpu_custom_call" | custom-call | tf_op jit(solution)/shard_map/pallas_call | solution.py:214
  (24 shorter events, 3.3 us)
Async XLA Ops:
  3.7 8.5 %collective-permute-start = (bf16[528,128]{1,0:T(8,128)(2,1)}, bf16[528,128]{1,0:T(8,128)(2,1)S(1)}, u32[]{:S(2)}, u32[]{:S(2)}) collective-permute-start(bf16[528,128]{1,0:T(8,128)(2,1)} %get-tuple-element.21), channel_id=1, source_target_pairs={{0,4},{4,0},{1,5},{5,1},{2,6},{6,2},{3,7},{7,3},{8,12},{12,8},{9,1... | collective-permute-start | bytes 405512 | tf_op jit(solution)/shard_map/ppermute | solution.py:239
  5.0 13.7 %collective-permute-start.4 = (bf16[512,128]{1,0:T(8,128)(2,1)}, bf16[512,128]{1,0:T(8,128)(2,1)S(1)}, u32[]{:S(2)}, u32[]{:S(2)}) collective-permute-start(bf16[512,128]{1,0:T(8,128)(2,1)} %get-tuple-element.22), channel_id=1, source_target_pairs={{0,32},{8,40},{16,48},{24,56},{32,0},{40,8},{48,16},{56,24},{1,33}... | collective-permute-start | bytes 393224 | tf_op jit(solution)/shard_map/ppermute | solution.py:240
  12.2 6.5 %copy-start = (bf16[512,128]{1,0:T(8,128)(2,1)S(1)}, bf16[512,128]{1,0:T(8,128)(2,1)}, u32[]{:S(2)}) copy-start(bf16[512,128]{1,0:T(8,128)(2,1)} %get-tuple-element.22) | copy-start | bytes 393220
  13.2 11.6 %collective-permute-start.3 = (bf16[2,528,128]{2,1,0:T(8,128)(2,1)S(1)}, bf16[2,528,128]{2,1,0:T(8,128)(2,1)S(1)}, u32[]{:S(2)}, u32[]{:S(2)}) collective-permute-start(bf16[2,528,128]{2,1,0:T(8,128)(2,1)S(1)} %pad_maximum_fusion.refs_0_), channel_id=1, source_target_pairs={{0,48},{8,24},{16,0},{24,40},{32,16},{40,56},{48,32},{56,8},{1,49}... | collective-permute-start | bytes 811016 | tf_op jit(solution)/shard_map/ppermute | solution.py:241
  16.7 14.1 %collective-permute-start.2 = (bf16[2,528,128]{2,1,0:T(8,128)(2,1)S(1)}, bf16[2,528,128]{2,1,0:T(8,128)(2,1)S(1)}, u32[]{:S(2)}, u32[]{:S(2)}) collective-permute-start(bf16[2,528,128]{2,1,0:T(8,128)(2,1)S(1)} %pad_maximum_fusion.refs_0_), channel_id=1, source_target_pairs={{0,56},{8,0},{16,8},{24,16},{32,24},{40,32},{48,40},{56,48},{1,57}... | collective-permute-start | bytes 811016 | tf_op jit(solution)/shard_map/ppermute | solution.py:241
  16.9 13.8 %collective-permute-start.1 = (bf16[2,528,128]{2,1,0:T(8,128)(2,1)S(1)}, bf16[2,528,128]{2,1,0:T(8,128)(2,1)S(1)}, u32[]{:S(2)}, u32[]{:S(2)}) collective-permute-start(bf16[2,528,128]{2,1,0:T(8,128)(2,1)S(1)} %pad_maximum_fusion.refs_0_), channel_id=1, source_target_pairs={{0,8},{8,16},{16,24},{24,32},{32,40},{40,48},{48,56},{56,0},{1,9},... | collective-permute-start | bytes 811016 | tf_op jit(solution)/shard_map/ppermute | solution.py:241
  18.7 3.3 %copy-start.1 = (s32[128]{0:T(128)S(1)}, s32[128]{0:T(128)}, u32[]{:S(2)}) copy-start(s32[128]{0:T(128)} %refs_0_.1) | copy-start | bytes 1540
  18.8 14.6 %collective-permute-start.7 = (bf16[2,512,128]{2,1,0:T(8,128)(2,1)S(1)}, bf16[2,512,128]{2,1,0:T(8,128)(2,1)S(1)}, u32[]{:S(2)}, u32[]{:S(2)}) collective-permute-start(bf16[2,512,128]{2,1,0:T(8,128)(2,1)S(1)} %pad_maximum_fusion.1.refs_4_), channel_id=1, source_target_pairs={{0,128},{64,192},{128,0},{192,64},{1,129},{65,193},{129,1},{193,65... | collective-permute-start | bytes 786440 | tf_op jit(solution)/shard_map/ppermute | solution.py:242
  22.1 17.3 %collective-permute-start.6 = (bf16[2,512,128]{2,1,0:T(8,128)(2,1)S(1)}, bf16[2,512,128]{2,1,0:T(8,128)(2,1)S(1)}, u32[]{:S(2)}, u32[]{:S(2)}) collective-permute-start(bf16[2,512,128]{2,1,0:T(8,128)(2,1)S(1)} %pad_maximum_fusion.1.refs_4_), channel_id=1, source_target_pairs={{0,64},{64,128},{128,192},{192,0},{1,65},{65,129},{129,193},{193,1... | collective-permute-start | bytes 786440 | tf_op jit(solution)/shard_map/ppermute | solution.py:242
  24.8 18.4 %collective-permute-start.5 = (bf16[2,512,128]{2,1,0:T(8,128)(2,1)S(1)}, bf16[2,512,128]{2,1,0:T(8,128)(2,1)S(1)}, u32[]{:S(2)}, u32[]{:S(2)}) collective-permute-start(bf16[2,512,128]{2,1,0:T(8,128)(2,1)S(1)} %pad_maximum_fusion.1.refs_4_), channel_id=1, source_target_pairs={{0,192},{64,0},{128,64},{192,128},{1,193},{65,1},{129,65},{193,129... | collective-permute-start | bytes 786440 | tf_op jit(solution)/shard_map/ppermute | solution.py:242
  36.0 9.3 %collective-permute-start.8 = (bf16[2,512,128]{2,1,0:T(8,128)(2,1)S(1)}, bf16[2,512,128]{2,1,0:T(8,128)(2,1)S(1)}, u32[]{:S(2)}, u32[]{:S(2)}) collective-permute-start(bf16[2,512,128]{2,1,0:T(8,128)(2,1)S(1)} %get-tuple-element.27), channel_id=1, source_target_pairs={{0,128},{64,192},{128,0},{192,64},{1,129},{65,193},{129,1},{193,65... | collective-permute-start | bytes 786440 | tf_op jit(solution)/shard_map/ppermute | solution.py:263
  42.0 12.5 %collective-permute-start.13 = (bf16[2,512,128]{2,1,0:T(8,128)(2,1)S(1)}, bf16[2,512,128]{2,1,0:T(8,128)(2,1)S(1)}, u32[]{:S(2)}, u32[]{:S(2)}) collective-permute-start(bf16[2,512,128]{2,1,0:T(8,128)(2,1)S(1)} %get-tuple-element.35), channel_id=1, source_target_pairs={{0,192},{64,0},{128,64},{192,128},{1,193},{65,1},{129,65},{193,129... | collective-permute-start | bytes 786440 | tf_op jit(solution)/shard_map/ppermute | solution.py:263
  48.0 9.1 %collective-permute-start.14 = (bf16[2,512,128]{2,1,0:T(8,128)(2,1)S(1)}, bf16[2,512,128]{2,1,0:T(8,128)(2,1)S(1)}, u32[]{:S(2)}, u32[]{:S(2)}) collective-permute-start(bf16[2,512,128]{2,1,0:T(8,128)(2,1)S(1)} %get-tuple-element.36), channel_id=1, source_target_pairs={{0,64},{64,128},{128,192},{192,0},{1,65},{65,129},{129,193},{193,1... | collective-permute-start | bytes 786440 | tf_op jit(solution)/shard_map/ppermute | solution.py:267
  51.4 10.1 %collective-permute-start.9 = (bf16[2,256,128]{2,1,0:T(8,128)(2,1)S(1)}, bf16[2,256,128]{2,1,0:T(8,128)(2,1)S(1)}, u32[]{:S(2)}, u32[]{:S(2)}) collective-permute-start(bf16[2,256,128]{2,1,0:T(8,128)(2,1)S(1)} %get-tuple-element.29), channel_id=1, source_target_pairs={{0,56},{8,0},{16,8},{24,16},{32,24},{40,32},{48,40},{56,48},{1,57}... | collective-permute-start | bytes 393224 | tf_op jit(solution)/shard_map/ppermute | solution.py:268
  54.1 13.2 %collective-permute-start.10 = (bf16[2,256,128]{2,1,0:T(8,128)(2,1)S(1)}, bf16[2,256,128]{2,1,0:T(8,128)(2,1)S(1)}, u32[]{:S(2)}, u32[]{:S(2)}) collective-permute-start(bf16[2,256,128]{2,1,0:T(8,128)(2,1)S(1)} %get-tuple-element.30), channel_id=1, source_target_pairs={{0,8},{8,16},{16,24},{24,32},{32,40},{40,48},{48,56},{56,0},{1,9},... | collective-permute-start | bytes 393224 | tf_op jit(solution)/shard_map/ppermute | solution.py:268
  54.1 13.2 %collective-permute-start.11 = (bf16[2,256,128]{2,1,0:T(8,128)(2,1)S(1)}, bf16[2,256,128]{2,1,0:T(8,128)(2,1)S(1)}, u32[]{:S(2)}, u32[]{:S(2)}) collective-permute-start(bf16[2,256,128]{2,1,0:T(8,128)(2,1)S(1)} %get-tuple-element.31), channel_id=1, source_target_pairs={{48,0},{24,8},{0,16},{40,24},{16,32},{56,40},{32,48},{8,56},{49,1}... | collective-permute-start | bytes 393224 | tf_op jit(solution)/shard_map/ppermute | solution.py:268
  57.3 14.5 %collective-permute-start.15 = (bf16[512,128]{1,0:T(8,128)(2,1)S(1)}, bf16[512,128]{1,0:T(8,128)(2,1)S(1)}, u32[]{:S(2)}, u32[]{:S(2)}) collective-permute-start(bf16[512,128]{1,0:T(8,128)(2,1)S(1)} %get-tuple-element.38), channel_id=1, source_target_pairs={{0,32},{8,40},{16,48},{24,56},{32,0},{40,8},{48,16},{56,24},{1,33}... | collective-permute-start | bytes 393224 | tf_op jit(solution)/shard_map/ppermute | solution.py:275
  67.4 4.4 %collective-permute-start.12 = (bf16[256,128]{1,0:T(8,128)(2,1)S(1)}, bf16[256,128]{1,0:T(8,128)(2,1)S(1)}, u32[]{:S(2)}, u32[]{:S(2)}) collective-permute-start(bf16[256,128]{1,0:T(8,128)(2,1)S(1)} %get-tuple-element.33), channel_id=1, source_target_pairs={{0,4},{4,0},{1,5},{5,1},{2,6},{6,2},{3,7},{7,3},{8,12},{12,8},{9,1... | collective-permute-start | bytes 196616 | tf_op jit(solution)/shard_map/ppermute | solution.py:277

commit v4 on v3

--- a/solution.py
+++ b/solution.py
@@ -94,15 +94,21 @@
     return dot(p.astype(BF16), g), dot(ds, q), dot(kt, ds)
 
 
-def grad_kernel(turn, info_ref, *refs):
-    q_refs, y_ref, refs = refs[:4], refs[4], refs[5:]
-    if turn > 0:
-        dqin_ref, refs = refs[0], refs[1:]
-    if turn < 3:
-        dq_ref, dkv_ref, dv_acc, dk_acc = refs
-    else:
-        kept_ref, back_ref, refs = refs[0], refs[1], refs[2:]
-        dq_refs, (dkv_ref, sum_ref, dv_acc, dk_acc) = refs[:4], refs[4:]
+def grad_kernel(turn, groups, first, ends, info_ref, *refs):
+    refs = list(refs)
+
+    def take(count):
+        taken = refs[:count]
+        del refs[:count]
+        return taken
+
+    q_refs, (y_ref,) = take(len(groups)), take(1)
+    dqin_refs = take(0 if first else len(groups))
+    (dkvin_ref,) = take(1) if ends == "close" else (None,)
+    kept_ref, back_ref = take(2) if ends == "last" else (None, None)
+    dq_refs, (dkv_ref,) = take(len(groups)), take(1)
+    (sum_ref,) = take(1) if ends == "last" else (None,)
+    dv_acc, dk_acc = refs
     y, z, x = place(info_ref)
     y_at = ring(y + Y_FROM[turn], 4)
     z_at = (z, ring(z + 7, 8), ring(z + 1, 8), ring(z + jnp.where(lax.rem(z, 2) == 0, 2, 6), 8))
@@ -119,18 +125,17 @@
         dv_acc[rows] = dv if fresh else dv_acc[rows] + dv
         dk_acc[rows] = dk if fresh else dk_acc[rows] + dk
 
-    for pair in range(2):
-        chunks = [(s, a) for s in (2 * pair, 2 * pair + 1) for a in range(2)]
+    for turn_at, (group, q_ref) in enumerate(zip(groups, q_refs)):
 
         def rows(at):
-            return jnp.concatenate([q_refs[s][a, at : at + BLK, :] for s, a in chunks], 0)
-
-        stats = [q_refs[s][a, 4 * BLK :, :].astype(F32) for s, a in chunks]
+            return jnp.concatenate([q_ref[s, at : at + BLK, :] for s in range(4)], 0)
+
+        stats = [q_ref[s, 4 * BLK :, :].astype(F32) for s in range(4)]
         lse_low, lse_high, delta_low, delta_high = (
             jnp.concatenate([st[r : r + 1, :] for st in stats], 1) * (LOG2E if r < 2 else 1.0) for r in range(4)
         )
-        low_i = [low_block(info_ref, device_row(y, z_at[s], 1 - x if a else x))[0] for s, a in chunks]
-        own = turn == 0 and pair == 0
+        low_i = [low_block(info_ref, device_row(y, z_at[s], 1 - x if group else x))[0] for s in range(4)]
+        own = turn == 0 and group == 0
 
         def hide(j, low):
             parts = []
@@ -141,7 +146,7 @@
             return jnp.concatenate(parts, 1)
 
         q_low, q_high, g_low, g_high = (rows(b * BLK) for b in range(4))
-        fresh = pair == 0
+        fresh = turn_at == 0
         dv, dk, dq_high = tile(k_low, v_low, kt_low, q_high, g_high, [lse_high] * 2, delta_high)
         add(0, dv, dk, fresh)
         lses = [lse_high + hide(j, False) for j in range(2)]
@@ -151,23 +156,25 @@
         lses = [lse_low + hide(j, True) for j in range(2)]
         dv, dk, dq_low = tile(k_low, v_low, kt_low, q_low, g_low, lses, delta_low, own)
         add(0, dv, dk, False)
-        columns = slice(pair * 4 * BLK, (pair + 1) * 4 * BLK)
+        ref = dq_refs[turn_at]
         for b, dq in ((0, dq_low), (1, dq_high)):
-            if turn > 0:
-                dq = dqin_ref[b, :, columns] + dq
-            if turn < 3:
-                dq_ref[b, :, columns] = dq
+            if not first:
+                dq = dqin_refs[turn_at][b] + dq
+            if ends == "last":
+                for s in range(4):
+                    ref[s, b * BLK : (b + 1) * BLK, :] = dq[:, s * BLK : (s + 1) * BLK].T.astype(ref.dtype)
             else:
-                for n, (s, a) in enumerate(chunks):
-                    ref = dq_refs[s]
-                    ref[a, b * BLK : (b + 1) * BLK, :] = dq[:, n * BLK : (n + 1) * BLK].T.astype(ref.dtype)
+                ref[b] = dq
 
     for j in range(2):
         for b in range(2):
             source = slice((2 * b + j) * BLK, (2 * b + j + 1) * BLK)
-            dkv_ref[j, b * BLK : (b + 1) * BLK, :] = dk_acc[source].astype(dkv_ref.dtype)
-            dkv_ref[j, (2 + b) * BLK : (3 + b) * BLK, :] = dv_acc[source].astype(dkv_ref.dtype)
-    if turn == 3:
+            for at, part in ((b, dk_acc[source]), (2 + b, dv_acc[source])):
+                rows = slice(at * BLK, (at + 1) * BLK)
+                if ends == "close":
+                    part = dkvin_ref[j, rows, :] + part
+                dkv_ref[j, rows, :] = part.astype(dkv_ref.dtype)
+    if ends == "last":
         sum_ref[...] = kept_ref[...] + back_ref[...].astype(F32)
 
 
@@ -180,18 +187,25 @@
         out_ref[...] = total.astype(out_ref.dtype)
 
 
-def last_kernel(info_ref, dq_ref, dqx_ref, dkv_ref, dkvz_ref, q_ref, k_ref, v_ref):
+def cross_kernel(own_ref, back_ref, keep_ref, *send_refs):
+    for s, out_ref in enumerate((keep_ref, *send_refs)):
+        out_ref[...] = (own_ref[s] + back_ref[s].astype(F32)).astype(out_ref.dtype)
+
+
+def last_kernel(info_ref, dq_ref, dqa_ref, dqb_ref, dqc_ref, dkv_ref, dkvz_ref, q_ref, k_ref, v_ref):
     _, swapped = low_block(info_ref, device_row(*place(info_ref)))
     for part in range(2):
         to = pl.multiple_of(jnp.where(swapped, (1 - part) * BLK, part * BLK), BLK)
-        at = part * BLK
-
-        def total(ref, other, start):
-            return ref[start : start + BLK, :] + other[start : start + BLK, :].astype(F32)
-
-        q_ref[pl.ds(to, BLK), :] = (total(dq_ref, dqx_ref, at) * FACTOR).astype(BF16)
-        k_ref[pl.ds(to, BLK), :] = (total(dkv_ref, dkvz_ref, at) * FACTOR).astype(BF16)
-        v_ref[pl.ds(to, BLK), :] = total(dkv_ref, dkvz_ref, 2 * BLK + at).astype(BF16)
+
+        def total(ref, others, at):
+            out = ref[at : at + BLK, :]
+            for other in others:
+                out += other[at : at + BLK, :].astype(F32)
+            return out
+
+        q_ref[pl.ds(to, BLK), :] = (total(dq_ref, (dqa_ref, dqb_ref, dqc_ref), part * BLK) * FACTOR).astype(BF16)
+        k_ref[pl.ds(to, BLK), :] = (total(dkv_ref, (dkvz_ref,), part * BLK) * FACTOR).astype(BF16)
+        v_ref[pl.ds(to, BLK), :] = total(dkv_ref, (dkvz_ref,), (2 + part) * BLK).astype(BF16)
 
 
 def z_step(step):
@@ -236,47 +250,54 @@
         in_specs=[pl.BlockSpec(memory_space=pltpu.HBM)] * len(operands),
         vmem_limit=PREP_VMEM,
     )
-    q0 = jnp.stack([mine_q, lax.ppermute(mine_q, "kx", X_SWAP)])
-    k0 = jnp.stack([mine_k, lax.ppermute(mine_k, "kz", z_step(4))])
-    q_sets = [q0] + [lax.ppermute(q0, "kz", p) for p in (z_step(1), z_step(-1), Z_PAIRS)]
+    other_k = lax.ppermute(mine_k, "kz", z_step(4))
+    arrived = [lax.ppermute(mine_q, "kz", p) for p in (z_step(1), z_step(-1), Z_PAIRS)]
+    q_mine = jnp.pad(mine_q[None], ((0, 3), (0, 0), (0, 0)))
+    for s, part in enumerate(arrived):
+        q_mine = lax.dynamic_update_slice(q_mine, part[None], (s + 1, 0, 0))
+    q_mine, other_k = lax.optimization_barrier((q_mine, other_k))
+    k0 = jnp.stack([mine_k, other_k])
+    q_sets = [q_mine, lax.ppermute(q_mine, "kx", X_SWAP)]
     k_sets = [k0] + [lax.ppermute(k0, "pb", y_step(-s)) for s in Y_FROM[1:]]
 
     acc = pltpu.VMEM((4 * BLK, DIM), F32)
-    dq_acc = ((2, DIM, 8 * BLK), F32)
+    dq_acc = ((2, DIM, 4 * BLK), F32)
     dkv_acc = ((2, K_ROWS, DIM), F32)
-    cost = pl.CostEstimate(flops=16 * 2 * 5 * 4 * BLK**3 // 2, bytes_accessed=1 << 20, transcendentals=0)
-    back = []
-    for turn in range(4):
-        operands = q_sets + [k_sets[turn]] + ([dq] if turn else [])
-        outs = [dq_acc, dkv_acc if turn == 0 else ((2, K_ROWS, DIM), BF16)]
-        options = dict(input_output_aliases={6: 0}) if turn else {}
-        if turn == 3:
-            operands += [kept, back[0]]
-            outs = [((2, 2 * BLK, DIM), F32 if s == 0 else BF16) for s in range(4)] + [outs[1], dkv_acc]
-            options = {}
-        kernel = functools.partial(grad_kernel, turn)
-        *dq, part = call(kernel, outs, operands, info, [acc, acc], cost_estimate=cost, **options)
-        if turn == 0:
-            (dq,), kept = dq, part
-        elif turn < 3:
-            (dq,) = dq
-            back.append(lax.ppermute(part, "pb", y_step(Y_FROM[turn])))
-        else:
-            *dq, last = dq
-            kept = part
-            back.append(lax.ppermute(last, "pb", y_step(Y_FROM[turn])))
-    dq_back = [lax.ppermute(dq[t], "kz", p) for t, p in ((1, z_step(-1)), (2, z_step(1)), (3, Z_BACK))]
-
-    def meet(own, partners):
-        shape = own.shape[1:]
-        return call(meet_kernel, [(shape, F32), (shape, BF16)], [own] + partners)
-
-    dkv_keep, dkv_send = meet(kept, back[1:])
-    dkv_last = lax.ppermute(dkv_send, "kz", z_step(4))
-    dq_keep, dq_send = meet(dq[0], dq_back)
-    dq_last = lax.ppermute(dq_send, "kx", X_SWAP)
-    grads = [((2 * BLK, DIM), BF16)] * 3
-    return tuple(call(last_kernel, grads, (dq_keep, dq_last, dkv_keep, dkv_last), info))
+    dkv_out = ((2, K_ROWS, DIM), BF16)
+
+    def grad(turn, groups, first, ends, operands, outs):
+        flops = 10 * len(groups) * 3 * (2 * BLK) * (4 * BLK) * DIM
+        return call(
+            functools.partial(grad_kernel, turn, groups, first, ends),
+            outs,
+            [q_sets[g] for g in groups] + [k_sets[turn]] + operands,
+            info,
+            [acc, acc],
+            cost_estimate=pl.CostEstimate(flops=flops, bytes_accessed=1 << 20, transcendentals=0),
+        )
+
+    def send_back(turn, part):
+        return lax.ppermute(part, "pb", y_step(Y_FROM[turn]))
+
+    dq0, kept = grad(0, (0,), True, "", [], [dq_acc, dkv_acc])
+    dq1, kept = grad(0, (1,), True, "close", [kept], [dq_acc, dkv_acc])
+    *dqs, part = grad(1, (0, 1), False, "", [dq0, dq1], [dq_acc, dq_acc, dkv_out])
+    back1 = send_back(1, part)
+    *dqs, part = grad(2, (0, 1), False, "", dqs, [dq_acc, dq_acc, dkv_out])
+    back2 = send_back(2, part)
+    dq_out = (4, 2 * BLK, DIM)
+    dq_keep, dq_send, part, kept = grad(
+        3, (0, 1), False, "last", dqs + [kept, back1], [(dq_out, F32), (dq_out, BF16), dkv_out, dkv_acc]
+    )
+    back3 = send_back(3, part)
+    dq_back = lax.ppermute(dq_send, "kx", X_SWAP)
+    chunk = (2 * BLK, DIM)
+    dq_keep, *dq_send = call(cross_kernel, [(chunk, F32)] + [(chunk, BF16)] * 3, (dq_keep, dq_back))
+    dq_back = [lax.ppermute(d, "kz", p) for d, p in zip(dq_send, (z_step(-1), z_step(1), Z_BACK))]
+    shape = (K_ROWS, DIM)
+    dkv_keep, dkv_send = call(meet_kernel, [(shape, F32), (shape, BF16)], [kept, back2, back3])
+    dkv_back = lax.ppermute(dkv_send, "kz", z_step(4))
+    return tuple(call(last_kernel, [(chunk, BF16)] * 3, (dq_keep, *dq_back, dkv_keep, dkv_back), info))
 
 
 def solution(mesh):

time: 73.1 us -> 76.6 us (1.048)
  waiting for transfers between devices: 18.9 us -> 21.6 us
  local copies, waits for them, and re-layouts: 0.01 us -> 1.03 us
  other arithmetic: 1.68 us -> 0.7 us
    ppermute x13, waiting for transfers between devices: 18.8 us -> 21.6 us  [the longest x3 6.48 us: send_back(): return lax.ppermute(part, 'pb', y_step(Y_FROM[turn]))]
    another operation x2 -> x1, other arithmetic: 0.99 us -> 0.03 us  [body(): k0 = jnp.stack([mine_k, other_k])]
    pad x0 -> x1, local copies, waits for them, and re-layouts: none -> 0.97 us  [body(): q_mine = jnp.pad(mine_q[None], ((0, 3), (0, 0), (0, 0)))]
    pallas_call x8 -> x9, Pallas kernels: 14.4 us -> 15 us  [call(): pl.pallas_call(kernel, out_shape=[jax.ShapeDtypeStruct(s, t) for s, t in...]
  transfers between devices with their start and end apart: 16 -> 16, of which waited for: 6 -> 7; matrix products, arithmetic and copies ran while one was open for 1% -> 1% of each run, Pallas kernels for 15% -> 15%
where the time goes in v4:
time: 76.6 us; the launch traced here: 76.2 us
  starting transfers between devices  37.1 us (48%)
  waiting for transfers between devices  21.6 us (28%)
  Pallas kernels  15 us (20%)
  local copies, waits for them, and re-layouts  1.03 us (1%)
  between operations  0.77 us (1%)
    pallas_call x9, Pallas kernels, call(): pl.pallas_call(kernel, out_shape=[jax.ShapeDtypeStruct(s, t) for s, t in...  15 us
    ppermute x3, starting transfers between devices, send_back(): return lax.ppermute(part, 'pb', y_step(Y_FROM[turn]))  8.1 us
    ppermute x3, starting transfers between devices, body(): lax.ppermute(d, 'kz', p)  7.96 us
    ppermute x3, starting transfers between devices, body(): lax.ppermute(mine_q, 'kz', p)  7.4 us
    ppermute x3, starting transfers between devices, body(): k_sets = [k0] + [lax.ppermute(k0, 'pb', y_step(-s)) for s in Y_FROM[1:]]  6.53 us
    ppermute x3, waiting for transfers between devices, send_back(): return lax.ppermute(part, 'pb', y_step(Y_FROM[turn]))  6.48 us
    ppermute x1, starting transfers between devices, body(): other_k = lax.ppermute(mine_k, 'kz', z_step(4))  4.58 us
    ppermute x3, waiting for transfers between devices, body(): lax.ppermute(mine_q, 'kz', p)  4.33 us
  transfers between devices with their start and end apart: 16, of which 7 were waited for; matrix products, arithmetic and copies ran while one was open for 1% of the time, Pallas kernels for 15%

profile of v4, /device:TPU:4, one launch (start us, length us, event | category | flops | bytes accessed | tf_op | source)
XLA Modules:
  0.0 76.2 jit_solution(7451978665814375814)
XLA Ops:
  1.2 2.5 %shard_map.94 = (bf16[528,128]{1,0:T(8,128)(2,1)}, bf16[512,128]{1,0:T(8,128)(2,1)}) custom-call(s32[3]{0:T(128)} %pad_add_fusion.1.where_ref, s32[128]{0:T(128)} %refs_0_.1, bf16[256,128]{1,0:T(8,128)(2,1)} %refs_1_.1, bf16[256,128]{1,0:T(8,128)(2,1)} %refs_2_.1, bf16[256,128]{1,0:T(8,128)(2,1)} %refs_3_.1, bf16[256,128]{1,0:T(8,128)(2,1)} %refs_4_.1, ...), custom_call_target="tpu_custom_call" | custom-call | tf_op jit(solution)/shard_map/pallas_call | solution.py:228
  3.7 2.0 %collective-permute-start = (bf16[528,128]{1,0:T(8,128)(2,1)}, bf16[528,128]{1,0:T(8,128)(2,1)S(1)}, u32[]{:S(2)}, u32[]{:S(2)}) collective-permute-start(bf16[528,128]{1,0:T(8,128)(2,1)} %get-tuple-element.27), channel_id=1, source_target_pairs={{0,8},{8,16},{16,24},{24,32},{32,40},{40,48},{48,56},{56,0},{1,9},... | collective-permute-start | bytes 405512 | tf_op jit(solution)/shard_map/ppermute | solution.py:254
  5.7 5.4 %collective-permute-start.2 = (bf16[528,128]{1,0:T(8,128)(2,1)}, bf16[528,128]{1,0:T(8,128)(2,1)S(1)}, u32[]{:S(2)}, u32[]{:S(2)}) collective-permute-start(bf16[528,128]{1,0:T(8,128)(2,1)} %get-tuple-element.27), channel_id=1, source_target_pairs={{0,48},{8,24},{16,0},{24,40},{32,16},{40,56},{48,32},{56,8},{1,49}... | collective-permute-start | bytes 405512 | tf_op jit(solution)/shard_map/ppermute | solution.py:254
  11.1 4.6 %collective-permute-start.3 = (bf16[512,128]{1,0:T(8,128)(2,1)}, bf16[512,128]{1,0:T(8,128)(2,1)S(1)}, u32[]{:S(2)}, u32[]{:S(2)}) collective-permute-start(bf16[512,128]{1,0:T(8,128)(2,1)} %get-tuple-element.28), channel_id=1, source_target_pairs={{0,32},{8,40},{16,48},{24,56},{32,0},{40,8},{48,16},{56,24},{1,33}... | collective-permute-start | bytes 393224 | tf_op jit(solution)/shard_map/ppermute | solution.py:253
  16.7 4.3 %collective-permute-done.1 = bf16[528,128]{1,0:T(8,128)(2,1)S(1)} collective-permute-done((bf16[528,128]{1,0:T(8,128)(2,1)}, bf16[528,128]{1,0:T(8,128)(2,1)S(1)}, u32[]{:S(2)}, u32[]{:S(2)}) %collective-permute-start.1) | collective-permute-done | bytes 135200 | tf_op jit(solution)/shard_map/ppermute | solution.py:254
  21.1 4.0 %collective-permute-done.3 = bf16[512,128]{1,0:T(8,128)(2,1)S(1)} collective-permute-done((bf16[512,128]{1,0:T(8,128)(2,1)}, bf16[512,128]{1,0:T(8,128)(2,1)S(1)}, u32[]{:S(2)}, u32[]{:S(2)}) %collective-permute-start.3) | collective-permute-done | bytes 131104 | tf_op jit(solution)/shard_map/ppermute | solution.py:253
  25.1 1.2 %collective-permute-start.4 = (bf16[4,528,128]{2,1,0:T(8,128)(2,1)S(1)}, bf16[4,528,128]{2,1,0:T(8,128)(2,1)S(1)}, u32[]{:S(2)}, u32[]{:S(2)}) collective-permute-start(bf16[4,528,128]{2,1,0:T(8,128)(2,1)S(1)} %bitcast_dynamic-update-slice_fusion.refs_0_), channel_id=1, source_target_pairs={{0,4},{4,0},{1,5},{5,1},{2,6},{6,2},{3,7},{7,3},{8,12},{12,8},{9,1... | collective-permute-start | bytes 1622024 | tf_op jit(solution)/shard_map/ppermute | solution.py:260
  26.3 3.3 %collective-permute-start.7 = (bf16[2,512,128]{2,1,0:T(8,128)(2,1)S(1)}, bf16[2,512,128]{2,1,0:T(8,128)(2,1)S(1)}, u32[]{:S(2)}, u32[]{:S(2)}) collective-permute-start(bf16[2,512,128]{2,1,0:T(8,128)(2,1)S(1)} %pad_maximum_fusion.refs_1_), channel_id=1, source_target_pairs={{0,128},{64,192},{128,0},{192,64},{1,129},{65,193},{129,1},{193,65... | collective-permute-start | bytes 786440 | tf_op jit(solution)/shard_map/ppermute | solution.py:261
  30.3 2.6 %collective-permute-start.5 = (bf16[2,512,128]{2,1,0:T(8,128)(2,1)S(1)}, bf16[2,512,128]{2,1,0:T(8,128)(2,1)S(1)}, u32[]{:S(2)}, u32[]{:S(2)}) collective-permute-start(bf16[2,512,128]{2,1,0:T(8,128)(2,1)S(1)} %pad_maximum_fusion.refs_1_), channel_id=1, source_target_pairs={{0,192},{64,0},{128,64},{192,128},{1,193},{65,1},{129,65},{193,129... | collective-permute-start | bytes 786440 | tf_op jit(solution)/shard_map/ppermute | solution.py:261
  32.9 1.6 %shard_map.95 = (f32[2,128,512]{2,1,0:T(8,128)S(1)}, f32[2,512,128]{2,1,0:T(8,128)S(1)}) custom-call(s32[131]{0:T(256)S(1)} %pad_add_fusion.info_ref, bf16[4,528,128]{2,1,0:T(8,128)(2,1)S(1)} %bitcast_dynamic-update-slice_fusion.refs_0_, bf16[2,512,128]{2,1,0:T(8,128)(2,1)S(1)} %pad_maximum_fusion.refs_1_), custom_call_target="tpu_custom_call" | custom-call | flops 503316480 | bytes 1048576 | tf_op jit(solution)/shard_map/pallas_call | solution.py:228
  34.5 2.7 %collective-permute-done.4.refs_0_.refs_1_ = bf16[4,528,128]{2,1,0:T(8,128)(2,1)S(1)} collective-permute-done((bf16[4,528,128]{2,1,0:T(8,128)(2,1)S(1)}, bf16[4,528,128]{2,1,0:T(8,128)(2,1)S(1)}, u32[]{:S(2)}, u32[]{:S(2)}) %collective-permute-start.4) | collective-permute-done | bytes 540704 | tf_op jit(solution)/shard_map/ppermute | solution.py:260
  37.3 1.6 %shard_map.96 = (f32[2,128,512]{2,1,0:T(8,128)S(1)}, f32[2,512,128]{2,1,0:T(8,128)S(1)}) custom-call(s32[131]{0:T(256)S(1)} %pad_add_fusion.info_ref, bf16[4,528,128]{2,1,0:T(8,128)(2,1)S(1)} %collective-permute-done.4.refs_0_.refs_1_, bf16[2,512,128]{2,1,0:T(8,128)(2,1)S(1)} %pad_maximum_fusion.refs_1_, f32[2,512,128]{2,1,0:T(8,128)S(1)} %get-tuple-element.32.refs_2_), custom_call_target="tpu_custom_call" | custom-call | flops 503316480 | bytes 1048576 | tf_op jit(solution)/shard_map/pallas_call | solution.py:228
  38.9 2.6 %shard_map.97 = (f32[2,128,512]{2,1,0:T(8,128)S(1)}, f32[2,128,512]{2,1,0:T(8,128)S(1)}, bf16[2,512,128]{2,1,0:T(8,128)(2,1)S(1)}) custom-call(s32[131]{0:T(256)S(1)} %pad_add_fusion.info_ref, bf16[4,528,128]{2,1,0:T(8,128)(2,1)S(1)} %bitcast_dynamic-update-slice_fusion.refs_0_, bf16[4,528,128]{2,1,0:T(8,128)(2,1)S(1)} %collective-permute-done.4.refs_0_.refs_1_, ...), custom_call_target="tpu_custom_call" | custom-call | flops 1006632960 | bytes 1048576 | tf_op jit(solution)/shard_map/pallas_call | solution.py:228
  41.5 3.5 %collective-permute-start.8 = (bf16[2,512,128]{2,1,0:T(8,128)(2,1)S(1)}, bf16[2,512,128]{2,1,0:T(8,128)(2,1)S(1)}, u32[]{:S(2)}, u32[]{:S(2)}) collective-permute-start(bf16[2,512,128]{2,1,0:T(8,128)(2,1)S(1)} %get-tuple-element.39), channel_id=1, source_target_pairs={{0,128},{64,192},{128,0},{192,64},{1,129},{65,193},{129,1},{193,65... | collective-permute-start | bytes 786440 | tf_op jit(solution)/shard_map/ppermute | solution.py:280
  45.0 2.6 %shard_map.98 = (f32[2,128,512]{2,1,0:T(8,128)S(1)}, f32[2,128,512]{2,1,0:T(8,128)S(1)}, bf16[2,512,128]{2,1,0:T(8,128)(2,1)S(1)}) custom-call(s32[131]{0:T(256)S(1)} %pad_add_fusion.info_ref, bf16[4,528,128]{2,1,0:T(8,128)(2,1)S(1)} %bitcast_dynamic-update-slice_fusion.refs_0_, bf16[4,528,128]{2,1,0:T(8,128)(2,1)S(1)} %collective-permute-done.4.refs_0_.refs_1_, ...), custom_call_target="tpu_custom_call" | custom-call | flops 1006632960 | bytes 1048576 | tf_op jit(solution)/shard_map/pallas_call | solution.py:228
  47.5 1.1 %collective-permute-start.13 = (bf16[2,512,128]{2,1,0:T(8,128)(2,1)S(1)}, bf16[2,512,128]{2,1,0:T(8,128)(2,1)S(1)}, u32[]{:S(2)}, u32[]{:S(2)}) collective-permute-start(bf16[2,512,128]{2,1,0:T(8,128)(2,1)S(1)} %get-tuple-element.47), channel_id=1, source_target_pairs={{0,192},{64,0},{128,64},{192,128},{1,193},{65,1},{129,65},{193,129... | collective-permute-start | bytes 786440 | tf_op jit(solution)/shard_map/ppermute | solution.py:280
  49.6 2.7 %shard_map.99 = (f32[4,256,128]{2,1,0:T(8,128)S(1)}, bf16[4,256,128]{2,1,0:T(8,128)(2,1)S(1)}, bf16[2,512,128]{2,1,0:T(8,128)(2,1)S(1)}, f32[2,512,128]{2,1,0:T(8,128)S(1)}) custom-call(s32[131]{0:T(256)S(1)} %pad_add_fusion.info_ref, bf16[4,528,128]{2,1,0:T(8,128)(2,1)S(1)} %bitcast_dynamic-update-slice_fusion.refs_0_, ...), custom_call_target="tpu_custom_call" | custom-call | flops 1006632960 | bytes 1048576 | tf_op jit(solution)/shard_map/pallas_call | solution.py:228
  52.4 3.5 %collective-permute-start.14 = (bf16[2,512,128]{2,1,0:T(8,128)(2,1)S(1)}, bf16[2,512,128]{2,1,0:T(8,128)(2,1)S(1)}, u32[]{:S(2)}, u32[]{:S(2)}) collective-permute-start(bf16[2,512,128]{2,1,0:T(8,128)(2,1)S(1)} %get-tuple-element.48), channel_id=1, source_target_pairs={{0,64},{64,128},{128,192},{192,0},{1,65},{65,129},{129,193},{193,1... | collective-permute-start | bytes 786440 | tf_op jit(solution)/shard_map/ppermute | solution.py:280
  55.9 1.2 %collective-permute-start.9 = (bf16[4,256,128]{2,1,0:T(8,128)(2,1)S(1)}, bf16[4,256,128]{2,1,0:T(8,128)(2,1)S(1)}, u32[]{:S(2)}, u32[]{:S(2)}) collective-permute-start(bf16[4,256,128]{2,1,0:T(8,128)(2,1)S(1)} %get-tuple-element.41), channel_id=1, source_target_pairs={{0,4},{4,0},{1,5},{5,1},{2,6},{6,2},{3,7},{7,3},{8,12},{12,8},{9,1... | collective-permute-start | bytes 786440 | tf_op jit(solution)/shard_map/ppermute | solution.py:293
  57.1 5.5 %collective-permute-done.14.refs_1_ = bf16[2,512,128]{2,1,0:T(8,128)(2,1)S(1)} collective-permute-done((bf16[2,512,128]{2,1,0:T(8,128)(2,1)S(1)}, bf16[2,512,128]{2,1,0:T(8,128)(2,1)S(1)}, u32[]{:S(2)}, u32[]{:S(2)}) %collective-permute-start.14) | collective-permute-done | bytes 262176 | tf_op jit(solution)/shard_map/ppermute | solution.py:280
  62.9 5.7 %collective-permute-start.10 = (bf16[256,128]{1,0:T(8,128)(2,1)S(1)}, bf16[256,128]{1,0:T(8,128)(2,1)S(1)}, u32[]{:S(2)}, u32[]{:S(2)}) collective-permute-start(bf16[256,128]{1,0:T(8,128)(2,1)S(1)} %get-tuple-element.43), channel_id=1, source_target_pairs={{0,56},{8,0},{16,8},{24,16},{32,24},{40,32},{48,40},{56,48},{1,57}... | collective-permute-start | bytes 196616 | tf_op jit(solution)/shard_map/ppermute | solution.py:296
  68.6 2.3 %collective-permute-start.12 = (bf16[256,128]{1,0:T(8,128)(2,1)S(1)}, bf16[256,128]{1,0:T(8,128)(2,1)S(1)}, u32[]{:S(2)}, u32[]{:S(2)}) collective-permute-start(bf16[256,128]{1,0:T(8,128)(2,1)S(1)} %get-tuple-element.45), channel_id=1, source_target_pairs={{48,0},{24,8},{0,16},{40,24},{16,32},{56,40},{32,48},{8,56},{49,1}... | collective-permute-start | bytes 196616 | tf_op jit(solution)/shard_map/ppermute | solution.py:296
  70.8 3.2 %collective-permute-done.11.dqb_ref = bf16[256,128]{1,0:T(8,128)(2,1)S(1)} collective-permute-done((bf16[256,128]{1,0:T(8,128)(2,1)S(1)}, bf16[256,128]{1,0:T(8,128)(2,1)S(1)}, u32[]{:S(2)}, u32[]{:S(2)}) %collective-permute-start.11) | collective-permute-done | bytes 65568 | tf_op jit(solution)/shard_map/ppermute | solution.py:296
  74.9 1.3 %shard_map.102 = (bf16[256,128]{1,0:T(8,128)(2,1)}, bf16[256,128]{1,0:T(8,128)(2,1)}, bf16[256,128]{1,0:T(8,128)(2,1)}) custom-call(s32[131]{0:T(256)S(1)} %pad_add_fusion.info_ref, f32[256,128]{1,0:T(8,128)S(1)} %get-tuple-element.42.dq_ref, bf16[256,128]{1,0:T(8,128)(2,1)S(1)} %collective-permute-done.10.dqa_ref, ...), custom_call_target="tpu_custom_call" | custom-call | tf_op jit(solution)/shard_map/pallas_call | solution.py:228
  (28 shorter events, 4.6 us)
Async XLA Ops:
  3.7 13.0 %collective-permute-start = (bf16[528,128]{1,0:T(8,128)(2,1)}, bf16[528,128]{1,0:T(8,128)(2,1)S(1)}, u32[]{:S(2)}, u32[]{:S(2)}) collective-permute-start(bf16[528,128]{1,0:T(8,128)(2,1)} %get-tuple-element.27), channel_id=1, source_target_pairs={{0,8},{8,16},{16,24},{24,32},{32,40},{40,48},{48,56},{56,0},{1,9},... | collective-permute-start | bytes 405512 | tf_op jit(solution)/shard_map/ppermute | solution.py:254
  5.7 15.4 %collective-permute-start.2 = (bf16[528,128]{1,0:T(8,128)(2,1)}, bf16[528,128]{1,0:T(8,128)(2,1)S(1)}, u32[]{:S(2)}, u32[]{:S(2)}) collective-permute-start(bf16[528,128]{1,0:T(8,128)(2,1)} %get-tuple-element.27), channel_id=1, source_target_pairs={{0,48},{8,24},{16,0},{24,40},{32,16},{40,56},{48,32},{56,8},{1,49}... | collective-permute-start | bytes 405512 | tf_op jit(solution)/shard_map/ppermute | solution.py:254
  11.1 9.9 %collective-permute-start.1 = (bf16[528,128]{1,0:T(8,128)(2,1)}, bf16[528,128]{1,0:T(8,128)(2,1)S(1)}, u32[]{:S(2)}, u32[]{:S(2)}) collective-permute-start(bf16[528,128]{1,0:T(8,128)(2,1)} %get-tuple-element.27), channel_id=1, source_target_pairs={{0,56},{8,0},{16,8},{24,16},{32,24},{40,32},{48,40},{56,48},{1,57}... | collective-permute-start | bytes 405512 | tf_op jit(solution)/shard_map/ppermute | solution.py:254
  11.1 14.0 %collective-permute-start.3 = (bf16[512,128]{1,0:T(8,128)(2,1)}, bf16[512,128]{1,0:T(8,128)(2,1)S(1)}, u32[]{:S(2)}, u32[]{:S(2)}) collective-permute-start(bf16[512,128]{1,0:T(8,128)(2,1)} %get-tuple-element.28), channel_id=1, source_target_pairs={{0,32},{8,40},{16,48},{24,56},{32,0},{40,8},{48,16},{56,24},{1,33}... | collective-permute-start | bytes 393224 | tf_op jit(solution)/shard_map/ppermute | solution.py:253
  21.0 5.2 %copy-start = (bf16[512,128]{1,0:T(8,128)(2,1)S(1)}, bf16[512,128]{1,0:T(8,128)(2,1)}, u32[]{:S(2)}) copy-start(bf16[512,128]{1,0:T(8,128)(2,1)} %get-tuple-element.28) | copy-start | bytes 393220
  25.1 12.2 %collective-permute-start.4 = (bf16[4,528,128]{2,1,0:T(8,128)(2,1)S(1)}, bf16[4,528,128]{2,1,0:T(8,128)(2,1)S(1)}, u32[]{:S(2)}, u32[]{:S(2)}) collective-permute-start(bf16[4,528,128]{2,1,0:T(8,128)(2,1)S(1)} %bitcast_dynamic-update-slice_fusion.refs_0_), channel_id=1, source_target_pairs={{0,4},{4,0},{1,5},{5,1},{2,6},{6,2},{3,7},{7,3},{8,12},{12,8},{9,1... | collective-permute-start | bytes 1622024 | tf_op jit(solution)/shard_map/ppermute | solution.py:260
  26.3 3.3 %copy-start.1 = (s32[128]{0:T(128)S(1)}, s32[128]{0:T(128)}, u32[]{:S(2)}) copy-start(s32[128]{0:T(128)} %refs_0_.1) | copy-start | bytes 1540
  26.3 12.6 %collective-permute-start.7 = (bf16[2,512,128]{2,1,0:T(8,128)(2,1)S(1)}, bf16[2,512,128]{2,1,0:T(8,128)(2,1)S(1)}, u32[]{:S(2)}, u32[]{:S(2)}) collective-permute-start(bf16[2,512,128]{2,1,0:T(8,128)(2,1)S(1)} %pad_maximum_fusion.refs_1_), channel_id=1, source_target_pairs={{0,128},{64,192},{128,0},{192,64},{1,129},{65,193},{129,1},{193,65... | collective-permute-start | bytes 786440 | tf_op jit(solution)/shard_map/ppermute | solution.py:261
  29.7 15.3 %collective-permute-start.6 = (bf16[2,512,128]{2,1,0:T(8,128)(2,1)S(1)}, bf16[2,512,128]{2,1,0:T(8,128)(2,1)S(1)}, u32[]{:S(2)}, u32[]{:S(2)}) collective-permute-start(bf16[2,512,128]{2,1,0:T(8,128)(2,1)S(1)} %pad_maximum_fusion.refs_1_), channel_id=1, source_target_pairs={{0,64},{64,128},{128,192},{192,0},{1,65},{65,129},{129,193},{193,1... | collective-permute-start | bytes 786440 | tf_op jit(solution)/shard_map/ppermute | solution.py:261
  30.3 18.3 %collective-permute-start.5 = (bf16[2,512,128]{2,1,0:T(8,128)(2,1)S(1)}, bf16[2,512,128]{2,1,0:T(8,128)(2,1)S(1)}, u32[]{:S(2)}, u32[]{:S(2)}) collective-permute-start(bf16[2,512,128]{2,1,0:T(8,128)(2,1)S(1)} %pad_maximum_fusion.refs_1_), channel_id=1, source_target_pairs={{0,192},{64,0},{128,64},{192,128},{1,193},{65,1},{129,65},{193,129... | collective-permute-start | bytes 786440 | tf_op jit(solution)/shard_map/ppermute | solution.py:261
  41.5 8.1 %collective-permute-start.8 = (bf16[2,512,128]{2,1,0:T(8,128)(2,1)S(1)}, bf16[2,512,128]{2,1,0:T(8,128)(2,1)S(1)}, u32[]{:S(2)}, u32[]{:S(2)}) collective-permute-start(bf16[2,512,128]{2,1,0:T(8,128)(2,1)S(1)} %get-tuple-element.39), channel_id=1, source_target_pairs={{0,128},{64,192},{128,0},{192,64},{1,129},{65,193},{129,1},{193,65... | collective-permute-start | bytes 786440 | tf_op jit(solution)/shard_map/ppermute | solution.py:280
  47.5 9.5 %collective-permute-start.13 = (bf16[2,512,128]{2,1,0:T(8,128)(2,1)S(1)}, bf16[2,512,128]{2,1,0:T(8,128)(2,1)S(1)}, u32[]{:S(2)}, u32[]{:S(2)}) collective-permute-start(bf16[2,512,128]{2,1,0:T(8,128)(2,1)S(1)} %get-tuple-element.47), channel_id=1, source_target_pairs={{0,192},{64,0},{128,64},{192,128},{1,193},{65,1},{129,65},{193,129... | collective-permute-start | bytes 786440 | tf_op jit(solution)/shard_map/ppermute | solution.py:280
  52.4 10.2 %collective-permute-start.14 = (bf16[2,512,128]{2,1,0:T(8,128)(2,1)S(1)}, bf16[2,512,128]{2,1,0:T(8,128)(2,1)S(1)}, u32[]{:S(2)}, u32[]{:S(2)}) collective-permute-start(bf16[2,512,128]{2,1,0:T(8,128)(2,1)S(1)} %get-tuple-element.48), channel_id=1, source_target_pairs={{0,64},{64,128},{128,192},{192,0},{1,65},{65,129},{129,193},{193,1... | collective-permute-start | bytes 786440 | tf_op jit(solution)/shard_map/ppermute | solution.py:280
  55.9 6.9 %collective-permute-start.9 = (bf16[4,256,128]{2,1,0:T(8,128)(2,1)S(1)}, bf16[4,256,128]{2,1,0:T(8,128)(2,1)S(1)}, u32[]{:S(2)}, u32[]{:S(2)}) collective-permute-start(bf16[4,256,128]{2,1,0:T(8,128)(2,1)S(1)} %get-tuple-element.41), channel_id=1, source_target_pairs={{0,4},{4,0},{1,5},{5,1},{2,6},{6,2},{3,7},{7,3},{8,12},{12,8},{9,1... | collective-permute-start | bytes 786440 | tf_op jit(solution)/shard_map/ppermute | solution.py:293
  62.7 12.3 %collective-permute-start.15 = (bf16[512,128]{1,0:T(8,128)(2,1)S(1)}, bf16[512,128]{1,0:T(8,128)(2,1)S(1)}, u32[]{:S(2)}, u32[]{:S(2)}) collective-permute-start(bf16[512,128]{1,0:T(8,128)(2,1)S(1)} %get-tuple-element.50), channel_id=1, source_target_pairs={{0,32},{8,40},{16,48},{24,56},{32,0},{40,8},{48,16},{56,24},{1,33}... | collective-permute-start | bytes 393224 | tf_op jit(solution)/shard_map/ppermute | solution.py:299
  62.9 8.0 %collective-permute-start.10 = (bf16[256,128]{1,0:T(8,128)(2,1)S(1)}, bf16[256,128]{1,0:T(8,128)(2,1)S(1)}, u32[]{:S(2)}, u32[]{:S(2)}) collective-permute-start(bf16[256,128]{1,0:T(8,128)(2,1)S(1)} %get-tuple-element.43), channel_id=1, source_target_pairs={{0,56},{8,0},{16,8},{24,16},{32,24},{40,32},{48,40},{56,48},{1,57}... | collective-permute-start | bytes 196616 | tf_op jit(solution)/shard_map/ppermute | solution.py:296
  68.6 5.5 %collective-permute-start.11 = (bf16[256,128]{1,0:T(8,128)(2,1)S(1)}, bf16[256,128]{1,0:T(8,128)(2,1)S(1)}, u32[]{:S(2)}, u32[]{:S(2)}) collective-permute-start(bf16[256,128]{1,0:T(8,128)(2,1)S(1)} %get-tuple-element.44), channel_id=1, source_target_pairs={{0,8},{8,16},{16,24},{24,32},{32,40},{40,48},{48,56},{56,0},{1,9},... | collective-permute-start | bytes 196616 | tf_op jit(solution)/shard_map/ppermute | solution.py:296
  68.6 6.4 %collective-permute-start.12 = (bf16[256,128]{1,0:T(8,128)(2,1)S(1)}, bf16[256,128]{1,0:T(8,128)(2,1)S(1)}, u32[]{:S(2)}, u32[]{:S(2)}) collective-permute-start(bf16[256,128]{1,0:T(8,128)(2,1)S(1)} %get-tuple-element.45), channel_id=1, source_target_pairs={{48,0},{24,8},{0,16},{40,24},{16,32},{56,40},{32,48},{8,56},{49,1}... | collective-permute-start | bytes 196616 | tf_op jit(solution)/shard_map/ppermute | solution.py:296

commit v5 on v3

v5 whole, which is shorter than its diff:
```python
import functools
import math

import jax
import jax.numpy as jnp
from jax import lax
from jax.experimental import pallas as pl
from jax.experimental.pallas import tpu as pltpu
from jax.sharding import Mesh, PartitionSpec as P

F32 = jnp.float32
BF16 = jnp.bfloat16
BLK = 128
DIM = 128
LOG2E = math.log2(math.e)
FACTOR = 1.0 / math.sqrt(DIM)
VMEM_LIMIT = 48 * 1024 * 1024
PREP_VMEM = 62 * 1024 * 1024
FLOPS = 10 * 2 * 3 * (2 * BLK) * (4 * BLK) * DIM
HIDE = 1e30
Y_FROM = (0, 2, 3, 1)
NT = (((1,), (1,)), ((), ()))
Q_ROWS = 4 * BLK + 16
K_ROWS = 4 * BLK


def dot(a, b):
    return jnp.dot(a, b, preferred_element_type=F32)


def dot_nt(a, b):
    return lax.dot_general(a, b, NT, preferred_element_type=F32)


def ring(value, size):
    return lax.rem(value + size, size)


def blocks(fold_ref, y, z, x):
    device = y * 16 + z * 2 + x
    first = fold_ref[2 * device]
    second = fold_ref[2 * device + 1]
    low = pl.multiple_of(jnp.where(second < first, BLK, 0), BLK)
    high = pl.multiple_of(jnp.where(second < first, 0, BLK), BLK)
    return jnp.minimum(first, second), (low, high)


def prep_kernel(q_ref, k_ref, v_ref, o_ref, g_ref, lse_ref, qout_ref, kout_ref, g_buf, o_buf, lse_buf, stats_buf, sems):
    half = 2 * BLK
    loads = [
        pltpu.make_async_copy(s, d, sems.at[n])
        for n, (s, d) in enumerate(((g_ref, g_buf), (o_ref, o_buf), (lse_ref, lse_buf)))
    ]
    moves = [
        pltpu.make_async_copy(s, d, sems.at[3 + n])
        for n, (s, d) in enumerate(
            (
                (q_ref, qout_ref.at[:half]),
                (g_ref, qout_ref.at[half : 2 * half]),
                (k_ref, kout_ref.at[:half]),
                (v_ref, kout_ref.at[half:]),
            )
        )
    ]
    for copy in loads + moves:
        copy.start()
    for copy in loads:
        copy.wait()
    lse = lse_buf[...].astype(F32)
    rows = [lse[:, :BLK], lse[:, BLK:]]
    for start in (0, BLK):
        prod = g_buf[start : start + BLK, :].astype(F32) * o_buf[start : start + BLK, :].astype(F32)
        rows.append(jnp.sum(prod.T, axis=0, keepdims=True))
    stats_buf[...] = jnp.concatenate(rows + [jnp.zeros((12, DIM), F32)], axis=0).astype(BF16)
    moves.append(pltpu.make_async_copy(stats_buf, qout_ref.at[2 * half :], sems.at[7]))
    moves[-1].start()
    for copy in moves:
        copy.wait()


def tile(k, v, kt, q, g, lses, delta, diagonal=None):
    s = dot_nt(k, q)
    probs = []
    for b, lse in enumerate(lses):
        p = jnp.exp2(s[b * BLK : (b + 1) * BLK] * (FACTOR * LOG2E) - lse)
        if b == diagonal:
            shape = (BLK, BLK)
            seen = lax.broadcasted_iota(jnp.int32, shape, 0) <= lax.broadcasted_iota(jnp.int32, shape, 1)
            p = jnp.concatenate([jnp.where(seen, p[:, :BLK], 0.0), p[:, BLK:]], 1)
        probs.append(p)
    p = jnp.concatenate(probs, 0)
    dp = dot_nt(v, g)
    ds = (p * (dp - delta)).astype(BF16)
    return dot(p.astype(BF16), g), dot(ds, q), dot(kt, ds)


def grad_kernel(turn, js, first, final, fold_ref, *refs):
    q_refs, y_ref, refs = refs[:4], refs[4], refs[5:]
    if not first:
        dqin_ref, refs = refs[0], refs[1:]
    if final:
        dq_refs, (dkv_ref, dv_acc, dk_acc) = refs[:4], refs[4:]
    else:
        dq_ref, dkv_ref, dv_acc, dk_acc = refs
    y, z, x = (lax.axis_index(name) for name in ("pb", "kz", "kx"))
    y_at = ring(y + Y_FROM[turn], 4)
    z_at = (z, ring(z + 7, 8), ring(z + 1, 8), ring(z + jnp.where(lax.rem(z, 2) == 0, 2, 6), 8))
    low_j, starts_j = zip(*(blocks(fold_ref, y_at, ring(z + 4 * j, 8), x) for j in js))
    count = len(js)
    half = count * BLK

    def keys(array):
        parts = [
            y_ref[n, pl.ds(array * 2 * BLK + starts_j[n][b], BLK), :] for b in range(2) for n in range(count)
        ]
        return jnp.concatenate(parts, 0)

    k, v = keys(0), keys(1)
    kt = k.T

    for pair in range(2):
        chunks = [(s, a) for s in (2 * pair, 2 * pair + 1) for a in range(2)]
        low_i, starts_i = zip(*(blocks(fold_ref, y, z_at[s], 1 - x if a else x) for s, a in chunks))

        def queries(array, b):
            parts = [q_refs[s][a, pl.ds(array * 2 * BLK + at[b], BLK), :] for (s, a), at in zip(chunks, starts_i)]
            return jnp.concatenate(parts, 0)

        def stats(row, scale):
            low, high = [], []
            for (s, a), at in zip(chunks, starts_i):
                both = q_refs[s][a, 4 * BLK :, :].astype(F32)
                upper, lower = both[row : row + 1, :], both[row + 1 : row + 2, :]
                low.append(jnp.where(at[0] == 0, upper, lower) * scale)
                high.append(jnp.where(at[0] == 0, lower, upper) * scale)
            return jnp.concatenate(low, 1), jnp.concatenate(high, 1)

        lse_low, lse_high = stats(0, LOG2E)
        delta_low, delta_high = stats(2, 1.0)
        own = turn == 0 and js[0] == 0 and pair == 0

        def hide(m, low):
            parts = []
            for n, li in enumerate(low_i):
                seen = low_j[m] < li if low else li < low_j[m]
                hidden = jnp.float32(0.0) if own and n == 0 and m == 0 else jnp.where(seen, 0.0, HIDE)
                parts.append(jnp.full((1, BLK), hidden, F32))
            return jnp.concatenate(parts, 1)

        lses = [lse_high] * count + [lse_high + hide(m, False) for m in range(count)]
        dv, dk, dq_high = tile(
            k, v, kt, queries(0, 1), queries(1, 1), lses, delta_high, count if own else None
        )
        dv_acc[...] = dv if pair == 0 else dv_acc[...] + dv
        dk_acc[...] = dk if pair == 0 else dk_acc[...] + dk
        lses = [lse_low + hide(m, True) for m in range(count)]
        dv, dk, dq_low = tile(
            k[:half], v[:half], kt[:, :half], queries(0, 0), queries(1, 0), lses, delta_low, 0 if own else None
        )
        dv_acc[:half] += dv
        dk_acc[:half] += dk
        columns = slice(pair * 4 * BLK, (pair + 1) * 4 * BLK)
        for b, dq in ((0, dq_low), (1, dq_high)):
            if not first:
                dq = dqin_ref[b, :, columns] + dq
            if not final:
                dq_ref[b, :, columns] = dq
            else:
                for n, (s, a) in enumerate(chunks):
                    ref = dq_refs[s]
                    ref[a, pl.ds(starts_i[n][b], BLK), :] = dq[:, n * BLK : (n + 1) * BLK].T.astype(ref.dtype)

    for n in range(count):
        for b in range(2):
            source = slice(b * half + n * BLK, b * half + (n + 1) * BLK)
            at = starts_j[n][b]
            dkv_ref[n, pl.ds(at, BLK), :] = dk_acc[source].astype(dkv_ref.dtype)
            dkv_ref[n, pl.ds(2 * BLK + at, BLK), :] = dv_acc[source].astype(dkv_ref.dtype)


def meet_kernel(own_ref, other_ref, *refs):
    *back_refs, keep_ref, send_ref = refs
    for part, (start_ref, out_ref) in enumerate(((own_ref, keep_ref), (other_ref, send_ref))):
        total = start_ref[...]
        for ref in back_refs:
            total += ref[part].astype(F32)
        out_ref[...] = total.astype(out_ref.dtype)


def last_kernel(dq_ref, dqx_ref, dkv_ref, dkvz_ref, q_ref, k_ref, v_ref):
    q_ref[...] = ((dq_ref[...] + dqx_ref[...].astype(F32)) * FACTOR).astype(BF16)
    dkv = dkv_ref[...] + dkvz_ref[...].astype(F32)
    k_ref[...] = (dkv[: 2 * BLK] * FACTOR).astype(BF16)
    v_ref[...] = dkv[2 * BLK :].astype(BF16)


def z_step(step):
    return [(i, (i + step) % 8) for i in range(8)]


def y_step(step):
    return [(i, (i + step) % 4) for i in range(4)]


Z_PAIRS = [(i, (i - 2) % 8 if i % 2 == 0 else (i + 2) % 8) for i in range(8)]
Z_BACK = [(b, a) for a, b in Z_PAIRS]
X_SWAP = [(0, 1), (1, 0)]


def call(kernel, outs, operands, fold=None, scratch=(), in_specs=None, vmem_limit=VMEM_LIMIT, **options):
    smem = pl.BlockSpec(memory_space=pltpu.SMEM)
    vmem = pl.BlockSpec(memory_space=pltpu.VMEM)
    scalars = [] if fold is None else [fold]
    return pl.pallas_call(
        kernel,
        out_shape=[jax.ShapeDtypeStruct(s, t) for s, t in outs],
        in_specs=[smem] * len(scalars) + (in_specs or [vmem] * len(operands)),
        out_specs=[pl.BlockSpec(memory_space=pltpu.HBM) if in_specs else vmem] * len(outs),
        scratch_shapes=list(scratch),
        compiler_params=pltpu.CompilerParams(vmem_limit_bytes=vmem_limit),
        **options,
    )(*scalars, *operands)


def body(queries, key_rows, value_rows, outputs, out_grad, saved_lse, fold_map):
    operands = (queries, key_rows, value_rows, outputs, out_grad, saved_lse.T)
    rows = pltpu.VMEM((2 * BLK, DIM), BF16)
    mine_q, mine_k = call(
        prep_kernel,
        [((Q_ROWS, DIM), BF16), ((K_ROWS, DIM), BF16)],
        operands,
        scratch=[
            rows,
            rows,
            pltpu.VMEM((1, 2 * BLK), BF16),
            pltpu.VMEM((Q_ROWS - 4 * BLK, DIM), BF16),
            pltpu.SemaphoreType.DMA((8,)),
        ],
        in_specs=[pl.BlockSpec(memory_space=pltpu.HBM)] * len(operands),
        vmem_limit=PREP_VMEM,
    )
    other_k = lax.ppermute(mine_k, "kz", z_step(4))
    q0 = jnp.stack([mine_q, lax.ppermute(mine_q, "kx", X_SWAP)])
    _, other_k = lax.optimization_barrier((q0, other_k))
    k0 = jnp.stack([mine_k, other_k])
    q_sets = [q0] + [lax.ppermute(q0, "kz", p) for p in (z_step(1), z_step(-1), Z_PAIRS)]
    k_sets = [k0] + [lax.ppermute(k0, "pb", y_step(-s)) for s in Y_FROM[1:]]

    dq = []
    dkv = {}
    order = ((0, (0,)), (1, (0, 1)), (2, (0, 1)), (3, (0, 1)), (0, (1,)))
    for turn, js in order:
        first, final = (turn, js) == order[0], (turn, js) == order[-1]
        key_set = (mine_k, other_k)[js[0]][None] if turn == 0 else k_sets[turn]
        outs = [((2, DIM, 8 * BLK), F32)]
        if final:
            outs = [((2, 2 * BLK, DIM), F32 if s == 0 else BF16) for s in range(4)]
        acc = pltpu.VMEM((2 * len(js) * BLK, DIM), F32)
        *dq, part = call(
            functools.partial(grad_kernel, turn, js, first, final),
            outs + [((len(js), K_ROWS, DIM), BF16 if turn else F32)],
            q_sets + [key_set] + ([] if first else dq),
            fold_map,
            [acc, acc],
            cost_estimate=pl.CostEstimate(flops=FLOPS * len(js) // 2, bytes_accessed=1 << 20, transcendentals=0),
            input_output_aliases={} if first or final else {6: 0},
        )
        dkv[turn, js] = lax.ppermute(part, "pb", y_step(Y_FROM[turn])) if turn else part[0]
    dq_back = [lax.ppermute(dq[t], "kz", p) for t, p in ((1, z_step(-1)), (2, z_step(1)), (3, Z_BACK))]

    def meet(own, other, partners):
        return call(meet_kernel, [(own.shape, F32), (own.shape, BF16)], [own, other] + partners)

    dkv_keep, dkv_send = meet(dkv[0, (0,)], dkv[0, (1,)], [dkv[t, (0, 1)] for t in (1, 2, 3)])
    dkv_last = lax.ppermute(dkv_send, "kz", z_step(4))
    dq_keep, dq_send = meet(dq[0][0], dq[0][1], dq_back)
    dq_last = lax.ppermute(dq_send, "kx", X_SWAP)
    return tuple(call(last_kernel, [((2 * BLK, DIM), BF16)] * 3, (dq_keep, dq_last, dkv_keep, dkv_last)))


def solution(mesh):
    fine = Mesh(mesh.devices.reshape(4, 8, 2, 2, 2), ("pb", "kz", "kx", "hx", "hc"))
    rows = P(("pb", "kz", "kx"), ("hx", "hc"))
    return jax.shard_map(
        body,
        mesh=fine,
        in_specs=(rows,) * 6 + (P(),),
        out_specs=(rows,) * 3,
        check_vma=False,
    )
```

time: 73.1 us -> 75.1 us (1.027); the launches traced: 73 us -> 73.7 us
  Pallas kernels: 14.4 us -> 22.1 us
  waiting for transfers between devices: 18.9 us -> 14.5 us
  starting transfers between devices: 37.3 us -> 35.3 us
    pallas_call x8 -> x9, Pallas kernels: 14.4 us -> 22.1 us  [call(): pl.pallas_call(kernel, out_shape=[jax.ShapeDtypeStruct(s, t) for s, t in...]
    ppermute x3, waiting for transfers between devices: 5.86 us -> 0.01 us  [body(): lax.ppermute(dq[t], 'kz', p)]
    ppermute x4, starting transfers between devices: 15.1 us -> 12.5 us  [the longest x1 7.19 us: body(): other_k = lax.ppermute(mine_k, 'kz', z_step(4))]
    ppermute x1, waiting for transfers between devices: 0.01 us -> 1.18 us  [body(): dkv_last = lax.ppermute(dkv_send, 'kz', z_step(4))]
  transfers between devices with their start and end apart: 16 -> 16, of which waited for: 6 -> 6; matrix products, arithmetic and copies ran while one was open for 1% -> 1% of each run, Pallas kernels for 15% -> 13%
where the time goes in v5:
time: 75.1 us; the launch traced here: 73.7 us
  starting transfers between devices  35.3 us (47%)
  Pallas kernels  22.1 us (29%)
  waiting for transfers between devices  14.5 us (19%)
  other arithmetic  0.99 us (1%)
  between operations  0.76 us (1%)
    pallas_call x9, Pallas kernels, call(): pl.pallas_call(kernel, out_shape=[jax.ShapeDtypeStruct(s, t) for s, t in...  22.1 us
    ppermute x1, starting transfers between devices, body(): other_k = lax.ppermute(mine_k, 'kz', z_step(4))  7.19 us
    ppermute x3, starting transfers between devices, body(): k_sets = [k0] + [lax.ppermute(k0, 'pb', y_step(-s)) for s in Y_FROM[1:]]  6.97 us
    ppermute x3, starting transfers between devices, body(): lax.ppermute(q0, 'kz', p)  5.55 us
    ppermute x3, starting transfers between devices, body(): lax.ppermute(part, 'pb', y_step(Y_FROM[turn]))  5.27 us
    ppermute x3, waiting for transfers between devices, body(): lax.ppermute(q0, 'kz', p)  5.02 us
    ppermute x3, waiting for transfers between devices, body(): lax.ppermute(part, 'pb', y_step(Y_FROM[turn]))  4.87 us
    ppermute x1, starting transfers between devices, body(): dkv_last = lax.ppermute(dkv_send, 'kz', z_step(4))  4.56 us
  transfers between devices with their start and end apart: 16, of which 6 were waited for; matrix products, arithmetic and copies ran while one was open for 1% of the time, Pallas kernels for 13%

profile of v5, /device:TPU:4, one launch (start us, length us, event | category | flops | bytes accessed | tf_op | source)
XLA Modules:
  0.0 73.7 jit_solution(6687029217639083324)
XLA Ops:
  0.6 9.1 %shard_map.94 = (bf16[528,128]{1,0:T(8,128)(2,1)}, bf16[512,128]{1,0:T(8,128)(2,1)}) custom-call(bf16[256,128]{1,0:T(8,128)(2,1)} %q_ref.1, bf16[256,128]{1,0:T(8,128)(2,1)} %k_ref.1, bf16[256,128]{1,0:T(8,128)(2,1)} %v_ref.1, bf16[256,128]{1,0:T(8,128)(2,1)} %o_ref.1, bf16[256,128]{1,0:T(8,128)(2,1)} %g_ref.1, bf16[1,256]{1,0:T(2,128)(2,1)} %bitcast.19), custom_call_target="tpu_custom_call" | custom-call | tf_op jit(solution)/shard_map/pallas_call | solution.py:214
  9.8 1.3 %collective-permute-start = (bf16[528,128]{1,0:T(8,128)(2,1)}, bf16[528,128]{1,0:T(8,128)(2,1)S(1)}, u32[]{:S(2)}, u32[]{:S(2)}) collective-permute-start(bf16[528,128]{1,0:T(8,128)(2,1)} %get-tuple-element.23), channel_id=1, source_target_pairs={{0,4},{4,0},{1,5},{5,1},{2,6},{6,2},{3,7},{7,3},{8,12},{12,8},{9,1... | collective-permute-start | bytes 405512 | tf_op jit(solution)/shard_map/ppermute | solution.py:243
  11.0 7.2 %collective-permute-start.4 = (bf16[512,128]{1,0:T(8,128)(2,1)}, bf16[512,128]{1,0:T(8,128)(2,1)S(1)}, u32[]{:S(2)}, u32[]{:S(2)}) collective-permute-start(bf16[512,128]{1,0:T(8,128)(2,1)} %get-tuple-element.24), channel_id=1, source_target_pairs={{0,32},{8,40},{16,48},{24,56},{32,0},{40,8},{48,16},{56,24},{1,33}... | collective-permute-start | bytes 393224 | tf_op jit(solution)/shard_map/ppermute | solution.py:242
  18.2 1.0 %pad_maximum_fusion.refs_0_ = bf16[2,528,128]{2,1,0:T(8,128)(2,1)S(1)} fusion(bf16[1,528,128]{2,1,0:T(8,128)(2,1)S(1)} %bitcast.18, bf16[1,528,128]{2,1,0:T(8,128)(2,1)} %bitcast.17), kind=kLoop, calls=%fused_computation | loop fusion | flops 135168 | bytes 540672 | tf_op jit(solution)/shard_map/stack | solution.py:243
  19.2 3.5 %collective-permute-start.3 = (bf16[2,528,128]{2,1,0:T(8,128)(2,1)S(1)}, bf16[2,528,128]{2,1,0:T(8,128)(2,1)S(1)}, u32[]{:S(2)}, u32[]{:S(2)}) collective-permute-start(bf16[2,528,128]{2,1,0:T(8,128)(2,1)S(1)} %pad_maximum_fusion.refs_0_), channel_id=1, source_target_pairs={{0,48},{8,24},{16,0},{24,40},{32,16},{40,56},{48,32},{56,8},{1,49}... | collective-permute-start | bytes 811016 | tf_op jit(solution)/shard_map/ppermute | solution.py:246
  23.0 1.8 %collective-permute-start.1 = (bf16[2,528,128]{2,1,0:T(8,128)(2,1)S(1)}, bf16[2,528,128]{2,1,0:T(8,128)(2,1)S(1)}, u32[]{:S(2)}, u32[]{:S(2)}) collective-permute-start(bf16[2,528,128]{2,1,0:T(8,128)(2,1)S(1)} %pad_maximum_fusion.refs_0_), channel_id=1, source_target_pairs={{0,8},{8,16},{16,24},{24,32},{32,40},{40,48},{48,56},{56,0},{1,9},... | collective-permute-start | bytes 811016 | tf_op jit(solution)/shard_map/ppermute | solution.py:246
  24.8 3.3 %collective-permute-start.7 = (bf16[2,512,128]{2,1,0:T(8,128)(2,1)S(1)}, bf16[2,512,128]{2,1,0:T(8,128)(2,1)S(1)}, u32[]{:S(2)}, u32[]{:S(2)}) collective-permute-start(bf16[2,512,128]{2,1,0:T(8,128)(2,1)S(1)} %pad_maximum_fusion.1), channel_id=1, source_target_pairs={{0,128},{64,192},{128,0},{192,64},{1,129},{65,193},{129,1},{193,65... | collective-permute-start | bytes 786440 | tf_op jit(solution)/shard_map/ppermute | solution.py:247
  28.8 2.1 %collective-permute-done.3.refs_3_ = bf16[2,528,128]{2,1,0:T(8,128)(2,1)S(1)} collective-permute-done((bf16[2,528,128]{2,1,0:T(8,128)(2,1)S(1)}, bf16[2,528,128]{2,1,0:T(8,128)(2,1)S(1)}, u32[]{:S(2)}, u32[]{:S(2)}) %collective-permute-start.3) | collective-permute-done | bytes 270368 | tf_op jit(solution)/shard_map/ppermute | solution.py:246
  30.9 3.0 %collective-permute-start.5 = (bf16[2,512,128]{2,1,0:T(8,128)(2,1)S(1)}, bf16[2,512,128]{2,1,0:T(8,128)(2,1)S(1)}, u32[]{:S(2)}, u32[]{:S(2)}) collective-permute-start(bf16[2,512,128]{2,1,0:T(8,128)(2,1)S(1)} %pad_maximum_fusion.1), channel_id=1, source_target_pairs={{0,192},{64,0},{128,64},{192,128},{1,193},{65,1},{129,65},{193,129... | collective-permute-start | bytes 786440 | tf_op jit(solution)/shard_map/ppermute | solution.py:247
  33.9 2.9 %collective-permute-done.2.refs_2_ = bf16[2,528,128]{2,1,0:T(8,128)(2,1)S(1)} collective-permute-done((bf16[2,528,128]{2,1,0:T(8,128)(2,1)S(1)}, bf16[2,528,128]{2,1,0:T(8,128)(2,1)S(1)}, u32[]{:S(2)}, u32[]{:S(2)}) %collective-permute-start.2) | collective-permute-done | bytes 270368 | tf_op jit(solution)/shard_map/ppermute | solution.py:246
  36.8 1.8 %shard_map.95 = (f32[2,128,1024]{2,1,0:T(8,128)S(1)}, f32[1,512,128]{2,1,0:T(8,128)S(1)}) custom-call(s32[128]{0:T(128)S(1)} %copy-done.1, bf16[2,528,128]{2,1,0:T(8,128)(2,1)S(1)} %pad_maximum_fusion.refs_0_, bf16[2,528,128]{2,1,0:T(8,128)(2,1)S(1)} %collective-permute-done.1.refs_1_, bf16[2,528,128]{2,1,0:T(8,128)(2,1)S(1)} %collective-permute-done.2.refs_2_, ...), custom_call_target="tpu_custom_call" | custom-call | flops 503316480 | bytes 1048576 | tf_op jit(solution)/shard_map/pallas_call | solution.py:214
  38.6 2.8 %shard_map.96 = (f32[2,128,1024]{2,1,0:T(8,128)S(1)}, bf16[2,512,128]{2,1,0:T(8,128)(2,1)S(1)}) custom-call(s32[128]{0:T(128)S(1)} %copy-done.1, bf16[2,528,128]{2,1,0:T(8,128)(2,1)S(1)} %pad_maximum_fusion.refs_0_, bf16[2,528,128]{2,1,0:T(8,128)(2,1)S(1)} %collective-permute-done.1.refs_1_, ...), custom_call_target="tpu_custom_call", output_to_operand_aliasing={{0}: (6, {})} | custom-call | flops 1006632960 | bytes 1048576 | tf_op jit(solution)/shard_map/pallas_call | solution.py:214
  41.4 2.8 %shard_map.97 = (f32[2,128,1024]{2,1,0:T(8,128)S(1)}, bf16[2,512,128]{2,1,0:T(8,128)(2,1)S(1)}) custom-call(s32[128]{0:T(128)S(1)} %copy-done.1, bf16[2,528,128]{2,1,0:T(8,128)(2,1)S(1)} %pad_maximum_fusion.refs_0_, bf16[2,528,128]{2,1,0:T(8,128)(2,1)S(1)} %collective-permute-done.1.refs_1_, ...), custom_call_target="tpu_custom_call", output_to_operand_aliasing={{0}: (6, {})} | custom-call | flops 1006632960 | bytes 1048576 | tf_op jit(solution)/shard_map/pallas_call | solution.py:214
  44.2 2.8 %shard_map.98 = (f32[2,128,1024]{2,1,0:T(8,128)S(1)}, bf16[2,512,128]{2,1,0:T(8,128)(2,1)S(1)}) custom-call(s32[128]{0:T(128)S(1)} %copy-done.1, bf16[2,528,128]{2,1,0:T(8,128)(2,1)S(1)} %pad_maximum_fusion.refs_0_, bf16[2,528,128]{2,1,0:T(8,128)(2,1)S(1)} %collective-permute-done.1.refs_1_, ...), custom_call_target="tpu_custom_call", output_to_operand_aliasing={{0}: (6, {})} | custom-call | flops 1006632960 | bytes 1048576 | tf_op jit(solution)/shard_map/pallas_call | solution.py:214
  47.0 1.6 %collective-permute-start.14 = (bf16[2,512,128]{2,1,0:T(8,128)(2,1)S(1)}, bf16[2,512,128]{2,1,0:T(8,128)(2,1)S(1)}, u32[]{:S(2)}, u32[]{:S(2)}) collective-permute-start(bf16[2,512,128]{2,1,0:T(8,128)(2,1)S(1)} %get-tuple-element.40), channel_id=1, source_target_pairs={{0,64},{64,128},{128,192},{192,0},{1,65},{65,129},{129,193},{193,1... | collective-permute-start | bytes 786440 | tf_op jit(solution)/shard_map/ppermute | solution.py:268
  48.6 1.7 %collective-permute-start.13 = (bf16[2,512,128]{2,1,0:T(8,128)(2,1)S(1)}, bf16[2,512,128]{2,1,0:T(8,128)(2,1)S(1)}, u32[]{:S(2)}, u32[]{:S(2)}) collective-permute-start(bf16[2,512,128]{2,1,0:T(8,128)(2,1)S(1)} %get-tuple-element.39), channel_id=1, source_target_pairs={{0,192},{64,0},{128,64},{192,128},{1,193},{65,1},{129,65},{193,129... | collective-permute-start | bytes 786440 | tf_op jit(solution)/shard_map/ppermute | solution.py:268
  50.3 2.0 %collective-permute-start.12 = (bf16[2,512,128]{2,1,0:T(8,128)(2,1)S(1)}, bf16[2,512,128]{2,1,0:T(8,128)(2,1)S(1)}, u32[]{:S(2)}, u32[]{:S(2)}) collective-permute-start(bf16[2,512,128]{2,1,0:T(8,128)(2,1)S(1)} %get-tuple-element.38), channel_id=1, source_target_pairs={{0,128},{64,192},{128,0},{192,64},{1,129},{65,193},{129,1},{193,65... | collective-permute-start | bytes 786440 | tf_op jit(solution)/shard_map/ppermute | solution.py:268
  52.2 1.9 %shard_map.99 = (f32[2,256,128]{2,1,0:T(8,128)S(1)}, bf16[2,256,128]{2,1,0:T(8,128)(2,1)S(1)}, bf16[2,256,128]{2,1,0:T(8,128)(2,1)S(1)}, bf16[2,256,128]{2,1,0:T(8,128)(2,1)S(1)}, f32[1,512,128]{2,1,0:T(8,128)S(1)}) custom-call(s32[128]{0:T(128)S(1)} %copy-done.1, bf16[2,528,128]{2,1,0:T(8,128)(2,1)S(1)} %pad_maximum_fusion.refs_0_, ...), custom_call_target="tpu_custom_call" | custom-call | flops 503316480 | bytes 1048576 | tf_op jit(solution)/shard_map/pallas_call | solution.py:214
  54.2 2.9 %collective-permute-start.8 = (bf16[2,256,128]{2,1,0:T(8,128)(2,1)S(1)}, bf16[2,256,128]{2,1,0:T(8,128)(2,1)S(1)}, u32[]{:S(2)}, u32[]{:S(2)}) collective-permute-start(bf16[2,256,128]{2,1,0:T(8,128)(2,1)S(1)} %get-tuple-element.31), channel_id=1, source_target_pairs={{0,56},{8,0},{16,8},{24,16},{32,24},{40,32},{48,40},{56,48},{1,57}... | collective-permute-start | bytes 393224 | tf_op jit(solution)/shard_map/ppermute | solution.py:269
  57.8 3.1 %collective-permute-done.13.refs_1_ = bf16[2,512,128]{2,1,0:T(8,128)(2,1)S(1)} collective-permute-done((bf16[2,512,128]{2,1,0:T(8,128)(2,1)S(1)}, bf16[2,512,128]{2,1,0:T(8,128)(2,1)S(1)}, u32[]{:S(2)}, u32[]{:S(2)}) %collective-permute-start.13) | collective-permute-done | bytes 262176 | tf_op jit(solution)/shard_map/ppermute | solution.py:268
  60.9 1.8 %collective-permute-done.12.refs_0_ = bf16[2,512,128]{2,1,0:T(8,128)(2,1)S(1)} collective-permute-done((bf16[2,512,128]{2,1,0:T(8,128)(2,1)S(1)}, bf16[2,512,128]{2,1,0:T(8,128)(2,1)S(1)}, u32[]{:S(2)}, u32[]{:S(2)}) %collective-permute-start.12) | collective-permute-done | bytes 262176 | tf_op jit(solution)/shard_map/ppermute | solution.py:268
  62.8 4.6 %collective-permute-start.15 = (bf16[512,128]{1,0:T(8,128)(2,1)S(1)}, bf16[512,128]{1,0:T(8,128)(2,1)S(1)}, u32[]{:S(2)}, u32[]{:S(2)}) collective-permute-start(bf16[512,128]{1,0:T(8,128)(2,1)S(1)} %get-tuple-element.42), channel_id=1, source_target_pairs={{0,32},{8,40},{16,48},{24,56},{32,0},{40,8},{48,16},{56,24},{1,33}... | collective-permute-start | bytes 393224 | tf_op jit(solution)/shard_map/ppermute | solution.py:275
  68.4 3.5 %collective-permute-done.11.dqx_ref = bf16[256,128]{1,0:T(8,128)(2,1)S(1)} collective-permute-done((bf16[256,128]{1,0:T(8,128)(2,1)S(1)}, bf16[256,128]{1,0:T(8,128)(2,1)S(1)}, u32[]{:S(2)}, u32[]{:S(2)}) %collective-permute-start.11) | collective-permute-done | bytes 65568 | tf_op jit(solution)/shard_map/ppermute | solution.py:277
  71.8 1.2 %collective-permute-done.15.dkvz_ref = bf16[512,128]{1,0:T(8,128)(2,1)S(1)} collective-permute-done((bf16[512,128]{1,0:T(8,128)(2,1)S(1)}, bf16[512,128]{1,0:T(8,128)(2,1)S(1)}, u32[]{:S(2)}, u32[]{:S(2)}) %collective-permute-start.15) | collective-permute-done | bytes 131104 | tf_op jit(solution)/shard_map/ppermute | solution.py:275
  (24 shorter events, 3.5 us)
Async XLA Ops:
  9.8 8.5 %collective-permute-start = (bf16[528,128]{1,0:T(8,128)(2,1)}, bf16[528,128]{1,0:T(8,128)(2,1)S(1)}, u32[]{:S(2)}, u32[]{:S(2)}) collective-permute-start(bf16[528,128]{1,0:T(8,128)(2,1)} %get-tuple-element.23), channel_id=1, source_target_pairs={{0,4},{4,0},{1,5},{5,1},{2,6},{6,2},{3,7},{7,3},{8,12},{12,8},{9,1... | collective-permute-start | bytes 405512 | tf_op jit(solution)/shard_map/ppermute | solution.py:243
  11.0 13.7 %collective-permute-start.4 = (bf16[512,128]{1,0:T(8,128)(2,1)}, bf16[512,128]{1,0:T(8,128)(2,1)S(1)}, u32[]{:S(2)}, u32[]{:S(2)}) collective-permute-start(bf16[512,128]{1,0:T(8,128)(2,1)} %get-tuple-element.24), channel_id=1, source_target_pairs={{0,32},{8,40},{16,48},{24,56},{32,0},{40,8},{48,16},{56,24},{1,33}... | collective-permute-start | bytes 393224 | tf_op jit(solution)/shard_map/ppermute | solution.py:242
  18.2 6.5 %copy-start = (bf16[512,128]{1,0:T(8,128)(2,1)S(1)}, bf16[512,128]{1,0:T(8,128)(2,1)}, u32[]{:S(2)}) copy-start(bf16[512,128]{1,0:T(8,128)(2,1)} %get-tuple-element.24) | copy-start | bytes 393220
  19.2 11.6 %collective-permute-start.3 = (bf16[2,528,128]{2,1,0:T(8,128)(2,1)S(1)}, bf16[2,528,128]{2,1,0:T(8,128)(2,1)S(1)}, u32[]{:S(2)}, u32[]{:S(2)}) collective-permute-start(bf16[2,528,128]{2,1,0:T(8,128)(2,1)S(1)} %pad_maximum_fusion.refs_0_), channel_id=1, source_target_pairs={{0,48},{8,24},{16,0},{24,40},{32,16},{40,56},{48,32},{56,8},{1,49}... | collective-permute-start | bytes 811016 | tf_op jit(solution)/shard_map/ppermute | solution.py:246
  22.7 14.1 %collective-permute-start.2 = (bf16[2,528,128]{2,1,0:T(8,128)(2,1)S(1)}, bf16[2,528,128]{2,1,0:T(8,128)(2,1)S(1)}, u32[]{:S(2)}, u32[]{:S(2)}) collective-permute-start(bf16[2,528,128]{2,1,0:T(8,128)(2,1)S(1)} %pad_maximum_fusion.refs_0_), channel_id=1, source_target_pairs={{0,56},{8,0},{16,8},{24,16},{32,24},{40,32},{48,40},{56,48},{1,57}... | collective-permute-start | bytes 811016 | tf_op jit(solution)/shard_map/ppermute | solution.py:246
  23.0 13.8 %collective-permute-start.1 = (bf16[2,528,128]{2,1,0:T(8,128)(2,1)S(1)}, bf16[2,528,128]{2,1,0:T(8,128)(2,1)S(1)}, u32[]{:S(2)}, u32[]{:S(2)}) collective-permute-start(bf16[2,528,128]{2,1,0:T(8,128)(2,1)S(1)} %pad_maximum_fusion.refs_0_), channel_id=1, source_target_pairs={{0,8},{8,16},{16,24},{24,32},{32,40},{40,48},{48,56},{56,0},{1,9},... | collective-permute-start | bytes 811016 | tf_op jit(solution)/shard_map/ppermute | solution.py:246
  24.8 12.0 %copy-start.1 = (s32[128]{0:T(128)S(1)}, s32[128]{0:T(128)}, u32[]{:S(2)}) copy-start(s32[128]{0:T(128)} %fold_ref.9) | copy-start | bytes 1540
  24.8 13.8 %collective-permute-start.7 = (bf16[2,512,128]{2,1,0:T(8,128)(2,1)S(1)}, bf16[2,512,128]{2,1,0:T(8,128)(2,1)S(1)}, u32[]{:S(2)}, u32[]{:S(2)}) collective-permute-start(bf16[2,512,128]{2,1,0:T(8,128)(2,1)S(1)} %pad_maximum_fusion.1), channel_id=1, source_target_pairs={{0,128},{64,192},{128,0},{192,64},{1,129},{65,193},{129,1},{193,65... | collective-permute-start | bytes 786440 | tf_op jit(solution)/shard_map/ppermute | solution.py:247
  28.1 13.3 %collective-permute-start.6 = (bf16[2,512,128]{2,1,0:T(8,128)(2,1)S(1)}, bf16[2,512,128]{2,1,0:T(8,128)(2,1)S(1)}, u32[]{:S(2)}, u32[]{:S(2)}) collective-permute-start(bf16[2,512,128]{2,1,0:T(8,128)(2,1)S(1)} %pad_maximum_fusion.1), channel_id=1, source_target_pairs={{0,64},{64,128},{128,192},{192,0},{1,65},{65,129},{129,193},{193,1... | collective-permute-start | bytes 786440 | tf_op jit(solution)/shard_map/ppermute | solution.py:247
  30.9 13.3 %collective-permute-start.5 = (bf16[2,512,128]{2,1,0:T(8,128)(2,1)S(1)}, bf16[2,512,128]{2,1,0:T(8,128)(2,1)S(1)}, u32[]{:S(2)}, u32[]{:S(2)}) collective-permute-start(bf16[2,512,128]{2,1,0:T(8,128)(2,1)S(1)} %pad_maximum_fusion.1), channel_id=1, source_target_pairs={{0,192},{64,0},{128,64},{192,128},{1,193},{65,1},{129,65},{193,129... | collective-permute-start | bytes 786440 | tf_op jit(solution)/shard_map/ppermute | solution.py:247
  47.0 10.1 %collective-permute-start.14 = (bf16[2,512,128]{2,1,0:T(8,128)(2,1)S(1)}, bf16[2,512,128]{2,1,0:T(8,128)(2,1)S(1)}, u32[]{:S(2)}, u32[]{:S(2)}) collective-permute-start(bf16[2,512,128]{2,1,0:T(8,128)(2,1)S(1)} %get-tuple-element.40), channel_id=1, source_target_pairs={{0,64},{64,128},{128,192},{192,0},{1,65},{65,129},{129,193},{193,1... | collective-permute-start | bytes 786440 | tf_op jit(solution)/shard_map/ppermute | solution.py:268
  48.6 12.3 %collective-permute-start.13 = (bf16[2,512,128]{2,1,0:T(8,128)(2,1)S(1)}, bf16[2,512,128]{2,1,0:T(8,128)(2,1)S(1)}, u32[]{:S(2)}, u32[]{:S(2)}) collective-permute-start(bf16[2,512,128]{2,1,0:T(8,128)(2,1)S(1)} %get-tuple-element.39), channel_id=1, source_target_pairs={{0,192},{64,0},{128,64},{192,128},{1,193},{65,1},{129,65},{193,129... | collective-permute-start | bytes 786440 | tf_op jit(solution)/shard_map/ppermute | solution.py:268
  50.3 12.4 %collective-permute-start.12 = (bf16[2,512,128]{2,1,0:T(8,128)(2,1)S(1)}, bf16[2,512,128]{2,1,0:T(8,128)(2,1)S(1)}, u32[]{:S(2)}, u32[]{:S(2)}) collective-permute-start(bf16[2,512,128]{2,1,0:T(8,128)(2,1)S(1)} %get-tuple-element.38), channel_id=1, source_target_pairs={{0,128},{64,192},{128,0},{192,64},{1,129},{65,193},{129,1},{193,65... | collective-permute-start | bytes 786440 | tf_op jit(solution)/shard_map/ppermute | solution.py:268
  54.2 13.2 %collective-permute-start.8 = (bf16[2,256,128]{2,1,0:T(8,128)(2,1)S(1)}, bf16[2,256,128]{2,1,0:T(8,128)(2,1)S(1)}, u32[]{:S(2)}, u32[]{:S(2)}) collective-permute-start(bf16[2,256,128]{2,1,0:T(8,128)(2,1)S(1)} %get-tuple-element.31), channel_id=1, source_target_pairs={{0,56},{8,0},{16,8},{24,16},{32,24},{40,32},{48,40},{56,48},{1,57}... | collective-permute-start | bytes 393224 | tf_op jit(solution)/shard_map/ppermute | solution.py:269
  57.1 10.3 %collective-permute-start.9 = (bf16[2,256,128]{2,1,0:T(8,128)(2,1)S(1)}, bf16[2,256,128]{2,1,0:T(8,128)(2,1)S(1)}, u32[]{:S(2)}, u32[]{:S(2)}) collective-permute-start(bf16[2,256,128]{2,1,0:T(8,128)(2,1)S(1)} %get-tuple-element.32), channel_id=1, source_target_pairs={{0,8},{8,16},{16,24},{24,32},{32,40},{40,48},{48,56},{56,0},{1,9},... | collective-permute-start | bytes 393224 | tf_op jit(solution)/shard_map/ppermute | solution.py:269
  57.1 10.3 %collective-permute-start.10 = (bf16[2,256,128]{2,1,0:T(8,128)(2,1)S(1)}, bf16[2,256,128]{2,1,0:T(8,128)(2,1)S(1)}, u32[]{:S(2)}, u32[]{:S(2)}) collective-permute-start(bf16[2,256,128]{2,1,0:T(8,128)(2,1)S(1)} %get-tuple-element.33), channel_id=1, source_target_pairs={{48,0},{24,8},{0,16},{40,24},{16,32},{56,40},{32,48},{8,56},{49,1}... | collective-permute-start | bytes 393224 | tf_op jit(solution)/shard_map/ppermute | solution.py:269
  62.8 10.2 %collective-permute-start.15 = (bf16[512,128]{1,0:T(8,128)(2,1)S(1)}, bf16[512,128]{1,0:T(8,128)(2,1)S(1)}, u32[]{:S(2)}, u32[]{:S(2)}) collective-permute-start(bf16[512,128]{1,0:T(8,128)(2,1)S(1)} %get-tuple-element.42), channel_id=1, source_target_pairs={{0,32},{8,40},{16,48},{24,56},{32,0},{40,8},{48,16},{56,24},{1,33}... | collective-permute-start | bytes 393224 | tf_op jit(solution)/shard_map/ppermute | solution.py:275
  67.5 4.4 %collective-permute-start.11 = (bf16[256,128]{1,0:T(8,128)(2,1)S(1)}, bf16[256,128]{1,0:T(8,128)(2,1)S(1)}, u32[]{:S(2)}, u32[]{:S(2)}) collective-permute-start(bf16[256,128]{1,0:T(8,128)(2,1)S(1)} %get-tuple-element.35), channel_id=1, source_target_pairs={{0,4},{4,0},{1,5},{5,1},{2,6},{6,2},{3,7},{7,3},{8,12},{12,8},{9,1... | collective-permute-start | bytes 196616 | tf_op jit(solution)/shard_map/ppermute | solution.py:277

commit v6 on v5

--- a/solution.py
+++ b/solution.py
@@ -45,36 +45,30 @@
     return jnp.minimum(first, second), (low, high)
 
 
-def prep_kernel(q_ref, k_ref, v_ref, o_ref, g_ref, lse_ref, qout_ref, kout_ref, g_buf, o_buf, lse_buf, stats_buf, sems):
+def prep_kernel(*refs):
+    sources, (qout_ref, kout_ref), buffers, (stats_buf, sems) = refs[:6], refs[6:8], refs[8:14], refs[14:]
     half = 2 * BLK
-    loads = [
-        pltpu.make_async_copy(s, d, sems.at[n])
-        for n, (s, d) in enumerate(((g_ref, g_buf), (o_ref, o_buf), (lse_ref, lse_buf)))
-    ]
-    moves = [
-        pltpu.make_async_copy(s, d, sems.at[3 + n])
-        for n, (s, d) in enumerate(
-            (
-                (q_ref, qout_ref.at[:half]),
-                (g_ref, qout_ref.at[half : 2 * half]),
-                (k_ref, kout_ref.at[:half]),
-                (v_ref, kout_ref.at[half:]),
-            )
-        )
-    ]
-    for copy in loads + moves:
+    targets = (qout_ref.at[half : 2 * half], None, None, kout_ref.at[:half], kout_ref.at[half:], qout_ref.at[:half])
+    loads = [pltpu.make_async_copy(s, d, sems.at[n]) for n, (s, d) in enumerate(zip(sources, buffers))]
+    stores = [pltpu.make_async_copy(s, d, sems.at[6 + n]) for n, (s, d) in enumerate(zip(buffers, targets)) if d is not None]
+    for copy in loads:
         copy.start()
-    for copy in loads:
-        copy.wait()
+    for n in (0, 1, 2):
+        loads[n].wait()
+    stores[0].start()
+    g_buf, o_buf, lse_buf = buffers[:3]
     lse = lse_buf[...].astype(F32)
     rows = [lse[:, :BLK], lse[:, BLK:]]
     for start in (0, BLK):
         prod = g_buf[start : start + BLK, :].astype(F32) * o_buf[start : start + BLK, :].astype(F32)
         rows.append(jnp.sum(prod.T, axis=0, keepdims=True))
+    for n in (3, 4, 5):
+        loads[n].wait()
+        stores[n - 2].start()
     stats_buf[...] = jnp.concatenate(rows + [jnp.zeros((12, DIM), F32)], axis=0).astype(BF16)
-    moves.append(pltpu.make_async_copy(stats_buf, qout_ref.at[2 * half :], sems.at[7]))
-    moves[-1].start()
-    for copy in moves:
+    stores.append(pltpu.make_async_copy(stats_buf, qout_ref.at[2 * half :], sems.at[7]))
+    stores[-1].start()
+    for copy in stores:
         copy.wait()
 
 
@@ -99,7 +93,8 @@
     if not first:
         dqin_ref, refs = refs[0], refs[1:]
     if final:
-        dq_refs, (dkv_ref, dv_acc, dk_acc) = refs[:4], refs[4:]
+        kept_ref, back_ref, refs = refs[0], refs[1], refs[2:]
+        dq_refs, (sum_ref, dkv_ref, dv_acc, dk_acc) = refs[:4], refs[4:]
     else:
         dq_ref, dkv_ref, dv_acc, dk_acc = refs
     y, z, x = (lax.axis_index(name) for name in ("pb", "kz", "kx"))
@@ -174,8 +169,14 @@
         for b in range(2):
             source = slice(b * half + n * BLK, b * half + (n + 1) * BLK)
             at = starts_j[n][b]
-            dkv_ref[n, pl.ds(at, BLK), :] = dk_acc[source].astype(dkv_ref.dtype)
-            dkv_ref[n, pl.ds(2 * BLK + at, BLK), :] = dv_acc[source].astype(dkv_ref.dtype)
+            for array, acc in ((0, dk_acc), (1, dv_acc)):
+                rows = pl.ds(array * 2 * BLK + at, BLK)
+                part = acc[source]
+                if final:
+                    part = part + back_ref[1, rows, :].astype(F32)
+                dkv_ref[n, rows, :] = part.astype(dkv_ref.dtype)
+    if final:
+        sum_ref[...] = kept_ref[...] + back_ref[0].astype(F32)
 
 
 def meet_kernel(own_ref, other_ref, *refs):
@@ -223,24 +224,19 @@
 
 
 def body(queries, key_rows, value_rows, outputs, out_grad, saved_lse, fold_map):
-    operands = (queries, key_rows, value_rows, outputs, out_grad, saved_lse.T)
-    rows = pltpu.VMEM((2 * BLK, DIM), BF16)
+    operands = (out_grad, outputs, saved_lse.T, key_rows, value_rows, queries)
+    buffers = [pltpu.VMEM(a.shape, a.dtype) for a in operands]
     mine_q, mine_k = call(
         prep_kernel,
         [((Q_ROWS, DIM), BF16), ((K_ROWS, DIM), BF16)],
         operands,
-        scratch=[
-            rows,
-            rows,
-            pltpu.VMEM((1, 2 * BLK), BF16),
-            pltpu.VMEM((Q_ROWS - 4 * BLK, DIM), BF16),
-            pltpu.SemaphoreType.DMA((8,)),
-        ],
+        scratch=buffers + [pltpu.VMEM((Q_ROWS - 4 * BLK, DIM), BF16), pltpu.SemaphoreType.DMA((12,))],
         in_specs=[pl.BlockSpec(memory_space=pltpu.HBM)] * len(operands),
         vmem_limit=PREP_VMEM,
     )
     other_k = lax.ppermute(mine_k, "kz", z_step(4))
-    q0 = jnp.stack([mine_q, lax.ppermute(mine_q, "kx", X_SWAP)])
+    q0 = lax.optimization_barrier(jnp.pad(mine_q[None], ((0, 1), (0, 0), (0, 0))))
+    q0 = lax.dynamic_update_slice(q0, lax.ppermute(mine_q, "kx", X_SWAP)[None], (1, 0, 0))
     _, other_k = lax.optimization_barrier((q0, other_k))
     k0 = jnp.stack([mine_k, other_k])
     q_sets = [q0] + [lax.ppermute(q0, "kz", p) for p in (z_step(1), z_step(-1), Z_PAIRS)]
@@ -254,12 +250,12 @@
         key_set = (mine_k, other_k)[js[0]][None] if turn == 0 else k_sets[turn]
         outs = [((2, DIM, 8 * BLK), F32)]
         if final:
-            outs = [((2, 2 * BLK, DIM), F32 if s == 0 else BF16) for s in range(4)]
+            outs = [((2, 2 * BLK, DIM), F32 if s == 0 else BF16) for s in range(4)] + [((K_ROWS, DIM), F32)]
         acc = pltpu.VMEM((2 * len(js) * BLK, DIM), F32)
         *dq, part = call(
             functools.partial(grad_kernel, turn, js, first, final),
             outs + [((len(js), K_ROWS, DIM), BF16 if turn else F32)],
-            q_sets + [key_set] + ([] if first else dq),
+            q_sets + [key_set] + ([] if first else dq) + ([dkv[0, (0,)], dkv[1, (0, 1)]] if final else []),
             fold_map,
             [acc, acc],
             cost_estimate=pl.CostEstimate(flops=FLOPS * len(js) // 2, bytes_accessed=1 << 20, transcendentals=0),
@@ -271,7 +267,7 @@
     def meet(own, other, partners):
         return call(meet_kernel, [(own.shape, F32), (own.shape, BF16)], [own, other] + partners)
 
-    dkv_keep, dkv_send = meet(dkv[0, (0,)], dkv[0, (1,)], [dkv[t, (0, 1)] for t in (1, 2, 3)])
+    dkv_keep, dkv_send = meet(dq[4], dkv[0, (1,)], [dkv[t, (0, 1)] for t in (2, 3)])
     dkv_last = lax.ppermute(dkv_send, "kz", z_step(4))
     dq_keep, dq_send = meet(dq[0][0], dq[0][1], dq_back)
     dq_last = lax.ppermute(dq_send, "kx", X_SWAP)

time: 75.1 us -> 67.8 us (0.903); the launches traced: 73.7 us -> 67.6 us
  Pallas kernels: 22.1 us -> 14.7 us
  starting transfers between devices: 35.3 us -> 37.8 us
  waiting for transfers between devices: 14.5 us -> 13.4 us
  other arithmetic: 0.99 us -> 0.03 us
  local copies, waits for them, and re-layouts: 0.03 us -> 0.98 us
    pallas_call x9, Pallas kernels: 22.1 us -> 14.7 us  [call(): pl.pallas_call(kernel, out_shape=[jax.ShapeDtypeStruct(s, t) for s, t in...]
    ppermute x3, waiting for transfers between devices: 4.87 us -> 0.01 us  [body(): lax.ppermute(part, 'pb', y_step(Y_FROM[turn]))]
    ppermute x3, waiting for transfers between devices: 0.01 us -> 3.97 us  [body(): lax.ppermute(dq[t], 'kz', p)]
    ppermute x1, starting transfers between devices: 4.56 us -> 6.52 us  [body(): dkv_last = lax.ppermute(dkv_send, 'kz', z_step(4))]
    ppermute x3, starting transfers between devices: 5.27 us -> 6.78 us  [body(): lax.ppermute(part, 'pb', y_step(Y_FROM[turn]))]
    another operation x1 -> x0, other arithmetic: 0.97 us -> none  [body(): q0 = jnp.stack([mine_q, lax.ppermute(mine_q, 'kx', X_SWAP)])]
    ppermute x3, starting transfers between devices: 5.55 us -> 4.59 us  [body(): lax.ppermute(q0, 'kz', p)]
    ppermute x3, waiting for transfers between devices: 5.02 us -> 5.97 us  [body(): lax.ppermute(q0, 'kz', p)]
  transfers between devices with their start and end apart: 16 -> 16, of which waited for: 6 -> 6; matrix products, arithmetic and copies ran while one was open for 1% -> 1% of each run, Pallas kernels for 13% -> 18%
where the time goes in v6:
time: 67.8 us; the launch traced here: 67.6 us
  starting transfers between devices  37.8 us (56%)
  Pallas kernels  14.7 us (22%)
  waiting for transfers between devices  13.4 us (20%)
  local copies, waits for them, and re-layouts  0.98 us (1%)
  between operations  0.75 us (1%)
    pallas_call x9, Pallas kernels, call(): pl.pallas_call(kernel, out_shape=[jax.ShapeDtypeStruct(s, t) for s, t in...  14.7 us
    ppermute x1, starting transfers between devices, body(): other_k = lax.ppermute(mine_k, 'kz', z_step(4))  7.19 us
    ppermute x3, starting transfers between devices, body(): k_sets = [k0] + [lax.ppermute(k0, 'pb', y_step(-s)) for s in Y_FROM[1:]]  6.97 us
    ppermute x3, starting transfers between devices, body(): lax.ppermute(part, 'pb', y_step(Y_FROM[turn]))  6.78 us
    ppermute x1, starting transfers between devices, body(): dkv_last = lax.ppermute(dkv_send, 'kz', z_step(4))  6.52 us
    ppermute x3, waiting for transfers between devices, body(): lax.ppermute(q0, 'kz', p)  5.97 us
    ppermute x3, starting transfers between devices, body(): lax.ppermute(q0, 'kz', p)  4.59 us
    ppermute x3, waiting for transfers between devices, body(): lax.ppermute(dq[t], 'kz', p)  3.97 us
  transfers between devices with their start and end apart: 16, of which 6 were waited for; matrix products, arithmetic and copies ran while one was open for 1% of the time, Pallas kernels for 18%

profile of v6, /device:TPU:4, one launch (start us, length us, event | category | flops | bytes accessed | tf_op | source)
XLA Modules:
  0.0 67.6 jit_solution(10799183935848718598)
XLA Ops:
  0.6 1.8 %shard_map.94 = (bf16[528,128]{1,0:T(8,128)(2,1)}, bf16[512,128]{1,0:T(8,128)(2,1)}) custom-call(bf16[256,128]{1,0:T(8,128)(2,1)} %refs_0_.1, bf16[256,128]{1,0:T(8,128)(2,1)} %refs_1_.1, bf16[1,256]{1,0:T(2,128)(2,1)} %bitcast.19, bf16[256,128]{1,0:T(8,128)(2,1)} %refs_3_.1, bf16[256,128]{1,0:T(8,128)(2,1)} %refs_4_.1, bf16[256,128]{1,0:T(8,128)(2,1)} %refs_5_.1), custom_call_target="tpu_custom_call" | custom-call | tf_op jit(solution)/shard_map/pallas_call | solution.py:215
  2.4 1.3 %collective-permute-start = (bf16[528,128]{1,0:T(8,128)(2,1)}, bf16[528,128]{1,0:T(8,128)(2,1)S(1)}, u32[]{:S(2)}, u32[]{:S(2)}) collective-permute-start(bf16[528,128]{1,0:T(8,128)(2,1)} %get-tuple-element.24), channel_id=1, source_target_pairs={{0,4},{4,0},{1,5},{5,1},{2,6},{6,2},{3,7},{7,3},{8,12},{12,8},{9,1... | collective-permute-start | bytes 405512 | tf_op jit(solution)/shard_map/ppermute | solution.py:239
  3.7 7.2 %collective-permute-start.4 = (bf16[512,128]{1,0:T(8,128)(2,1)}, bf16[512,128]{1,0:T(8,128)(2,1)S(1)}, u32[]{:S(2)}, u32[]{:S(2)}) collective-permute-start(bf16[512,128]{1,0:T(8,128)(2,1)} %get-tuple-element.25), channel_id=1, source_target_pairs={{0,32},{8,40},{16,48},{24,56},{32,0},{40,8},{48,16},{56,24},{1,33}... | collective-permute-start | bytes 393224 | tf_op jit(solution)/shard_map/ppermute | solution.py:237
  10.9 0.9 %pad.4 = bf16[2,528,128]{2,1,0:T(8,128)(2,1)S(1)} pad(bf16[1,528,128]{2,1,0:T(8,128)(2,1)} %bitcast.18, bf16[]{:T(256)} %constant.1.clone.1), padding=0_1x0_0x0_0 | pad | bytes 405506 | tf_op jit(solution)/shard_map/jit(_pad)/pad | solution.py:238
  11.9 2.6 %collective-permute-start.3 = (bf16[2,528,128]{2,1,0:T(8,128)(2,1)S(1)}, bf16[2,528,128]{2,1,0:T(8,128)(2,1)S(1)}, u32[]{:S(2)}, u32[]{:S(2)}) collective-permute-start(bf16[2,528,128]{2,1,0:T(8,128)(2,1)S(1)} %bitcast_dynamic-update-slice_fusion.refs_0_), channel_id=1, source_target_pairs={{0,48},{8,24},{16,0},{24,40},{32,16},{40,56},{48,32},{56,8},{1,49}... | collective-permute-start | bytes 811016 | tf_op jit(solution)/shard_map/ppermute | solution.py:242
  14.4 1.2 %collective-permute-start.2 = (bf16[2,528,128]{2,1,0:T(8,128)(2,1)S(1)}, bf16[2,528,128]{2,1,0:T(8,128)(2,1)S(1)}, u32[]{:S(2)}, u32[]{:S(2)}) collective-permute-start(bf16[2,528,128]{2,1,0:T(8,128)(2,1)S(1)} %bitcast_dynamic-update-slice_fusion.refs_0_), channel_id=1, source_target_pairs={{0,56},{8,0},{16,8},{24,16},{32,24},{40,32},{48,40},{56,48},{1,57}... | collective-permute-start | bytes 811016 | tf_op jit(solution)/shard_map/ppermute | solution.py:242
  15.6 0.8 %collective-permute-start.1 = (bf16[2,528,128]{2,1,0:T(8,128)(2,1)S(1)}, bf16[2,528,128]{2,1,0:T(8,128)(2,1)S(1)}, u32[]{:S(2)}, u32[]{:S(2)}) collective-permute-start(bf16[2,528,128]{2,1,0:T(8,128)(2,1)S(1)} %bitcast_dynamic-update-slice_fusion.refs_0_), channel_id=1, source_target_pairs={{0,8},{8,16},{16,24},{24,32},{32,40},{40,48},{48,56},{56,0},{1,9},... | collective-permute-start | bytes 811016 | tf_op jit(solution)/shard_map/ppermute | solution.py:242
  16.5 3.3 %collective-permute-start.7 = (bf16[2,512,128]{2,1,0:T(8,128)(2,1)S(1)}, bf16[2,512,128]{2,1,0:T(8,128)(2,1)S(1)}, u32[]{:S(2)}, u32[]{:S(2)}) collective-permute-start(bf16[2,512,128]{2,1,0:T(8,128)(2,1)S(1)} %pad_maximum_fusion), channel_id=1, source_target_pairs={{0,128},{64,192},{128,0},{192,64},{1,129},{65,193},{129,1},{193,65... | collective-permute-start | bytes 786440 | tf_op jit(solution)/shard_map/ppermute | solution.py:243
  20.5 3.0 %collective-permute-done.3.refs_3_ = bf16[2,528,128]{2,1,0:T(8,128)(2,1)S(1)} collective-permute-done((bf16[2,528,128]{2,1,0:T(8,128)(2,1)S(1)}, bf16[2,528,128]{2,1,0:T(8,128)(2,1)S(1)}, u32[]{:S(2)}, u32[]{:S(2)}) %collective-permute-start.3) | collective-permute-done | bytes 270368 | tf_op jit(solution)/shard_map/ppermute | solution.py:242
  23.5 3.0 %collective-permute-start.5 = (bf16[2,512,128]{2,1,0:T(8,128)(2,1)S(1)}, bf16[2,512,128]{2,1,0:T(8,128)(2,1)S(1)}, u32[]{:S(2)}, u32[]{:S(2)}) collective-permute-start(bf16[2,512,128]{2,1,0:T(8,128)(2,1)S(1)} %pad_maximum_fusion), channel_id=1, source_target_pairs={{0,192},{64,0},{128,64},{192,128},{1,193},{65,1},{129,65},{193,129... | collective-permute-start | bytes 786440 | tf_op jit(solution)/shard_map/ppermute | solution.py:243
  26.5 2.9 %collective-permute-done.2.refs_2_ = bf16[2,528,128]{2,1,0:T(8,128)(2,1)S(1)} collective-permute-done((bf16[2,528,128]{2,1,0:T(8,128)(2,1)S(1)}, bf16[2,528,128]{2,1,0:T(8,128)(2,1)S(1)}, u32[]{:S(2)}, u32[]{:S(2)}) %collective-permute-start.2) | collective-permute-done | bytes 270368 | tf_op jit(solution)/shard_map/ppermute | solution.py:242
  29.4 1.8 %shard_map.95 = (f32[2,128,1024]{2,1,0:T(8,128)S(1)}, f32[1,512,128]{2,1,0:T(8,128)S(1)}) custom-call(s32[128]{0:T(128)S(1)} %copy-done.1, bf16[2,528,128]{2,1,0:T(8,128)(2,1)S(1)} %bitcast_dynamic-update-slice_fusion.refs_0_, bf16[2,528,128]{2,1,0:T(8,128)(2,1)S(1)} %collective-permute-done.1.refs_1_, ...), custom_call_target="tpu_custom_call" | custom-call | flops 503316480 | bytes 1048576 | tf_op jit(solution)/shard_map/pallas_call | solution.py:215
  31.3 2.8 %shard_map.96 = (f32[2,128,1024]{2,1,0:T(8,128)S(1)}, bf16[2,512,128]{2,1,0:T(8,128)(2,1)S(1)}) custom-call(s32[128]{0:T(128)S(1)} %copy-done.1, bf16[2,528,128]{2,1,0:T(8,128)(2,1)S(1)} %bitcast_dynamic-update-slice_fusion.refs_0_, bf16[2,528,128]{2,1,0:T(8,128)(2,1)S(1)} %collective-permute-done.1.refs_1_, ...), custom_call_target="tpu_custom_call", output_to_operand_aliasing={{0}: (6, {})} | custom-call | flops 1006632960 | bytes 1048576 | tf_op jit(solution)/shard_map/pallas_call | solution.py:215
  34.0 3.5 %collective-permute-start.8 = (bf16[2,512,128]{2,1,0:T(8,128)(2,1)S(1)}, bf16[2,512,128]{2,1,0:T(8,128)(2,1)S(1)}, u32[]{:S(2)}, u32[]{:S(2)}) collective-permute-start(bf16[2,512,128]{2,1,0:T(8,128)(2,1)S(1)} %get-tuple-element.32), channel_id=1, source_target_pairs={{0,128},{64,192},{128,0},{192,64},{1,129},{65,193},{129,1},{193,65... | collective-permute-start | bytes 786440 | tf_op jit(solution)/shard_map/ppermute | solution.py:264
  37.5 2.8 %shard_map.97 = (f32[2,128,1024]{2,1,0:T(8,128)S(1)}, bf16[2,512,128]{2,1,0:T(8,128)(2,1)S(1)}) custom-call(s32[128]{0:T(128)S(1)} %copy-done.1, bf16[2,528,128]{2,1,0:T(8,128)(2,1)S(1)} %bitcast_dynamic-update-slice_fusion.refs_0_, bf16[2,528,128]{2,1,0:T(8,128)(2,1)S(1)} %collective-permute-done.1.refs_1_, ...), custom_call_target="tpu_custom_call", output_to_operand_aliasing={{0}: (6, {})} | custom-call | flops 1006632960 | bytes 1048576 | tf_op jit(solution)/shard_map/pallas_call | solution.py:215
  40.3 2.7 %shard_map.98 = (f32[2,128,1024]{2,1,0:T(8,128)S(1)}, bf16[2,512,128]{2,1,0:T(8,128)(2,1)S(1)}) custom-call(s32[128]{0:T(128)S(1)} %copy-done.1, bf16[2,528,128]{2,1,0:T(8,128)(2,1)S(1)} %bitcast_dynamic-update-slice_fusion.refs_0_, bf16[2,528,128]{2,1,0:T(8,128)(2,1)S(1)} %collective-permute-done.1.refs_1_, ...), custom_call_target="tpu_custom_call", output_to_operand_aliasing={{0}: (6, {})} | custom-call | flops 1006632960 | bytes 1048576 | tf_op jit(solution)/shard_map/pallas_call | solution.py:215
  43.8 2.6 %collective-permute-start.13 = (bf16[2,512,128]{2,1,0:T(8,128)(2,1)S(1)}, bf16[2,512,128]{2,1,0:T(8,128)(2,1)S(1)}, u32[]{:S(2)}, u32[]{:S(2)}) collective-permute-start(bf16[2,512,128]{2,1,0:T(8,128)(2,1)S(1)} %get-tuple-element.41), channel_id=1, source_target_pairs={{0,192},{64,0},{128,64},{192,128},{1,193},{65,1},{129,65},{193,129... | collective-permute-start | bytes 786440 | tf_op jit(solution)/shard_map/ppermute | solution.py:264
  46.4 2.0 %shard_map.99 = (f32[2,256,128]{2,1,0:T(8,128)S(1)}, bf16[2,256,128]{2,1,0:T(8,128)(2,1)S(1)}, bf16[2,256,128]{2,1,0:T(8,128)(2,1)S(1)}, bf16[2,256,128]{2,1,0:T...) custom-call(s32[128]{0:T(128)S(1)} %copy-done.1, ...), custom_call_target="tpu_custom_call" | custom-call | flops 503316480 | bytes 1048576 | tf_op jit(solution)/shard_map/pallas_call | solution.py:215
  48.3 3.0 %collective-permute-start.9 = (bf16[2,256,128]{2,1,0:T(8,128)(2,1)S(1)}, bf16[2,256,128]{2,1,0:T(8,128)(2,1)S(1)}, u32[]{:S(2)}, u32[]{:S(2)}) collective-permute-start(bf16[2,256,128]{2,1,0:T(8,128)(2,1)S(1)} %get-tuple-element.34), channel_id=1, source_target_pairs={{0,56},{8,0},{16,8},{24,16},{32,24},{40,32},{48,40},{56,48},{1,57}... | collective-permute-start | bytes 393224 | tf_op jit(solution)/shard_map/ppermute | solution.py:265
  52.0 6.5 %collective-permute-start.15 = (bf16[512,128]{1,0:T(8,128)(2,1)S(1)}, bf16[512,128]{1,0:T(8,128)(2,1)S(1)}, u32[]{:S(2)}, u32[]{:S(2)}) collective-permute-start(bf16[512,128]{1,0:T(8,128)(2,1)S(1)} %get-tuple-element.44), channel_id=1, source_target_pairs={{0,32},{8,40},{16,48},{24,56},{32,0},{40,8},{48,16},{56,24},{1,33}... | collective-permute-start | bytes 393224 | tf_op jit(solution)/shard_map/ppermute | solution.py:271
  58.5 1.8 %collective-permute-done.10.refs_1_ = bf16[2,256,128]{2,1,0:T(8,128)(2,1)S(1)} collective-permute-done((bf16[2,256,128]{2,1,0:T(8,128)(2,1)S(1)}, bf16[2,256,128]{2,1,0:T(8,128)(2,1)S(1)}, u32[]{:S(2)}, u32[]{:S(2)}) %collective-permute-start.10) | collective-permute-done | bytes 131104 | tf_op jit(solution)/shard_map/ppermute | solution.py:265
  60.4 2.2 %collective-permute-done.11.refs_2_ = bf16[2,256,128]{2,1,0:T(8,128)(2,1)S(1)} collective-permute-done((bf16[2,256,128]{2,1,0:T(8,128)(2,1)S(1)}, bf16[2,256,128]{2,1,0:T(8,128)(2,1)S(1)}, u32[]{:S(2)}, u32[]{:S(2)}) %collective-permute-start.11) | collective-permute-done | bytes 131104 | tf_op jit(solution)/shard_map/ppermute | solution.py:265
  62.6 0.9 %collective-permute-start.12 = (bf16[256,128]{1,0:T(8,128)(2,1)S(1)}, bf16[256,128]{1,0:T(8,128)(2,1)S(1)}, u32[]{:S(2)}, u32[]{:S(2)}) collective-permute-start(bf16[256,128]{1,0:T(8,128)(2,1)S(1)} %get-tuple-element.38), channel_id=1, source_target_pairs={{0,4},{4,0},{1,5},{5,1},{2,6},{6,2},{3,7},{7,3},{8,12},{12,8},{9,1... | collective-permute-start | bytes 196616 | tf_op jit(solution)/shard_map/ppermute | solution.py:273
  64.1 2.9 %collective-permute-done.12.dqx_ref = bf16[256,128]{1,0:T(8,128)(2,1)S(1)} collective-permute-done((bf16[256,128]{1,0:T(8,128)(2,1)S(1)}, bf16[256,128]{1,0:T(8,128)(2,1)S(1)}, u32[]{:S(2)}, u32[]{:S(2)}) %collective-permute-start.12) | collective-permute-done | bytes 65568 | tf_op jit(solution)/shard_map/ppermute | solution.py:273
  (25 shorter events, 3.5 us)
Async XLA Ops:
  2.4 9.4 %collective-permute-start = (bf16[528,128]{1,0:T(8,128)(2,1)}, bf16[528,128]{1,0:T(8,128)(2,1)S(1)}, u32[]{:S(2)}, u32[]{:S(2)}) collective-permute-start(bf16[528,128]{1,0:T(8,128)(2,1)} %get-tuple-element.24), channel_id=1, source_target_pairs={{0,4},{4,0},{1,5},{5,1},{2,6},{6,2},{3,7},{7,3},{8,12},{12,8},{9,1... | collective-permute-start | bytes 405512 | tf_op jit(solution)/shard_map/ppermute | solution.py:239
  3.7 12.8 %collective-permute-start.4 = (bf16[512,128]{1,0:T(8,128)(2,1)}, bf16[512,128]{1,0:T(8,128)(2,1)S(1)}, u32[]{:S(2)}, u32[]{:S(2)}) collective-permute-start(bf16[512,128]{1,0:T(8,128)(2,1)} %get-tuple-element.25), channel_id=1, source_target_pairs={{0,32},{8,40},{16,48},{24,56},{32,0},{40,8},{48,16},{56,24},{1,33}... | collective-permute-start | bytes 393224 | tf_op jit(solution)/shard_map/ppermute | solution.py:237
  11.8 4.6 %copy-start = (bf16[512,128]{1,0:T(8,128)(2,1)S(1)}, bf16[512,128]{1,0:T(8,128)(2,1)}, u32[]{:S(2)}) copy-start(bf16[512,128]{1,0:T(8,128)(2,1)} %get-tuple-element.25) | copy-start | bytes 393220
  11.9 11.6 %collective-permute-start.3 = (bf16[2,528,128]{2,1,0:T(8,128)(2,1)S(1)}, bf16[2,528,128]{2,1,0:T(8,128)(2,1)S(1)}, u32[]{:S(2)}, u32[]{:S(2)}) collective-permute-start(bf16[2,528,128]{2,1,0:T(8,128)(2,1)S(1)} %bitcast_dynamic-update-slice_fusion.refs_0_), channel_id=1, source_target_pairs={{0,48},{8,24},{16,0},{24,40},{32,16},{40,56},{48,32},{56,8},{1,49}... | collective-permute-start | bytes 811016 | tf_op jit(solution)/shard_map/ppermute | solution.py:242
  14.4 15.0 %collective-permute-start.2 = (bf16[2,528,128]{2,1,0:T(8,128)(2,1)S(1)}, bf16[2,528,128]{2,1,0:T(8,128)(2,1)S(1)}, u32[]{:S(2)}, u32[]{:S(2)}) collective-permute-start(bf16[2,528,128]{2,1,0:T(8,128)(2,1)S(1)} %bitcast_dynamic-update-slice_fusion.refs_0_), channel_id=1, source_target_pairs={{0,56},{8,0},{16,8},{24,16},{32,24},{40,32},{48,40},{56,48},{1,57}... | collective-permute-start | bytes 811016 | tf_op jit(solution)/shard_map/ppermute | solution.py:242
  15.6 13.8 %collective-permute-start.1 = (bf16[2,528,128]{2,1,0:T(8,128)(2,1)S(1)}, bf16[2,528,128]{2,1,0:T(8,128)(2,1)S(1)}, u32[]{:S(2)}, u32[]{:S(2)}) collective-permute-start(bf16[2,528,128]{2,1,0:T(8,128)(2,1)S(1)} %bitcast_dynamic-update-slice_fusion.refs_0_), channel_id=1, source_target_pairs={{0,8},{8,16},{16,24},{24,32},{32,40},{40,48},{48,56},{56,0},{1,9},... | collective-permute-start | bytes 811016 | tf_op jit(solution)/shard_map/ppermute | solution.py:242
  16.5 13.0 %copy-start.1 = (s32[128]{0:T(128)S(1)}, s32[128]{0:T(128)}, u32[]{:S(2)}) copy-start(s32[128]{0:T(128)} %fold_ref.9) | copy-start | bytes 1540
  16.5 14.8 %collective-permute-start.7 = (bf16[2,512,128]{2,1,0:T(8,128)(2,1)S(1)}, bf16[2,512,128]{2,1,0:T(8,128)(2,1)S(1)}, u32[]{:S(2)}, u32[]{:S(2)}) collective-permute-start(bf16[2,512,128]{2,1,0:T(8,128)(2,1)S(1)} %pad_maximum_fusion), channel_id=1, source_target_pairs={{0,128},{64,192},{128,0},{192,64},{1,129},{65,193},{129,1},{193,65... | collective-permute-start | bytes 786440 | tf_op jit(solution)/shard_map/ppermute | solution.py:243
  19.8 17.7 %collective-permute-start.6 = (bf16[2,512,128]{2,1,0:T(8,128)(2,1)S(1)}, bf16[2,512,128]{2,1,0:T(8,128)(2,1)S(1)}, u32[]{:S(2)}, u32[]{:S(2)}) collective-permute-start(bf16[2,512,128]{2,1,0:T(8,128)(2,1)S(1)} %pad_maximum_fusion), channel_id=1, source_target_pairs={{0,64},{64,128},{128,192},{192,0},{1,65},{65,129},{129,193},{193,1... | collective-permute-start | bytes 786440 | tf_op jit(solution)/shard_map/ppermute | solution.py:243
  23.5 16.8 %collective-permute-start.5 = (bf16[2,512,128]{2,1,0:T(8,128)(2,1)S(1)}, bf16[2,512,128]{2,1,0:T(8,128)(2,1)S(1)}, u32[]{:S(2)}, u32[]{:S(2)}) collective-permute-start(bf16[2,512,128]{2,1,0:T(8,128)(2,1)S(1)} %pad_maximum_fusion), channel_id=1, source_target_pairs={{0,192},{64,0},{128,64},{192,128},{1,193},{65,1},{129,65},{193,129... | collective-permute-start | bytes 786440 | tf_op jit(solution)/shard_map/ppermute | solution.py:243
  34.0 12.3 %collective-permute-start.8 = (bf16[2,512,128]{2,1,0:T(8,128)(2,1)S(1)}, bf16[2,512,128]{2,1,0:T(8,128)(2,1)S(1)}, u32[]{:S(2)}, u32[]{:S(2)}) collective-permute-start(bf16[2,512,128]{2,1,0:T(8,128)(2,1)S(1)} %get-tuple-element.32), channel_id=1, source_target_pairs={{0,128},{64,192},{128,0},{192,64},{1,129},{65,193},{129,1},{193,65... | collective-permute-start | bytes 786440 | tf_op jit(solution)/shard_map/ppermute | solution.py:264
  43.0 8.8 %collective-permute-start.14 = (bf16[2,512,128]{2,1,0:T(8,128)(2,1)S(1)}, bf16[2,512,128]{2,1,0:T(8,128)(2,1)S(1)}, u32[]{:S(2)}, u32[]{:S(2)}) collective-permute-start(bf16[2,512,128]{2,1,0:T(8,128)(2,1)S(1)} %get-tuple-element.42), channel_id=1, source_target_pairs={{0,64},{64,128},{128,192},{192,0},{1,65},{65,129},{129,193},{193,1... | collective-permute-start | bytes 786440 | tf_op jit(solution)/shard_map/ppermute | solution.py:264
  43.8 8.1 %collective-permute-start.13 = (bf16[2,512,128]{2,1,0:T(8,128)(2,1)S(1)}, bf16[2,512,128]{2,1,0:T(8,128)(2,1)S(1)}, u32[]{:S(2)}, u32[]{:S(2)}) collective-permute-start(bf16[2,512,128]{2,1,0:T(8,128)(2,1)S(1)} %get-tuple-element.41), channel_id=1, source_target_pairs={{0,192},{64,0},{128,64},{192,128},{1,193},{65,1},{129,65},{193,129... | collective-permute-start | bytes 786440 | tf_op jit(solution)/shard_map/ppermute | solution.py:264
  48.3 10.2 %collective-permute-start.9 = (bf16[2,256,128]{2,1,0:T(8,128)(2,1)S(1)}, bf16[2,256,128]{2,1,0:T(8,128)(2,1)S(1)}, u32[]{:S(2)}, u32[]{:S(2)}) collective-permute-start(bf16[2,256,128]{2,1,0:T(8,128)(2,1)S(1)} %get-tuple-element.34), channel_id=1, source_target_pairs={{0,56},{8,0},{16,8},{24,16},{32,24},{40,32},{48,40},{56,48},{1,57}... | collective-permute-start | bytes 393224 | tf_op jit(solution)/shard_map/ppermute | solution.py:265
  51.3 9.0 %collective-permute-start.10 = (bf16[2,256,128]{2,1,0:T(8,128)(2,1)S(1)}, bf16[2,256,128]{2,1,0:T(8,128)(2,1)S(1)}, u32[]{:S(2)}, u32[]{:S(2)}) collective-permute-start(bf16[2,256,128]{2,1,0:T(8,128)(2,1)S(1)} %get-tuple-element.35), channel_id=1, source_target_pairs={{0,8},{8,16},{16,24},{24,32},{32,40},{40,48},{48,56},{56,0},{1,9},... | collective-permute-start | bytes 393224 | tf_op jit(solution)/shard_map/ppermute | solution.py:265
  51.3 11.2 %collective-permute-start.11 = (bf16[2,256,128]{2,1,0:T(8,128)(2,1)S(1)}, bf16[2,256,128]{2,1,0:T(8,128)(2,1)S(1)}, u32[]{:S(2)}, u32[]{:S(2)}) collective-permute-start(bf16[2,256,128]{2,1,0:T(8,128)(2,1)S(1)} %get-tuple-element.36), channel_id=1, source_target_pairs={{48,0},{24,8},{0,16},{40,24},{16,32},{56,40},{32,48},{8,56},{49,1}... | collective-permute-start | bytes 393224 | tf_op jit(solution)/shard_map/ppermute | solution.py:265
  52.0 12.1 %collective-permute-start.15 = (bf16[512,128]{1,0:T(8,128)(2,1)S(1)}, bf16[512,128]{1,0:T(8,128)(2,1)S(1)}, u32[]{:S(2)}, u32[]{:S(2)}) collective-permute-start(bf16[512,128]{1,0:T(8,128)(2,1)S(1)} %get-tuple-element.44), channel_id=1, source_target_pairs={{0,32},{8,40},{16,48},{24,56},{32,0},{40,8},{48,16},{56,24},{1,33}... | collective-permute-start | bytes 393224 | tf_op jit(solution)/shard_map/ppermute | solution.py:271
  62.6 4.4 %collective-permute-start.12 = (bf16[256,128]{1,0:T(8,128)(2,1)S(1)}, bf16[256,128]{1,0:T(8,128)(2,1)S(1)}, u32[]{:S(2)}, u32[]{:S(2)}) collective-permute-start(bf16[256,128]{1,0:T(8,128)(2,1)S(1)} %get-tuple-element.38), channel_id=1, source_target_pairs={{0,4},{4,0},{1,5},{5,1},{2,6},{6,2},{3,7},{7,3},{8,12},{12,8},{9,1... | collective-permute-start | bytes 196616 | tf_op jit(solution)/shard_map/ppermute | solution.py:273

commit v7 on v6

v7 whole, which is shorter than its diff:
```python
import functools
import math

import jax
import jax.numpy as jnp
from jax import lax
from jax.experimental import pallas as pl
from jax.experimental.pallas import tpu as pltpu
from jax.sharding import Mesh, PartitionSpec as P

F32 = jnp.float32
BF16 = jnp.bfloat16
BLK = 128
DIM = 128
LOG2E = math.log2(math.e)
FACTOR = 1.0 / math.sqrt(DIM)
VMEM_LIMIT = 48 * 1024 * 1024
PREP_VMEM = 62 * 1024 * 1024
FLOPS = 10 * 2 * 3 * (2 * BLK) * (4 * BLK) * DIM
HIDE = 1e30
Y_FROM = (0, 2, 3, 1)
NT = (((1,), (1,)), ((), ()))
ROWS = 4 * BLK + 16


def dot(a, b):
    return jnp.dot(a, b, preferred_element_type=F32)


def dot_nt(a, b):
    return lax.dot_general(a, b, NT, preferred_element_type=F32)


def prep_kernel(*refs):
    sources, (qout_ref, kout_ref), buffers, refs = refs[:7], refs[7:9], refs[9:16], refs[16:]
    qrows_buf, krows_buf, load_sems, store_sems = refs
    loads = [pltpu.make_async_copy(s, d, load_sems.at[n]) for n, (s, d) in enumerate(zip(sources, buffers))]
    for copy in loads:
        copy.start()
    stores = []

    def store(source, target):
        stores.append(pltpu.make_async_copy(source, target, store_sems.at[len(stores)]))
        stores[-1].start()

    def store_blocks(n, out_ref, at):
        loads[n].wait()
        store(buffers[n].at[pl.ds(low_at, BLK)], out_ref.at[at : at + BLK])
        store(buffers[n].at[pl.ds(high_at, BLK)], out_ref.at[at + BLK : at + 2 * BLK])

    fold_ref, g_buf, o_buf, lse_buf = buffers[:4]
    device = lax.axis_index("pb") * 16 + lax.axis_index("kz") * 2 + lax.axis_index("kx")
    loads[0].wait()
    first, second = fold_ref[2 * device], fold_ref[2 * device + 1]
    swapped = second < first
    low_at = pl.multiple_of(jnp.where(swapped, BLK, 0), BLK)
    high_at = pl.multiple_of(jnp.where(swapped, 0, BLK), BLK)
    low = jnp.minimum(first, second).astype(F32)
    krows_buf[...] = jnp.full(krows_buf.shape, low, F32).astype(BF16)
    store(krows_buf, kout_ref.at[4 * BLK :])
    store_blocks(1, qout_ref, 2 * BLK)
    loads[2].wait()
    loads[3].wait()
    lse = lse_buf[...].astype(F32)
    rows = [jnp.where(swapped, lse[:, BLK:], lse[:, :BLK]), jnp.where(swapped, lse[:, :BLK], lse[:, BLK:])]
    for at in (low_at, high_at):
        prod = g_buf[pl.ds(at, BLK), :].astype(F32) * o_buf[pl.ds(at, BLK), :].astype(F32)
        rows.append(jnp.sum(prod.T, axis=0, keepdims=True))
    rows.append(jnp.full((1, DIM), low, F32))
    rows.append(jnp.full((1, DIM), jnp.where(swapped, 1.0, 0.0), F32))
    qrows_buf[...] = jnp.concatenate(rows + [jnp.zeros((10, DIM), F32)], axis=0).astype(BF16)
    store(qrows_buf, qout_ref.at[4 * BLK :])
    store_blocks(6, qout_ref, 0)
    store_blocks(4, kout_ref, 0)
    store_blocks(5, kout_ref, 2 * BLK)
    for copy in stores:
        copy.wait()


def tile(k, v, kt, q, g, lses, delta, diagonal=None):
    s = dot_nt(k, q)
    probs = []
    for b, lse in enumerate(lses):
        p = jnp.exp2(s[b * BLK : (b + 1) * BLK] * (FACTOR * LOG2E) - lse)
        if b == diagonal:
            shape = (BLK, BLK)
            seen = lax.broadcasted_iota(jnp.int32, shape, 0) <= lax.broadcasted_iota(jnp.int32, shape, 1)
            p = jnp.concatenate([jnp.where(seen, p[:, :BLK], 0.0), p[:, BLK:]], 1)
        probs.append(p)
    p = jnp.concatenate(probs, 0)
    dp = dot_nt(v, g)
    ds = (p * (dp - delta)).astype(BF16)
    return dot(p.astype(BF16), g), dot(ds, q), dot(kt, ds)


def grad_kernel(js, plan, own, *refs):
    refs = list(refs)

    def take(count):
        taken = refs[:count]
        del refs[:count]
        return taken

    q_refs, (y_ref,) = take(2 * len(plan)), take(1)
    dqin_refs = [None if first else take(1)[0] for first, _ in plan]
    dq_refs = [take(2 if last else 1) for _, last in plan]
    dkv_ref, dv_acc, dk_acc = refs
    count = len(js)
    half = count * BLK

    def keys(array):
        at = array * 2 * BLK
        return jnp.concatenate([y_ref[j, at + b * BLK : at + (b + 1) * BLK, :] for b in range(2) for j in js], 0)

    k, v = keys(0), keys(1)
    kt = k.T
    low_j = [jnp.concatenate([y_ref[j, 4 * BLK :, :].astype(F32)[0:1, :]] * 4, 1) for j in js]

    for n, (first, last) in enumerate(plan):
        pair = q_refs[2 * n : 2 * n + 2]
        chunks = [(ref, a) for ref in pair for a in range(2)]

        def queries(array, b):
            at = (2 * array + b) * BLK
            return jnp.concatenate([ref[a, at : at + BLK, :] for ref, a in chunks], 0)

        tiles = [ref[a, 4 * BLK :, :].astype(F32) for ref, a in chunks]
        lse_low, lse_high, delta_low, delta_high, low_i = (
            jnp.concatenate([t[r : r + 1, :] for t in tiles], 1) for r in range(5)
        )
        lse_low, lse_high = lse_low * LOG2E, lse_high * LOG2E
        diagonal = own and n == 0

        lses = [lse_high] * count + [lse_high + jnp.where(low_i <= low, 0.0, HIDE) for low in low_j]
        dv, dk, dq_high = tile(
            k, v, kt, queries(0, 1), queries(1, 1), lses, delta_high, count if diagonal else None
        )
        dv_acc[...] = dv if n == 0 else dv_acc[...] + dv
        dk_acc[...] = dk if n == 0 else dk_acc[...] + dk
        lses = [lse_low + jnp.where(low <= low_i, 0.0, HIDE) for low in low_j]
        dv, dk, dq_low = tile(
            k[:half], v[:half], kt[:, :half], queries(0, 0), queries(1, 0), lses, delta_low, 0 if diagonal else None
        )
        dv_acc[:half] += dv
        dk_acc[:half] += dk
        for b, dq in ((0, dq_low), (1, dq_high)):
            if not first:
                dq = dqin_refs[n][b] + dq
            if not last:
                dq_refs[n][0][b] = dq
            else:
                for c in range(4):
                    ref = dq_refs[n][c // 2]
                    ref[c % 2, b * BLK : (b + 1) * BLK, :] = dq[:, c * BLK : (c + 1) * BLK].T.astype(ref.dtype)

    for m in range(count):
        for b in range(2):
            source = slice(b * half + m * BLK, b * half + (m + 1) * BLK)
            for array, acc in ((0, dk_acc), (1, dv_acc)):
                at = (2 * array + b) * BLK
                dkv_ref[m, at : at + BLK, :] = acc[source].astype(dkv_ref.dtype)


def meet_kernel(parts, *refs):
    out_refs = refs[-2:]
    for half, out_ref in enumerate(out_refs):
        total = None
        for ref, index in zip(refs, parts):
            if index[half] is not None:
                part = ref[index[half]].astype(F32)
                total = part if total is None else total + part
        out_ref[...] = total.astype(out_ref.dtype)


def last_kernel(rows_ref, dq_ref, dqx_ref, dkv_ref, dkvz_ref, q_ref, k_ref, v_ref):
    swapped = rows_ref[0, 4 * BLK :, :].astype(F32)[5:6, :] > 0.5

    def restore(out_ref, total):
        low, high = total[:BLK], total[BLK:]
        out_ref[:BLK, :] = jnp.where(swapped, high, low).astype(BF16)
        out_ref[BLK:, :] = jnp.where(swapped, low, high).astype(BF16)

    restore(q_ref, (dq_ref[...] + dqx_ref[...].astype(F32)) * FACTOR)
    dkv = dkv_ref[...] + dkvz_ref[...].astype(F32)
    restore(k_ref, dkv[: 2 * BLK] * FACTOR)
    restore(v_ref, dkv[2 * BLK :])


def z_step(step):
    return [(i, (i + step) % 8) for i in range(8)]


def y_step(step):
    return [(i, (i + step) % 4) for i in range(4)]


Z_PAIRS = [(i, (i - 2) % 8 if i % 2 == 0 else (i + 2) % 8) for i in range(8)]
Z_BACK = [(b, a) for a, b in Z_PAIRS]
X_SWAP = [(0, 1), (1, 0)]


def call(kernel, outs, operands, scratch=(), hbm=False, **options):
    space = pl.BlockSpec(memory_space=pltpu.HBM if hbm else pltpu.VMEM)
    return pl.pallas_call(
        kernel,
        out_shape=[jax.ShapeDtypeStruct(s, t) for s, t in outs],
        in_specs=[space] * len(operands),
        out_specs=[space] * len(outs),
        scratch_shapes=list(scratch),
        compiler_params=pltpu.CompilerParams(vmem_limit_bytes=PREP_VMEM if hbm else VMEM_LIMIT),
        **options,
    )(*operands)


def body(queries, key_rows, value_rows, outputs, out_grad, saved_lse, fold_map):
    operands = (fold_map, out_grad, outputs, saved_lse.T, key_rows, value_rows, queries)
    buffers = [(pltpu.SMEM if n == 0 else pltpu.VMEM)(a.shape, a.dtype) for n, a in enumerate(operands)]
    rows = pltpu.VMEM((ROWS - 4 * BLK, DIM), BF16)
    sems = [pltpu.SemaphoreType.DMA((7,)), pltpu.SemaphoreType.DMA((10,))]
    payload = ((ROWS, DIM), BF16)
    mine_q, mine_k = call(prep_kernel, [payload] * 2, operands, buffers + [rows] * 2 + sems, hbm=True)

    def beside(mine, other):
        both = lax.optimization_barrier(jnp.pad(mine[None], ((0, 1), (0, 0), (0, 0))))
        return lax.dynamic_update_slice(both, other[None], (1, 0, 0))

    other_k = lax.ppermute(mine_k, "kz", z_step(4))
    q0 = beside(mine_q, lax.ppermute(mine_q, "kx", X_SWAP))
    _, other_k = lax.optimization_barrier((q0, other_k))
    k0 = jnp.stack([mine_k, other_k])
    q_sets = [q0] + [lax.ppermute(q0, "kz", p) for p in (z_step(1), z_step(-1), Z_PAIRS)]
    k_sets = [k0] + [lax.ppermute(k0, "pb", y_step(-s)) for s in Y_FROM[1:]]
    q_pairs = ([q_sets[0], q_sets[3]], [q_sets[1], q_sets[2]])

    def grad(turn, js, pairs, dq_in, last, dkv_type):
        plan = tuple((d is None, e) for d, e in zip(dq_in, last))
        outs = []
        for pair, end in zip(pairs, last):
            if end:
                outs += [((2, 2 * BLK, DIM), F32 if (pair, s) == (0, 0) else BF16) for s in range(2)]
            else:
                outs.append(((2, DIM, 4 * BLK), F32))
        acc = pltpu.VMEM((2 * len(js) * BLK, DIM), F32)
        units = len(js) * len(pairs)
        *dq, part = call(
            functools.partial(grad_kernel, js, plan, turn == 0 and js[0] == 0 and pairs[0] == 0),
            outs + [((len(js), 4 * BLK, DIM), dkv_type)],
            [q for p in pairs for q in q_pairs[p]] + [k_sets[turn]] + [d for d in dq_in if d is not None],
            [acc, acc],
            cost_estimate=pl.CostEstimate(flops=FLOPS * units // 4, bytes_accessed=1 << 20, transcendentals=0),
        )
        return dq, part

    def send_back(turn, part):
        return lax.ppermute(part, "pb", y_step(Y_FROM[turn]))

    (dq0,), own = grad(0, (0, 1), (0,), (None,), (False,), F32)
    (dq1,), own_a = grad(0, (0,), (1,), (None,), (False,), F32)
    (dq0, dq1), part = grad(1, (0, 1), (0, 1), (dq0, dq1), (False, False), BF16)
    back = [send_back(1, part)]
    (dq0, dq1), part = grad(2, (0, 1), (0, 1), (dq0, dq1), (False, False), BF16)
    back.append(send_back(2, part))
    (dq_keep, dq_z2, dq1), part = grad(3, (0, 1), (0, 1), (dq0, dq1), (True, False), BF16)
    back.append(send_back(3, part))
    dq1, back[0] = lax.optimization_barrier((dq1, back[0]))
    (dq_left, dq_right), own_b = grad(0, (1,), (1,), (dq1,), (True,), F32)
    dq_back = [lax.ppermute(d, "kz", p) for d, p in ((dq_left, z_step(-1)), (dq_right, z_step(1)), (dq_z2, Z_BACK))]

    def meet(operands, parts, shape):
        return call(functools.partial(meet_kernel, parts), [(shape, F32), (shape, BF16)], operands)

    both = (0, 1)
    dkv_keep, dkv_send = meet([own, own_a, own_b] + back, [both, (0, None), (None, 0)] + [both] * 3, (4 * BLK, DIM))
    dkv_last = lax.ppermute(dkv_send, "kz", z_step(4))
    dq_keep, dq_send = meet([dq_keep] + dq_back, [both] * 4, (2 * BLK, DIM))
    dq_last = lax.ppermute(dq_send, "kx", X_SWAP)
    return tuple(call(last_kernel, [((2 * BLK, DIM), BF16)] * 3, (q0, dq_keep, dq_last, dkv_keep, dkv_last)))


def solution(mesh):
    fine = Mesh(mesh.devices.reshape(4, 8, 2, 2, 2), ("pb", "kz", "kx", "hx", "hc"))
    rows = P(("pb", "kz", "kx"), ("hx", "hc"))
    return jax.shard_map(
        body,
        mesh=fine,
        in_specs=(rows,) * 6 + (P(),),
        out_specs=(rows,) * 3,
        check_vma=False,
    )
```

time: 67.8 us -> 62.8 us (0.926)
  the two profiles are of different devices: /device:TPU:4 before, /device:TPU:56 now
where the time goes in v7:
time: 62.8 us; the launch traced here: 62.6 us
  waiting for transfers between devices  25.6 us (41%)
  starting transfers between devices  23.8 us (38%)
  Pallas kernels  11.5 us (18%)
  local copies, waits for them, and re-layouts  0.96 us (2%)
  between operations  0.77 us (1%)
    pallas_call x10, Pallas kernels, call(): pl.pallas_call(kernel, out_shape=[jax.ShapeDtypeStruct(s, t) for s, t in...  11.5 us
    ppermute x3, waiting for transfers between devices, body(): lax.ppermute(q0, 'kz', p)  7.38 us
    ppermute x1, starting transfers between devices, body(): other_k = lax.ppermute(mine_k, 'kz', z_step(4))  6.29 us
    ppermute x1, waiting for transfers between devices, body(): dkv_last = lax.ppermute(dkv_send, 'kz', z_step(4))  5.87 us
    ppermute x3, waiting for transfers between devices, body(): k_sets = [k0] + [lax.ppermute(k0, 'pb', y_step(-s)) for s in Y_FROM[1:]]  5.4 us
    ppermute x3, starting transfers between devices, body(): k_sets = [k0] + [lax.ppermute(k0, 'pb', y_step(-s)) for s in Y_FROM[1:]]  4.25 us
    ppermute x3, starting transfers between devices, body(): lax.ppermute(q0, 'kz', p)  3.57 us
    ppermute x3, starting transfers between devices, send_back(): return lax.ppermute(part, 'pb', y_step(Y_FROM[turn]))  3.31 us
  transfers between devices with their start and end apart: 16, of which 7 were waited for; matrix products, arithmetic and copies ran while one was open for 2% of the time, Pallas kernels for 14%

profile of v7, /device:TPU:56, one launch (start us, length us, event | category | flops | bytes accessed | tf_op | source)
XLA Modules:
  0.0 62.6 jit_solution(2347122485511879152)
XLA Ops:
  0.6 1.8 %shard_map.94 = (bf16[528,128]{1,0:T(8,128)(2,1)}, bf16[528,128]{1,0:T(8,128)(2,1)}) custom-call(s32[128]{0:T(128)} %refs_0_.1, bf16[256,128]{1,0:T(8,128)(2,1)} %refs_1_.1, bf16[256,128]{1,0:T(8,128)(2,1)} %refs_2_.1, bf16[1,256]{1,0:T(2,128)(2,1)} %bitcast.9, bf16[256,128]{1,0:T(8,128)(2,1)} %refs_4_.1, bf16[256,128]{1,0:T(8,128)(2,1)} %refs_5_.1, ...), custom_call_target="tpu_custom_call" | custom-call | tf_op jit(solution)/shard_map/pallas_call | solution.py:204
  2.5 1.6 %collective-permute-start = (bf16[528,128]{1,0:T(8,128)(2,1)}, bf16[528,128]{1,0:T(8,128)(2,1)S(1)}, u32[]{:S(2)}, u32[]{:S(2)}) collective-permute-start(bf16[528,128]{1,0:T(8,128)(2,1)} %get-tuple-element.29), channel_id=1, source_target_pairs={{0,4},{4,0},{1,5},{5,1},{2,6},{6,2},{3,7},{7,3},{8,12},{12,8},{9,1... | collective-permute-start | bytes 405512 | tf_op jit(solution)/shard_map/ppermute | solution.py:228
  4.0 6.3 %collective-permute-start.4 = (bf16[528,128]{1,0:T(8,128)(2,1)}, bf16[528,128]{1,0:T(8,128)(2,1)S(1)}, u32[]{:S(2)}, u32[]{:S(2)}) collective-permute-start(bf16[528,128]{1,0:T(8,128)(2,1)} %get-tuple-element.30), channel_id=1, source_target_pairs={{0,32},{8,40},{16,48},{24,56},{32,0},{40,8},{48,16},{56,24},{1,33}... | collective-permute-start | bytes 405512 | tf_op jit(solution)/shard_map/ppermute | solution.py:227
  10.3 0.9 %pad.4 = bf16[2,528,128]{2,1,0:T(8,128)(2,1)S(1)} pad(bf16[1,528,128]{2,1,0:T(8,128)(2,1)} %bitcast.6, bf16[]{:T(256)} %constant.1.clone.1), padding=0_1x0_0x0_0 | pad | bytes 405506 | tf_op jit(solution)/shard_map/jit(_pad)/pad | solution.py:224
  11.3 1.1 %collective-permute-start.2 = (bf16[2,528,128]{2,1,0:T(8,128)(2,1)S(1)}, bf16[2,528,128]{2,1,0:T(8,128)(2,1)S(1)}, u32[]{:S(2)}, u32[]{:S(2)}) collective-permute-start(bf16[2,528,128]{2,1,0:T(8,128)(2,1)S(1)} %bitcast_dynamic-update-slice_fusion.refs_0_.rows_ref), channel_id=1, source_target_pairs={{0,8},{8,16},{16,24},{24,32},{32,40},{40,48},{48,56},{56,0},{1,9},... | collective-permute-start | bytes 811016 | tf_op jit(solution)/shard_map/ppermute | solution.py:231
  12.4 1.0 %collective-permute-start.3 = (bf16[2,528,128]{2,1,0:T(8,128)(2,1)S(1)}, bf16[2,528,128]{2,1,0:T(8,128)(2,1)S(1)}, u32[]{:S(2)}, u32[]{:S(2)}) collective-permute-start(bf16[2,528,128]{2,1,0:T(8,128)(2,1)S(1)} %bitcast_dynamic-update-slice_fusion.refs_0_.rows_ref), channel_id=1, source_target_pairs={{0,56},{8,0},{16,8},{24,16},{32,24},{40,32},{48,40},{56,48},{1,57}... | collective-permute-start | bytes 811016 | tf_op jit(solution)/shard_map/ppermute | solution.py:231
  13.4 1.5 %collective-permute-start.1 = (bf16[2,528,128]{2,1,0:T(8,128)(2,1)S(1)}, bf16[2,528,128]{2,1,0:T(8,128)(2,1)S(1)}, u32[]{:S(2)}, u32[]{:S(2)}) collective-permute-start(bf16[2,528,128]{2,1,0:T(8,128)(2,1)S(1)} %bitcast_dynamic-update-slice_fusion.refs_0_.rows_ref), channel_id=1, source_target_pairs={{0,48},{8,24},{16,0},{24,40},{32,16},{40,56},{48,32},{56,8},{1,49}... | collective-permute-start | bytes 811016 | tf_op jit(solution)/shard_map/ppermute | solution.py:231
  14.9 2.5 %collective-permute-done.4 = bf16[528,128]{1,0:T(8,128)(2,1)S(1)} collective-permute-done((bf16[528,128]{1,0:T(8,128)(2,1)}, bf16[528,128]{1,0:T(8,128)(2,1)S(1)}, u32[]{:S(2)}, u32[]{:S(2)}) %collective-permute-start.4) | collective-permute-done | bytes 135200 | tf_op jit(solution)/shard_map/ppermute | solution.py:227
  17.4 1.3 %collective-permute-start.7 = (bf16[2,528,128]{2,1,0:T(8,128)(2,1)S(1)}, bf16[2,528,128]{2,1,0:T(8,128)(2,1)S(1)}, u32[]{:S(2)}, u32[]{:S(2)}) collective-permute-start(bf16[2,528,128]{2,1,0:T(8,128)(2,1)S(1)} %pad_maximum_fusion.refs_2_), channel_id=1, source_target_pairs={{0,128},{64,192},{128,0},{192,64},{1,129},{65,193},{129,1},{193,65... | collective-permute-start | bytes 811016 | tf_op jit(solution)/shard_map/ppermute | solution.py:232
  18.8 2.2 %collective-permute-start.6 = (bf16[2,528,128]{2,1,0:T(8,128)(2,1)S(1)}, bf16[2,528,128]{2,1,0:T(8,128)(2,1)S(1)}, u32[]{:S(2)}, u32[]{:S(2)}) collective-permute-start(bf16[2,528,128]{2,1,0:T(8,128)(2,1)S(1)} %pad_maximum_fusion.refs_2_), channel_id=1, source_target_pairs={{0,64},{64,128},{128,192},{192,0},{1,65},{65,129},{129,193},{193,1... | collective-permute-start | bytes 811016 | tf_op jit(solution)/shard_map/ppermute | solution.py:232
  20.9 7.4 %collective-permute-done.2.refs_0_.refs_2_ = bf16[2,528,128]{2,1,0:T(8,128)(2,1)S(1)} collective-permute-done((bf16[2,528,128]{2,1,0:T(8,128)(2,1)S(1)}, bf16[2,528,128]{2,1,0:T(8,128)(2,1)S(1)}, u32[]{:S(2)}, u32[]{:S(2)}) %collective-permute-start.2) | collective-permute-done | bytes 270368 | tf_op jit(solution)/shard_map/ppermute | solution.py:231
  29.8 1.1 %shard_map.95 = (f32[2,128,512]{2,1,0:T(8,128)S(1)}, f32[2,512,128]{2,1,0:T(8,128)S(1)}) custom-call(bf16[2,528,128]{2,1,0:T(8,128)(2,1)S(1)} %bitcast_dynamic-update-slice_fusion.refs_0_.rows_ref, bf16[2,528,128]{2,1,0:T(8,128)(2,1)S(1)} %collective-permute-done.1.refs_1_, bf16[2,528,128]{2,1,0:T(8,128)(2,1)S(1)} %pad_maximum_fusion.refs_2_), custom_call_target="tpu_custom_call" | custom-call | flops 503316480 | bytes 1048576 | tf_op jit(solution)/shard_map/pallas_call | solution.py:204
  30.9 2.0 %shard_map.97 = (f32[2,128,512]{2,1,0:T(8,128)S(1)}, f32[2,128,512]{2,1,0:T(8,128)S(1)}, bf16[2,512,128]{2,1,0:T(8,128)(2,1)S(1)}) custom-call(bf16[2,528,128]{2,1,0:T(8,128)(2,1)S(1)} %bitcast_dynamic-update-slice_fusion.refs_0_.rows_ref, bf16[2,528,128]{2,1,0:T(8,128)(2,1)S(1)} %collective-permute-done.1.refs_1_, ...), custom_call_target="tpu_custom_call" | custom-call | flops 1006632960 | bytes 1048576 | tf_op jit(solution)/shard_map/pallas_call | solution.py:204
  32.9 1.2 %collective-permute-start.8 = (bf16[2,512,128]{2,1,0:T(8,128)(2,1)S(1)}, bf16[2,512,128]{2,1,0:T(8,128)(2,1)S(1)}, u32[]{:S(2)}, u32[]{:S(2)}) collective-permute-start(bf16[2,512,128]{2,1,0:T(8,128)(2,1)S(1)} %get-tuple-element.40), channel_id=1, source_target_pairs={{0,128},{64,192},{128,0},{192,64},{1,129},{65,193},{129,1},{193,65... | collective-permute-start | bytes 786440 | tf_op jit(solution)/shard_map/ppermute | solution.py:255
  34.2 2.0 %shard_map.98 = (f32[2,128,512]{2,1,0:T(8,128)S(1)}, f32[2,128,512]{2,1,0:T(8,128)S(1)}, bf16[2,512,128]{2,1,0:T(8,128)(2,1)S(1)}) custom-call(bf16[2,528,128]{2,1,0:T(8,128)(2,1)S(1)} %bitcast_dynamic-update-slice_fusion.refs_0_.rows_ref, bf16[2,528,128]{2,1,0:T(8,128)(2,1)S(1)} %collective-permute-done.1.refs_1_, ...), custom_call_target="tpu_custom_call" | custom-call | flops 1006632960 | bytes 1048576 | tf_op jit(solution)/shard_map/pallas_call | solution.py:204
  36.2 5.4 %collective-permute-done.5.refs_4_ = bf16[2,528,128]{2,1,0:T(8,128)(2,1)S(1)} collective-permute-done((bf16[2,528,128]{2,1,0:T(8,128)(2,1)S(1)}, bf16[2,528,128]{2,1,0:T(8,128)(2,1)S(1)}, u32[]{:S(2)}, u32[]{:S(2)}) %collective-permute-start.5) | collective-permute-done | bytes 270368 | tf_op jit(solution)/shard_map/ppermute | solution.py:232
  41.6 2.0 %shard_map.99 = (f32[2,256,128]{2,1,0:T(8,128)S(1)}, bf16[2,256,128]{2,1,0:T(8,128)(2,1)S(1)}, f32[2,128,512]{2,1,0:T(8,128)S(1)}, bf16[2,512,128]{2,1,0:T(8,128)(2,1)S(1)}) custom-call(bf16[2,528,128]{2,1,0:T(8,128)(2,1)S(1)} %bitcast_dynamic-update-slice_fusion.refs_0_.rows_ref, bf16[2,528,128]{2,1,0:T(8,128)(2,1)S(1)} %collective-permute-done.1.refs_1_, ...), custom_call_target="tpu_custom_call" | custom-call | flops 1006632960 | bytes 1048576 | tf_op jit(solution)/shard_map/pallas_call | solution.py:204
  43.7 2.0 %collective-permute-start.13 = (bf16[2,512,128]{2,1,0:T(8,128)(2,1)S(1)}, bf16[2,512,128]{2,1,0:T(8,128)(2,1)S(1)}, u32[]{:S(2)}, u32[]{:S(2)}) collective-permute-start(bf16[2,512,128]{2,1,0:T(8,128)(2,1)S(1)} %get-tuple-element.51), channel_id=1, source_target_pairs={{0,192},{64,0},{128,64},{192,128},{1,193},{65,1},{129,65},{193,129... | collective-permute-start | bytes 786440 | tf_op jit(solution)/shard_map/ppermute | solution.py:255
  46.7 2.0 %collective-permute-start.9 = (bf16[2,256,128]{2,1,0:T(8,128)(2,1)S(1)}, bf16[2,256,128]{2,1,0:T(8,128)(2,1)S(1)}, u32[]{:S(2)}, u32[]{:S(2)}) collective-permute-start(bf16[2,256,128]{2,1,0:T(8,128)(2,1)S(1)} %get-tuple-element.42), channel_id=1, source_target_pairs={{0,56},{8,0},{16,8},{24,16},{32,24},{40,32},{48,40},{56,48},{1,57}... | collective-permute-start | bytes 393224 | tf_op jit(solution)/shard_map/ppermute | solution.py:267
  48.7 1.4 %collective-permute-done.14.refs_5_ = bf16[2,512,128]{2,1,0:T(8,128)(2,1)S(1)} collective-permute-done((bf16[2,512,128]{2,1,0:T(8,128)(2,1)S(1)}, bf16[2,512,128]{2,1,0:T(8,128)(2,1)S(1)}, u32[]{:S(2)}, u32[]{:S(2)}) %collective-permute-start.14) | collective-permute-done | bytes 262176 | tf_op jit(solution)/shard_map/ppermute | solution.py:255
  50.1 1.3 %collective-permute-done.13.refs_4_ = bf16[2,512,128]{2,1,0:T(8,128)(2,1)S(1)} collective-permute-done((bf16[2,512,128]{2,1,0:T(8,128)(2,1)S(1)}, bf16[2,512,128]{2,1,0:T(8,128)(2,1)S(1)}, u32[]{:S(2)}, u32[]{:S(2)}) %collective-permute-start.13) | collective-permute-done | bytes 262176 | tf_op jit(solution)/shard_map/ppermute | solution.py:255
  51.6 2.1 %collective-permute-start.15 = (bf16[512,128]{1,0:T(8,128)(2,1)S(1)}, bf16[512,128]{1,0:T(8,128)(2,1)S(1)}, u32[]{:S(2)}, u32[]{:S(2)}) collective-permute-start(bf16[512,128]{1,0:T(8,128)(2,1)S(1)} %get-tuple-element.54), channel_id=1, source_target_pairs={{0,32},{8,40},{16,48},{24,56},{32,0},{40,8},{48,16},{56,24},{1,33}... | collective-permute-start | bytes 393224 | tf_op jit(solution)/shard_map/ppermute | solution.py:274
  53.7 1.7 %collective-permute-done.9.refs_1_ = bf16[2,256,128]{2,1,0:T(8,128)(2,1)S(1)} collective-permute-done((bf16[2,256,128]{2,1,0:T(8,128)(2,1)S(1)}, bf16[2,256,128]{2,1,0:T(8,128)(2,1)S(1)}, u32[]{:S(2)}, u32[]{:S(2)}) %collective-permute-start.9) | collective-permute-done | bytes 131104 | tf_op jit(solution)/shard_map/ppermute | solution.py:267
  56.0 5.9 %collective-permute-done.15.dkvz_ref = bf16[512,128]{1,0:T(8,128)(2,1)S(1)} collective-permute-done((bf16[512,128]{1,0:T(8,128)(2,1)S(1)}, bf16[512,128]{1,0:T(8,128)(2,1)S(1)}, u32[]{:S(2)}, u32[]{:S(2)}) %collective-permute-start.15) | collective-permute-done | bytes 131104 | tf_op jit(solution)/shard_map/ppermute | solution.py:274
  (23 shorter events, 4.0 us)
Async XLA Ops:
  2.5 8.8 %collective-permute-start = (bf16[528,128]{1,0:T(8,128)(2,1)}, bf16[528,128]{1,0:T(8,128)(2,1)S(1)}, u32[]{:S(2)}, u32[]{:S(2)}) collective-permute-start(bf16[528,128]{1,0:T(8,128)(2,1)} %get-tuple-element.29), channel_id=1, source_target_pairs={{0,4},{4,0},{1,5},{5,1},{2,6},{6,2},{3,7},{7,3},{8,12},{12,8},{9,1... | collective-permute-start | bytes 405512 | tf_op jit(solution)/shard_map/ppermute | solution.py:228
  4.0 13.4 %collective-permute-start.4 = (bf16[528,128]{1,0:T(8,128)(2,1)}, bf16[528,128]{1,0:T(8,128)(2,1)S(1)}, u32[]{:S(2)}, u32[]{:S(2)}) collective-permute-start(bf16[528,128]{1,0:T(8,128)(2,1)} %get-tuple-element.30), channel_id=1, source_target_pairs={{0,32},{8,40},{16,48},{24,56},{32,0},{40,8},{48,16},{56,24},{1,33}... | collective-permute-start | bytes 405512 | tf_op jit(solution)/shard_map/ppermute | solution.py:227
  11.3 6.1 %copy-start = (bf16[528,128]{1,0:T(8,128)(2,1)S(1)}, bf16[528,128]{1,0:T(8,128)(2,1)}, u32[]{:S(2)}) copy-start(bf16[528,128]{1,0:T(8,128)(2,1)} %get-tuple-element.30) | copy-start | bytes 405508
  11.3 17.0 %collective-permute-start.2 = (bf16[2,528,128]{2,1,0:T(8,128)(2,1)S(1)}, bf16[2,528,128]{2,1,0:T(8,128)(2,1)S(1)}, u32[]{:S(2)}, u32[]{:S(2)}) collective-permute-start(bf16[2,528,128]{2,1,0:T(8,128)(2,1)S(1)} %bitcast_dynamic-update-slice_fusion.refs_0_.rows_ref), channel_id=1, source_target_pairs={{0,8},{8,16},{16,24},{24,32},{32,40},{40,48},{48,56},{56,0},{1,9},... | collective-permute-start | bytes 811016 | tf_op jit(solution)/shard_map/ppermute | solution.py:231
  12.4 16.7 %collective-permute-start.3 = (bf16[2,528,128]{2,1,0:T(8,128)(2,1)S(1)}, bf16[2,528,128]{2,1,0:T(8,128)(2,1)S(1)}, u32[]{:S(2)}, u32[]{:S(2)}) collective-permute-start(bf16[2,528,128]{2,1,0:T(8,128)(2,1)S(1)} %bitcast_dynamic-update-slice_fusion.refs_0_.rows_ref), channel_id=1, source_target_pairs={{0,56},{8,0},{16,8},{24,16},{32,24},{40,32},{48,40},{56,48},{1,57}... | collective-permute-start | bytes 811016 | tf_op jit(solution)/shard_map/ppermute | solution.py:231
  13.4 16.4 %collective-permute-start.1 = (bf16[2,528,128]{2,1,0:T(8,128)(2,1)S(1)}, bf16[2,528,128]{2,1,0:T(8,128)(2,1)S(1)}, u32[]{:S(2)}, u32[]{:S(2)}) collective-permute-start(bf16[2,528,128]{2,1,0:T(8,128)(2,1)S(1)} %bitcast_dynamic-update-slice_fusion.refs_0_.rows_ref), channel_id=1, source_target_pairs={{0,48},{8,24},{16,0},{24,40},{32,16},{40,56},{48,32},{56,8},{1,49}... | collective-permute-start | bytes 811016 | tf_op jit(solution)/shard_map/ppermute | solution.py:231
  17.4 13.5 %collective-permute-start.7 = (bf16[2,528,128]{2,1,0:T(8,128)(2,1)S(1)}, bf16[2,528,128]{2,1,0:T(8,128)(2,1)S(1)}, u32[]{:S(2)}, u32[]{:S(2)}) collective-permute-start(bf16[2,528,128]{2,1,0:T(8,128)(2,1)S(1)} %pad_maximum_fusion.refs_2_), channel_id=1, source_target_pairs={{0,128},{64,192},{128,0},{192,64},{1,129},{65,193},{129,1},{193,65... | collective-permute-start | bytes 811016 | tf_op jit(solution)/shard_map/ppermute | solution.py:232
  18.8 15.4 %collective-permute-start.6 = (bf16[2,528,128]{2,1,0:T(8,128)(2,1)S(1)}, bf16[2,528,128]{2,1,0:T(8,128)(2,1)S(1)}, u32[]{:S(2)}, u32[]{:S(2)}) collective-permute-start(bf16[2,528,128]{2,1,0:T(8,128)(2,1)S(1)} %pad_maximum_fusion.refs_2_), channel_id=1, source_target_pairs={{0,64},{64,128},{128,192},{192,0},{1,65},{65,129},{129,193},{193,1... | collective-permute-start | bytes 811016 | tf_op jit(solution)/shard_map/ppermute | solution.py:232
  28.3 13.3 %collective-permute-start.5 = (bf16[2,528,128]{2,1,0:T(8,128)(2,1)S(1)}, bf16[2,528,128]{2,1,0:T(8,128)(2,1)S(1)}, u32[]{:S(2)}, u32[]{:S(2)}) collective-permute-start(bf16[2,528,128]{2,1,0:T(8,128)(2,1)S(1)} %pad_maximum_fusion.refs_2_), channel_id=1, source_target_pairs={{0,192},{64,0},{128,64},{192,128},{1,193},{65,1},{129,65},{193,129... | collective-permute-start | bytes 811016 | tf_op jit(solution)/shard_map/ppermute | solution.py:232
  32.9 12.8 %collective-permute-start.8 = (bf16[2,512,128]{2,1,0:T(8,128)(2,1)S(1)}, bf16[2,512,128]{2,1,0:T(8,128)(2,1)S(1)}, u32[]{:S(2)}, u32[]{:S(2)}) collective-permute-start(bf16[2,512,128]{2,1,0:T(8,128)(2,1)S(1)} %get-tuple-element.40), channel_id=1, source_target_pairs={{0,128},{64,192},{128,0},{192,64},{1,129},{65,193},{129,1},{193,65... | collective-permute-start | bytes 786440 | tf_op jit(solution)/shard_map/ppermute | solution.py:255
  43.6 6.4 %collective-permute-start.14 = (bf16[2,512,128]{2,1,0:T(8,128)(2,1)S(1)}, bf16[2,512,128]{2,1,0:T(8,128)(2,1)S(1)}, u32[]{:S(2)}, u32[]{:S(2)}) collective-permute-start(bf16[2,512,128]{2,1,0:T(8,128)(2,1)S(1)} %get-tuple-element.52), channel_id=1, source_target_pairs={{0,64},{64,128},{128,192},{192,0},{1,65},{65,129},{129,193},{193,1... | collective-permute-start | bytes 786440 | tf_op jit(solution)/shard_map/ppermute | solution.py:255
  43.7 7.7 %collective-permute-start.13 = (bf16[2,512,128]{2,1,0:T(8,128)(2,1)S(1)}, bf16[2,512,128]{2,1,0:T(8,128)(2,1)S(1)}, u32[]{:S(2)}, u32[]{:S(2)}) collective-permute-start(bf16[2,512,128]{2,1,0:T(8,128)(2,1)S(1)} %get-tuple-element.51), channel_id=1, source_target_pairs={{0,192},{64,0},{128,64},{192,128},{1,193},{65,1},{129,65},{193,129... | collective-permute-start | bytes 786440 | tf_op jit(solution)/shard_map/ppermute | solution.py:255
  45.8 7.9 %collective-permute-start.11 = (bf16[2,256,128]{2,1,0:T(8,128)(2,1)S(1)}, bf16[2,256,128]{2,1,0:T(8,128)(2,1)S(1)}, u32[]{:S(2)}, u32[]{:S(2)}) collective-permute-start(bf16[2,256,128]{2,1,0:T(8,128)(2,1)S(1)} %get-tuple-element.44), channel_id=1, source_target_pairs={{48,0},{24,8},{0,16},{40,24},{16,32},{56,40},{32,48},{8,56},{49,1}... | collective-permute-start | bytes 393224 | tf_op jit(solution)/shard_map/ppermute | solution.py:267
  46.6 7.1 %collective-permute-start.10 = (bf16[2,256,128]{2,1,0:T(8,128)(2,1)S(1)}, bf16[2,256,128]{2,1,0:T(8,128)(2,1)S(1)}, u32[]{:S(2)}, u32[]{:S(2)}) collective-permute-start(bf16[2,256,128]{2,1,0:T(8,128)(2,1)S(1)} %get-tuple-element.43), channel_id=1, source_target_pairs={{0,8},{8,16},{16,24},{24,32},{32,40},{40,48},{48,56},{56,0},{1,9},... | collective-permute-start | bytes 393224 | tf_op jit(solution)/shard_map/ppermute | solution.py:267
  46.7 8.7 %collective-permute-start.9 = (bf16[2,256,128]{2,1,0:T(8,128)(2,1)S(1)}, bf16[2,256,128]{2,1,0:T(8,128)(2,1)S(1)}, u32[]{:S(2)}, u32[]{:S(2)}) collective-permute-start(bf16[2,256,128]{2,1,0:T(8,128)(2,1)S(1)} %get-tuple-element.42), channel_id=1, source_target_pairs={{0,56},{8,0},{16,8},{24,16},{32,24},{40,32},{48,40},{56,48},{1,57}... | collective-permute-start | bytes 393224 | tf_op jit(solution)/shard_map/ppermute | solution.py:267
  51.6 10.3 %collective-permute-start.15 = (bf16[512,128]{1,0:T(8,128)(2,1)S(1)}, bf16[512,128]{1,0:T(8,128)(2,1)S(1)}, u32[]{:S(2)}, u32[]{:S(2)}) collective-permute-start(bf16[512,128]{1,0:T(8,128)(2,1)S(1)} %get-tuple-element.54), channel_id=1, source_target_pairs={{0,32},{8,40},{16,48},{24,56},{32,0},{40,8},{48,16},{56,24},{1,33}... | collective-permute-start | bytes 393224 | tf_op jit(solution)/shard_map/ppermute | solution.py:274
  55.4 6.5 %collective-permute-start.12 = (bf16[256,128]{1,0:T(8,128)(2,1)S(1)}, bf16[256,128]{1,0:T(8,128)(2,1)S(1)}, u32[]{:S(2)}, u32[]{:S(2)}) collective-permute-start(bf16[256,128]{1,0:T(8,128)(2,1)S(1)} %get-tuple-element.46), channel_id=1, source_target_pairs={{0,4},{4,0},{1,5},{5,1},{2,6},{6,2},{3,7},{7,3},{8,12},{12,8},{9,1... | collective-permute-start | bytes 196616 | tf_op jit(solution)/shard_map/ppermute | solution.py:276

commit v8 on v7

--- a/solution.py
+++ b/solution.py
@@ -16,7 +16,7 @@
 FACTOR = 1.0 / math.sqrt(DIM)
 VMEM_LIMIT = 48 * 1024 * 1024
 PREP_VMEM = 62 * 1024 * 1024
-FLOPS = 10 * 2 * 3 * (2 * BLK) * (4 * BLK) * DIM
+COST = pl.CostEstimate(flops=500000000, bytes_accessed=1000000, transcendentals=0)
 HIDE = 1e30
 Y_FROM = (0, 2, 3, 1)
 NT = (((1,), (1,)), ((), ()))
@@ -93,7 +93,7 @@
     return dot(p.astype(BF16), g), dot(ds, q), dot(kt, ds)
 
 
-def grad_kernel(js, plan, own, *refs):
+def grad_kernel(js, plan, own, add, split, *refs):
     refs = list(refs)
 
     def take(count):
@@ -103,8 +103,10 @@
 
     q_refs, (y_ref,) = take(2 * len(plan)), take(1)
     dqin_refs = [None if first else take(1)[0] for first, _ in plan]
+    addin_ref = refs.pop(0) if add else None
     dq_refs = [take(2 if last else 1) for _, last in plan]
-    dkv_ref, dv_acc, dk_acc = refs
+    dkv_refs = take(len(js)) if split else [refs.pop(0)]
+    dv_acc, dk_acc = refs
     count = len(js)
     half = count * BLK
 
@@ -157,8 +159,14 @@
         for b in range(2):
             source = slice(b * half + m * BLK, b * half + (m + 1) * BLK)
             for array, acc in ((0, dk_acc), (1, dv_acc)):
-                at = (2 * array + b) * BLK
-                dkv_ref[m, at : at + BLK, :] = acc[source].astype(dkv_ref.dtype)
+                rows = slice((2 * array + b) * BLK, (2 * array + b + 1) * BLK)
+                part = acc[source]
+                if add:
+                    part = addin_ref[m, rows, :] + part
+                if split:
+                    dkv_refs[m][rows, :] = part.astype(BF16)
+                else:
+                    dkv_refs[0][m, rows, :] = part.astype(dkv_refs[0].dtype)
 
 
 def meet_kernel(parts, *refs):
@@ -172,7 +180,7 @@
         out_ref[...] = total.astype(out_ref.dtype)
 
 
-def last_kernel(rows_ref, dq_ref, dqx_ref, dkv_ref, dkvz_ref, q_ref, k_ref, v_ref):
+def last_kernel(rows_ref, dq_ref, dqx_ref, dkv_ref, dkvz_ref, dkvy_ref, dkvyz_ref, q_ref, k_ref, v_ref):
     swapped = rows_ref[0, 4 * BLK :, :].astype(F32)[5:6, :] > 0.5
 
     def restore(out_ref, total):
@@ -181,7 +189,9 @@
         out_ref[BLK:, :] = jnp.where(swapped, low, high).astype(BF16)
 
     restore(q_ref, (dq_ref[...] + dqx_ref[...].astype(F32)) * FACTOR)
-    dkv = dkv_ref[...] + dkvz_ref[...].astype(F32)
+    dkv = dkv_ref[...]
+    for ref in (dkvz_ref, dkvy_ref, dkvyz_ref):
+        dkv += ref[...].astype(F32)
     restore(k_ref, dkv[: 2 * BLK] * FACTOR)
     restore(v_ref, dkv[2 * BLK :])
 
@@ -232,7 +242,7 @@
     k_sets = [k0] + [lax.ppermute(k0, "pb", y_step(-s)) for s in Y_FROM[1:]]
     q_pairs = ([q_sets[0], q_sets[3]], [q_sets[1], q_sets[2]])
 
-    def grad(turn, js, pairs, dq_in, last, dkv_type):
+    def grad(turn, js, pairs, dq_in, last, dkv_type, add=None, split=False):
         plan = tuple((d is None, e) for d, e in zip(dq_in, last))
         outs = []
         for pair, end in zip(pairs, last):
@@ -240,41 +250,46 @@
                 outs += [((2, 2 * BLK, DIM), F32 if (pair, s) == (0, 0) else BF16) for s in range(2)]
             else:
                 outs.append(((2, DIM, 4 * BLK), F32))
+        dkv_out = [((4 * BLK, DIM), BF16)] * len(js) if split else [((len(js), 4 * BLK, DIM), dkv_type)]
         acc = pltpu.VMEM((2 * len(js) * BLK, DIM), F32)
-        units = len(js) * len(pairs)
-        *dq, part = call(
-            functools.partial(grad_kernel, js, plan, turn == 0 and js[0] == 0 and pairs[0] == 0),
-            outs + [((len(js), 4 * BLK, DIM), dkv_type)],
-            [q for p in pairs for q in q_pairs[p]] + [k_sets[turn]] + [d for d in dq_in if d is not None],
+        results = call(
+            functools.partial(grad_kernel, js, plan, turn == 0 and pairs[0] == 0, add is not None, split),
+            outs + dkv_out,
+            [q for p in pairs for q in q_pairs[p]] + [k_sets[turn]] + [d for d in (*dq_in, add) if d is not None],
             [acc, acc],
-            cost_estimate=pl.CostEstimate(flops=FLOPS * units // 4, bytes_accessed=1 << 20, transcendentals=0),
+            cost_estimate=COST,
         )
-        return dq, part
+        return results[: len(outs)], results[len(outs) :]
 
     def send_back(turn, part):
         return lax.ppermute(part, "pb", y_step(Y_FROM[turn]))
 
-    (dq0,), own = grad(0, (0, 1), (0,), (None,), (False,), F32)
-    (dq1,), own_a = grad(0, (0,), (1,), (None,), (False,), F32)
-    (dq0, dq1), part = grad(1, (0, 1), (0, 1), (dq0, dq1), (False, False), BF16)
-    back = [send_back(1, part)]
-    (dq0, dq1), part = grad(2, (0, 1), (0, 1), (dq0, dq1), (False, False), BF16)
-    back.append(send_back(2, part))
-    (dq_keep, dq_z2, dq1), part = grad(3, (0, 1), (0, 1), (dq0, dq1), (True, False), BF16)
-    back.append(send_back(3, part))
-    dq1, back[0] = lax.optimization_barrier((dq1, back[0]))
-    (dq_left, dq_right), own_b = grad(0, (1,), (1,), (dq1,), (True,), F32)
-    dq_back = [lax.ppermute(d, "kz", p) for d, p in ((dq_left, z_step(-1)), (dq_right, z_step(1)), (dq_z2, Z_BACK))]
+    both = (0, 1)
+    (dq1,), (own1,) = grad(0, both, (1,), (None,), (False,), F32)
+    k_sets[0], own1 = lax.optimization_barrier((k_sets[0], own1))
+    (dq0,), (own0,) = grad(0, both, (0,), (None,), (False,), F32)
+    (dq0, dq1), (part,) = grad(1, both, both, (dq0, dq1), (False, False), BF16)
+    back1 = send_back(1, part)
+    (dq0, dq1), (part,) = grad(2, both, both, (dq0, dq1), (False, False), BF16)
+    back2 = send_back(2, part)
+    (dq_keep, *dqs), (part, part_far) = grad(3, both, both, (dq0, dq1), (True, True), BF16, split=True)
+    back3 = send_back(3, part)
+    far = [(y * 8 + z, (y + Y_FROM[3]) % 4 * 8 + (z + 4) % 8) for y in range(4) for z in range(8)]
+    back_far = lax.ppermute(part_far, ("pb", "kz"), far)
+    dqs[0], back1 = lax.optimization_barrier((dqs[0], back1))
+    dq_back = [lax.ppermute(d, "kz", p) for d, p in zip(dqs, (Z_BACK, z_step(-1), z_step(1)))]
 
     def meet(operands, parts, shape):
         return call(functools.partial(meet_kernel, parts), [(shape, F32), (shape, BF16)], operands)
 
-    both = (0, 1)
-    dkv_keep, dkv_send = meet([own, own_a, own_b] + back, [both, (0, None), (None, 0)] + [both] * 3, (4 * BLK, DIM))
+    dkv_keep, dkv_send = meet(
+        [own0, own1, back1, back2], [both] * 4, (4 * BLK, DIM)
+    )
     dkv_last = lax.ppermute(dkv_send, "kz", z_step(4))
     dq_keep, dq_send = meet([dq_keep] + dq_back, [both] * 4, (2 * BLK, DIM))
     dq_last = lax.ppermute(dq_send, "kx", X_SWAP)
-    return tuple(call(last_kernel, [((2 * BLK, DIM), BF16)] * 3, (q0, dq_keep, dq_last, dkv_keep, dkv_last)))
+    operands = (q0, dq_keep, dq_last, dkv_keep, dkv_last, back3, back_far)
+    return tuple(call(last_kernel, [((2 * BLK, DIM), BF16)] * 3, operands))
 
 
 def solution(mesh):

time: 62.8 us -> 66.2 us (1.054)
  the two profiles are of different devices: /device:TPU:56 before, /device:TPU:32 now
where the time goes in v8:
time: 66.2 us; the launch traced here: 66.1 us
  starting transfers between devices  32.9 us (50%)
  waiting for transfers between devices  20.3 us (31%)
  Pallas kernels  11.1 us (17%)
  local copies, waits for them, and re-layouts  0.96 us (1%)
  between operations  0.75 us (1%)
    pallas_call x9, Pallas kernels, call(): pl.pallas_call(kernel, out_shape=[jax.ShapeDtypeStruct(s, t) for s, t in...  11.1 us
    ppermute x1, waiting for transfers between devices, body(): back_far = lax.ppermute(part_far, ('pb', 'kz'), far)  9.87 us
    ppermute x3, starting transfers between devices, body(): k_sets = [k0] + [lax.ppermute(k0, 'pb', y_step(-s)) for s in Y_FROM[1:]]  6.97 us
    ppermute x3, waiting for transfers between devices, body(): lax.ppermute(q0, 'kz', p)  6.93 us
    ppermute x1, starting transfers between devices, body(): other_k = lax.ppermute(mine_k, 'kz', z_step(4))  6.29 us
    ppermute x1, starting transfers between devices, body(): back_far = lax.ppermute(part_far, ('pb', 'kz'), far)  6.02 us
    ppermute x3, starting transfers between devices, body(): lax.ppermute(d, 'kz', p)  4.13 us
    ppermute x3, starting transfers between devices, body(): lax.ppermute(q0, 'kz', p)  3.58 us
  transfers between devices with their start and end apart: 17, of which 5 were waited for; matrix products, arithmetic and copies ran while one was open for 1% of the time, Pallas kernels for 13%

profile of v8, /device:TPU:32, one launch (start us, length us, event | category | flops | bytes accessed | tf_op | source)
XLA Modules:
  0.0 66.1 jit_solution(11437391089773267601)
XLA Ops:
  0.6 1.8 %shard_map.94 = (bf16[528,128]{1,0:T(8,128)(2,1)}, bf16[528,128]{1,0:T(8,128)(2,1)}) custom-call(s32[128]{0:T(128)} %refs_0_.1, bf16[256,128]{1,0:T(8,128)(2,1)} %refs_1_.1, bf16[256,128]{1,0:T(8,128)(2,1)} %refs_2_.1, bf16[1,256]{1,0:T(2,128)(2,1)} %bitcast.9, bf16[256,128]{1,0:T(8,128)(2,1)} %refs_4_.1, bf16[256,128]{1,0:T(8,128)(2,1)} %refs_5_.1, ...), custom_call_target="tpu_custom_call" | custom-call | tf_op jit(solution)/shard_map/pallas_call | solution.py:214
  2.5 1.6 %collective-permute-start = (bf16[528,128]{1,0:T(8,128)(2,1)}, bf16[528,128]{1,0:T(8,128)(2,1)S(1)}, u32[]{:S(2)}, u32[]{:S(2)}) collective-permute-start(bf16[528,128]{1,0:T(8,128)(2,1)} %get-tuple-element.30), channel_id=1, source_target_pairs={{0,4},{4,0},{1,5},{5,1},{2,6},{6,2},{3,7},{7,3},{8,12},{12,8},{9,1... | collective-permute-start | bytes 405512 | tf_op jit(solution)/shard_map/ppermute | solution.py:238
  4.0 6.3 %collective-permute-start.4 = (bf16[528,128]{1,0:T(8,128)(2,1)}, bf16[528,128]{1,0:T(8,128)(2,1)S(1)}, u32[]{:S(2)}, u32[]{:S(2)}) collective-permute-start(bf16[528,128]{1,0:T(8,128)(2,1)} %get-tuple-element.31), channel_id=1, source_target_pairs={{0,32},{8,40},{16,48},{24,56},{32,0},{40,8},{48,16},{56,24},{1,33}... | collective-permute-start | bytes 405512 | tf_op jit(solution)/shard_map/ppermute | solution.py:237
  10.3 0.9 %pad.4 = bf16[2,528,128]{2,1,0:T(8,128)(2,1)S(1)} pad(bf16[1,528,128]{2,1,0:T(8,128)(2,1)} %bitcast.6, bf16[]{:T(256)} %constant.1.clone.1), padding=0_1x0_0x0_0 | pad | bytes 405506 | tf_op jit(solution)/shard_map/jit(_pad)/pad | solution.py:234
  11.3 1.1 %collective-permute-start.2 = (bf16[2,528,128]{2,1,0:T(8,128)(2,1)S(1)}, bf16[2,528,128]{2,1,0:T(8,128)(2,1)S(1)}, u32[]{:S(2)}, u32[]{:S(2)}) collective-permute-start(bf16[2,528,128]{2,1,0:T(8,128)(2,1)S(1)} %bitcast_dynamic-update-slice_fusion.refs_0_.rows_ref), channel_id=1, source_target_pairs={{0,8},{8,16},{16,24},{24,32},{32,40},{40,48},{48,56},{56,0},{1,9},... | collective-permute-start | bytes 811016 | tf_op jit(solution)/shard_map/ppermute | solution.py:241
  12.4 1.0 %collective-permute-start.3 = (bf16[2,528,128]{2,1,0:T(8,128)(2,1)S(1)}, bf16[2,528,128]{2,1,0:T(8,128)(2,1)S(1)}, u32[]{:S(2)}, u32[]{:S(2)}) collective-permute-start(bf16[2,528,128]{2,1,0:T(8,128)(2,1)S(1)} %bitcast_dynamic-update-slice_fusion.refs_0_.rows_ref), channel_id=1, source_target_pairs={{0,56},{8,0},{16,8},{24,16},{32,24},{40,32},{48,40},{56,48},{1,57}... | collective-permute-start | bytes 811016 | tf_op jit(solution)/shard_map/ppermute | solution.py:241
  13.4 1.5 %collective-permute-start.1 = (bf16[2,528,128]{2,1,0:T(8,128)(2,1)S(1)}, bf16[2,528,128]{2,1,0:T(8,128)(2,1)S(1)}, u32[]{:S(2)}, u32[]{:S(2)}) collective-permute-start(bf16[2,528,128]{2,1,0:T(8,128)(2,1)S(1)} %bitcast_dynamic-update-slice_fusion.refs_0_.rows_ref), channel_id=1, source_target_pairs={{0,48},{8,24},{16,0},{24,40},{32,16},{40,56},{48,32},{56,8},{1,49}... | collective-permute-start | bytes 811016 | tf_op jit(solution)/shard_map/ppermute | solution.py:241
  14.9 2.5 %collective-permute-done.4 = bf16[528,128]{1,0:T(8,128)(2,1)S(1)} collective-permute-done((bf16[528,128]{1,0:T(8,128)(2,1)}, bf16[528,128]{1,0:T(8,128)(2,1)S(1)}, u32[]{:S(2)}, u32[]{:S(2)}) %collective-permute-start.4) | collective-permute-done | bytes 135200 | tf_op jit(solution)/shard_map/ppermute | solution.py:237
  17.4 3.3 %collective-permute-start.7 = (bf16[2,528,128]{2,1,0:T(8,128)(2,1)S(1)}, bf16[2,528,128]{2,1,0:T(8,128)(2,1)S(1)}, u32[]{:S(2)}, u32[]{:S(2)}) collective-permute-start(bf16[2,528,128]{2,1,0:T(8,128)(2,1)S(1)} %pad_maximum_fusion.refs_2_), channel_id=1, source_target_pairs={{0,128},{64,192},{128,0},{192,64},{1,129},{65,193},{129,1},{193,65... | collective-permute-start | bytes 811016 | tf_op jit(solution)/shard_map/ppermute | solution.py:242
  21.4 6.9 %collective-permute-done.2.refs_0_.refs_2_ = bf16[2,528,128]{2,1,0:T(8,128)(2,1)S(1)} collective-permute-done((bf16[2,528,128]{2,1,0:T(8,128)(2,1)S(1)}, bf16[2,528,128]{2,1,0:T(8,128)(2,1)S(1)}, u32[]{:S(2)}, u32[]{:S(2)}) %collective-permute-start.2) | collective-permute-done | bytes 270368 | tf_op jit(solution)/shard_map/ppermute | solution.py:241
  28.3 3.0 %collective-permute-start.5 = (bf16[2,528,128]{2,1,0:T(8,128)(2,1)S(1)}, bf16[2,528,128]{2,1,0:T(8,128)(2,1)S(1)}, u32[]{:S(2)}, u32[]{:S(2)}) collective-permute-start(bf16[2,528,128]{2,1,0:T(8,128)(2,1)S(1)} %pad_maximum_fusion.refs_2_), channel_id=1, source_target_pairs={{0,192},{64,0},{128,64},{192,128},{1,193},{65,1},{129,65},{193,129... | collective-permute-start | bytes 811016 | tf_op jit(solution)/shard_map/ppermute | solution.py:242
  31.3 1.1 %shard_map.95 = (f32[2,128,512]{2,1,0:T(8,128)S(1)}, f32[2,512,128]{2,1,0:T(8,128)S(1)}) custom-call(bf16[2,528,128]{2,1,0:T(8,128)(2,1)S(1)} %collective-permute-done.2.refs_0_.refs_2_, bf16[2,528,128]{2,1,0:T(8,128)(2,1)S(1)} %collective-permute-done.3.refs_1_.refs_3_, bf16[2,528,128]{2,1,0:T(8,128)(2,1)S(1)} %pad_maximum_fusion.refs_2_), custom_call_target="tpu_custom_call" | custom-call | flops 500000000 | bytes 1000000 | tf_op jit(solution)/shard_map/pallas_call | solution.py:214
  32.4 1.1 %shard_map.96 = (f32[2,128,512]{2,1,0:T(8,128)S(1)}, f32[2,512,128]{2,1,0:T(8,128)S(1)}) custom-call(bf16[2,528,128]{2,1,0:T(8,128)(2,1)S(1)} %bitcast_dynamic-update-slice_fusion.refs_0_.rows_ref, bf16[2,528,128]{2,1,0:T(8,128)(2,1)S(1)} %collective-permute-done.1.refs_1_, bf16[2,528,128]{2,1,0:T(8,128)(2,1)S(1)} %pad_maximum_fusion.refs_2_), custom_call_target="tpu_custom_call" | custom-call | flops 500000000 | bytes 1000000 | tf_op jit(solution)/shard_map/pallas_call | solution.py:214
  33.5 2.0 %shard_map.97 = (f32[2,128,512]{2,1,0:T(8,128)S(1)}, f32[2,128,512]{2,1,0:T(8,128)S(1)}, bf16[2,512,128]{2,1,0:T(8,128)(2,1)S(1)}) custom-call(bf16[2,528,128]{2,1,0:T(8,128)(2,1)S(1)} %bitcast_dynamic-update-slice_fusion.refs_0_.rows_ref, bf16[2,528,128]{2,1,0:T(8,128)(2,1)S(1)} %collective-permute-done.1.refs_1_, ...), custom_call_target="tpu_custom_call" | custom-call | flops 500000000 | bytes 1000000 | tf_op jit(solution)/shard_map/pallas_call | solution.py:214
  35.6 0.9 %collective-permute-start.8 = (bf16[2,512,128]{2,1,0:T(8,128)(2,1)S(1)}, bf16[2,512,128]{2,1,0:T(8,128)(2,1)S(1)}, u32[]{:S(2)}, u32[]{:S(2)}) collective-permute-start(bf16[2,512,128]{2,1,0:T(8,128)(2,1)S(1)} %get-tuple-element.43), channel_id=1, source_target_pairs={{0,128},{64,192},{128,0},{192,64},{1,129},{65,193},{129,1},{193,65... | collective-permute-start | bytes 786440 | tf_op jit(solution)/shard_map/ppermute | solution.py:265
  36.5 2.0 %shard_map.98 = (f32[2,128,512]{2,1,0:T(8,128)S(1)}, f32[2,128,512]{2,1,0:T(8,128)S(1)}, bf16[2,512,128]{2,1,0:T(8,128)(2,1)S(1)}) custom-call(bf16[2,528,128]{2,1,0:T(8,128)(2,1)S(1)} %bitcast_dynamic-update-slice_fusion.refs_0_.rows_ref, bf16[2,528,128]{2,1,0:T(8,128)(2,1)S(1)} %collective-permute-done.1.refs_1_, ...), custom_call_target="tpu_custom_call" | custom-call | flops 500000000 | bytes 1000000 | tf_op jit(solution)/shard_map/pallas_call | solution.py:214
  38.5 1.1 %collective-permute-start.13 = (bf16[2,512,128]{2,1,0:T(8,128)(2,1)S(1)}, bf16[2,512,128]{2,1,0:T(8,128)(2,1)S(1)}, u32[]{:S(2)}, u32[]{:S(2)}) collective-permute-start(bf16[2,512,128]{2,1,0:T(8,128)(2,1)S(1)} %get-tuple-element.52), channel_id=1, source_target_pairs={{0,192},{64,0},{128,64},{192,128},{1,193},{65,1},{129,65},{193,129... | collective-permute-start | bytes 786440 | tf_op jit(solution)/shard_map/ppermute | solution.py:265
  39.7 2.1 %shard_map.99 = (f32[2,256,128]{2,1,0:T(8,128)S(1)}, bf16[2,256,128]{2,1,0:T(8,128)(2,1)S(1)}, bf16[2,256,128]{2,1,0:T(8,128)(2,1)S(1)}, bf16[2,256,128]{2,1,0:T...) custom-call(bf16[2,528,128]{2,1,0:T(8,128)(2,1)S(1)} %bitcast_dynamic-update-slice_fusion.refs_0_.rows_ref, ...), custom_call_target="tpu_custom_call" | custom-call | flops 500000000 | bytes 1000000 | tf_op jit(solution)/shard_map/pallas_call | solution.py:214
  41.8 1.4 %collective-permute-start.10 = (bf16[2,256,128]{2,1,0:T(8,128)(2,1)S(1)}, bf16[2,256,128]{2,1,0:T(8,128)(2,1)S(1)}, u32[]{:S(2)}, u32[]{:S(2)}) collective-permute-start(bf16[2,256,128]{2,1,0:T(8,128)(2,1)S(1)} %get-tuple-element.45), channel_id=1, source_target_pairs={{0,56},{8,0},{16,8},{24,16},{32,24},{40,32},{48,40},{56,48},{1,57}... | collective-permute-start | bytes 393224 | tf_op jit(solution)/shard_map/ppermute | solution.py:280
  43.9 2.0 %collective-permute-start.9 = (bf16[2,256,128]{2,1,0:T(8,128)(2,1)S(1)}, bf16[2,256,128]{2,1,0:T(8,128)(2,1)S(1)}, u32[]{:S(2)}, u32[]{:S(2)}) collective-permute-start(bf16[2,256,128]{2,1,0:T(8,128)(2,1)S(1)} %get-tuple-element.44), channel_id=1, source_target_pairs={{48,0},{24,8},{0,16},{40,24},{16,32},{56,40},{32,48},{8,56},{49,1}... | collective-permute-start | bytes 393224 | tf_op jit(solution)/shard_map/ppermute | solution.py:280
  46.0 1.0 %collective-permute-start.15 = (bf16[512,128]{1,0:T(8,128)(2,1)S(1)}, bf16[512,128]{1,0:T(8,128)(2,1)S(1)}, u32[]{:S(2)}, u32[]{:S(2)}) collective-permute-start(bf16[512,128]{1,0:T(8,128)(2,1)S(1)} %get-tuple-element.55), channel_id=1, source_target_pairs={{0,64},{64,128},{128,192},{192,0},{1,65},{65,129},{129,193},{193,1... | collective-permute-start | bytes 393224 | tf_op jit(solution)/shard_map/ppermute | solution.py:265
  47.3 6.0 %collective-permute-start.16 = (bf16[512,128]{1,0:T(8,128)(2,1)S(1)}, bf16[512,128]{1,0:T(8,128)(2,1)S(1)}, u32[]{:S(2)}, u32[]{:S(2)}) collective-permute-start(bf16[512,128]{1,0:T(8,128)(2,1)S(1)} %get-tuple-element.56), channel_id=1, source_target_pairs={{0,96},{8,104},{16,112},{24,120},{32,64},{40,72},{48,80},{56,88},{... | collective-permute-start | bytes 393224 | tf_op jit(solution)/shard_map/ppermute | solution.py:278
  53.4 0.7 %collective-permute-start.14 = (bf16[512,128]{1,0:T(8,128)(2,1)S(1)}, bf16[512,128]{1,0:T(8,128)(2,1)S(1)}, u32[]{:S(2)}, u32[]{:S(2)}) collective-permute-start(bf16[512,128]{1,0:T(8,128)(2,1)S(1)} %get-tuple-element.54), channel_id=1, source_target_pairs={{0,32},{8,40},{16,48},{24,56},{32,0},{40,8},{48,16},{56,24},{1,33}... | collective-permute-start | bytes 393224 | tf_op jit(solution)/shard_map/ppermute | solution.py:288
  54.9 9.9 %collective-permute-done.16.dkvyz_ref = bf16[512,128]{1,0:T(8,128)(2,1)S(1)} collective-permute-done((bf16[512,128]{1,0:T(8,128)(2,1)S(1)}, bf16[512,128]{1,0:T(8,128)(2,1)S(1)}, u32[]{:S(2)}, u32[]{:S(2)}) %collective-permute-start.16) | collective-permute-done | bytes 131104 | tf_op jit(solution)/shard_map/ppermute | solution.py:278
  (24 shorter events, 4.0 us)
Async XLA Ops:
  2.5 8.8 %collective-permute-start = (bf16[528,128]{1,0:T(8,128)(2,1)}, bf16[528,128]{1,0:T(8,128)(2,1)S(1)}, u32[]{:S(2)}, u32[]{:S(2)}) collective-permute-start(bf16[528,128]{1,0:T(8,128)(2,1)} %get-tuple-element.30), channel_id=1, source_target_pairs={{0,4},{4,0},{1,5},{5,1},{2,6},{6,2},{3,7},{7,3},{8,12},{12,8},{9,1... | collective-permute-start | bytes 405512 | tf_op jit(solution)/shard_map/ppermute | solution.py:238
  4.0 13.4 %collective-permute-start.4 = (bf16[528,128]{1,0:T(8,128)(2,1)}, bf16[528,128]{1,0:T(8,128)(2,1)S(1)}, u32[]{:S(2)}, u32[]{:S(2)}) collective-permute-start(bf16[528,128]{1,0:T(8,128)(2,1)} %get-tuple-element.31), channel_id=1, source_target_pairs={{0,32},{8,40},{16,48},{24,56},{32,0},{40,8},{48,16},{56,24},{1,33}... | collective-permute-start | bytes 405512 | tf_op jit(solution)/shard_map/ppermute | solution.py:237
  11.3 6.2 %copy-start = (bf16[528,128]{1,0:T(8,128)(2,1)S(1)}, bf16[528,128]{1,0:T(8,128)(2,1)}, u32[]{:S(2)}) copy-start(bf16[528,128]{1,0:T(8,128)(2,1)} %get-tuple-element.31) | copy-start | bytes 405508
  11.3 17.0 %collective-permute-start.2 = (bf16[2,528,128]{2,1,0:T(8,128)(2,1)S(1)}, bf16[2,528,128]{2,1,0:T(8,128)(2,1)S(1)}, u32[]{:S(2)}, u32[]{:S(2)}) collective-permute-start(bf16[2,528,128]{2,1,0:T(8,128)(2,1)S(1)} %bitcast_dynamic-update-slice_fusion.refs_0_.rows_ref), channel_id=1, source_target_pairs={{0,8},{8,16},{16,24},{24,32},{32,40},{40,48},{48,56},{56,0},{1,9},... | collective-permute-start | bytes 811016 | tf_op jit(solution)/shard_map/ppermute | solution.py:241
  12.4 18.9 %collective-permute-start.3 = (bf16[2,528,128]{2,1,0:T(8,128)(2,1)S(1)}, bf16[2,528,128]{2,1,0:T(8,128)(2,1)S(1)}, u32[]{:S(2)}, u32[]{:S(2)}) collective-permute-start(bf16[2,528,128]{2,1,0:T(8,128)(2,1)S(1)} %bitcast_dynamic-update-slice_fusion.refs_0_.rows_ref), channel_id=1, source_target_pairs={{0,56},{8,0},{16,8},{24,16},{32,24},{40,32},{48,40},{56,48},{1,57}... | collective-permute-start | bytes 811016 | tf_op jit(solution)/shard_map/ppermute | solution.py:241
  13.4 19.0 %collective-permute-start.1 = (bf16[2,528,128]{2,1,0:T(8,128)(2,1)S(1)}, bf16[2,528,128]{2,1,0:T(8,128)(2,1)S(1)}, u32[]{:S(2)}, u32[]{:S(2)}) collective-permute-start(bf16[2,528,128]{2,1,0:T(8,128)(2,1)S(1)} %bitcast_dynamic-update-slice_fusion.refs_0_.rows_ref), channel_id=1, source_target_pairs={{0,48},{8,24},{16,0},{24,40},{32,16},{40,56},{48,32},{56,8},{1,49}... | collective-permute-start | bytes 811016 | tf_op jit(solution)/shard_map/ppermute | solution.py:241
  17.4 16.1 %collective-permute-start.7 = (bf16[2,528,128]{2,1,0:T(8,128)(2,1)S(1)}, bf16[2,528,128]{2,1,0:T(8,128)(2,1)S(1)}, u32[]{:S(2)}, u32[]{:S(2)}) collective-permute-start(bf16[2,528,128]{2,1,0:T(8,128)(2,1)S(1)} %pad_maximum_fusion.refs_2_), channel_id=1, source_target_pairs={{0,128},{64,192},{128,0},{192,64},{1,129},{65,193},{129,1},{193,65... | collective-permute-start | bytes 811016 | tf_op jit(solution)/shard_map/ppermute | solution.py:242
  20.7 15.8 %collective-permute-start.6 = (bf16[2,528,128]{2,1,0:T(8,128)(2,1)S(1)}, bf16[2,528,128]{2,1,0:T(8,128)(2,1)S(1)}, u32[]{:S(2)}, u32[]{:S(2)}) collective-permute-start(bf16[2,528,128]{2,1,0:T(8,128)(2,1)S(1)} %pad_maximum_fusion.refs_2_), channel_id=1, source_target_pairs={{0,64},{64,128},{128,192},{192,0},{1,65},{65,129},{129,193},{193,1... | collective-permute-start | bytes 811016 | tf_op jit(solution)/shard_map/ppermute | solution.py:242
  28.3 11.4 %collective-permute-start.5 = (bf16[2,528,128]{2,1,0:T(8,128)(2,1)S(1)}, bf16[2,528,128]{2,1,0:T(8,128)(2,1)S(1)}, u32[]{:S(2)}, u32[]{:S(2)}) collective-permute-start(bf16[2,528,128]{2,1,0:T(8,128)(2,1)S(1)} %pad_maximum_fusion.refs_2_), channel_id=1, source_target_pairs={{0,192},{64,0},{128,64},{192,128},{1,193},{65,1},{129,65},{193,129... | collective-permute-start | bytes 811016 | tf_op jit(solution)/shard_map/ppermute | solution.py:242
  35.6 8.3 %collective-permute-start.8 = (bf16[2,512,128]{2,1,0:T(8,128)(2,1)S(1)}, bf16[2,512,128]{2,1,0:T(8,128)(2,1)S(1)}, u32[]{:S(2)}, u32[]{:S(2)}) collective-permute-start(bf16[2,512,128]{2,1,0:T(8,128)(2,1)S(1)} %get-tuple-element.43), channel_id=1, source_target_pairs={{0,128},{64,192},{128,0},{192,64},{1,129},{65,193},{129,1},{193,65... | collective-permute-start | bytes 786440 | tf_op jit(solution)/shard_map/ppermute | solution.py:265
  38.5 8.7 %collective-permute-start.13 = (bf16[2,512,128]{2,1,0:T(8,128)(2,1)S(1)}, bf16[2,512,128]{2,1,0:T(8,128)(2,1)S(1)}, u32[]{:S(2)}, u32[]{:S(2)}) collective-permute-start(bf16[2,512,128]{2,1,0:T(8,128)(2,1)S(1)} %get-tuple-element.52), channel_id=1, source_target_pairs={{0,192},{64,0},{128,64},{192,128},{1,193},{65,1},{129,65},{193,129... | collective-permute-start | bytes 786440 | tf_op jit(solution)/shard_map/ppermute | solution.py:265
  41.8 11.6 %collective-permute-start.10 = (bf16[2,256,128]{2,1,0:T(8,128)(2,1)S(1)}, bf16[2,256,128]{2,1,0:T(8,128)(2,1)S(1)}, u32[]{:S(2)}, u32[]{:S(2)}) collective-permute-start(bf16[2,256,128]{2,1,0:T(8,128)(2,1)S(1)} %get-tuple-element.45), channel_id=1, source_target_pairs={{0,56},{8,0},{16,8},{24,16},{32,24},{40,32},{48,40},{56,48},{1,57}... | collective-permute-start | bytes 393224 | tf_op jit(solution)/shard_map/ppermute | solution.py:280
  43.2 11.0 %collective-permute-start.11 = (bf16[2,256,128]{2,1,0:T(8,128)(2,1)S(1)}, bf16[2,256,128]{2,1,0:T(8,128)(2,1)S(1)}, u32[]{:S(2)}, u32[]{:S(2)}) collective-permute-start(bf16[2,256,128]{2,1,0:T(8,128)(2,1)S(1)} %get-tuple-element.46), channel_id=1, source_target_pairs={{0,8},{8,16},{16,24},{24,32},{32,40},{40,48},{48,56},{56,0},{1,9},... | collective-permute-start | bytes 393224 | tf_op jit(solution)/shard_map/ppermute | solution.py:280
  43.9 10.3 %collective-permute-start.9 = (bf16[2,256,128]{2,1,0:T(8,128)(2,1)S(1)}, bf16[2,256,128]{2,1,0:T(8,128)(2,1)S(1)}, u32[]{:S(2)}, u32[]{:S(2)}) collective-permute-start(bf16[2,256,128]{2,1,0:T(8,128)(2,1)S(1)} %get-tuple-element.44), channel_id=1, source_target_pairs={{48,0},{24,8},{0,16},{40,24},{16,32},{56,40},{32,48},{8,56},{49,1}... | collective-permute-start | bytes 393224 | tf_op jit(solution)/shard_map/ppermute | solution.py:280
  46.0 8.9 %collective-permute-start.15 = (bf16[512,128]{1,0:T(8,128)(2,1)S(1)}, bf16[512,128]{1,0:T(8,128)(2,1)S(1)}, u32[]{:S(2)}, u32[]{:S(2)}) collective-permute-start(bf16[512,128]{1,0:T(8,128)(2,1)S(1)} %get-tuple-element.55), channel_id=1, source_target_pairs={{0,64},{64,128},{128,192},{192,0},{1,65},{65,129},{129,193},{193,1... | collective-permute-start | bytes 393224 | tf_op jit(solution)/shard_map/ppermute | solution.py:265
  47.3 17.5 %collective-permute-start.16 = (bf16[512,128]{1,0:T(8,128)(2,1)S(1)}, bf16[512,128]{1,0:T(8,128)(2,1)S(1)}, u32[]{:S(2)}, u32[]{:S(2)}) collective-permute-start(bf16[512,128]{1,0:T(8,128)(2,1)S(1)} %get-tuple-element.56), channel_id=1, source_target_pairs={{0,96},{8,104},{16,112},{24,120},{32,64},{40,72},{48,80},{56,88},{... | collective-permute-start | bytes 393224 | tf_op jit(solution)/shard_map/ppermute | solution.py:278
  53.4 11.9 %collective-permute-start.14 = (bf16[512,128]{1,0:T(8,128)(2,1)S(1)}, bf16[512,128]{1,0:T(8,128)(2,1)S(1)}, u32[]{:S(2)}, u32[]{:S(2)}) collective-permute-start(bf16[512,128]{1,0:T(8,128)(2,1)S(1)} %get-tuple-element.54), channel_id=1, source_target_pairs={{0,32},{8,40},{16,48},{24,56},{32,0},{40,8},{48,16},{56,24},{1,33}... | collective-permute-start | bytes 393224 | tf_op jit(solution)/shard_map/ppermute | solution.py:288
  54.3 11.1 %collective-permute-start.12 = (bf16[256,128]{1,0:T(8,128)(2,1)S(1)}, bf16[256,128]{1,0:T(8,128)(2,1)S(1)}, u32[]{:S(2)}, u32[]{:S(2)}) collective-permute-start(bf16[256,128]{1,0:T(8,128)(2,1)S(1)} %get-tuple-element.48), channel_id=1, source_target_pairs={{0,4},{4,0},{1,5},{5,1},{2,6},{6,2},{3,7},{7,3},{8,12},{12,8},{9,1... | collective-permute-start | bytes 196616 | tf_op jit(solution)/shard_map/ppermute | solution.py:290

commit v9 on v8

--- a/solution.py
+++ b/solution.py
@@ -180,7 +180,7 @@
         out_ref[...] = total.astype(out_ref.dtype)
 
 
-def last_kernel(rows_ref, dq_ref, dqx_ref, dkv_ref, dkvz_ref, dkvy_ref, dkvyz_ref, q_ref, k_ref, v_ref):
+def last_kernel(rows_ref, dq_ref, dqx_ref, dkv_ref, dkvz_ref, q_ref, k_ref, v_ref):
     swapped = rows_ref[0, 4 * BLK :, :].astype(F32)[5:6, :] > 0.5
 
     def restore(out_ref, total):
@@ -189,9 +189,7 @@
         out_ref[BLK:, :] = jnp.where(swapped, low, high).astype(BF16)
 
     restore(q_ref, (dq_ref[...] + dqx_ref[...].astype(F32)) * FACTOR)
-    dkv = dkv_ref[...]
-    for ref in (dkvz_ref, dkvy_ref, dkvyz_ref):
-        dkv += ref[...].astype(F32)
+    dkv = dkv_ref[...] + dkvz_ref[...].astype(F32)
     restore(k_ref, dkv[: 2 * BLK] * FACTOR)
     restore(v_ref, dkv[2 * BLK :])
 
@@ -265,30 +263,30 @@
         return lax.ppermute(part, "pb", y_step(Y_FROM[turn]))
 
     both = (0, 1)
-    (dq1,), (own1,) = grad(0, both, (1,), (None,), (False,), F32)
-    k_sets[0], own1 = lax.optimization_barrier((k_sets[0], own1))
-    (dq0,), (own0,) = grad(0, both, (0,), (None,), (False,), F32)
-    (dq0, dq1), (part,) = grad(1, both, both, (dq0, dq1), (False, False), BF16)
+    (dq1,), (own_a,) = grad(0, (0,), (1,), (None,), (False,), F32)
+    q_pairs[0][1], dq1 = lax.optimization_barrier((q_pairs[0][1], dq1))
+    (dq1,), (own_b,) = grad(0, (1,), (1,), (dq1,), (False,), F32)
+    (dq0, dq1), (part,) = grad(1, both, both, (None, dq1), (False, False), BF16)
     back1 = send_back(1, part)
     (dq0, dq1), (part,) = grad(2, both, both, (dq0, dq1), (False, False), BF16)
     back2 = send_back(2, part)
-    (dq_keep, *dqs), (part, part_far) = grad(3, both, both, (dq0, dq1), (True, True), BF16, split=True)
+    (dq0, *dqs), (part,) = grad(3, both, both, (dq0, dq1), (False, True), BF16)
     back3 = send_back(3, part)
-    far = [(y * 8 + z, (y + Y_FROM[3]) % 4 * 8 + (z + 4) % 8) for y in range(4) for z in range(8)]
-    back_far = lax.ppermute(part_far, ("pb", "kz"), far)
-    dqs[0], back1 = lax.optimization_barrier((dqs[0], back1))
+    (dq_keep, dq_z2), (own0,) = grad(0, both, (0,), (dq0,), (True,), F32)
+    dq_z2, back1, back2 = lax.optimization_barrier((dq_z2, back1, back2))
+    dqs.insert(0, dq_z2)
     dq_back = [lax.ppermute(d, "kz", p) for d, p in zip(dqs, (Z_BACK, z_step(-1), z_step(1)))]
 
     def meet(operands, parts, shape):
         return call(functools.partial(meet_kernel, parts), [(shape, F32), (shape, BF16)], operands)
 
     dkv_keep, dkv_send = meet(
-        [own0, own1, back1, back2], [both] * 4, (4 * BLK, DIM)
+        [own0, own_a, own_b, back1, back2, back3], [both, (0, None), (None, 0)] + [both] * 3, (4 * BLK, DIM)
     )
     dkv_last = lax.ppermute(dkv_send, "kz", z_step(4))
     dq_keep, dq_send = meet([dq_keep] + dq_back, [both] * 4, (2 * BLK, DIM))
     dq_last = lax.ppermute(dq_send, "kx", X_SWAP)
-    operands = (q0, dq_keep, dq_last, dkv_keep, dkv_last, back3, back_far)
+    operands = (q0, dq_keep, dq_last, dkv_keep, dkv_last)
     return tuple(call(last_kernel, [((2 * BLK, DIM), BF16)] * 3, operands))
 
 

time: 66.2 us -> 64.4 us (0.973)
  the two profiles are of different devices: /device:TPU:32 before, /device:TPU:8 now
where the time goes in v9:
time: 64.4 us; the launch traced here: 64.3 us
  starting transfers between devices  29 us (45%)
  waiting for transfers between devices  21.9 us (34%)
  Pallas kernels  11.6 us (18%)
  local copies, waits for them, and re-layouts  0.96 us (1%)
  between operations  0.77 us (1%)
    pallas_call x10, Pallas kernels, call(): pl.pallas_call(kernel, out_shape=[jax.ShapeDtypeStruct(s, t) for s, t in...  11.6 us
    ppermute x3, waiting for transfers between devices, body(): lax.ppermute(q0, 'kz', p)  9.65 us
    ppermute x1, starting transfers between devices, body(): other_k = lax.ppermute(mine_k, 'kz', z_step(4))  7.19 us
    ppermute x1, starting transfers between devices, body(): dkv_last = lax.ppermute(dkv_send, 'kz', z_step(4))  5.43 us
    ppermute x3, starting transfers between devices, send_back(): return lax.ppermute(part, 'pb', y_step(Y_FROM[turn]))  5.08 us
    ppermute x3, starting transfers between devices, body(): lax.ppermute(q0, 'kz', p)  4.3 us
    ppermute x3, waiting for transfers between devices, send_back(): return lax.ppermute(part, 'pb', y_step(Y_FROM[turn]))  3.71 us
    ppermute x3, waiting for transfers between devices, body(): lax.ppermute(d, 'kz', p)  3.36 us
  transfers between devices with their start and end apart: 16, of which 8 were waited for; matrix products, arithmetic and copies ran while one was open for 2% of the time, Pallas kernels for 14%

profile of v9, /device:TPU:8, one launch (start us, length us, event | category | flops | bytes accessed | tf_op | source)
XLA Modules:
  0.0 64.3 jit_solution(14727618656307481908)
XLA Ops:
  0.6 1.8 %shard_map.94 = (bf16[528,128]{1,0:T(8,128)(2,1)}, bf16[528,128]{1,0:T(8,128)(2,1)}) custom-call(s32[128]{0:T(128)} %refs_0_.1, bf16[256,128]{1,0:T(8,128)(2,1)} %refs_1_.1, bf16[256,128]{1,0:T(8,128)(2,1)} %refs_2_.1, bf16[1,256]{1,0:T(2,128)(2,1)} %bitcast.9, bf16[256,128]{1,0:T(8,128)(2,1)} %refs_4_.1, bf16[256,128]{1,0:T(8,128)(2,1)} %refs_5_.1, ...), custom_call_target="tpu_custom_call" | custom-call | tf_op jit(solution)/shard_map/pallas_call | solution.py:212
  2.5 1.6 %collective-permute-start = (bf16[528,128]{1,0:T(8,128)(2,1)}, bf16[528,128]{1,0:T(8,128)(2,1)S(1)}, u32[]{:S(2)}, u32[]{:S(2)}) collective-permute-start(bf16[528,128]{1,0:T(8,128)(2,1)} %get-tuple-element.32), channel_id=1, source_target_pairs={{0,4},{4,0},{1,5},{5,1},{2,6},{6,2},{3,7},{7,3},{8,12},{12,8},{9,1... | collective-permute-start | bytes 405512 | tf_op jit(solution)/shard_map/ppermute | solution.py:236
  4.0 7.2 %collective-permute-start.4 = (bf16[528,128]{1,0:T(8,128)(2,1)}, bf16[528,128]{1,0:T(8,128)(2,1)S(1)}, u32[]{:S(2)}, u32[]{:S(2)}) collective-permute-start(bf16[528,128]{1,0:T(8,128)(2,1)} %get-tuple-element.33), channel_id=1, source_target_pairs={{0,32},{8,40},{16,48},{24,56},{32,0},{40,8},{48,16},{56,24},{1,33}... | collective-permute-start | bytes 405512 | tf_op jit(solution)/shard_map/ppermute | solution.py:235
  11.2 0.9 %pad.4 = bf16[2,528,128]{2,1,0:T(8,128)(2,1)S(1)} pad(bf16[1,528,128]{2,1,0:T(8,128)(2,1)} %bitcast.6, bf16[]{:T(256)} %constant.1.clone.1), padding=0_1x0_0x0_0 | pad | bytes 405506 | tf_op jit(solution)/shard_map/jit(_pad)/pad | solution.py:232
  12.2 1.1 %collective-permute-start.2 = (bf16[2,528,128]{2,1,0:T(8,128)(2,1)S(1)}, bf16[2,528,128]{2,1,0:T(8,128)(2,1)S(1)}, u32[]{:S(2)}, u32[]{:S(2)}) collective-permute-start(bf16[2,528,128]{2,1,0:T(8,128)(2,1)S(1)} %bitcast_dynamic-update-slice_fusion.refs_0_.rows_ref), channel_id=1, source_target_pairs={{0,8},{8,16},{16,24},{24,32},{32,40},{40,48},{48,56},{56,0},{1,9},... | collective-permute-start | bytes 811016 | tf_op jit(solution)/shard_map/ppermute | solution.py:239
  13.3 2.2 %collective-permute-start.3 = (bf16[2,528,128]{2,1,0:T(8,128)(2,1)S(1)}, bf16[2,528,128]{2,1,0:T(8,128)(2,1)S(1)}, u32[]{:S(2)}, u32[]{:S(2)}) collective-permute-start(bf16[2,528,128]{2,1,0:T(8,128)(2,1)S(1)} %bitcast_dynamic-update-slice_fusion.refs_0_.rows_ref), channel_id=1, source_target_pairs={{0,56},{8,0},{16,8},{24,16},{32,24},{40,32},{48,40},{56,48},{1,57}... | collective-permute-start | bytes 811016 | tf_op jit(solution)/shard_map/ppermute | solution.py:239
  15.5 1.0 %collective-permute-start.1 = (bf16[2,528,128]{2,1,0:T(8,128)(2,1)S(1)}, bf16[2,528,128]{2,1,0:T(8,128)(2,1)S(1)}, u32[]{:S(2)}, u32[]{:S(2)}) collective-permute-start(bf16[2,528,128]{2,1,0:T(8,128)(2,1)S(1)} %bitcast_dynamic-update-slice_fusion.refs_0_.rows_ref), channel_id=1, source_target_pairs={{0,48},{8,24},{16,0},{24,40},{32,16},{40,56},{48,32},{56,8},{1,49}... | collective-permute-start | bytes 811016 | tf_op jit(solution)/shard_map/ppermute | solution.py:239
  16.5 0.9 %collective-permute-done.4 = bf16[528,128]{1,0:T(8,128)(2,1)S(1)} collective-permute-done((bf16[528,128]{1,0:T(8,128)(2,1)}, bf16[528,128]{1,0:T(8,128)(2,1)S(1)}, u32[]{:S(2)}, u32[]{:S(2)}) %collective-permute-start.4) | collective-permute-done | bytes 135200 | tf_op jit(solution)/shard_map/ppermute | solution.py:235
  17.5 2.4 %collective-permute-start.7 = (bf16[2,528,128]{2,1,0:T(8,128)(2,1)S(1)}, bf16[2,528,128]{2,1,0:T(8,128)(2,1)S(1)}, u32[]{:S(2)}, u32[]{:S(2)}) collective-permute-start(bf16[2,528,128]{2,1,0:T(8,128)(2,1)S(1)} %pad_maximum_fusion.refs_2_), channel_id=1, source_target_pairs={{0,128},{64,192},{128,0},{192,64},{1,129},{65,193},{129,1},{193,65... | collective-permute-start | bytes 811016 | tf_op jit(solution)/shard_map/ppermute | solution.py:240
  19.8 3.4 %collective-permute-done.2.refs_0_.refs_2_ = bf16[2,528,128]{2,1,0:T(8,128)(2,1)S(1)} collective-permute-done((bf16[2,528,128]{2,1,0:T(8,128)(2,1)S(1)}, bf16[2,528,128]{2,1,0:T(8,128)(2,1)S(1)}, u32[]{:S(2)}, u32[]{:S(2)}) %collective-permute-start.2) | collective-permute-done | bytes 270368 | tf_op jit(solution)/shard_map/ppermute | solution.py:239
  23.7 6.2 %collective-permute-done.3.refs_1_.refs_3_ = bf16[2,528,128]{2,1,0:T(8,128)(2,1)S(1)} collective-permute-done((bf16[2,528,128]{2,1,0:T(8,128)(2,1)S(1)}, bf16[2,528,128]{2,1,0:T(8,128)(2,1)S(1)}, u32[]{:S(2)}, u32[]{:S(2)}) %collective-permute-start.3) | collective-permute-done | bytes 270368 | tf_op jit(solution)/shard_map/ppermute | solution.py:239
  31.4 2.0 %shard_map.97 = (f32[2,128,512]{2,1,0:T(8,128)S(1)}, f32[2,128,512]{2,1,0:T(8,128)S(1)}, bf16[2,512,128]{2,1,0:T(8,128)(2,1)S(1)}) custom-call(bf16[2,528,128]{2,1,0:T(8,128)(2,1)S(1)} %bitcast_dynamic-update-slice_fusion.refs_0_.rows_ref, bf16[2,528,128]{2,1,0:T(8,128)(2,1)S(1)} %collective-permute-done.1.refs_1_, ...), custom_call_target="tpu_custom_call" | custom-call | flops 500000000 | bytes 1000000 | tf_op jit(solution)/shard_map/pallas_call | solution.py:212
  33.5 2.0 %shard_map.98 = (f32[2,128,512]{2,1,0:T(8,128)S(1)}, f32[2,128,512]{2,1,0:T(8,128)S(1)}, bf16[2,512,128]{2,1,0:T(8,128)(2,1)S(1)}) custom-call(bf16[2,528,128]{2,1,0:T(8,128)(2,1)S(1)} %bitcast_dynamic-update-slice_fusion.refs_0_.rows_ref, bf16[2,528,128]{2,1,0:T(8,128)(2,1)S(1)} %collective-permute-done.1.refs_1_, ...), custom_call_target="tpu_custom_call" | custom-call | flops 500000000 | bytes 1000000 | tf_op jit(solution)/shard_map/pallas_call | solution.py:212
  36.1 2.6 %collective-permute-start.8 = (bf16[2,512,128]{2,1,0:T(8,128)(2,1)S(1)}, bf16[2,512,128]{2,1,0:T(8,128)(2,1)S(1)}, u32[]{:S(2)}, u32[]{:S(2)}) collective-permute-start(bf16[2,512,128]{2,1,0:T(8,128)(2,1)S(1)} %get-tuple-element.46), channel_id=1, source_target_pairs={{0,128},{64,192},{128,0},{192,64},{1,129},{65,193},{129,1},{193,65... | collective-permute-start | bytes 786440 | tf_op jit(solution)/shard_map/ppermute | solution.py:263
  38.6 2.1 %shard_map.99 = (f32[2,128,512]{2,1,0:T(8,128)S(1)}, bf16[2,256,128]{2,1,0:T(8,128)(2,1)S(1)}, bf16[2,256,128]{2,1,0:T(8,128)(2,1)S(1)}, bf16[2,512,128]{2,1,0:T(8,128)(2,1)S(1)}) custom-call(bf16[2,528,128]{2,1,0:T(8,128)(2,1)S(1)} %bitcast_dynamic-update-slice_fusion.refs_0_.rows_ref, bf16[2,528,128]{2,1,0:T(8,128)(2,1)S(1)} %collective-permute-done.1.refs_1_, ...), custom_call_target="tpu_custom_call" | custom-call | flops 500000000 | bytes 1000000 | tf_op jit(solution)/shard_map/pallas_call | solution.py:212
  40.8 2.0 %collective-permute-start.14 = (bf16[2,512,128]{2,1,0:T(8,128)(2,1)S(1)}, bf16[2,512,128]{2,1,0:T(8,128)(2,1)S(1)}, u32[]{:S(2)}, u32[]{:S(2)}) collective-permute-start(bf16[2,512,128]{2,1,0:T(8,128)(2,1)S(1)} %get-tuple-element.58), channel_id=1, source_target_pairs={{0,64},{64,128},{128,192},{192,0},{1,65},{65,129},{129,193},{193,1... | collective-permute-start | bytes 786440 | tf_op jit(solution)/shard_map/ppermute | solution.py:263
  42.8 0.7 %collective-permute-start.11 = (bf16[2,256,128]{2,1,0:T(8,128)(2,1)S(1)}, bf16[2,256,128]{2,1,0:T(8,128)(2,1)S(1)}, u32[]{:S(2)}, u32[]{:S(2)}) collective-permute-start(bf16[2,256,128]{2,1,0:T(8,128)(2,1)S(1)} %get-tuple-element.49), channel_id=1, source_target_pairs={{0,56},{8,0},{16,8},{24,16},{32,24},{40,32},{48,40},{56,48},{1,57}... | collective-permute-start | bytes 393224 | tf_op jit(solution)/shard_map/ppermute | solution.py:278
  43.5 1.3 %collective-permute-start.12 = (bf16[2,256,128]{2,1,0:T(8,128)(2,1)S(1)}, bf16[2,256,128]{2,1,0:T(8,128)(2,1)S(1)}, u32[]{:S(2)}, u32[]{:S(2)}) collective-permute-start(bf16[2,256,128]{2,1,0:T(8,128)(2,1)S(1)} %get-tuple-element.50), channel_id=1, source_target_pairs={{0,8},{8,16},{16,24},{24,32},{32,40},{40,48},{48,56},{56,0},{1,9},... | collective-permute-start | bytes 393224 | tf_op jit(solution)/shard_map/ppermute | solution.py:278
  44.8 1.2 %shard_map.100 = (f32[2,256,128]{2,1,0:T(8,128)S(1)}, bf16[2,256,128]{2,1,0:T(8,128)(2,1)S(1)}, f32[2,512,128]{2,1,0:T(8,128)S(1)}) custom-call(bf16[2,528,128]{2,1,0:T(8,128)(2,1)S(1)} %bitcast_dynamic-update-slice_fusion.refs_0_.rows_ref, bf16[2,528,128]{2,1,0:T(8,128)(2,1)S(1)} %collective-permute-done.1.refs_1_, ...), custom_call_target="tpu_custom_call" | custom-call | flops 500000000 | bytes 1000000 | tf_op jit(solution)/shard_map/pallas_call | solution.py:212
  46.0 3.3 %collective-permute-done.8.refs_3_ = bf16[2,512,128]{2,1,0:T(8,128)(2,1)S(1)} collective-permute-done((bf16[2,512,128]{2,1,0:T(8,128)(2,1)S(1)}, bf16[2,512,128]{2,1,0:T(8,128)(2,1)S(1)}, u32[]{:S(2)}, u32[]{:S(2)}) %collective-permute-start.8) | collective-permute-done | bytes 262176 | tf_op jit(solution)/shard_map/ppermute | solution.py:263
  50.4 5.4 %collective-permute-start.15 = (bf16[512,128]{1,0:T(8,128)(2,1)S(1)}, bf16[512,128]{1,0:T(8,128)(2,1)S(1)}, u32[]{:S(2)}, u32[]{:S(2)}) collective-permute-start(bf16[512,128]{1,0:T(8,128)(2,1)S(1)} %get-tuple-element.60), channel_id=1, source_target_pairs={{0,32},{8,40},{16,48},{24,56},{32,0},{40,8},{48,16},{56,24},{1,33}... | collective-permute-start | bytes 393224 | tf_op jit(solution)/shard_map/ppermute | solution.py:286
  55.8 3.4 %collective-permute-done.10.refs_1_ = bf16[2,256,128]{2,1,0:T(8,128)(2,1)S(1)} collective-permute-done((bf16[2,256,128]{2,1,0:T(8,128)(2,1)S(1)}, bf16[2,256,128]{2,1,0:T(8,128)(2,1)S(1)}, u32[]{:S(2)}, u32[]{:S(2)}) %collective-permute-start.10) | collective-permute-done | bytes 131104 | tf_op jit(solution)/shard_map/ppermute | solution.py:278
  59.3 3.1 %collective-permute-done.15.dkvz_ref = bf16[512,128]{1,0:T(8,128)(2,1)S(1)} collective-permute-done((bf16[512,128]{1,0:T(8,128)(2,1)S(1)}, bf16[512,128]{1,0:T(8,128)(2,1)S(1)}, u32[]{:S(2)}, u32[]{:S(2)}) %collective-permute-start.15) | collective-permute-done | bytes 131104 | tf_op jit(solution)/shard_map/ppermute | solution.py:286
  62.4 1.2 %collective-permute-done.13.dqx_ref = bf16[256,128]{1,0:T(8,128)(2,1)S(1)} collective-permute-done((bf16[256,128]{1,0:T(8,128)(2,1)S(1)}, bf16[256,128]{1,0:T(8,128)(2,1)S(1)}, u32[]{:S(2)}, u32[]{:S(2)}) %collective-permute-start.13) | collective-permute-done | bytes 65568 | tf_op jit(solution)/shard_map/ppermute | solution.py:288
  (23 shorter events, 4.4 us)
Async XLA Ops:
  2.5 9.7 %collective-permute-start = (bf16[528,128]{1,0:T(8,128)(2,1)}, bf16[528,128]{1,0:T(8,128)(2,1)S(1)}, u32[]{:S(2)}, u32[]{:S(2)}) collective-permute-start(bf16[528,128]{1,0:T(8,128)(2,1)} %get-tuple-element.32), channel_id=1, source_target_pairs={{0,4},{4,0},{1,5},{5,1},{2,6},{6,2},{3,7},{7,3},{8,12},{12,8},{9,1... | collective-permute-start | bytes 405512 | tf_op jit(solution)/shard_map/ppermute | solution.py:236
  4.0 13.4 %collective-permute-start.4 = (bf16[528,128]{1,0:T(8,128)(2,1)}, bf16[528,128]{1,0:T(8,128)(2,1)S(1)}, u32[]{:S(2)}, u32[]{:S(2)}) collective-permute-start(bf16[528,128]{1,0:T(8,128)(2,1)} %get-tuple-element.33), channel_id=1, source_target_pairs={{0,32},{8,40},{16,48},{24,56},{32,0},{40,8},{48,16},{56,24},{1,33}... | collective-permute-start | bytes 405512 | tf_op jit(solution)/shard_map/ppermute | solution.py:235
  12.2 5.3 %copy-start = (bf16[528,128]{1,0:T(8,128)(2,1)S(1)}, bf16[528,128]{1,0:T(8,128)(2,1)}, u32[]{:S(2)}) copy-start(bf16[528,128]{1,0:T(8,128)(2,1)} %get-tuple-element.33) | copy-start | bytes 405508
  12.2 11.1 %collective-permute-start.2 = (bf16[2,528,128]{2,1,0:T(8,128)(2,1)S(1)}, bf16[2,528,128]{2,1,0:T(8,128)(2,1)S(1)}, u32[]{:S(2)}, u32[]{:S(2)}) collective-permute-start(bf16[2,528,128]{2,1,0:T(8,128)(2,1)S(1)} %bitcast_dynamic-update-slice_fusion.refs_0_.rows_ref), channel_id=1, source_target_pairs={{0,8},{8,16},{16,24},{24,32},{32,40},{40,48},{48,56},{56,0},{1,9},... | collective-permute-start | bytes 811016 | tf_op jit(solution)/shard_map/ppermute | solution.py:239
  13.3 16.7 %collective-permute-start.3 = (bf16[2,528,128]{2,1,0:T(8,128)(2,1)S(1)}, bf16[2,528,128]{2,1,0:T(8,128)(2,1)S(1)}, u32[]{:S(2)}, u32[]{:S(2)}) collective-permute-start(bf16[2,528,128]{2,1,0:T(8,128)(2,1)S(1)} %bitcast_dynamic-update-slice_fusion.refs_0_.rows_ref), channel_id=1, source_target_pairs={{0,56},{8,0},{16,8},{24,16},{32,24},{40,32},{48,40},{56,48},{1,57}... | collective-permute-start | bytes 811016 | tf_op jit(solution)/shard_map/ppermute | solution.py:239
  15.5 15.2 %collective-permute-start.1 = (bf16[2,528,128]{2,1,0:T(8,128)(2,1)S(1)}, bf16[2,528,128]{2,1,0:T(8,128)(2,1)S(1)}, u32[]{:S(2)}, u32[]{:S(2)}) collective-permute-start(bf16[2,528,128]{2,1,0:T(8,128)(2,1)S(1)} %bitcast_dynamic-update-slice_fusion.refs_0_.rows_ref), channel_id=1, source_target_pairs={{0,48},{8,24},{16,0},{24,40},{32,16},{40,56},{48,32},{56,8},{1,49}... | collective-permute-start | bytes 811016 | tf_op jit(solution)/shard_map/ppermute | solution.py:239
  17.5 14.0 %collective-permute-start.7 = (bf16[2,528,128]{2,1,0:T(8,128)(2,1)S(1)}, bf16[2,528,128]{2,1,0:T(8,128)(2,1)S(1)}, u32[]{:S(2)}, u32[]{:S(2)}) collective-permute-start(bf16[2,528,128]{2,1,0:T(8,128)(2,1)S(1)} %pad_maximum_fusion.refs_2_), channel_id=1, source_target_pairs={{0,128},{64,192},{128,0},{192,64},{1,129},{65,193},{129,1},{193,65... | collective-permute-start | bytes 811016 | tf_op jit(solution)/shard_map/ppermute | solution.py:240
  19.8 13.6 %collective-permute-start.6 = (bf16[2,528,128]{2,1,0:T(8,128)(2,1)S(1)}, bf16[2,528,128]{2,1,0:T(8,128)(2,1)S(1)}, u32[]{:S(2)}, u32[]{:S(2)}) collective-permute-start(bf16[2,528,128]{2,1,0:T(8,128)(2,1)S(1)} %pad_maximum_fusion.refs_2_), channel_id=1, source_target_pairs={{0,64},{64,128},{128,192},{192,0},{1,65},{65,129},{129,193},{193,1... | collective-permute-start | bytes 811016 | tf_op jit(solution)/shard_map/ppermute | solution.py:240
  23.3 15.4 %collective-permute-start.5 = (bf16[2,528,128]{2,1,0:T(8,128)(2,1)S(1)}, bf16[2,528,128]{2,1,0:T(8,128)(2,1)S(1)}, u32[]{:S(2)}, u32[]{:S(2)}) collective-permute-start(bf16[2,528,128]{2,1,0:T(8,128)(2,1)S(1)} %pad_maximum_fusion.refs_2_), channel_id=1, source_target_pairs={{0,192},{64,0},{128,64},{192,128},{1,193},{65,1},{129,65},{193,129... | collective-permute-start | bytes 811016 | tf_op jit(solution)/shard_map/ppermute | solution.py:240
  35.5 10.5 %collective-permute-start.9 = (bf16[2,512,128]{2,1,0:T(8,128)(2,1)S(1)}, bf16[2,512,128]{2,1,0:T(8,128)(2,1)S(1)}, u32[]{:S(2)}, u32[]{:S(2)}) collective-permute-start(bf16[2,512,128]{2,1,0:T(8,128)(2,1)S(1)} %get-tuple-element.47), channel_id=1, source_target_pairs={{0,192},{64,0},{128,64},{192,128},{1,193},{65,1},{129,65},{193,129... | collective-permute-start | bytes 786440 | tf_op jit(solution)/shard_map/ppermute | solution.py:263
  36.1 13.3 %collective-permute-start.8 = (bf16[2,512,128]{2,1,0:T(8,128)(2,1)S(1)}, bf16[2,512,128]{2,1,0:T(8,128)(2,1)S(1)}, u32[]{:S(2)}, u32[]{:S(2)}) collective-permute-start(bf16[2,512,128]{2,1,0:T(8,128)(2,1)S(1)} %get-tuple-element.46), channel_id=1, source_target_pairs={{0,128},{64,192},{128,0},{192,64},{1,129},{65,193},{129,1},{193,65... | collective-permute-start | bytes 786440 | tf_op jit(solution)/shard_map/ppermute | solution.py:263
  40.8 9.4 %collective-permute-start.14 = (bf16[2,512,128]{2,1,0:T(8,128)(2,1)S(1)}, bf16[2,512,128]{2,1,0:T(8,128)(2,1)S(1)}, u32[]{:S(2)}, u32[]{:S(2)}) collective-permute-start(bf16[2,512,128]{2,1,0:T(8,128)(2,1)S(1)} %get-tuple-element.58), channel_id=1, source_target_pairs={{0,64},{64,128},{128,192},{192,0},{1,65},{65,129},{129,193},{193,1... | collective-permute-start | bytes 786440 | tf_op jit(solution)/shard_map/ppermute | solution.py:263
  42.8 13.0 %collective-permute-start.11 = (bf16[2,256,128]{2,1,0:T(8,128)(2,1)S(1)}, bf16[2,256,128]{2,1,0:T(8,128)(2,1)S(1)}, u32[]{:S(2)}, u32[]{:S(2)}) collective-permute-start(bf16[2,256,128]{2,1,0:T(8,128)(2,1)S(1)} %get-tuple-element.49), channel_id=1, source_target_pairs={{0,56},{8,0},{16,8},{24,16},{32,24},{40,32},{48,40},{56,48},{1,57}... | collective-permute-start | bytes 393224 | tf_op jit(solution)/shard_map/ppermute | solution.py:278
  43.5 12.3 %collective-permute-start.12 = (bf16[2,256,128]{2,1,0:T(8,128)(2,1)S(1)}, bf16[2,256,128]{2,1,0:T(8,128)(2,1)S(1)}, u32[]{:S(2)}, u32[]{:S(2)}) collective-permute-start(bf16[2,256,128]{2,1,0:T(8,128)(2,1)S(1)} %get-tuple-element.50), channel_id=1, source_target_pairs={{0,8},{8,16},{16,24},{24,32},{32,40},{40,48},{48,56},{56,0},{1,9},... | collective-permute-start | bytes 393224 | tf_op jit(solution)/shard_map/ppermute | solution.py:278
  49.3 9.8 %collective-permute-start.10 = (bf16[2,256,128]{2,1,0:T(8,128)(2,1)S(1)}, bf16[2,256,128]{2,1,0:T(8,128)(2,1)S(1)}, u32[]{:S(2)}, u32[]{:S(2)}) collective-permute-start(bf16[2,256,128]{2,1,0:T(8,128)(2,1)S(1)} %get-tuple-element.48), channel_id=1, source_target_pairs={{48,0},{24,8},{0,16},{40,24},{16,32},{56,40},{32,48},{8,56},{49,1}... | collective-permute-start | bytes 393224 | tf_op jit(solution)/shard_map/ppermute | solution.py:278
  50.4 12.0 %collective-permute-start.15 = (bf16[512,128]{1,0:T(8,128)(2,1)S(1)}, bf16[512,128]{1,0:T(8,128)(2,1)S(1)}, u32[]{:S(2)}, u32[]{:S(2)}) collective-permute-start(bf16[512,128]{1,0:T(8,128)(2,1)S(1)} %get-tuple-element.60), channel_id=1, source_target_pairs={{0,32},{8,40},{16,48},{24,56},{32,0},{40,8},{48,16},{56,24},{1,33}... | collective-permute-start | bytes 393224 | tf_op jit(solution)/shard_map/ppermute | solution.py:286
  59.2 4.4 %collective-permute-start.13 = (bf16[256,128]{1,0:T(8,128)(2,1)S(1)}, bf16[256,128]{1,0:T(8,128)(2,1)S(1)}, u32[]{:S(2)}, u32[]{:S(2)}) collective-permute-start(bf16[256,128]{1,0:T(8,128)(2,1)S(1)} %get-tuple-element.52), channel_id=1, source_target_pairs={{0,4},{4,0},{1,5},{5,1},{2,6},{6,2},{3,7},{7,3},{8,12},{12,8},{9,1... | collective-permute-start | bytes 196616 | tf_op jit(solution)/shard_map/ppermute | solution.py:288

commit v10 on v9

--- a/solution.py
+++ b/solution.py
@@ -272,8 +272,9 @@
     back2 = send_back(2, part)
     (dq0, *dqs), (part,) = grad(3, both, both, (dq0, dq1), (False, True), BF16)
     back3 = send_back(3, part)
+    dq0, back1 = lax.optimization_barrier((dq0, back1))
     (dq_keep, dq_z2), (own0,) = grad(0, both, (0,), (dq0,), (True,), F32)
-    dq_z2, back1, back2 = lax.optimization_barrier((dq_z2, back1, back2))
+    dq_z2, back2 = lax.optimization_barrier((dq_z2, back2))
     dqs.insert(0, dq_z2)
     dq_back = [lax.ppermute(d, "kz", p) for d, p in zip(dqs, (Z_BACK, z_step(-1), z_step(1)))]
 

time: 64.4 us -> 63.9 us (level)
  the two profiles are of different devices: /device:TPU:8 before, /device:TPU:24 now
where the time goes in v10:
time: 63.9 us; the launch traced here: 63.7 us
  starting transfers between devices  33.2 us (52%)
  waiting for transfers between devices  17.2 us (27%)
  Pallas kernels  11.6 us (18%)
  local copies, waits for them, and re-layouts  0.96 us (2%)
  between operations  0.76 us (1%)
    pallas_call x10, Pallas kernels, call(): pl.pallas_call(kernel, out_shape=[jax.ShapeDtypeStruct(s, t) for s, t in...  11.6 us
    ppermute x3, waiting for transfers between devices, body(): lax.ppermute(q0, 'kz', p)  8.24 us
    ppermute x1, starting transfers between devices, body(): other_k = lax.ppermute(mine_k, 'kz', z_step(4))  7.19 us
    ppermute x1, waiting for transfers between devices, body(): dkv_last = lax.ppermute(dkv_send, 'kz', z_step(4))  6.08 us
    ppermute x3, starting transfers between devices, body(): lax.ppermute(d, 'kz', p)  5.25 us
    ppermute x1, starting transfers between devices, body(): dkv_last = lax.ppermute(dkv_send, 'kz', z_step(4))  4.95 us
    ppermute x3, starting transfers between devices, send_back(): return lax.ppermute(part, 'pb', y_step(Y_FROM[turn]))  4.88 us
    ppermute x3, starting transfers between devices, body(): lax.ppermute(q0, 'kz', p)  4.3 us
  transfers between devices with their start and end apart: 16, of which 6 were waited for; matrix products, arithmetic and copies ran while one was open for 2% of the time, Pallas kernels for 14%

profile of v10, /device:TPU:24, one launch (start us, length us, event | category | flops | bytes accessed | tf_op | source)
XLA Modules:
  0.0 63.7 jit_solution(719930533240419181)
XLA Ops:
  0.6 1.8 %shard_map.94 = (bf16[528,128]{1,0:T(8,128)(2,1)}, bf16[528,128]{1,0:T(8,128)(2,1)}) custom-call(s32[128]{0:T(128)} %refs_0_.1, bf16[256,128]{1,0:T(8,128)(2,1)} %refs_1_.1, bf16[256,128]{1,0:T(8,128)(2,1)} %refs_2_.1, bf16[1,256]{1,0:T(2,128)(2,1)} %bitcast.9, bf16[256,128]{1,0:T(8,128)(2,1)} %refs_4_.1, bf16[256,128]{1,0:T(8,128)(2,1)} %refs_5_.1, ...), custom_call_target="tpu_custom_call" | custom-call | tf_op jit(solution)/shard_map/pallas_call | solution.py:212
  2.5 1.6 %collective-permute-start = (bf16[528,128]{1,0:T(8,128)(2,1)}, bf16[528,128]{1,0:T(8,128)(2,1)S(1)}, u32[]{:S(2)}, u32[]{:S(2)}) collective-permute-start(bf16[528,128]{1,0:T(8,128)(2,1)} %get-tuple-element.33), channel_id=1, source_target_pairs={{0,4},{4,0},{1,5},{5,1},{2,6},{6,2},{3,7},{7,3},{8,12},{12,8},{9,1... | collective-permute-start | bytes 405512 | tf_op jit(solution)/shard_map/ppermute | solution.py:236
  4.0 7.2 %collective-permute-start.4 = (bf16[528,128]{1,0:T(8,128)(2,1)}, bf16[528,128]{1,0:T(8,128)(2,1)S(1)}, u32[]{:S(2)}, u32[]{:S(2)}) collective-permute-start(bf16[528,128]{1,0:T(8,128)(2,1)} %get-tuple-element.34), channel_id=1, source_target_pairs={{0,32},{8,40},{16,48},{24,56},{32,0},{40,8},{48,16},{56,24},{1,33}... | collective-permute-start | bytes 405512 | tf_op jit(solution)/shard_map/ppermute | solution.py:235
  11.2 0.9 %pad.4 = bf16[2,528,128]{2,1,0:T(8,128)(2,1)S(1)} pad(bf16[1,528,128]{2,1,0:T(8,128)(2,1)} %bitcast.6, bf16[]{:T(256)} %constant.1.clone.1), padding=0_1x0_0x0_0 | pad | bytes 405506 | tf_op jit(solution)/shard_map/jit(_pad)/pad | solution.py:232
  12.2 1.1 %collective-permute-start.2 = (bf16[2,528,128]{2,1,0:T(8,128)(2,1)S(1)}, bf16[2,528,128]{2,1,0:T(8,128)(2,1)S(1)}, u32[]{:S(2)}, u32[]{:S(2)}) collective-permute-start(bf16[2,528,128]{2,1,0:T(8,128)(2,1)S(1)} %bitcast_dynamic-update-slice_fusion.refs_0_.rows_ref), channel_id=1, source_target_pairs={{0,8},{8,16},{16,24},{24,32},{32,40},{40,48},{48,56},{56,0},{1,9},... | collective-permute-start | bytes 811016 | tf_op jit(solution)/shard_map/ppermute | solution.py:239
  13.3 2.2 %collective-permute-start.3 = (bf16[2,528,128]{2,1,0:T(8,128)(2,1)S(1)}, bf16[2,528,128]{2,1,0:T(8,128)(2,1)S(1)}, u32[]{:S(2)}, u32[]{:S(2)}) collective-permute-start(bf16[2,528,128]{2,1,0:T(8,128)(2,1)S(1)} %bitcast_dynamic-update-slice_fusion.refs_0_.rows_ref), channel_id=1, source_target_pairs={{0,56},{8,0},{16,8},{24,16},{32,24},{40,32},{48,40},{56,48},{1,57}... | collective-permute-start | bytes 811016 | tf_op jit(solution)/shard_map/ppermute | solution.py:239
  15.5 1.0 %collective-permute-start.1 = (bf16[2,528,128]{2,1,0:T(8,128)(2,1)S(1)}, bf16[2,528,128]{2,1,0:T(8,128)(2,1)S(1)}, u32[]{:S(2)}, u32[]{:S(2)}) collective-permute-start(bf16[2,528,128]{2,1,0:T(8,128)(2,1)S(1)} %bitcast_dynamic-update-slice_fusion.refs_0_.rows_ref), channel_id=1, source_target_pairs={{0,48},{8,24},{16,0},{24,40},{32,16},{40,56},{48,32},{56,8},{1,49}... | collective-permute-start | bytes 811016 | tf_op jit(solution)/shard_map/ppermute | solution.py:239
  16.5 0.9 %collective-permute-done.4 = bf16[528,128]{1,0:T(8,128)(2,1)S(1)} collective-permute-done((bf16[528,128]{1,0:T(8,128)(2,1)}, bf16[528,128]{1,0:T(8,128)(2,1)S(1)}, u32[]{:S(2)}, u32[]{:S(2)}) %collective-permute-start.4) | collective-permute-done | bytes 135200 | tf_op jit(solution)/shard_map/ppermute | solution.py:235
  17.5 1.3 %collective-permute-start.7 = (bf16[2,528,128]{2,1,0:T(8,128)(2,1)S(1)}, bf16[2,528,128]{2,1,0:T(8,128)(2,1)S(1)}, u32[]{:S(2)}, u32[]{:S(2)}) collective-permute-start(bf16[2,528,128]{2,1,0:T(8,128)(2,1)S(1)} %pad_maximum_fusion.refs_2_), channel_id=1, source_target_pairs={{0,128},{64,192},{128,0},{192,64},{1,129},{65,193},{129,1},{193,65... | collective-permute-start | bytes 811016 | tf_op jit(solution)/shard_map/ppermute | solution.py:240
  18.8 2.2 %collective-permute-start.6 = (bf16[2,528,128]{2,1,0:T(8,128)(2,1)S(1)}, bf16[2,528,128]{2,1,0:T(8,128)(2,1)S(1)}, u32[]{:S(2)}, u32[]{:S(2)}) collective-permute-start(bf16[2,528,128]{2,1,0:T(8,128)(2,1)S(1)} %pad_maximum_fusion.refs_2_), channel_id=1, source_target_pairs={{0,64},{64,128},{128,192},{192,0},{1,65},{65,129},{129,193},{193,1... | collective-permute-start | bytes 811016 | tf_op jit(solution)/shard_map/ppermute | solution.py:240
  21.0 2.3 %collective-permute-done.2.refs_0_.refs_2_ = bf16[2,528,128]{2,1,0:T(8,128)(2,1)S(1)} collective-permute-done((bf16[2,528,128]{2,1,0:T(8,128)(2,1)S(1)}, bf16[2,528,128]{2,1,0:T(8,128)(2,1)S(1)}, u32[]{:S(2)}, u32[]{:S(2)}) %collective-permute-start.2) | collective-permute-done | bytes 270368 | tf_op jit(solution)/shard_map/ppermute | solution.py:239
  24.0 5.9 %collective-permute-done.3.refs_1_.refs_3_ = bf16[2,528,128]{2,1,0:T(8,128)(2,1)S(1)} collective-permute-done((bf16[2,528,128]{2,1,0:T(8,128)(2,1)S(1)}, bf16[2,528,128]{2,1,0:T(8,128)(2,1)S(1)}, u32[]{:S(2)}, u32[]{:S(2)}) %collective-permute-start.3) | collective-permute-done | bytes 270368 | tf_op jit(solution)/shard_map/ppermute | solution.py:239
  31.4 2.0 %shard_map.97 = (f32[2,128,512]{2,1,0:T(8,128)S(1)}, f32[2,128,512]{2,1,0:T(8,128)S(1)}, bf16[2,512,128]{2,1,0:T(8,128)(2,1)S(1)}) custom-call(bf16[2,528,128]{2,1,0:T(8,128)(2,1)S(1)} %bitcast_dynamic-update-slice_fusion.refs_0_.rows_ref, bf16[2,528,128]{2,1,0:T(8,128)(2,1)S(1)} %collective-permute-done.1.refs_1_, ...), custom_call_target="tpu_custom_call" | custom-call | flops 500000000 | bytes 1000000 | tf_op jit(solution)/shard_map/pallas_call | solution.py:212
  33.5 1.3 %collective-permute-start.8 = (bf16[2,512,128]{2,1,0:T(8,128)(2,1)S(1)}, bf16[2,512,128]{2,1,0:T(8,128)(2,1)S(1)}, u32[]{:S(2)}, u32[]{:S(2)}) collective-permute-start(bf16[2,512,128]{2,1,0:T(8,128)(2,1)S(1)} %get-tuple-element.45), channel_id=1, source_target_pairs={{0,128},{64,192},{128,0},{192,64},{1,129},{65,193},{129,1},{193,65... | collective-permute-start | bytes 786440 | tf_op jit(solution)/shard_map/ppermute | solution.py:263
  34.8 2.0 %shard_map.98 = (f32[2,128,512]{2,1,0:T(8,128)S(1)}, f32[2,128,512]{2,1,0:T(8,128)S(1)}, bf16[2,512,128]{2,1,0:T(8,128)(2,1)S(1)}) custom-call(bf16[2,528,128]{2,1,0:T(8,128)(2,1)S(1)} %bitcast_dynamic-update-slice_fusion.refs_0_.rows_ref, bf16[2,528,128]{2,1,0:T(8,128)(2,1)S(1)} %collective-permute-done.1.refs_1_, ...), custom_call_target="tpu_custom_call" | custom-call | flops 500000000 | bytes 1000000 | tf_op jit(solution)/shard_map/pallas_call | solution.py:212
  37.1 2.1 %shard_map.99 = (f32[2,128,512]{2,1,0:T(8,128)S(1)}, bf16[2,256,128]{2,1,0:T(8,128)(2,1)S(1)}, bf16[2,256,128]{2,1,0:T(8,128)(2,1)S(1)}, bf16[2,512,128]{2,1,0:T(8,128)(2,1)S(1)}) custom-call(bf16[2,528,128]{2,1,0:T(8,128)(2,1)S(1)} %bitcast_dynamic-update-slice_fusion.refs_0_.rows_ref, bf16[2,528,128]{2,1,0:T(8,128)(2,1)S(1)} %collective-permute-done.1.refs_1_, ...), custom_call_target="tpu_custom_call" | custom-call | flops 500000000 | bytes 1000000 | tf_op jit(solution)/shard_map/pallas_call | solution.py:212
  39.3 3.3 %collective-permute-start.14 = (bf16[2,512,128]{2,1,0:T(8,128)(2,1)S(1)}, bf16[2,512,128]{2,1,0:T(8,128)(2,1)S(1)}, u32[]{:S(2)}, u32[]{:S(2)}) collective-permute-start(bf16[2,512,128]{2,1,0:T(8,128)(2,1)S(1)} %get-tuple-element.60), channel_id=1, source_target_pairs={{0,64},{64,128},{128,192},{192,0},{1,65},{65,129},{129,193},{193,1... | collective-permute-start | bytes 786440 | tf_op jit(solution)/shard_map/ppermute | solution.py:263
  43.3 3.1 %collective-permute-start.12 = (bf16[2,256,128]{2,1,0:T(8,128)(2,1)S(1)}, bf16[2,256,128]{2,1,0:T(8,128)(2,1)S(1)}, u32[]{:S(2)}, u32[]{:S(2)}) collective-permute-start(bf16[2,256,128]{2,1,0:T(8,128)(2,1)S(1)} %get-tuple-element.52), channel_id=1, source_target_pairs={{0,8},{8,16},{16,24},{24,32},{32,40},{40,48},{48,56},{56,0},{1,9},... | collective-permute-start | bytes 393224 | tf_op jit(solution)/shard_map/ppermute | solution.py:279
  46.5 1.2 %shard_map.100 = (f32[2,256,128]{2,1,0:T(8,128)S(1)}, bf16[2,256,128]{2,1,0:T(8,128)(2,1)S(1)}, f32[2,512,128]{2,1,0:T(8,128)S(1)}) custom-call(bf16[2,528,128]{2,1,0:T(8,128)(2,1)S(1)} %bitcast_dynamic-update-slice_fusion.refs_0_.rows_ref, bf16[2,528,128]{2,1,0:T(8,128)(2,1)S(1)} %collective-permute-done.1.refs_1_, ...), custom_call_target="tpu_custom_call" | custom-call | flops 500000000 | bytes 1000000 | tf_op jit(solution)/shard_map/pallas_call | solution.py:212
  47.8 1.4 %collective-permute-start.10 = (bf16[2,256,128]{2,1,0:T(8,128)(2,1)S(1)}, bf16[2,256,128]{2,1,0:T(8,128)(2,1)S(1)}, u32[]{:S(2)}, u32[]{:S(2)}) collective-permute-start(bf16[2,256,128]{2,1,0:T(8,128)(2,1)S(1)} %get-tuple-element.50), channel_id=1, source_target_pairs={{48,0},{24,8},{0,16},{40,24},{16,32},{56,40},{32,48},{8,56},{49,1}... | collective-permute-start | bytes 393224 | tf_op jit(solution)/shard_map/ppermute | solution.py:279
  49.3 5.0 %collective-permute-start.15 = (bf16[512,128]{1,0:T(8,128)(2,1)S(1)}, bf16[512,128]{1,0:T(8,128)(2,1)S(1)}, u32[]{:S(2)}, u32[]{:S(2)}) collective-permute-start(bf16[512,128]{1,0:T(8,128)(2,1)S(1)} %get-tuple-element.62), channel_id=1, source_target_pairs={{0,32},{8,40},{16,48},{24,56},{32,0},{40,8},{48,16},{56,24},{1,33}... | collective-permute-start | bytes 393224 | tf_op jit(solution)/shard_map/ppermute | solution.py:287
  54.3 1.8 %collective-permute-done.10.refs_1_ = bf16[2,256,128]{2,1,0:T(8,128)(2,1)S(1)} collective-permute-done((bf16[2,256,128]{2,1,0:T(8,128)(2,1)S(1)}, bf16[2,256,128]{2,1,0:T(8,128)(2,1)S(1)}, u32[]{:S(2)}, u32[]{:S(2)}) %collective-permute-start.10) | collective-permute-done | bytes 131104 | tf_op jit(solution)/shard_map/ppermute | solution.py:279
  56.1 0.8 %collective-permute-start.13 = (bf16[256,128]{1,0:T(8,128)(2,1)S(1)}, bf16[256,128]{1,0:T(8,128)(2,1)S(1)}, u32[]{:S(2)}, u32[]{:S(2)}) collective-permute-start(bf16[256,128]{1,0:T(8,128)(2,1)S(1)} %get-tuple-element.54), channel_id=1, source_target_pairs={{0,4},{4,0},{1,5},{5,1},{2,6},{6,2},{3,7},{7,3},{8,12},{12,8},{9,1... | collective-permute-start | bytes 196616 | tf_op jit(solution)/shard_map/ppermute | solution.py:289
  56.9 6.1 %collective-permute-done.15.dkvz_ref = bf16[512,128]{1,0:T(8,128)(2,1)S(1)} collective-permute-done((bf16[512,128]{1,0:T(8,128)(2,1)S(1)}, bf16[512,128]{1,0:T(8,128)(2,1)S(1)}, u32[]{:S(2)}, u32[]{:S(2)}) %collective-permute-start.15) | collective-permute-done | bytes 131104 | tf_op jit(solution)/shard_map/ppermute | solution.py:287
  (23 shorter events, 4.3 us)
Async XLA Ops:
  2.5 9.7 %collective-permute-start = (bf16[528,128]{1,0:T(8,128)(2,1)}, bf16[528,128]{1,0:T(8,128)(2,1)S(1)}, u32[]{:S(2)}, u32[]{:S(2)}) collective-permute-start(bf16[528,128]{1,0:T(8,128)(2,1)} %get-tuple-element.33), channel_id=1, source_target_pairs={{0,4},{4,0},{1,5},{5,1},{2,6},{6,2},{3,7},{7,3},{8,12},{12,8},{9,1... | collective-permute-start | bytes 405512 | tf_op jit(solution)/shard_map/ppermute | solution.py:236
  4.0 13.4 %collective-permute-start.4 = (bf16[528,128]{1,0:T(8,128)(2,1)}, bf16[528,128]{1,0:T(8,128)(2,1)S(1)}, u32[]{:S(2)}, u32[]{:S(2)}) collective-permute-start(bf16[528,128]{1,0:T(8,128)(2,1)} %get-tuple-element.34), channel_id=1, source_target_pairs={{0,32},{8,40},{16,48},{24,56},{32,0},{40,8},{48,16},{56,24},{1,33}... | collective-permute-start | bytes 405512 | tf_op jit(solution)/shard_map/ppermute | solution.py:235
  12.2 5.3 %copy-start = (bf16[528,128]{1,0:T(8,128)(2,1)S(1)}, bf16[528,128]{1,0:T(8,128)(2,1)}, u32[]{:S(2)}) copy-start(bf16[528,128]{1,0:T(8,128)(2,1)} %get-tuple-element.34) | copy-start | bytes 405508
  12.2 11.1 %collective-permute-start.2 = (bf16[2,528,128]{2,1,0:T(8,128)(2,1)S(1)}, bf16[2,528,128]{2,1,0:T(8,128)(2,1)S(1)}, u32[]{:S(2)}, u32[]{:S(2)}) collective-permute-start(bf16[2,528,128]{2,1,0:T(8,128)(2,1)S(1)} %bitcast_dynamic-update-slice_fusion.refs_0_.rows_ref), channel_id=1, source_target_pairs={{0,8},{8,16},{16,24},{24,32},{32,40},{40,48},{48,56},{56,0},{1,9},... | collective-permute-start | bytes 811016 | tf_op jit(solution)/shard_map/ppermute | solution.py:239
  13.3 16.7 %collective-permute-start.3 = (bf16[2,528,128]{2,1,0:T(8,128)(2,1)S(1)}, bf16[2,528,128]{2,1,0:T(8,128)(2,1)S(1)}, u32[]{:S(2)}, u32[]{:S(2)}) collective-permute-start(bf16[2,528,128]{2,1,0:T(8,128)(2,1)S(1)} %bitcast_dynamic-update-slice_fusion.refs_0_.rows_ref), channel_id=1, source_target_pairs={{0,56},{8,0},{16,8},{24,16},{32,24},{40,32},{48,40},{56,48},{1,57}... | collective-permute-start | bytes 811016 | tf_op jit(solution)/shard_map/ppermute | solution.py:239
  15.5 15.2 %collective-permute-start.1 = (bf16[2,528,128]{2,1,0:T(8,128)(2,1)S(1)}, bf16[2,528,128]{2,1,0:T(8,128)(2,1)S(1)}, u32[]{:S(2)}, u32[]{:S(2)}) collective-permute-start(bf16[2,528,128]{2,1,0:T(8,128)(2,1)S(1)} %bitcast_dynamic-update-slice_fusion.refs_0_.rows_ref), channel_id=1, source_target_pairs={{0,48},{8,24},{16,0},{24,40},{32,16},{40,56},{48,32},{56,8},{1,49}... | collective-permute-start | bytes 811016 | tf_op jit(solution)/shard_map/ppermute | solution.py:239
  17.5 14.0 %collective-permute-start.7 = (bf16[2,528,128]{2,1,0:T(8,128)(2,1)S(1)}, bf16[2,528,128]{2,1,0:T(8,128)(2,1)S(1)}, u32[]{:S(2)}, u32[]{:S(2)}) collective-permute-start(bf16[2,528,128]{2,1,0:T(8,128)(2,1)S(1)} %pad_maximum_fusion.refs_2_), channel_id=1, source_target_pairs={{0,128},{64,192},{128,0},{192,64},{1,129},{65,193},{129,1},{193,65... | collective-permute-start | bytes 811016 | tf_op jit(solution)/shard_map/ppermute | solution.py:240
  18.8 16.0 %collective-permute-start.6 = (bf16[2,528,128]{2,1,0:T(8,128)(2,1)S(1)}, bf16[2,528,128]{2,1,0:T(8,128)(2,1)S(1)}, u32[]{:S(2)}, u32[]{:S(2)}) collective-permute-start(bf16[2,528,128]{2,1,0:T(8,128)(2,1)S(1)} %pad_maximum_fusion.refs_2_), channel_id=1, source_target_pairs={{0,64},{64,128},{128,192},{192,0},{1,65},{65,129},{129,193},{193,1... | collective-permute-start | bytes 811016 | tf_op jit(solution)/shard_map/ppermute | solution.py:240
  23.3 13.8 %collective-permute-start.5 = (bf16[2,528,128]{2,1,0:T(8,128)(2,1)S(1)}, bf16[2,528,128]{2,1,0:T(8,128)(2,1)S(1)}, u32[]{:S(2)}, u32[]{:S(2)}) collective-permute-start(bf16[2,528,128]{2,1,0:T(8,128)(2,1)S(1)} %pad_maximum_fusion.refs_2_), channel_id=1, source_target_pairs={{0,192},{64,0},{128,64},{192,128},{1,193},{65,1},{129,65},{193,129... | collective-permute-start | bytes 811016 | tf_op jit(solution)/shard_map/ppermute | solution.py:240
  33.5 13.0 %collective-permute-start.8 = (bf16[2,512,128]{2,1,0:T(8,128)(2,1)S(1)}, bf16[2,512,128]{2,1,0:T(8,128)(2,1)S(1)}, u32[]{:S(2)}, u32[]{:S(2)}) collective-permute-start(bf16[2,512,128]{2,1,0:T(8,128)(2,1)S(1)} %get-tuple-element.45), channel_id=1, source_target_pairs={{0,128},{64,192},{128,0},{192,64},{1,129},{65,193},{129,1},{193,65... | collective-permute-start | bytes 786440 | tf_op jit(solution)/shard_map/ppermute | solution.py:263
  36.8 10.9 %collective-permute-start.9 = (bf16[2,512,128]{2,1,0:T(8,128)(2,1)S(1)}, bf16[2,512,128]{2,1,0:T(8,128)(2,1)S(1)}, u32[]{:S(2)}, u32[]{:S(2)}) collective-permute-start(bf16[2,512,128]{2,1,0:T(8,128)(2,1)S(1)} %get-tuple-element.49), channel_id=1, source_target_pairs={{0,192},{64,0},{128,64},{192,128},{1,193},{65,1},{129,65},{193,129... | collective-permute-start | bytes 786440 | tf_op jit(solution)/shard_map/ppermute | solution.py:263
  39.3 9.9 %collective-permute-start.14 = (bf16[2,512,128]{2,1,0:T(8,128)(2,1)S(1)}, bf16[2,512,128]{2,1,0:T(8,128)(2,1)S(1)}, u32[]{:S(2)}, u32[]{:S(2)}) collective-permute-start(bf16[2,512,128]{2,1,0:T(8,128)(2,1)S(1)} %get-tuple-element.60), channel_id=1, source_target_pairs={{0,64},{64,128},{128,192},{192,0},{1,65},{65,129},{129,193},{193,1... | collective-permute-start | bytes 786440 | tf_op jit(solution)/shard_map/ppermute | solution.py:263
  42.6 11.7 %collective-permute-start.11 = (bf16[2,256,128]{2,1,0:T(8,128)(2,1)S(1)}, bf16[2,256,128]{2,1,0:T(8,128)(2,1)S(1)}, u32[]{:S(2)}, u32[]{:S(2)}) collective-permute-start(bf16[2,256,128]{2,1,0:T(8,128)(2,1)S(1)} %get-tuple-element.51), channel_id=1, source_target_pairs={{0,56},{8,0},{16,8},{24,16},{32,24},{40,32},{48,40},{56,48},{1,57}... | collective-permute-start | bytes 393224 | tf_op jit(solution)/shard_map/ppermute | solution.py:279
  43.3 10.9 %collective-permute-start.12 = (bf16[2,256,128]{2,1,0:T(8,128)(2,1)S(1)}, bf16[2,256,128]{2,1,0:T(8,128)(2,1)S(1)}, u32[]{:S(2)}, u32[]{:S(2)}) collective-permute-start(bf16[2,256,128]{2,1,0:T(8,128)(2,1)S(1)} %get-tuple-element.52), channel_id=1, source_target_pairs={{0,8},{8,16},{16,24},{24,32},{32,40},{40,48},{48,56},{56,0},{1,9},... | collective-permute-start | bytes 393224 | tf_op jit(solution)/shard_map/ppermute | solution.py:279
  47.8 8.3 %collective-permute-start.10 = (bf16[2,256,128]{2,1,0:T(8,128)(2,1)S(1)}, bf16[2,256,128]{2,1,0:T(8,128)(2,1)S(1)}, u32[]{:S(2)}, u32[]{:S(2)}) collective-permute-start(bf16[2,256,128]{2,1,0:T(8,128)(2,1)S(1)} %get-tuple-element.50), channel_id=1, source_target_pairs={{48,0},{24,8},{0,16},{40,24},{16,32},{56,40},{32,48},{8,56},{49,1}... | collective-permute-start | bytes 393224 | tf_op jit(solution)/shard_map/ppermute | solution.py:279
  49.3 13.7 %collective-permute-start.15 = (bf16[512,128]{1,0:T(8,128)(2,1)S(1)}, bf16[512,128]{1,0:T(8,128)(2,1)S(1)}, u32[]{:S(2)}, u32[]{:S(2)}) collective-permute-start(bf16[512,128]{1,0:T(8,128)(2,1)S(1)} %get-tuple-element.62), channel_id=1, source_target_pairs={{0,32},{8,40},{16,48},{24,56},{32,0},{40,8},{48,16},{56,24},{1,33}... | collective-permute-start | bytes 393224 | tf_op jit(solution)/shard_map/ppermute | solution.py:287
  56.1 6.9 %collective-permute-start.13 = (bf16[256,128]{1,0:T(8,128)(2,1)S(1)}, bf16[256,128]{1,0:T(8,128)(2,1)S(1)}, u32[]{:S(2)}, u32[]{:S(2)}) collective-permute-start(bf16[256,128]{1,0:T(8,128)(2,1)S(1)} %get-tuple-element.54), channel_id=1, source_target_pairs={{0,4},{4,0},{1,5},{5,1},{2,6},{6,2},{3,7},{7,3},{8,12},{12,8},{9,1... | collective-permute-start | bytes 196616 | tf_op jit(solution)/shard_map/ppermute | solution.py:289

commit v11 on v9

--- a/solution.py
+++ b/solution.py
@@ -234,9 +234,9 @@
 
     other_k = lax.ppermute(mine_k, "kz", z_step(4))
     q0 = beside(mine_q, lax.ppermute(mine_q, "kx", X_SWAP))
-    _, other_k = lax.optimization_barrier((q0, other_k))
+    late_q, other_k = lax.optimization_barrier((q0, other_k))
     k0 = jnp.stack([mine_k, other_k])
-    q_sets = [q0] + [lax.ppermute(q0, "kz", p) for p in (z_step(1), z_step(-1), Z_PAIRS)]
+    q_sets = [q0] + [lax.ppermute(q, "kz", p) for q, p in ((q0, z_step(1)), (q0, z_step(-1)), (late_q, Z_PAIRS))]
     k_sets = [k0] + [lax.ppermute(k0, "pb", y_step(-s)) for s in Y_FROM[1:]]
     q_pairs = ([q_sets[0], q_sets[3]], [q_sets[1], q_sets[2]])
 
@@ -263,25 +263,28 @@
         return lax.ppermute(part, "pb", y_step(Y_FROM[turn]))
 
     both = (0, 1)
-    (dq1,), (own_a,) = grad(0, (0,), (1,), (None,), (False,), F32)
-    q_pairs[0][1], dq1 = lax.optimization_barrier((q_pairs[0][1], dq1))
-    (dq1,), (own_b,) = grad(0, (1,), (1,), (dq1,), (False,), F32)
-    (dq0, dq1), (part,) = grad(1, both, both, (None, dq1), (False, False), BF16)
-    back1 = send_back(1, part)
-    (dq0, dq1), (part,) = grad(2, both, both, (dq0, dq1), (False, False), BF16)
-    back2 = send_back(2, part)
-    (dq0, *dqs), (part,) = grad(3, both, both, (dq0, dq1), (False, True), BF16)
-    back3 = send_back(3, part)
-    (dq_keep, dq_z2), (own0,) = grad(0, both, (0,), (dq0,), (True,), F32)
-    dq_z2, back1, back2 = lax.optimization_barrier((dq_z2, back1, back2))
-    dqs.insert(0, dq_z2)
-    dq_back = [lax.ppermute(d, "kz", p) for d, p in zip(dqs, (Z_BACK, z_step(-1), z_step(1)))]
+    parts = []
+    dq1 = None
+    for turn in range(4):
+        dq1, (part,) = grad(turn, both, (1,), (dq1,), (turn == 3,), F32)
+        dq1 = dq1[0] if turn < 3 else dq1
+        parts.append(part)
+    dq_back = [lax.ppermute(d, "kz", p) for d, p in zip(dq1, (z_step(-1), z_step(1)))]
+    q_pairs[0][1], parts[3] = lax.optimization_barrier((q_pairs[0][1], parts[3]))
+    back = []
+    dq0 = None
+    for turn in (1, 2, 3):
+        (dq0,), (part,) = grad(turn, both, (0,), (dq0,), (False,), BF16, add=parts[turn])
+        back.append(send_back(turn, part))
+    dq0, back[0] = lax.optimization_barrier((dq0, back[0]))
+    (dq_keep, dq_z2), (own,) = grad(0, both, (0,), (dq0,), (True,), F32, add=parts[0])
+    dq_back.append(lax.ppermute(dq_z2, "kz", Z_BACK))
 
     def meet(operands, parts, shape):
         return call(functools.partial(meet_kernel, parts), [(shape, F32), (shape, BF16)], operands)
 
     dkv_keep, dkv_send = meet(
-        [own0, own_a, own_b, back1, back2, back3], [both, (0, None), (None, 0)] + [both] * 3, (4 * BLK, DIM)
+        [own] + back, [both] * 4, (4 * BLK, DIM)
     )
     dkv_last = lax.ppermute(dkv_send, "kz", z_step(4))
     dq_keep, dq_send = meet([dq_keep] + dq_back, [both] * 4, (2 * BLK, DIM))

time: 64.4 us -> 64 us (level)
  the two profiles are of different devices: /device:TPU:8 before, /device:TPU:4 now
where the time goes in v11:
time: 64 us; the launch traced here: 63.8 us
  starting transfers between devices  40.2 us (63%)
  Pallas kernels  11.8 us (18%)
  waiting for transfers between devices  10.1 us (16%)
  local copies, waits for them, and re-layouts  0.96 us (2%)
  between operations  0.77 us (1%)
    pallas_call x12, Pallas kernels, call(): pl.pallas_call(kernel, out_shape=[jax.ShapeDtypeStruct(s, t) for s, t in...  11.8 us
    ppermute x3, starting transfers between devices, body(): lax.ppermute(q, 'kz', p)  9 us
    ppermute x1, starting transfers between devices, body(): other_k = lax.ppermute(mine_k, 'kz', z_step(4))  7.19 us
    ppermute x3, starting transfers between devices, body(): k_sets = [k0] + [lax.ppermute(k0, 'pb', y_step(-s)) for s in Y_FROM[1:]]  6.52 us
    ppermute x2, starting transfers between devices, body(): lax.ppermute(d, 'kz', p)  5.32 us
    ppermute x1, waiting for transfers between devices, body(): dq_back.append(lax.ppermute(dq_z2, 'kz', Z_BACK))  4.76 us
    ppermute x1, starting transfers between devices, body(): dkv_last = lax.ppermute(dkv_send, 'kz', z_step(4))  4.36 us
    ppermute x3, starting transfers between devices, send_back(): return lax.ppermute(part, 'pb', y_step(Y_FROM[turn]))  4.26 us
  transfers between devices with their start and end apart: 16, of which 3 were waited for; matrix products, arithmetic and copies ran while one was open for 2% of the time, Pallas kernels for 13%

profile of v11, /device:TPU:4, one launch (start us, length us, event | category | flops | bytes accessed | tf_op | source)
XLA Modules:
  0.0 63.8 jit_solution(3732105959946680753)
XLA Ops:
  0.6 1.8 %shard_map.94 = (bf16[528,128]{1,0:T(8,128)(2,1)}, bf16[528,128]{1,0:T(8,128)(2,1)}) custom-call(s32[128]{0:T(128)} %refs_0_.1, bf16[256,128]{1,0:T(8,128)(2,1)} %refs_1_.1, bf16[256,128]{1,0:T(8,128)(2,1)} %refs_2_.1, bf16[1,256]{1,0:T(2,128)(2,1)} %bitcast.9, bf16[256,128]{1,0:T(8,128)(2,1)} %refs_4_.1, bf16[256,128]{1,0:T(8,128)(2,1)} %refs_5_.1, ...), custom_call_target="tpu_custom_call" | custom-call | tf_op jit(solution)/shard_map/pallas_call | solution.py:212
  2.5 1.3 %collective-permute-start = (bf16[528,128]{1,0:T(8,128)(2,1)}, bf16[528,128]{1,0:T(8,128)(2,1)S(1)}, u32[]{:S(2)}, u32[]{:S(2)}) collective-permute-start(bf16[528,128]{1,0:T(8,128)(2,1)} %get-tuple-element.33), channel_id=1, source_target_pairs={{0,4},{4,0},{1,5},{5,1},{2,6},{6,2},{3,7},{7,3},{8,12},{12,8},{9,1... | collective-permute-start | bytes 405512 | tf_op jit(solution)/shard_map/ppermute | solution.py:236
  3.7 7.2 %collective-permute-start.1 = (bf16[528,128]{1,0:T(8,128)(2,1)}, bf16[528,128]{1,0:T(8,128)(2,1)S(1)}, u32[]{:S(2)}, u32[]{:S(2)}) collective-permute-start(bf16[528,128]{1,0:T(8,128)(2,1)} %get-tuple-element.34), channel_id=1, source_target_pairs={{0,32},{8,40},{16,48},{24,56},{32,0},{40,8},{48,16},{56,24},{1,33}... | collective-permute-start | bytes 405512 | tf_op jit(solution)/shard_map/ppermute | solution.py:235
  11.9 1.1 %collective-permute-start.3 = (bf16[2,528,128]{2,1,0:T(8,128)(2,1)S(1)}, bf16[2,528,128]{2,1,0:T(8,128)(2,1)S(1)}, u32[]{:S(2)}, u32[]{:S(2)}) collective-permute-start(bf16[2,528,128]{2,1,0:T(8,128)(2,1)S(1)} %bitcast_dynamic-update-slice_fusion.refs_0_.rows_ref), channel_id=1, source_target_pairs={{0,8},{8,16},{16,24},{24,32},{32,40},{40,48},{48,56},{56,0},{1,9},... | collective-permute-start | bytes 811016 | tf_op jit(solution)/shard_map/ppermute | solution.py:239
  13.0 2.2 %collective-permute-start.4 = (bf16[2,528,128]{2,1,0:T(8,128)(2,1)S(1)}, bf16[2,528,128]{2,1,0:T(8,128)(2,1)S(1)}, u32[]{:S(2)}, u32[]{:S(2)}) collective-permute-start(bf16[2,528,128]{2,1,0:T(8,128)(2,1)S(1)} %bitcast_dynamic-update-slice_fusion.refs_0_.rows_ref), channel_id=1, source_target_pairs={{0,56},{8,0},{16,8},{24,16},{32,24},{40,32},{48,40},{56,48},{1,57}... | collective-permute-start | bytes 811016 | tf_op jit(solution)/shard_map/ppermute | solution.py:239
  15.2 1.9 %collective-permute-done.1 = bf16[528,128]{1,0:T(8,128)(2,1)S(1)} collective-permute-done((bf16[528,128]{1,0:T(8,128)(2,1)}, bf16[528,128]{1,0:T(8,128)(2,1)S(1)}, u32[]{:S(2)}, u32[]{:S(2)}) %collective-permute-start.1) | collective-permute-done | bytes 135200 | tf_op jit(solution)/shard_map/ppermute | solution.py:235
  17.2 3.3 %collective-permute-start.7 = (bf16[2,528,128]{2,1,0:T(8,128)(2,1)S(1)}, bf16[2,528,128]{2,1,0:T(8,128)(2,1)S(1)}, u32[]{:S(2)}, u32[]{:S(2)}) collective-permute-start(bf16[2,528,128]{2,1,0:T(8,128)(2,1)S(1)} %pad_maximum_fusion.refs_2_), channel_id=1, source_target_pairs={{0,128},{64,192},{128,0},{192,64},{1,129},{65,193},{129,1},{193,65... | collective-permute-start | bytes 811016 | tf_op jit(solution)/shard_map/ppermute | solution.py:240
  21.1 2.6 %collective-permute-start.5 = (bf16[2,528,128]{2,1,0:T(8,128)(2,1)S(1)}, bf16[2,528,128]{2,1,0:T(8,128)(2,1)S(1)}, u32[]{:S(2)}, u32[]{:S(2)}) collective-permute-start(bf16[2,528,128]{2,1,0:T(8,128)(2,1)S(1)} %pad_maximum_fusion.refs_2_), channel_id=1, source_target_pairs={{0,192},{64,0},{128,64},{192,128},{1,193},{65,1},{129,65},{193,129... | collective-permute-start | bytes 811016 | tf_op jit(solution)/shard_map/ppermute | solution.py:240
  23.7 5.7 %collective-permute-start.2 = (bf16[2,528,128]{2,1,0:T(8,128)(2,1)S(1)}, bf16[2,528,128]{2,1,0:T(8,128)(2,1)S(1)}, u32[]{:S(2)}, u32[]{:S(2)}) collective-permute-start(bf16[2,528,128]{2,1,0:T(8,128)(2,1)S(1)} %bitcast_dynamic-update-slice_fusion.refs_0_.rows_ref), channel_id=1, source_target_pairs={{0,48},{8,24},{16,0},{24,40},{32,16},{40,56},{48,32},{56,8},{1,49}... | collective-permute-start | bytes 811016 | tf_op jit(solution)/shard_map/ppermute | solution.py:239
  29.4 1.1 %shard_map.95 = (f32[2,128,512]{2,1,0:T(8,128)S(1)}, f32[2,512,128]{2,1,0:T(8,128)S(1)}) custom-call(bf16[2,528,128]{2,1,0:T(8,128)(2,1)S(1)} %collective-permute-done.3.refs_0_, bf16[2,528,128]{2,1,0:T(8,128)(2,1)S(1)} %collective-permute-done.4.refs_1_, bf16[2,528,128]{2,1,0:T(8,128)(2,1)S(1)} %pad_maximum_fusion.refs_2_), custom_call_target="tpu_custom_call" | custom-call | flops 500000000 | bytes 1000000 | tf_op jit(solution)/shard_map/pallas_call | solution.py:212
  30.5 1.1 %shard_map.96 = (f32[2,128,512]{2,1,0:T(8,128)S(1)}, f32[2,512,128]{2,1,0:T(8,128)S(1)}) custom-call(bf16[2,528,128]{2,1,0:T(8,128)(2,1)S(1)} %collective-permute-done.3.refs_0_, bf16[2,528,128]{2,1,0:T(8,128)(2,1)S(1)} %collective-permute-done.4.refs_1_, bf16[2,528,128]{2,1,0:T(8,128)(2,1)S(1)} %collective-permute-done.7.refs_2_, ...), custom_call_target="tpu_custom_call" | custom-call | flops 500000000 | bytes 1000000 | tf_op jit(solution)/shard_map/pallas_call | solution.py:212
  31.6 1.1 %shard_map.97 = (f32[2,128,512]{2,1,0:T(8,128)S(1)}, f32[2,512,128]{2,1,0:T(8,128)S(1)}) custom-call(bf16[2,528,128]{2,1,0:T(8,128)(2,1)S(1)} %collective-permute-done.3.refs_0_, bf16[2,528,128]{2,1,0:T(8,128)(2,1)S(1)} %collective-permute-done.4.refs_1_, bf16[2,528,128]{2,1,0:T(8,128)(2,1)S(1)} %collective-permute-done.6.refs_2_, ...), custom_call_target="tpu_custom_call" | custom-call | flops 500000000 | bytes 1000000 | tf_op jit(solution)/shard_map/pallas_call | solution.py:212
  32.7 1.2 %shard_map.98 = (bf16[2,256,128]{2,1,0:T(8,128)(2,1)S(1)}, bf16[2,256,128]{2,1,0:T(8,128)(2,1)S(1)}, f32[2,512,128]{2,1,0:T(8,128)S(1)}) custom-call(bf16[2,528,128]{2,1,0:T(8,128)(2,1)S(1)} %collective-permute-done.3.refs_0_, bf16[2,528,128]{2,1,0:T(8,128)(2,1)S(1)} %collective-permute-done.4.refs_1_, ...), custom_call_target="tpu_custom_call" | custom-call | flops 500000000 | bytes 1000000 | tf_op jit(solution)/shard_map/pallas_call | solution.py:212
  33.9 1.1 %shard_map.99 = (f32[2,128,512]{2,1,0:T(8,128)S(1)}, bf16[2,512,128]{2,1,0:T(8,128)(2,1)S(1)}) custom-call(bf16[2,528,128]{2,1,0:T(8,128)(2,1)S(1)} %bitcast_dynamic-update-slice_fusion.refs_0_.rows_ref, bf16[2,528,128]{2,1,0:T(8,128)(2,1)S(1)} %collective-permute-done.2.refs_1_, bf16[2,528,128]{2,1,0:T(8,128)(2,1)S(1)} %collective-permute-done.7.refs_2_, ...), custom_call_target="tpu_custom_call" | custom-call | flops 500000000 | bytes 1000000 | tf_op jit(solution)/shard_map/pallas_call | solution.py:212
  36.0 1.1 %shard_map.100 = (f32[2,128,512]{2,1,0:T(8,128)S(1)}, bf16[2,512,128]{2,1,0:T(8,128)(2,1)S(1)}) custom-call(bf16[2,528,128]{2,1,0:T(8,128)(2,1)S(1)} %bitcast_dynamic-update-slice_fusion.refs_0_.rows_ref, bf16[2,528,128]{2,1,0:T(8,128)(2,1)S(1)} %collective-permute-done.2.refs_1_, bf16[2,528,128]{2,1,0:T(8,128)(2,1)S(1)} %collective-permute-done.6.refs_2_, ...), custom_call_target="tpu_custom_call" | custom-call | flops 500000000 | bytes 1000000 | tf_op jit(solution)/shard_map/pallas_call | solution.py:212
  37.1 1.1 %shard_map.101 = (f32[2,128,512]{2,1,0:T(8,128)S(1)}, bf16[2,512,128]{2,1,0:T(8,128)(2,1)S(1)}) custom-call(bf16[2,528,128]{2,1,0:T(8,128)(2,1)S(1)} %bitcast_dynamic-update-slice_fusion.refs_0_.rows_ref, bf16[2,528,128]{2,1,0:T(8,128)(2,1)S(1)} %collective-permute-done.2.refs_1_, bf16[2,528,128]{2,1,0:T(8,128)(2,1)S(1)} %collective-permute-done.5.refs_2_, ...), custom_call_target="tpu_custom_call" | custom-call | flops 500000000 | bytes 1000000 | tf_op jit(solution)/shard_map/pallas_call | solution.py:212
  39.0 2.6 %collective-permute-start.13 = (bf16[2,512,128]{2,1,0:T(8,128)(2,1)S(1)}, bf16[2,512,128]{2,1,0:T(8,128)(2,1)S(1)}, u32[]{:S(2)}, u32[]{:S(2)}) collective-permute-start(bf16[2,512,128]{2,1,0:T(8,128)(2,1)S(1)} %get-tuple-element.59), channel_id=1, source_target_pairs={{0,192},{64,0},{128,64},{192,128},{1,193},{65,1},{129,65},{193,129... | collective-permute-start | bytes 786440 | tf_op jit(solution)/shard_map/ppermute | solution.py:263
  41.6 2.0 %collective-permute-start.10 = (bf16[2,256,128]{2,1,0:T(8,128)(2,1)S(1)}, bf16[2,256,128]{2,1,0:T(8,128)(2,1)S(1)}, u32[]{:S(2)}, u32[]{:S(2)}) collective-permute-start(bf16[2,256,128]{2,1,0:T(8,128)(2,1)S(1)} %get-tuple-element.53), channel_id=1, source_target_pairs={{0,8},{8,16},{16,24},{24,32},{32,40},{40,48},{48,56},{56,0},{1,9},... | collective-permute-start | bytes 393224 | tf_op jit(solution)/shard_map/ppermute | solution.py:272
  43.6 3.3 %collective-permute-start.9 = (bf16[2,256,128]{2,1,0:T(8,128)(2,1)S(1)}, bf16[2,256,128]{2,1,0:T(8,128)(2,1)S(1)}, u32[]{:S(2)}, u32[]{:S(2)}) collective-permute-start(bf16[2,256,128]{2,1,0:T(8,128)(2,1)S(1)} %get-tuple-element.52), channel_id=1, source_target_pairs={{0,56},{8,0},{16,8},{24,16},{32,24},{40,32},{48,40},{56,48},{1,57}... | collective-permute-start | bytes 393224 | tf_op jit(solution)/shard_map/ppermute | solution.py:272
  46.9 1.3 %shard_map.102 = (f32[2,256,128]{2,1,0:T(8,128)S(1)}, bf16[2,256,128]{2,1,0:T(8,128)(2,1)S(1)}, f32[2,512,128]{2,1,0:T(8,128)S(1)}) custom-call(bf16[2,528,128]{2,1,0:T(8,128)(2,1)S(1)} %bitcast_dynamic-update-slice_fusion.refs_0_.rows_ref, bf16[2,528,128]{2,1,0:T(8,128)(2,1)S(1)} %collective-permute-done.2.refs_1_, ...), custom_call_target="tpu_custom_call" | custom-call | flops 500000000 | bytes 1000000 | tf_op jit(solution)/shard_map/pallas_call | solution.py:212
  48.1 1.3 %collective-permute-start.11 = (bf16[2,256,128]{2,1,0:T(8,128)(2,1)S(1)}, bf16[2,256,128]{2,1,0:T(8,128)(2,1)S(1)}, u32[]{:S(2)}, u32[]{:S(2)}) collective-permute-start(bf16[2,256,128]{2,1,0:T(8,128)(2,1)S(1)} %get-tuple-element.54), channel_id=1, source_target_pairs={{48,0},{24,8},{0,16},{40,24},{16,32},{56,40},{32,48},{8,56},{49,1}... | collective-permute-start | bytes 393224 | tf_op jit(solution)/shard_map/ppermute | solution.py:281
  49.6 4.4 %collective-permute-start.15 = (bf16[512,128]{1,0:T(8,128)(2,1)S(1)}, bf16[512,128]{1,0:T(8,128)(2,1)S(1)}, u32[]{:S(2)}, u32[]{:S(2)}) collective-permute-start(bf16[512,128]{1,0:T(8,128)(2,1)S(1)} %get-tuple-element.62), channel_id=1, source_target_pairs={{0,32},{8,40},{16,48},{24,56},{32,0},{40,8},{48,16},{56,24},{1,33}... | collective-permute-start | bytes 393224 | tf_op jit(solution)/shard_map/ppermute | solution.py:289
  54.0 4.8 %collective-permute-done.11.refs_3_ = bf16[2,256,128]{2,1,0:T(8,128)(2,1)S(1)} collective-permute-done((bf16[2,256,128]{2,1,0:T(8,128)(2,1)S(1)}, bf16[2,256,128]{2,1,0:T(8,128)(2,1)S(1)}, u32[]{:S(2)}, u32[]{:S(2)}) %collective-permute-start.11) | collective-permute-done | bytes 131104 | tf_op jit(solution)/shard_map/ppermute | solution.py:281
  59.7 3.4 %collective-permute-done.12.dqx_ref = bf16[256,128]{1,0:T(8,128)(2,1)S(1)} collective-permute-done((bf16[256,128]{1,0:T(8,128)(2,1)S(1)}, bf16[256,128]{1,0:T(8,128)(2,1)S(1)}, u32[]{:S(2)}, u32[]{:S(2)}) %collective-permute-start.12) | collective-permute-done | bytes 65568 | tf_op jit(solution)/shard_map/ppermute | solution.py:291
  (25 shorter events, 5.2 us)
Async XLA Ops:
  2.5 9.4 %collective-permute-start = (bf16[528,128]{1,0:T(8,128)(2,1)}, bf16[528,128]{1,0:T(8,128)(2,1)S(1)}, u32[]{:S(2)}, u32[]{:S(2)}) collective-permute-start(bf16[528,128]{1,0:T(8,128)(2,1)} %get-tuple-element.33), channel_id=1, source_target_pairs={{0,4},{4,0},{1,5},{5,1},{2,6},{6,2},{3,7},{7,3},{8,12},{12,8},{9,1... | collective-permute-start | bytes 405512 | tf_op jit(solution)/shard_map/ppermute | solution.py:236
  3.7 13.4 %collective-permute-start.1 = (bf16[528,128]{1,0:T(8,128)(2,1)}, bf16[528,128]{1,0:T(8,128)(2,1)S(1)}, u32[]{:S(2)}, u32[]{:S(2)}) collective-permute-start(bf16[528,128]{1,0:T(8,128)(2,1)} %get-tuple-element.34), channel_id=1, source_target_pairs={{0,32},{8,40},{16,48},{24,56},{32,0},{40,8},{48,16},{56,24},{1,33}... | collective-permute-start | bytes 405512 | tf_op jit(solution)/shard_map/ppermute | solution.py:235
  11.9 5.3 %copy-start = (bf16[528,128]{1,0:T(8,128)(2,1)S(1)}, bf16[528,128]{1,0:T(8,128)(2,1)}, u32[]{:S(2)}) copy-start(bf16[528,128]{1,0:T(8,128)(2,1)} %get-tuple-element.34) | copy-start | bytes 405508
  11.9 11.8 %collective-permute-start.3 = (bf16[2,528,128]{2,1,0:T(8,128)(2,1)S(1)}, bf16[2,528,128]{2,1,0:T(8,128)(2,1)S(1)}, u32[]{:S(2)}, u32[]{:S(2)}) collective-permute-start(bf16[2,528,128]{2,1,0:T(8,128)(2,1)S(1)} %bitcast_dynamic-update-slice_fusion.refs_0_.rows_ref), channel_id=1, source_target_pairs={{0,8},{8,16},{16,24},{24,32},{32,40},{40,48},{48,56},{56,0},{1,9},... | collective-permute-start | bytes 811016 | tf_op jit(solution)/shard_map/ppermute | solution.py:239
  13.0 16.4 %collective-permute-start.4 = (bf16[2,528,128]{2,1,0:T(8,128)(2,1)S(1)}, bf16[2,528,128]{2,1,0:T(8,128)(2,1)S(1)}, u32[]{:S(2)}, u32[]{:S(2)}) collective-permute-start(bf16[2,528,128]{2,1,0:T(8,128)(2,1)S(1)} %bitcast_dynamic-update-slice_fusion.refs_0_.rows_ref), channel_id=1, source_target_pairs={{0,56},{8,0},{16,8},{24,16},{32,24},{40,32},{48,40},{56,48},{1,57}... | collective-permute-start | bytes 811016 | tf_op jit(solution)/shard_map/ppermute | solution.py:239
  17.2 13.3 %collective-permute-start.7 = (bf16[2,528,128]{2,1,0:T(8,128)(2,1)S(1)}, bf16[2,528,128]{2,1,0:T(8,128)(2,1)S(1)}, u32[]{:S(2)}, u32[]{:S(2)}) collective-permute-start(bf16[2,528,128]{2,1,0:T(8,128)(2,1)S(1)} %pad_maximum_fusion.refs_2_), channel_id=1, source_target_pairs={{0,128},{64,192},{128,0},{192,64},{1,129},{65,193},{129,1},{193,65... | collective-permute-start | bytes 811016 | tf_op jit(solution)/shard_map/ppermute | solution.py:240
  20.5 11.1 %collective-permute-start.6 = (bf16[2,528,128]{2,1,0:T(8,128)(2,1)S(1)}, bf16[2,528,128]{2,1,0:T(8,128)(2,1)S(1)}, u32[]{:S(2)}, u32[]{:S(2)}) collective-permute-start(bf16[2,528,128]{2,1,0:T(8,128)(2,1)S(1)} %pad_maximum_fusion.refs_2_), channel_id=1, source_target_pairs={{0,64},{64,128},{128,192},{192,0},{1,65},{65,129},{129,193},{193,1... | collective-permute-start | bytes 811016 | tf_op jit(solution)/shard_map/ppermute | solution.py:240
  21.1 11.6 %collective-permute-start.5 = (bf16[2,528,128]{2,1,0:T(8,128)(2,1)S(1)}, bf16[2,528,128]{2,1,0:T(8,128)(2,1)S(1)}, u32[]{:S(2)}, u32[]{:S(2)}) collective-permute-start(bf16[2,528,128]{2,1,0:T(8,128)(2,1)S(1)} %pad_maximum_fusion.refs_2_), channel_id=1, source_target_pairs={{0,192},{64,0},{128,64},{192,128},{1,193},{65,1},{129,65},{193,129... | collective-permute-start | bytes 811016 | tf_op jit(solution)/shard_map/ppermute | solution.py:240
  23.7 10.2 %collective-permute-start.2 = (bf16[2,528,128]{2,1,0:T(8,128)(2,1)S(1)}, bf16[2,528,128]{2,1,0:T(8,128)(2,1)S(1)}, u32[]{:S(2)}, u32[]{:S(2)}) collective-permute-start(bf16[2,528,128]{2,1,0:T(8,128)(2,1)S(1)} %bitcast_dynamic-update-slice_fusion.refs_0_.rows_ref), channel_id=1, source_target_pairs={{0,48},{8,24},{16,0},{24,40},{32,16},{40,56},{48,32},{56,8},{1,49}... | collective-permute-start | bytes 811016 | tf_op jit(solution)/shard_map/ppermute | solution.py:239
  35.0 11.8 %collective-permute-start.8 = (bf16[2,512,128]{2,1,0:T(8,128)(2,1)S(1)}, bf16[2,512,128]{2,1,0:T(8,128)(2,1)S(1)}, u32[]{:S(2)}, u32[]{:S(2)}) collective-permute-start(bf16[2,512,128]{2,1,0:T(8,128)(2,1)S(1)} %get-tuple-element.48), channel_id=1, source_target_pairs={{0,128},{64,192},{128,0},{192,64},{1,129},{65,193},{129,1},{193,65... | collective-permute-start | bytes 786440 | tf_op jit(solution)/shard_map/ppermute | solution.py:263
  38.2 11.2 %collective-permute-start.14 = (bf16[2,512,128]{2,1,0:T(8,128)(2,1)S(1)}, bf16[2,512,128]{2,1,0:T(8,128)(2,1)S(1)}, u32[]{:S(2)}, u32[]{:S(2)}) collective-permute-start(bf16[2,512,128]{2,1,0:T(8,128)(2,1)S(1)} %get-tuple-element.60), channel_id=1, source_target_pairs={{0,64},{64,128},{128,192},{192,0},{1,65},{65,129},{129,193},{193,1... | collective-permute-start | bytes 786440 | tf_op jit(solution)/shard_map/ppermute | solution.py:263
  39.0 10.5 %collective-permute-start.13 = (bf16[2,512,128]{2,1,0:T(8,128)(2,1)S(1)}, bf16[2,512,128]{2,1,0:T(8,128)(2,1)S(1)}, u32[]{:S(2)}, u32[]{:S(2)}) collective-permute-start(bf16[2,512,128]{2,1,0:T(8,128)(2,1)S(1)} %get-tuple-element.59), channel_id=1, source_target_pairs={{0,192},{64,0},{128,64},{192,128},{1,193},{65,1},{129,65},{193,129... | collective-permute-start | bytes 786440 | tf_op jit(solution)/shard_map/ppermute | solution.py:263
  41.6 12.4 %collective-permute-start.10 = (bf16[2,256,128]{2,1,0:T(8,128)(2,1)S(1)}, bf16[2,256,128]{2,1,0:T(8,128)(2,1)S(1)}, u32[]{:S(2)}, u32[]{:S(2)}) collective-permute-start(bf16[2,256,128]{2,1,0:T(8,128)(2,1)S(1)} %get-tuple-element.53), channel_id=1, source_target_pairs={{0,8},{8,16},{16,24},{24,32},{32,40},{40,48},{48,56},{56,0},{1,9},... | collective-permute-start | bytes 393224 | tf_op jit(solution)/shard_map/ppermute | solution.py:272
  43.6 10.4 %collective-permute-start.9 = (bf16[2,256,128]{2,1,0:T(8,128)(2,1)S(1)}, bf16[2,256,128]{2,1,0:T(8,128)(2,1)S(1)}, u32[]{:S(2)}, u32[]{:S(2)}) collective-permute-start(bf16[2,256,128]{2,1,0:T(8,128)(2,1)S(1)} %get-tuple-element.52), channel_id=1, source_target_pairs={{0,56},{8,0},{16,8},{24,16},{32,24},{40,32},{48,40},{56,48},{1,57}... | collective-permute-start | bytes 393224 | tf_op jit(solution)/shard_map/ppermute | solution.py:272
  48.1 10.6 %collective-permute-start.11 = (bf16[2,256,128]{2,1,0:T(8,128)(2,1)S(1)}, bf16[2,256,128]{2,1,0:T(8,128)(2,1)S(1)}, u32[]{:S(2)}, u32[]{:S(2)}) collective-permute-start(bf16[2,256,128]{2,1,0:T(8,128)(2,1)S(1)} %get-tuple-element.54), channel_id=1, source_target_pairs={{48,0},{24,8},{0,16},{40,24},{16,32},{56,40},{32,48},{8,56},{49,1}... | collective-permute-start | bytes 393224 | tf_op jit(solution)/shard_map/ppermute | solution.py:281
  49.6 10.1 %collective-permute-start.15 = (bf16[512,128]{1,0:T(8,128)(2,1)S(1)}, bf16[512,128]{1,0:T(8,128)(2,1)S(1)}, u32[]{:S(2)}, u32[]{:S(2)}) collective-permute-start(bf16[512,128]{1,0:T(8,128)(2,1)S(1)} %get-tuple-element.62), channel_id=1, source_target_pairs={{0,32},{8,40},{16,48},{24,56},{32,0},{40,8},{48,16},{56,24},{1,33}... | collective-permute-start | bytes 393224 | tf_op jit(solution)/shard_map/ppermute | solution.py:289
  58.8 4.4 %collective-permute-start.12 = (bf16[256,128]{1,0:T(8,128)(2,1)S(1)}, bf16[256,128]{1,0:T(8,128)(2,1)S(1)}, u32[]{:S(2)}, u32[]{:S(2)}) collective-permute-start(bf16[256,128]{1,0:T(8,128)(2,1)S(1)} %get-tuple-element.56), channel_id=1, source_target_pairs={{0,4},{4,0},{1,5},{5,1},{2,6},{6,2},{3,7},{7,3},{8,12},{12,8},{9,1... | collective-permute-start | bytes 196616 | tf_op jit(solution)/shard_map/ppermute | solution.py:291

commit v12 on v9

--- a/solution.py
+++ b/solution.py
@@ -232,11 +232,11 @@
         both = lax.optimization_barrier(jnp.pad(mine[None], ((0, 1), (0, 0), (0, 0))))
         return lax.dynamic_update_slice(both, other[None], (1, 0, 0))
 
-    other_k = lax.ppermute(mine_k, "kz", z_step(4))
-    q0 = beside(mine_q, lax.ppermute(mine_q, "kx", X_SWAP))
+    other_k = lax.ppermute(mine_k, "kx", X_SWAP)
+    q0 = beside(mine_q, lax.ppermute(mine_q, "kz", z_step(4)))
     _, other_k = lax.optimization_barrier((q0, other_k))
     k0 = jnp.stack([mine_k, other_k])
-    q_sets = [q0] + [lax.ppermute(q0, "kz", p) for p in (z_step(1), z_step(-1), Z_PAIRS)]
+    q_sets = [q0] + [lax.ppermute(q, "kz", p) for q, p in ((q0, z_step(1)), (q0, z_step(-1)), (q0, Z_PAIRS))]
     k_sets = [k0] + [lax.ppermute(k0, "pb", y_step(-s)) for s in Y_FROM[1:]]
     q_pairs = ([q_sets[0], q_sets[3]], [q_sets[1], q_sets[2]])
 
@@ -263,29 +263,29 @@
         return lax.ppermute(part, "pb", y_step(Y_FROM[turn]))
 
     both = (0, 1)
-    (dq1,), (own_a,) = grad(0, (0,), (1,), (None,), (False,), F32)
-    q_pairs[0][1], dq1 = lax.optimization_barrier((q_pairs[0][1], dq1))
-    (dq1,), (own_b,) = grad(0, (1,), (1,), (dq1,), (False,), F32)
-    (dq0, dq1), (part,) = grad(1, both, both, (None, dq1), (False, False), BF16)
-    back1 = send_back(1, part)
+    (dq1,), (own1,) = grad(0, both, (1,), (None,), (False,), F32)
+    (dq1,), (part,) = grad(1, both, (1,), (dq1,), (False,), F32)
+    q_pairs[0][1], part = lax.optimization_barrier((q_pairs[0][1], part))
+    (dq0,), (own0,) = grad(0, both, (0,), (None,), (False,), F32)
+    (dq0,), (part,) = grad(1, both, (0,), (dq0,), (False,), BF16, add=part)
+    back = [send_back(1, part)]
     (dq0, dq1), (part,) = grad(2, both, both, (dq0, dq1), (False, False), BF16)
-    back2 = send_back(2, part)
-    (dq0, *dqs), (part,) = grad(3, both, both, (dq0, dq1), (False, True), BF16)
-    back3 = send_back(3, part)
-    (dq_keep, dq_z2), (own0,) = grad(0, both, (0,), (dq0,), (True,), F32)
-    dq_z2, back1, back2 = lax.optimization_barrier((dq_z2, back1, back2))
-    dqs.insert(0, dq_z2)
+    back.append(send_back(2, part))
+    (dq_keep, *dqs), (part,) = grad(3, both, both, (dq0, dq1), (True, True), BF16)
+    back.append(send_back(3, part))
+    dqs[0], back[0] = lax.optimization_barrier((dqs[0], back[0]))
+    own = (own0, own1)
     dq_back = [lax.ppermute(d, "kz", p) for d, p in zip(dqs, (Z_BACK, z_step(-1), z_step(1)))]
 
     def meet(operands, parts, shape):
         return call(functools.partial(meet_kernel, parts), [(shape, F32), (shape, BF16)], operands)
 
     dkv_keep, dkv_send = meet(
-        [own0, own_a, own_b, back1, back2, back3], [both, (0, None), (None, 0)] + [both] * 3, (4 * BLK, DIM)
+        [*own, *back], [both] * 5, (4 * BLK, DIM)
     )
-    dkv_last = lax.ppermute(dkv_send, "kz", z_step(4))
+    dkv_last = lax.ppermute(dkv_send, "kx", X_SWAP)
     dq_keep, dq_send = meet([dq_keep] + dq_back, [both] * 4, (2 * BLK, DIM))
-    dq_last = lax.ppermute(dq_send, "kx", X_SWAP)
+    dq_last = lax.ppermute(dq_send, "kz", z_step(4))
     operands = (q0, dq_keep, dq_last, dkv_keep, dkv_last)
     return tuple(call(last_kernel, [((2 * BLK, DIM), BF16)] * 3, operands))
 

time: 64.4 us -> 64.5 us (level)
  the two profiles are of different devices: /device:TPU:8 before, /device:TPU:4 now
where the time goes in v12:
time: 64.5 us; the launch traced here: 64.3 us
  starting transfers between devices  40.2 us (62%)
  Pallas kernels  11.3 us (18%)
  waiting for transfers between devices  11.1 us (17%)
  local copies, waits for them, and re-layouts  0.96 us (1%)
  between operations  0.75 us (1%)
    pallas_call x10, Pallas kernels, call(): pl.pallas_call(kernel, out_shape=[jax.ShapeDtypeStruct(s, t) for s, t in...  11.3 us
    ppermute x3, starting transfers between devices, body(): lax.ppermute(q, 'kz', p)  9.65 us
    ppermute x1, starting transfers between devices, body(): q0 = beside(mine_q, lax.ppermute(mine_q, 'kz', z_step(4)))  7.28 us
    ppermute x3, starting transfers between devices, body(): k_sets = [k0] + [lax.ppermute(k0, 'pb', y_step(-s)) for s in Y_FROM[1:]]  6.52 us
    ppermute x3, starting transfers between devices, send_back(): return lax.ppermute(part, 'pb', y_step(Y_FROM[turn]))  6.21 us
    ppermute x3, waiting for transfers between devices, body(): lax.ppermute(d, 'kz', p)  4.71 us
    ppermute x1, waiting for transfers between devices, body(): dq_last = lax.ppermute(dq_send, 'kz', z_step(4))  4.56 us
    ppermute x3, starting transfers between devices, body(): lax.ppermute(d, 'kz', p)  4.42 us
  transfers between devices with their start and end apart: 16, of which 4 were waited for; matrix products, arithmetic and copies ran while one was open for 2% of the time, Pallas kernels for 14%

profile of v12, /device:TPU:4, one launch (start us, length us, event | category | flops | bytes accessed | tf_op | source)
XLA Modules:
  0.0 64.3 jit_solution(10165095698902701289)
XLA Ops:
  0.6 1.8 %shard_map.94 = (bf16[528,128]{1,0:T(8,128)(2,1)}, bf16[528,128]{1,0:T(8,128)(2,1)}) custom-call(s32[128]{0:T(128)} %refs_0_.1, bf16[256,128]{1,0:T(8,128)(2,1)} %refs_1_.1, bf16[256,128]{1,0:T(8,128)(2,1)} %refs_2_.1, bf16[1,256]{1,0:T(2,128)(2,1)} %bitcast.9, bf16[256,128]{1,0:T(8,128)(2,1)} %refs_4_.1, bf16[256,128]{1,0:T(8,128)(2,1)} %refs_5_.1, ...), custom_call_target="tpu_custom_call" | custom-call | tf_op jit(solution)/shard_map/pallas_call | solution.py:212
  2.5 7.3 %collective-permute-start = (bf16[528,128]{1,0:T(8,128)(2,1)}, bf16[528,128]{1,0:T(8,128)(2,1)S(1)}, u32[]{:S(2)}, u32[]{:S(2)}) collective-permute-start(bf16[528,128]{1,0:T(8,128)(2,1)} %get-tuple-element.30), channel_id=1, source_target_pairs={{0,32},{8,40},{16,48},{24,56},{32,0},{40,8},{48,16},{56,24},{1,33}... | collective-permute-start | bytes 405512 | tf_op jit(solution)/shard_map/ppermute | solution.py:236
  9.7 1.2 %collective-permute-start.4 = (bf16[528,128]{1,0:T(8,128)(2,1)}, bf16[528,128]{1,0:T(8,128)(2,1)S(1)}, u32[]{:S(2)}, u32[]{:S(2)}) collective-permute-start(bf16[528,128]{1,0:T(8,128)(2,1)} %get-tuple-element.31), channel_id=1, source_target_pairs={{0,4},{4,0},{1,5},{5,1},{2,6},{6,2},{3,7},{7,3},{8,12},{12,8},{9,1... | collective-permute-start | bytes 405512 | tf_op jit(solution)/shard_map/ppermute | solution.py:235
  10.9 0.9 %pad.4 = bf16[2,528,128]{2,1,0:T(8,128)(2,1)S(1)} pad(bf16[1,528,128]{2,1,0:T(8,128)(2,1)} %bitcast.6, bf16[]{:T(256)} %constant.1.clone.1), padding=0_1x0_0x0_0 | pad | bytes 405506 | tf_op jit(solution)/shard_map/jit(_pad)/pad | solution.py:232
  11.9 1.8 %collective-permute-done = bf16[528,128]{1,0:T(8,128)(2,1)S(1)} collective-permute-done((bf16[528,128]{1,0:T(8,128)(2,1)}, bf16[528,128]{1,0:T(8,128)(2,1)S(1)}, u32[]{:S(2)}, u32[]{:S(2)}) %collective-permute-start) | collective-permute-done | bytes 135200 | tf_op jit(solution)/shard_map/ppermute | solution.py:236
  13.6 3.9 %collective-permute-start.2 = (bf16[2,528,128]{2,1,0:T(8,128)(2,1)S(1)}, bf16[2,528,128]{2,1,0:T(8,128)(2,1)S(1)}, u32[]{:S(2)}, u32[]{:S(2)}) collective-permute-start(bf16[2,528,128]{2,1,0:T(8,128)(2,1)S(1)} %bitcast_dynamic-update-slice_fusion.refs_0_.rows_ref), channel_id=1, source_target_pairs={{0,8},{8,16},{16,24},{24,32},{32,40},{40,48},{48,56},{56,0},{1,9},... | collective-permute-start | bytes 811016 | tf_op jit(solution)/shard_map/ppermute | solution.py:239
  17.6 1.5 %collective-permute-start.3 = (bf16[2,528,128]{2,1,0:T(8,128)(2,1)S(1)}, bf16[2,528,128]{2,1,0:T(8,128)(2,1)S(1)}, u32[]{:S(2)}, u32[]{:S(2)}) collective-permute-start(bf16[2,528,128]{2,1,0:T(8,128)(2,1)S(1)} %bitcast_dynamic-update-slice_fusion.refs_0_.rows_ref), channel_id=1, source_target_pairs={{0,56},{8,0},{16,8},{24,16},{32,24},{40,32},{48,40},{56,48},{1,57}... | collective-permute-start | bytes 811016 | tf_op jit(solution)/shard_map/ppermute | solution.py:239
  19.1 3.3 %collective-permute-start.5 = (bf16[2,528,128]{2,1,0:T(8,128)(2,1)S(1)}, bf16[2,528,128]{2,1,0:T(8,128)(2,1)S(1)}, u32[]{:S(2)}, u32[]{:S(2)}) collective-permute-start(bf16[2,528,128]{2,1,0:T(8,128)(2,1)S(1)} %pad_maximum_fusion.refs_2_), channel_id=1, source_target_pairs={{0,128},{64,192},{128,0},{192,64},{1,129},{65,193},{129,1},{193,65... | collective-permute-start | bytes 811016 | tf_op jit(solution)/shard_map/ppermute | solution.py:240
  22.4 4.2 %collective-permute-start.1 = (bf16[2,528,128]{2,1,0:T(8,128)(2,1)S(1)}, bf16[2,528,128]{2,1,0:T(8,128)(2,1)S(1)}, u32[]{:S(2)}, u32[]{:S(2)}) collective-permute-start(bf16[2,528,128]{2,1,0:T(8,128)(2,1)S(1)} %bitcast_dynamic-update-slice_fusion.refs_0_.rows_ref), channel_id=1, source_target_pairs={{0,48},{8,24},{16,0},{24,40},{32,16},{40,56},{48,32},{56,8},{1,49}... | collective-permute-start | bytes 811016 | tf_op jit(solution)/shard_map/ppermute | solution.py:239
  27.3 2.6 %collective-permute-start.6 = (bf16[2,528,128]{2,1,0:T(8,128)(2,1)S(1)}, bf16[2,528,128]{2,1,0:T(8,128)(2,1)S(1)}, u32[]{:S(2)}, u32[]{:S(2)}) collective-permute-start(bf16[2,528,128]{2,1,0:T(8,128)(2,1)S(1)} %pad_maximum_fusion.refs_2_), channel_id=1, source_target_pairs={{0,192},{64,0},{128,64},{192,128},{1,193},{65,1},{129,65},{193,129... | collective-permute-start | bytes 811016 | tf_op jit(solution)/shard_map/ppermute | solution.py:240
  29.9 1.1 %shard_map.95 = (f32[2,128,512]{2,1,0:T(8,128)S(1)}, f32[2,512,128]{2,1,0:T(8,128)S(1)}) custom-call(bf16[2,528,128]{2,1,0:T(8,128)(2,1)S(1)} %collective-permute-done.2.refs_0_.refs_2_, bf16[2,528,128]{2,1,0:T(8,128)(2,1)S(1)} %collective-permute-done.3.refs_1_.refs_3_, bf16[2,528,128]{2,1,0:T(8,128)(2,1)S(1)} %pad_maximum_fusion.refs_2_), custom_call_target="tpu_custom_call" | custom-call | flops 500000000 | bytes 1000000 | tf_op jit(solution)/shard_map/pallas_call | solution.py:212
  31.0 1.1 %shard_map.96 = (f32[2,128,512]{2,1,0:T(8,128)S(1)}, f32[2,512,128]{2,1,0:T(8,128)S(1)}) custom-call(bf16[2,528,128]{2,1,0:T(8,128)(2,1)S(1)} %collective-permute-done.2.refs_0_.refs_2_, bf16[2,528,128]{2,1,0:T(8,128)(2,1)S(1)} %collective-permute-done.3.refs_1_.refs_3_, bf16[2,528,128]{2,1,0:T(8,128)(2,1)S(1)} %collective-permute-done.5.refs_2_, ...), custom_call_target="tpu_custom_call" | custom-call | flops 500000000 | bytes 1000000 | tf_op jit(solution)/shard_map/pallas_call | solution.py:212
  32.1 1.1 %shard_map.97 = (f32[2,128,512]{2,1,0:T(8,128)S(1)}, f32[2,512,128]{2,1,0:T(8,128)S(1)}) custom-call(bf16[2,528,128]{2,1,0:T(8,128)(2,1)S(1)} %bitcast_dynamic-update-slice_fusion.refs_0_.rows_ref, bf16[2,528,128]{2,1,0:T(8,128)(2,1)S(1)} %collective-permute-done.1.refs_1_, bf16[2,528,128]{2,1,0:T(8,128)(2,1)S(1)} %pad_maximum_fusion.refs_2_), custom_call_target="tpu_custom_call" | custom-call | flops 500000000 | bytes 1000000 | tf_op jit(solution)/shard_map/pallas_call | solution.py:212
  33.2 1.1 %shard_map.98 = (f32[2,128,512]{2,1,0:T(8,128)S(1)}, bf16[2,512,128]{2,1,0:T(8,128)(2,1)S(1)}) custom-call(bf16[2,528,128]{2,1,0:T(8,128)(2,1)S(1)} %bitcast_dynamic-update-slice_fusion.refs_0_.rows_ref, bf16[2,528,128]{2,1,0:T(8,128)(2,1)S(1)} %collective-permute-done.1.refs_1_, bf16[2,528,128]{2,1,0:T(8,128)(2,1)S(1)} %collective-permute-done.5.refs_2_, ...), custom_call_target="tpu_custom_call" | custom-call | flops 500000000 | bytes 1000000 | tf_op jit(solution)/shard_map/pallas_call | solution.py:212
  34.3 2.9 %collective-permute-start.8 = (bf16[2,512,128]{2,1,0:T(8,128)(2,1)S(1)}, bf16[2,512,128]{2,1,0:T(8,128)(2,1)S(1)}, u32[]{:S(2)}, u32[]{:S(2)}) collective-permute-start(bf16[2,512,128]{2,1,0:T(8,128)(2,1)S(1)} %get-tuple-element.44), channel_id=1, source_target_pairs={{0,128},{64,192},{128,0},{192,64},{1,129},{65,193},{129,1},{193,65... | collective-permute-start | bytes 786440 | tf_op jit(solution)/shard_map/ppermute | solution.py:263
  37.2 2.0 %shard_map.99 = (f32[2,128,512]{2,1,0:T(8,128)S(1)}, f32[2,128,512]{2,1,0:T(8,128)S(1)}, bf16[2,512,128]{2,1,0:T(8,128)(2,1)S(1)}) custom-call(bf16[2,528,128]{2,1,0:T(8,128)(2,1)S(1)} %bitcast_dynamic-update-slice_fusion.refs_0_.rows_ref, bf16[2,528,128]{2,1,0:T(8,128)(2,1)S(1)} %collective-permute-done.1.refs_1_, ...), custom_call_target="tpu_custom_call" | custom-call | flops 500000000 | bytes 1000000 | tf_op jit(solution)/shard_map/pallas_call | solution.py:212
  39.3 2.1 %shard_map.100 = (f32[2,256,128]{2,1,0:T(8,128)S(1)}, bf16[2,256,128]{2,1,0:T(8,128)(2,1)S(1)}, bf16[2,256,128]{2,1,0:T(8,128)(2,1)S(1)}, bf16[2,256,128]{2,1,0:T(8,128)(2,1)S(1)}, bf16[2,512,128]{2,1,0:T(8,128)(2,1)S(1)}) custom-call(bf16[2,528,128]{2,1,0:T(8,128)(2,1)S(1)} %bitcast_dynamic-update-slice_fusion.refs_0_.rows_ref, ...), custom_call_target="tpu_custom_call" | custom-call | flops 500000000 | bytes 1000000 | tf_op jit(solution)/shard_map/pallas_call | solution.py:212
  42.2 2.6 %collective-permute-start.13 = (bf16[2,512,128]{2,1,0:T(8,128)(2,1)S(1)}, bf16[2,512,128]{2,1,0:T(8,128)(2,1)S(1)}, u32[]{:S(2)}, u32[]{:S(2)}) collective-permute-start(bf16[2,512,128]{2,1,0:T(8,128)(2,1)S(1)} %get-tuple-element.53), channel_id=1, source_target_pairs={{0,192},{64,0},{128,64},{192,128},{1,193},{65,1},{129,65},{193,129... | collective-permute-start | bytes 786440 | tf_op jit(solution)/shard_map/ppermute | solution.py:263
  44.7 3.0 %collective-permute-start.10 = (bf16[2,256,128]{2,1,0:T(8,128)(2,1)S(1)}, bf16[2,256,128]{2,1,0:T(8,128)(2,1)S(1)}, u32[]{:S(2)}, u32[]{:S(2)}) collective-permute-start(bf16[2,256,128]{2,1,0:T(8,128)(2,1)S(1)} %get-tuple-element.46), channel_id=1, source_target_pairs={{0,56},{8,0},{16,8},{24,16},{32,24},{40,32},{48,40},{56,48},{1,57}... | collective-permute-start | bytes 393224 | tf_op jit(solution)/shard_map/ppermute | solution.py:278
  47.7 1.4 %collective-permute-start.9 = (bf16[2,256,128]{2,1,0:T(8,128)(2,1)S(1)}, bf16[2,256,128]{2,1,0:T(8,128)(2,1)S(1)}, u32[]{:S(2)}, u32[]{:S(2)}) collective-permute-start(bf16[2,256,128]{2,1,0:T(8,128)(2,1)S(1)} %get-tuple-element.45), channel_id=1, source_target_pairs={{48,0},{24,8},{0,16},{40,24},{16,32},{56,40},{32,48},{8,56},{49,1}... | collective-permute-start | bytes 393224 | tf_op jit(solution)/shard_map/ppermute | solution.py:278
  49.3 1.3 %collective-permute-start.15 = (bf16[512,128]{1,0:T(8,128)(2,1)S(1)}, bf16[512,128]{1,0:T(8,128)(2,1)S(1)}, u32[]{:S(2)}, u32[]{:S(2)}) collective-permute-start(bf16[512,128]{1,0:T(8,128)(2,1)S(1)} %get-tuple-element.56), channel_id=1, source_target_pairs={{0,4},{4,0},{1,5},{5,1},{2,6},{6,2},{3,7},{7,3},{8,12},{12,8},{9,1... | collective-permute-start | bytes 393224 | tf_op jit(solution)/shard_map/ppermute | solution.py:286
  51.5 3.8 %collective-permute-done.11.refs_3_ = bf16[2,256,128]{2,1,0:T(8,128)(2,1)S(1)} collective-permute-done((bf16[2,256,128]{2,1,0:T(8,128)(2,1)S(1)}, bf16[2,256,128]{2,1,0:T(8,128)(2,1)S(1)}, u32[]{:S(2)}, u32[]{:S(2)}) %collective-permute-start.11) | collective-permute-done | bytes 131104 | tf_op jit(solution)/shard_map/ppermute | solution.py:278
  55.4 3.7 %collective-permute-start.12 = (bf16[256,128]{1,0:T(8,128)(2,1)S(1)}, bf16[256,128]{1,0:T(8,128)(2,1)S(1)}, u32[]{:S(2)}, u32[]{:S(2)}) collective-permute-start(bf16[256,128]{1,0:T(8,128)(2,1)S(1)} %get-tuple-element.49), channel_id=1, source_target_pairs={{0,32},{8,40},{16,48},{24,56},{32,0},{40,8},{48,16},{56,24},{1,33}... | collective-permute-start | bytes 196616 | tf_op jit(solution)/shard_map/ppermute | solution.py:288
  59.1 4.6 %collective-permute-done.12.dqx_ref = bf16[256,128]{1,0:T(8,128)(2,1)S(1)} collective-permute-done((bf16[256,128]{1,0:T(8,128)(2,1)S(1)}, bf16[256,128]{1,0:T(8,128)(2,1)S(1)}, u32[]{:S(2)}, u32[]{:S(2)}) %collective-permute-start.12) | collective-permute-done | bytes 65568 | tf_op jit(solution)/shard_map/ppermute | solution.py:288
  (23 shorter events, 3.3 us)
Async XLA Ops:
  2.5 11.2 %collective-permute-start = (bf16[528,128]{1,0:T(8,128)(2,1)}, bf16[528,128]{1,0:T(8,128)(2,1)S(1)}, u32[]{:S(2)}, u32[]{:S(2)}) collective-permute-start(bf16[528,128]{1,0:T(8,128)(2,1)} %get-tuple-element.30), channel_id=1, source_target_pairs={{0,32},{8,40},{16,48},{24,56},{32,0},{40,8},{48,16},{56,24},{1,33}... | collective-permute-start | bytes 405512 | tf_op jit(solution)/shard_map/ppermute | solution.py:236
  9.7 9.4 %collective-permute-start.4 = (bf16[528,128]{1,0:T(8,128)(2,1)}, bf16[528,128]{1,0:T(8,128)(2,1)S(1)}, u32[]{:S(2)}, u32[]{:S(2)}) collective-permute-start(bf16[528,128]{1,0:T(8,128)(2,1)} %get-tuple-element.31), channel_id=1, source_target_pairs={{0,4},{4,0},{1,5},{5,1},{2,6},{6,2},{3,7},{7,3},{8,12},{12,8},{9,1... | collective-permute-start | bytes 405512 | tf_op jit(solution)/shard_map/ppermute | solution.py:235
  11.9 7.3 %copy-start = (bf16[528,128]{1,0:T(8,128)(2,1)S(1)}, bf16[528,128]{1,0:T(8,128)(2,1)}, u32[]{:S(2)}) copy-start(bf16[528,128]{1,0:T(8,128)(2,1)} %get-tuple-element.31) | copy-start | bytes 405508
  13.6 13.7 %collective-permute-start.2 = (bf16[2,528,128]{2,1,0:T(8,128)(2,1)S(1)}, bf16[2,528,128]{2,1,0:T(8,128)(2,1)S(1)}, u32[]{:S(2)}, u32[]{:S(2)}) collective-permute-start(bf16[2,528,128]{2,1,0:T(8,128)(2,1)S(1)} %bitcast_dynamic-update-slice_fusion.refs_0_.rows_ref), channel_id=1, source_target_pairs={{0,8},{8,16},{16,24},{24,32},{32,40},{40,48},{48,56},{56,0},{1,9},... | collective-permute-start | bytes 811016 | tf_op jit(solution)/shard_map/ppermute | solution.py:239
  17.6 12.3 %collective-permute-start.3 = (bf16[2,528,128]{2,1,0:T(8,128)(2,1)S(1)}, bf16[2,528,128]{2,1,0:T(8,128)(2,1)S(1)}, u32[]{:S(2)}, u32[]{:S(2)}) collective-permute-start(bf16[2,528,128]{2,1,0:T(8,128)(2,1)S(1)} %bitcast_dynamic-update-slice_fusion.refs_0_.rows_ref), channel_id=1, source_target_pairs={{0,56},{8,0},{16,8},{24,16},{32,24},{40,32},{48,40},{56,48},{1,57}... | collective-permute-start | bytes 811016 | tf_op jit(solution)/shard_map/ppermute | solution.py:239
  19.1 11.8 %collective-permute-start.5 = (bf16[2,528,128]{2,1,0:T(8,128)(2,1)S(1)}, bf16[2,528,128]{2,1,0:T(8,128)(2,1)S(1)}, u32[]{:S(2)}, u32[]{:S(2)}) collective-permute-start(bf16[2,528,128]{2,1,0:T(8,128)(2,1)S(1)} %pad_maximum_fusion.refs_2_), channel_id=1, source_target_pairs={{0,128},{64,192},{128,0},{192,64},{1,129},{65,193},{129,1},{193,65... | collective-permute-start | bytes 811016 | tf_op jit(solution)/shard_map/ppermute | solution.py:240
  22.4 9.6 %collective-permute-start.1 = (bf16[2,528,128]{2,1,0:T(8,128)(2,1)S(1)}, bf16[2,528,128]{2,1,0:T(8,128)(2,1)S(1)}, u32[]{:S(2)}, u32[]{:S(2)}) collective-permute-start(bf16[2,528,128]{2,1,0:T(8,128)(2,1)S(1)} %bitcast_dynamic-update-slice_fusion.refs_0_.rows_ref), channel_id=1, source_target_pairs={{0,48},{8,24},{16,0},{24,40},{32,16},{40,56},{48,32},{56,8},{1,49}... | collective-permute-start | bytes 811016 | tf_op jit(solution)/shard_map/ppermute | solution.py:239
  26.6 10.6 %collective-permute-start.7 = (bf16[2,528,128]{2,1,0:T(8,128)(2,1)S(1)}, bf16[2,528,128]{2,1,0:T(8,128)(2,1)S(1)}, u32[]{:S(2)}, u32[]{:S(2)}) collective-permute-start(bf16[2,528,128]{2,1,0:T(8,128)(2,1)S(1)} %pad_maximum_fusion.refs_2_), channel_id=1, source_target_pairs={{0,64},{64,128},{128,192},{192,0},{1,65},{65,129},{129,193},{193,1... | collective-permute-start | bytes 811016 | tf_op jit(solution)/shard_map/ppermute | solution.py:240
  27.3 11.9 %collective-permute-start.6 = (bf16[2,528,128]{2,1,0:T(8,128)(2,1)S(1)}, bf16[2,528,128]{2,1,0:T(8,128)(2,1)S(1)}, u32[]{:S(2)}, u32[]{:S(2)}) collective-permute-start(bf16[2,528,128]{2,1,0:T(8,128)(2,1)S(1)} %pad_maximum_fusion.refs_2_), channel_id=1, source_target_pairs={{0,192},{64,0},{128,64},{192,128},{1,193},{65,1},{129,65},{193,129... | collective-permute-start | bytes 811016 | tf_op jit(solution)/shard_map/ppermute | solution.py:240
  34.3 13.4 %collective-permute-start.8 = (bf16[2,512,128]{2,1,0:T(8,128)(2,1)S(1)}, bf16[2,512,128]{2,1,0:T(8,128)(2,1)S(1)}, u32[]{:S(2)}, u32[]{:S(2)}) collective-permute-start(bf16[2,512,128]{2,1,0:T(8,128)(2,1)S(1)} %get-tuple-element.44), channel_id=1, source_target_pairs={{0,128},{64,192},{128,0},{192,64},{1,129},{65,193},{129,1},{193,65... | collective-permute-start | bytes 786440 | tf_op jit(solution)/shard_map/ppermute | solution.py:263
  41.4 7.7 %collective-permute-start.14 = (bf16[2,512,128]{2,1,0:T(8,128)(2,1)S(1)}, bf16[2,512,128]{2,1,0:T(8,128)(2,1)S(1)}, u32[]{:S(2)}, u32[]{:S(2)}) collective-permute-start(bf16[2,512,128]{2,1,0:T(8,128)(2,1)S(1)} %get-tuple-element.54), channel_id=1, source_target_pairs={{0,64},{64,128},{128,192},{192,0},{1,65},{65,129},{129,193},{193,1... | collective-permute-start | bytes 786440 | tf_op jit(solution)/shard_map/ppermute | solution.py:263
  42.2 7.0 %collective-permute-start.13 = (bf16[2,512,128]{2,1,0:T(8,128)(2,1)S(1)}, bf16[2,512,128]{2,1,0:T(8,128)(2,1)S(1)}, u32[]{:S(2)}, u32[]{:S(2)}) collective-permute-start(bf16[2,512,128]{2,1,0:T(8,128)(2,1)S(1)} %get-tuple-element.53), channel_id=1, source_target_pairs={{0,192},{64,0},{128,64},{192,128},{1,193},{65,1},{129,65},{193,129... | collective-permute-start | bytes 786440 | tf_op jit(solution)/shard_map/ppermute | solution.py:263
  44.7 6.8 %collective-permute-start.10 = (bf16[2,256,128]{2,1,0:T(8,128)(2,1)S(1)}, bf16[2,256,128]{2,1,0:T(8,128)(2,1)S(1)}, u32[]{:S(2)}, u32[]{:S(2)}) collective-permute-start(bf16[2,256,128]{2,1,0:T(8,128)(2,1)S(1)} %get-tuple-element.46), channel_id=1, source_target_pairs={{0,56},{8,0},{16,8},{24,16},{32,24},{40,32},{48,40},{56,48},{1,57}... | collective-permute-start | bytes 393224 | tf_op jit(solution)/shard_map/ppermute | solution.py:278
  47.7 7.6 %collective-permute-start.11 = (bf16[2,256,128]{2,1,0:T(8,128)(2,1)S(1)}, bf16[2,256,128]{2,1,0:T(8,128)(2,1)S(1)}, u32[]{:S(2)}, u32[]{:S(2)}) collective-permute-start(bf16[2,256,128]{2,1,0:T(8,128)(2,1)S(1)} %get-tuple-element.47), channel_id=1, source_target_pairs={{0,8},{8,16},{16,24},{24,32},{32,40},{40,48},{48,56},{56,0},{1,9},... | collective-permute-start | bytes 393224 | tf_op jit(solution)/shard_map/ppermute | solution.py:278
  47.7 7.6 %collective-permute-start.9 = (bf16[2,256,128]{2,1,0:T(8,128)(2,1)S(1)}, bf16[2,256,128]{2,1,0:T(8,128)(2,1)S(1)}, u32[]{:S(2)}, u32[]{:S(2)}) collective-permute-start(bf16[2,256,128]{2,1,0:T(8,128)(2,1)S(1)} %get-tuple-element.45), channel_id=1, source_target_pairs={{48,0},{24,8},{0,16},{40,24},{16,32},{56,40},{32,48},{8,56},{49,1}... | collective-permute-start | bytes 393224 | tf_op jit(solution)/shard_map/ppermute | solution.py:278
  49.3 9.8 %collective-permute-start.15 = (bf16[512,128]{1,0:T(8,128)(2,1)S(1)}, bf16[512,128]{1,0:T(8,128)(2,1)S(1)}, u32[]{:S(2)}, u32[]{:S(2)}) collective-permute-start(bf16[512,128]{1,0:T(8,128)(2,1)S(1)} %get-tuple-element.56), channel_id=1, source_target_pairs={{0,4},{4,0},{1,5},{5,1},{2,6},{6,2},{3,7},{7,3},{8,12},{12,8},{9,1... | collective-permute-start | bytes 393224 | tf_op jit(solution)/shard_map/ppermute | solution.py:286
  55.4 8.3 %collective-permute-start.12 = (bf16[256,128]{1,0:T(8,128)(2,1)S(1)}, bf16[256,128]{1,0:T(8,128)(2,1)S(1)}, u32[]{:S(2)}, u32[]{:S(2)}) collective-permute-start(bf16[256,128]{1,0:T(8,128)(2,1)S(1)} %get-tuple-element.49), channel_id=1, source_target_pairs={{0,32},{8,40},{16,48},{24,56},{32,0},{40,8},{48,16},{56,24},{1,33}... | collective-permute-start | bytes 196616 | tf_op jit(solution)/shard_map/ppermute | solution.py:288

commit v13 on v11

--- a/solution.py
+++ b/solution.py
@@ -93,7 +93,7 @@
     return dot(p.astype(BF16), g), dot(ds, q), dot(kt, ds)
 
 
-def grad_kernel(js, plan, own, add, split, *refs):
+def grad_kernel(js, group, own, first, add, last, *refs):
     refs = list(refs)
 
     def take(count):
@@ -101,12 +101,11 @@
         del refs[:count]
         return taken
 
-    q_refs, (y_ref,) = take(2 * len(plan)), take(1)
-    dqin_refs = [None if first else take(1)[0] for first, _ in plan]
-    addin_ref = refs.pop(0) if add else None
-    dq_refs = [take(2 if last else 1) for _, last in plan]
-    dkv_refs = take(len(js)) if split else [refs.pop(0)]
-    dv_acc, dk_acc = refs
+    q_refs, (y_ref,) = take(2), take(1)
+    (dqin_ref,) = (None,) if first else take(1)
+    (addin_ref,) = take(1) if add else (None,)
+    (other_ref,) = take(1) if last else (None,)
+    dq_refs, (dkv_ref, dv_acc, dk_acc) = take(4 if last else 1), refs
     count = len(js)
     half = count * BLK
 
@@ -118,42 +117,40 @@
     kt = k.T
     low_j = [jnp.concatenate([y_ref[j, 4 * BLK :, :].astype(F32)[0:1, :]] * 4, 1) for j in js]
 
-    for n, (first, last) in enumerate(plan):
-        pair = q_refs[2 * n : 2 * n + 2]
-        chunks = [(ref, a) for ref in pair for a in range(2)]
-
-        def queries(array, b):
-            at = (2 * array + b) * BLK
-            return jnp.concatenate([ref[a, at : at + BLK, :] for ref, a in chunks], 0)
-
-        tiles = [ref[a, 4 * BLK :, :].astype(F32) for ref, a in chunks]
-        lse_low, lse_high, delta_low, delta_high, low_i = (
-            jnp.concatenate([t[r : r + 1, :] for t in tiles], 1) for r in range(5)
-        )
-        lse_low, lse_high = lse_low * LOG2E, lse_high * LOG2E
-        diagonal = own and n == 0
-
-        lses = [lse_high] * count + [lse_high + jnp.where(low_i <= low, 0.0, HIDE) for low in low_j]
-        dv, dk, dq_high = tile(
-            k, v, kt, queries(0, 1), queries(1, 1), lses, delta_high, count if diagonal else None
-        )
-        dv_acc[...] = dv if n == 0 else dv_acc[...] + dv
-        dk_acc[...] = dk if n == 0 else dk_acc[...] + dk
-        lses = [lse_low + jnp.where(low <= low_i, 0.0, HIDE) for low in low_j]
-        dv, dk, dq_low = tile(
-            k[:half], v[:half], kt[:, :half], queries(0, 0), queries(1, 0), lses, delta_low, 0 if diagonal else None
-        )
-        dv_acc[:half] += dv
-        dk_acc[:half] += dk
-        for b, dq in ((0, dq_low), (1, dq_high)):
-            if not first:
-                dq = dqin_refs[n][b] + dq
-            if not last:
-                dq_refs[n][0][b] = dq
-            else:
-                for c in range(4):
-                    ref = dq_refs[n][c // 2]
-                    ref[c % 2, b * BLK : (b + 1) * BLK, :] = dq[:, c * BLK : (c + 1) * BLK].T.astype(ref.dtype)
+    chunks = [(ref, c) for ref in q_refs for c in range(ref.shape[0])]
+
+    def queries(array, b):
+        at = (2 * array + b) * BLK
+        return jnp.concatenate([ref[a, at : at + BLK, :] for ref, a in chunks], 0)
+
+    tiles = [ref[a, 4 * BLK :, :].astype(F32) for ref, a in chunks]
+    lse_low, lse_high, delta_low, delta_high, low_i = (
+        jnp.concatenate([t[r : r + 1, :] for t in tiles], 1) for r in range(5)
+    )
+    lse_low, lse_high = lse_low * LOG2E, lse_high * LOG2E
+    diagonal = own
+
+    lses = [lse_high] * count + [lse_high + jnp.where(low_i <= low, 0.0, HIDE) for low in low_j]
+    dv, dk, dq_high = tile(
+        k, v, kt, queries(0, 1), queries(1, 1), lses, delta_high, count if diagonal else None
+    )
+    dv_acc[...] = dv
+    dk_acc[...] = dk
+    lses = [lse_low + jnp.where(low <= low_i, 0.0, HIDE) for low in low_j]
+    dv, dk, dq_low = tile(
+        k[:half], v[:half], kt[:, :half], queries(0, 0), queries(1, 0), lses, delta_low, 0 if diagonal else None
+    )
+    dv_acc[:half] += dv
+    dk_acc[:half] += dk
+    for b, dq in ((0, dq_low), (1, dq_high)):
+        if not first:
+            dq = dqin_ref[b] + dq
+        if not last:
+            dq_refs[0][b] = dq
+        else:
+            for a, part in ((group, dq), (1 - group, other_ref[b])):
+                for s, ref in enumerate(dq_refs):
+                    ref[a, b * BLK : (b + 1) * BLK, :] = part[:, s * BLK : (s + 1) * BLK].T.astype(ref.dtype)
 
     for m in range(count):
         for b in range(2):
@@ -163,10 +160,7 @@
                 part = acc[source]
                 if add:
                     part = addin_ref[m, rows, :] + part
-                if split:
-                    dkv_refs[m][rows, :] = part.astype(BF16)
-                else:
-                    dkv_refs[0][m, rows, :] = part.astype(dkv_refs[0].dtype)
+                dkv_ref[m, rows, :] = part.astype(dkv_ref.dtype)
 
 
 def meet_kernel(parts, *refs):
@@ -228,68 +222,65 @@
     payload = ((ROWS, DIM), BF16)
     mine_q, mine_k = call(prep_kernel, [payload] * 2, operands, buffers + [rows] * 2 + sems, hbm=True)
 
-    def beside(mine, other):
-        both = lax.optimization_barrier(jnp.pad(mine[None], ((0, 1), (0, 0), (0, 0))))
-        return lax.dynamic_update_slice(both, other[None], (1, 0, 0))
+    def gather(arrays):
+        out = jnp.pad(arrays[0][None], ((0, len(arrays) - 1), (0, 0), (0, 0)))
+        out = lax.optimization_barrier(out)
+        for n, array in enumerate(arrays[1:]):
+            out = lax.dynamic_update_slice(out, array[None], (n + 1, 0, 0))
+        return out
 
     other_k = lax.ppermute(mine_k, "kz", z_step(4))
-    q0 = beside(mine_q, lax.ppermute(mine_q, "kx", X_SWAP))
-    late_q, other_k = lax.optimization_barrier((q0, other_k))
-    k0 = jnp.stack([mine_k, other_k])
-    q_sets = [q0] + [lax.ppermute(q, "kz", p) for q, p in ((q0, z_step(1)), (q0, z_step(-1)), (late_q, Z_PAIRS))]
+    near = [lax.ppermute(mine_q, "kz", p) for p in (z_step(1), z_step(-1), Z_PAIRS)]
+    near = jnp.stack(near)
+    q_groups = [
+        (mine_q[None], near),
+        (lax.ppermute(mine_q, "kx", X_SWAP)[None], lax.ppermute(near, "kx", X_SWAP)),
+    ]
+    k0 = gather([mine_k, other_k])
     k_sets = [k0] + [lax.ppermute(k0, "pb", y_step(-s)) for s in Y_FROM[1:]]
-    q_pairs = ([q_sets[0], q_sets[3]], [q_sets[1], q_sets[2]])
-
-    def grad(turn, js, pairs, dq_in, last, dkv_type, add=None, split=False):
-        plan = tuple((d is None, e) for d, e in zip(dq_in, last))
-        outs = []
-        for pair, end in zip(pairs, last):
-            if end:
-                outs += [((2, 2 * BLK, DIM), F32 if (pair, s) == (0, 0) else BF16) for s in range(2)]
-            else:
-                outs.append(((2, DIM, 4 * BLK), F32))
-        dkv_out = [((4 * BLK, DIM), BF16)] * len(js) if split else [((len(js), 4 * BLK, DIM), dkv_type)]
-        acc = pltpu.VMEM((2 * len(js) * BLK, DIM), F32)
-        results = call(
-            functools.partial(grad_kernel, js, plan, turn == 0 and pairs[0] == 0, add is not None, split),
-            outs + dkv_out,
-            [q for p in pairs for q in q_pairs[p]] + [k_sets[turn]] + [d for d in (*dq_in, add) if d is not None],
+
+    def grad(turn, group, dq_in, add, dkv_type, other=None):
+        last = other is not None
+        outs = [((2, DIM, 4 * BLK), F32)]
+        if last:
+            outs = [((2, 2 * BLK, DIM), BF16 if s else F32) for s in range(4)]
+        acc = pltpu.VMEM((4 * BLK, DIM), F32)
+        own = turn == 0 and group == 0
+        *dq, part = call(
+            functools.partial(grad_kernel, (0, 1), group, own, dq_in is None, add is not None, last),
+            outs + [((2, 4 * BLK, DIM), dkv_type)],
+            [*q_groups[group], k_sets[turn]] + [d for d in (dq_in, add, other) if d is not None],
             [acc, acc],
             cost_estimate=COST,
         )
-        return results[: len(outs)], results[len(outs) :]
+        return (dq if last else dq[0]), part
 
     def send_back(turn, part):
         return lax.ppermute(part, "pb", y_step(Y_FROM[turn]))
 
     both = (0, 1)
     parts = []
-    dq1 = None
+    dq0 = dq1 = None
     for turn in range(4):
-        dq1, (part,) = grad(turn, both, (1,), (dq1,), (turn == 3,), F32)
-        dq1 = dq1[0] if turn < 3 else dq1
+        dq0, part = grad(turn, 0, dq0, None, F32)
         parts.append(part)
-    dq_back = [lax.ppermute(d, "kz", p) for d, p in zip(dq1, (z_step(-1), z_step(1)))]
-    q_pairs[0][1], parts[3] = lax.optimization_barrier((q_pairs[0][1], parts[3]))
+    q_groups[1], parts[1] = lax.optimization_barrier((q_groups[1], parts[1]))
     back = []
-    dq0 = None
     for turn in (1, 2, 3):
-        (dq0,), (part,) = grad(turn, both, (0,), (dq0,), (False,), BF16, add=parts[turn])
+        dq1, part = grad(turn, 1, dq1, parts[turn], BF16)
         back.append(send_back(turn, part))
-    dq0, back[0] = lax.optimization_barrier((dq0, back[0]))
-    (dq_keep, dq_z2), (own,) = grad(0, both, (0,), (dq0,), (True,), F32, add=parts[0])
-    dq_back.append(lax.ppermute(dq_z2, "kz", Z_BACK))
+    dq1, back[0] = lax.optimization_barrier((dq1, back[0]))
+    (dq_keep, *dqs), own = grad(0, 1, dq1, parts[0], F32, other=dq0)
+    dq_back = [lax.ppermute(d, "kz", p) for d, p in zip(dqs, (z_step(-1), z_step(1), Z_BACK))]
 
     def meet(operands, parts, shape):
         return call(functools.partial(meet_kernel, parts), [(shape, F32), (shape, BF16)], operands)
 
-    dkv_keep, dkv_send = meet(
-        [own] + back, [both] * 4, (4 * BLK, DIM)
-    )
+    dkv_keep, dkv_send = meet([own, *back], [both] * 4, (4 * BLK, DIM))
     dkv_last = lax.ppermute(dkv_send, "kz", z_step(4))
     dq_keep, dq_send = meet([dq_keep] + dq_back, [both] * 4, (2 * BLK, DIM))
     dq_last = lax.ppermute(dq_send, "kx", X_SWAP)
-    operands = (q0, dq_keep, dq_last, dkv_keep, dkv_last)
+    operands = (mine_q[None], dq_keep, dq_last, dkv_keep, dkv_last)
     return tuple(call(last_kernel, [((2 * BLK, DIM), BF16)] * 3, operands))
 
 

time: 64 us -> 74.9 us (1.17)
  waiting for transfers between devices: 10.1 us -> 33 us
  starting transfers between devices: 40.2 us -> 28.2 us
    ppermute x2 -> x3, waiting for transfers between devices: 0.01 us -> 10 us  [body(): lax.ppermute(d, 'kz', p)]
    ppermute x3, waiting for transfers between devices: 0.01 us -> 5.87 us  [body(): k_sets = [k0] + [lax.ppermute(k0, 'pb', y_step(-s)) for s in Y_FROM[1:]]]
    ppermute x1, starting transfers between devices: 7.19 us -> 2.56 us  [body(): other_k = lax.ppermute(mine_k, 'kz', z_step(4))]
    ppermute x3, waiting for transfers between devices: 0.01 us -> 4.63 us  [send_back(): return lax.ppermute(part, 'pb', y_step(Y_FROM[turn]))]
    ppermute x1, starting transfers between devices: 4.36 us -> 0.09 us  [body(): dkv_last = lax.ppermute(dkv_send, 'kz', z_step(4))]
    ppermute x2 -> x3, starting transfers between devices: 5.32 us -> 2.1 us  [body(): lax.ppermute(d, 'kz', p)]
    ppermute x1, waiting for transfers between devices: 1.91 us -> 4.1 us  [body(): other_k = lax.ppermute(mine_k, 'kz', z_step(4))]
  transfers between devices with their start and end apart: 16 -> 17, of which waited for: 3 -> 9; matrix products, arithmetic and copies ran while one was open for 2% -> 1% of each run, Pallas kernels for 13% -> 12%
where the time goes in v13:
time: 74.9 us; the launch traced here: 74.7 us
  waiting for transfers between devices  33 us (44%)
  starting transfers between devices  28.2 us (38%)
  Pallas kernels  11.7 us (16%)
  local copies, waits for them, and re-layouts  0.99 us (1%)
  between operations  0.77 us (1%)
    pallas_call x12, Pallas kernels, call(): pl.pallas_call(kernel, out_shape=[jax.ShapeDtypeStruct(s, t) for s, t in...  11.7 us
    ppermute x3, waiting for transfers between devices, body(): lax.ppermute(d, 'kz', p)  10 us
    ppermute x3, starting transfers between devices, body(): lax.ppermute(mine_q, 'kz', p)  8.4 us
    ppermute x3, starting transfers between devices, body(): k_sets = [k0] + [lax.ppermute(k0, 'pb', y_step(-s)) for s in Y_FROM[1:]]  6.52 us
    ppermute x3, waiting for transfers between devices, body(): k_sets = [k0] + [lax.ppermute(k0, 'pb', y_step(-s)) for s in Y_FROM[1:]]  5.87 us
    ppermute x3, waiting for transfers between devices, body(): lax.ppermute(mine_q, 'kz', p)  5.2 us
    ppermute x3, starting transfers between devices, send_back(): return lax.ppermute(part, 'pb', y_step(Y_FROM[turn]))  4.87 us
    ppermute x3, waiting for transfers between devices, send_back(): return lax.ppermute(part, 'pb', y_step(Y_FROM[turn]))  4.63 us
  transfers between devices with their start and end apart: 17, of which 9 were waited for; matrix products, arithmetic and copies ran while one was open for 1% of the time, Pallas kernels for 12%

profile of v13, /device:TPU:4, one launch (start us, length us, event | category | flops | bytes accessed | tf_op | source)
XLA Modules:
  0.0 74.7 jit_solution(12422941428206239463)
XLA Ops:
  0.6 1.8 %shard_map.94 = (bf16[528,128]{1,0:T(8,128)(2,1)}, bf16[528,128]{1,0:T(8,128)(2,1)}) custom-call(s32[128]{0:T(128)} %refs_0_.1, bf16[256,128]{1,0:T(8,128)(2,1)} %refs_1_.1, bf16[256,128]{1,0:T(8,128)(2,1)} %refs_2_.1, bf16[1,256]{1,0:T(2,128)(2,1)} %bitcast.22, bf16[256,128]{1,0:T(8,128)(2,1)} %refs_4_.1, bf16[256,128]{1,0:T(8,128)(2,1)} %refs_5_.1, ...), custom_call_target="tpu_custom_call" | custom-call | tf_op jit(solution)/shard_map/pallas_call | solution.py:206
  2.5 6.4 %collective-permute-start.3 = (bf16[528,128]{1,0:T(8,128)(2,1)}, bf16[528,128]{1,0:T(8,128)(2,1)S(1)}, u32[]{:S(2)}, u32[]{:S(2)}) collective-permute-start(bf16[528,128]{1,0:T(8,128)(2,1)} %get-tuple-element.33), channel_id=1, source_target_pairs={{0,48},{8,24},{16,0},{24,40},{32,16},{40,56},{48,32},{56,8},{1,49}... | collective-permute-start | bytes 405512 | tf_op jit(solution)/shard_map/ppermute | solution.py:233
  8.8 2.0 %collective-permute-start.1 = (bf16[528,128]{1,0:T(8,128)(2,1)}, bf16[528,128]{1,0:T(8,128)(2,1)S(1)}, u32[]{:S(2)}, u32[]{:S(2)}) collective-permute-start(bf16[528,128]{1,0:T(8,128)(2,1)} %get-tuple-element.33), channel_id=1, source_target_pairs={{0,8},{8,16},{16,24},{24,32},{32,40},{40,48},{48,56},{56,0},{1,9},... | collective-permute-start | bytes 405512 | tf_op jit(solution)/shard_map/ppermute | solution.py:233
  10.9 2.6 %collective-permute-start.5 = (bf16[528,128]{1,0:T(8,128)(2,1)}, bf16[528,128]{1,0:T(8,128)(2,1)S(1)}, u32[]{:S(2)}, u32[]{:S(2)}) collective-permute-start(bf16[528,128]{1,0:T(8,128)(2,1)} %get-tuple-element.34), channel_id=1, source_target_pairs={{0,32},{8,40},{16,48},{24,56},{32,0},{40,8},{48,16},{56,24},{1,33}... | collective-permute-start | bytes 405512 | tf_op jit(solution)/shard_map/ppermute | solution.py:232
  14.4 5.2 %collective-permute-done.2 = bf16[528,128]{1,0:T(8,128)(2,1)S(1)} collective-permute-done((bf16[528,128]{1,0:T(8,128)(2,1)}, bf16[528,128]{1,0:T(8,128)(2,1)S(1)}, u32[]{:S(2)}, u32[]{:S(2)}) %collective-permute-start.2) | collective-permute-done | bytes 135200 | tf_op jit(solution)/shard_map/ppermute | solution.py:233
  19.7 1.3 %collective-permute-start.4 = (bf16[3,528,128]{2,1,0:T(8,128)(2,1)S(1)}, bf16[3,528,128]{2,1,0:T(8,128)(2,1)S(1)}, u32[]{:S(2)}, u32[]{:S(2)}) collective-permute-start(bf16[3,528,128]{2,1,0:T(8,128)(2,1)S(1)} %pad_maximum_fusion.refs_1_), channel_id=1, source_target_pairs={{0,4},{4,0},{1,5},{5,1},{2,6},{6,2},{3,7},{7,3},{8,12},{12,8},{9,1... | collective-permute-start | bytes 1216520 | tf_op jit(solution)/shard_map/ppermute | solution.py:237
  20.9 4.1 %collective-permute-done.5 = bf16[528,128]{1,0:T(8,128)(2,1)S(1)} collective-permute-done((bf16[528,128]{1,0:T(8,128)(2,1)}, bf16[528,128]{1,0:T(8,128)(2,1)S(1)}, u32[]{:S(2)}, u32[]{:S(2)}) %collective-permute-start.5) | collective-permute-done | bytes 135200 | tf_op jit(solution)/shard_map/ppermute | solution.py:232
  25.1 3.3 %collective-permute-start.6 = (bf16[2,528,128]{2,1,0:T(8,128)(2,1)S(1)}, bf16[2,528,128]{2,1,0:T(8,128)(2,1)S(1)}, u32[]{:S(2)}, u32[]{:S(2)}) collective-permute-start(bf16[2,528,128]{2,1,0:T(8,128)(2,1)S(1)} %bitcast_dynamic-update-slice_fusion.refs_2_), channel_id=1, source_target_pairs={{0,128},{64,192},{128,0},{192,64},{1,129},{65,193},{129,1},{193,65... | collective-permute-start | bytes 811016 | tf_op jit(solution)/shard_map/ppermute | solution.py:240
  29.0 2.6 %collective-permute-start.7 = (bf16[2,528,128]{2,1,0:T(8,128)(2,1)S(1)}, bf16[2,528,128]{2,1,0:T(8,128)(2,1)S(1)}, u32[]{:S(2)}, u32[]{:S(2)}) collective-permute-start(bf16[2,528,128]{2,1,0:T(8,128)(2,1)S(1)} %bitcast_dynamic-update-slice_fusion.refs_2_), channel_id=1, source_target_pairs={{0,192},{64,0},{128,64},{192,128},{1,193},{65,1},{129,65},{193,129... | collective-permute-start | bytes 811016 | tf_op jit(solution)/shard_map/ppermute | solution.py:240
  31.6 1.2 %collective-permute-start = (bf16[528,128]{1,0:T(8,128)(2,1)S(1)}, bf16[528,128]{1,0:T(8,128)(2,1)S(1)}, u32[]{:S(2)}, u32[]{:S(2)}) collective-permute-start(bf16[528,128]{1,0:T(8,128)(2,1)S(1)} %copy-done), channel_id=1, source_target_pairs={{0,4},{4,0},{1,5},{5,1},{2,6},{6,2},{3,7},{7,3},{8,12},{12,8},{9,1... | collective-permute-start | bytes 405512 | tf_op jit(solution)/shard_map/ppermute | solution.py:237
  33.9 2.2 %collective-permute-done.6.refs_2_ = bf16[2,528,128]{2,1,0:T(8,128)(2,1)S(1)} collective-permute-done((bf16[2,528,128]{2,1,0:T(8,128)(2,1)S(1)}, bf16[2,528,128]{2,1,0:T(8,128)(2,1)S(1)}, u32[]{:S(2)}, u32[]{:S(2)}) %collective-permute-start.6) | collective-permute-done | bytes 270368 | tf_op jit(solution)/shard_map/ppermute | solution.py:240
  37.2 3.7 %collective-permute-done.8.refs_2_ = bf16[2,528,128]{2,1,0:T(8,128)(2,1)S(1)} collective-permute-done((bf16[2,528,128]{2,1,0:T(8,128)(2,1)S(1)}, bf16[2,528,128]{2,1,0:T(8,128)(2,1)S(1)}, u32[]{:S(2)}, u32[]{:S(2)}) %collective-permute-start.8) | collective-permute-done | bytes 270368 | tf_op jit(solution)/shard_map/ppermute | solution.py:240
  42.0 1.1 %shard_map.97 = (f32[2,128,512]{2,1,0:T(8,128)S(1)}, bf16[2,512,128]{2,1,0:T(8,128)(2,1)S(1)}) custom-call(bf16[1,528,128]{2,1,0:T(8,128)(2,1)S(1)} %bitcast.9, bf16[3,528,128]{2,1,0:T(8,128)(2,1)S(1)} %collective-permute-done.4.refs_1_, bf16[2,528,128]{2,1,0:T(8,128)(2,1)S(1)} %collective-permute-done.6.refs_2_, f32[2,512,128]{2,1,0:T(8,128)S(1)} %get-tuple-element.39.refs_3_), custom_call_target="tpu_custom_call" | custom-call | flops 500000000 | bytes 1000000 | tf_op jit(solution)/shard_map/pallas_call | solution.py:206
  43.1 2.7 %collective-permute-start.9 = (bf16[2,512,128]{2,1,0:T(8,128)(2,1)S(1)}, bf16[2,512,128]{2,1,0:T(8,128)(2,1)S(1)}, u32[]{:S(2)}, u32[]{:S(2)}) collective-permute-start(bf16[2,512,128]{2,1,0:T(8,128)(2,1)S(1)} %get-tuple-element.47), channel_id=1, source_target_pairs={{0,128},{64,192},{128,0},{192,64},{1,129},{65,193},{129,1},{193,65... | collective-permute-start | bytes 786440 | tf_op jit(solution)/shard_map/ppermute | solution.py:259
  46.9 1.1 %shard_map.99 = (f32[2,128,512]{2,1,0:T(8,128)S(1)}, bf16[2,512,128]{2,1,0:T(8,128)(2,1)S(1)}) custom-call(bf16[1,528,128]{2,1,0:T(8,128)(2,1)S(1)} %bitcast.10, bf16[3,528,128]{2,1,0:T(8,128)(2,1)S(1)} %collective-permute-done.4.refs_1_, bf16[2,528,128]{2,1,0:T(8,128)(2,1)S(1)} %collective-permute-done.8.refs_2_, ...), custom_call_target="tpu_custom_call" | custom-call | flops 500000000 | bytes 1000000 | tf_op jit(solution)/shard_map/pallas_call | solution.py:206
  48.1 2.1 %collective-permute-start.14 = (bf16[2,512,128]{2,1,0:T(8,128)(2,1)S(1)}, bf16[2,512,128]{2,1,0:T(8,128)(2,1)S(1)}, u32[]{:S(2)}, u32[]{:S(2)}) collective-permute-start(bf16[2,512,128]{2,1,0:T(8,128)(2,1)S(1)} %get-tuple-element.59), channel_id=1, source_target_pairs={{0,192},{64,0},{128,64},{192,128},{1,193},{65,1},{129,65},{193,129... | collective-permute-start | bytes 786440 | tf_op jit(solution)/shard_map/ppermute | solution.py:259
  51.4 2.3 %collective-permute-done.9.refs_1_ = bf16[2,512,128]{2,1,0:T(8,128)(2,1)S(1)} collective-permute-done((bf16[2,512,128]{2,1,0:T(8,128)(2,1)S(1)}, bf16[2,512,128]{2,1,0:T(8,128)(2,1)S(1)}, u32[]{:S(2)}, u32[]{:S(2)}) %collective-permute-start.9) | collective-permute-done | bytes 262176 | tf_op jit(solution)/shard_map/ppermute | solution.py:259
  53.7 1.3 %shard_map.102 = (f32[2,256,128]{2,1,0:T(8,128)S(1)}, bf16[2,256,128]{2,1,0:T(8,128)(2,1)S(1)}, bf16[2,256,128]{2,1,0:T(8,128)(2,1)S(1)}, bf16[2,256,128]{2,1,0:T(8,128)(2,1)S(1)}, f32[2,512,128]{2,1,0:T(8,128)S(1)}) custom-call(bf16[1,528,128]{2,1,0:T(8,128)(2,1)S(1)} %bitcast.12, bf16[3,528,128]{2,1,0:T(8,128)(2,1)S(1)} %collective-permute-done.4.refs_1_, ...), custom_call_target="tpu_custom_call" | custom-call | flops 500000000 | bytes 1000000 | tf_op jit(solution)/shard_map/pallas_call | solution.py:206
  55.0 2.0 %collective-permute-start.11 = (bf16[2,256,128]{2,1,0:T(8,128)(2,1)S(1)}, bf16[2,256,128]{2,1,0:T(8,128)(2,1)S(1)}, u32[]{:S(2)}, u32[]{:S(2)}) collective-permute-start(bf16[2,256,128]{2,1,0:T(8,128)(2,1)S(1)} %get-tuple-element.53), channel_id=1, source_target_pairs={{0,8},{8,16},{16,24},{24,32},{32,40},{40,48},{48,56},{56,0},{1,9},... | collective-permute-start | bytes 393224 | tf_op jit(solution)/shard_map/ppermute | solution.py:274
  57.0 2.3 %collective-permute-done.15.refs_3_ = bf16[2,512,128]{2,1,0:T(8,128)(2,1)S(1)} collective-permute-done((bf16[2,512,128]{2,1,0:T(8,128)(2,1)S(1)}, bf16[2,512,128]{2,1,0:T(8,128)(2,1)S(1)}, u32[]{:S(2)}, u32[]{:S(2)}) %collective-permute-start.15) | collective-permute-done | bytes 262176 | tf_op jit(solution)/shard_map/ppermute | solution.py:259
  59.6 2.2 %collective-permute-done.10.refs_1_ = bf16[2,256,128]{2,1,0:T(8,128)(2,1)S(1)} collective-permute-done((bf16[2,256,128]{2,1,0:T(8,128)(2,1)S(1)}, bf16[2,256,128]{2,1,0:T(8,128)(2,1)S(1)}, u32[]{:S(2)}, u32[]{:S(2)}) %collective-permute-start.10) | collective-permute-done | bytes 131104 | tf_op jit(solution)/shard_map/ppermute | solution.py:274
  61.8 7.8 %collective-permute-done.11.refs_2_ = bf16[2,256,128]{2,1,0:T(8,128)(2,1)S(1)} collective-permute-done((bf16[2,256,128]{2,1,0:T(8,128)(2,1)S(1)}, bf16[2,256,128]{2,1,0:T(8,128)(2,1)S(1)}, u32[]{:S(2)}, u32[]{:S(2)}) %collective-permute-start.11) | collective-permute-done | bytes 131104 | tf_op jit(solution)/shard_map/ppermute | solution.py:274
  69.7 1.2 %collective-permute-start.13 = (bf16[256,128]{1,0:T(8,128)(2,1)S(1)}, bf16[256,128]{1,0:T(8,128)(2,1)S(1)}, u32[]{:S(2)}, u32[]{:S(2)}) collective-permute-start(bf16[256,128]{1,0:T(8,128)(2,1)S(1)} %get-tuple-element.56), channel_id=1, source_target_pairs={{0,4},{4,0},{1,5},{5,1},{2,6},{6,2},{3,7},{7,3},{8,12},{12,8},{9,1... | collective-permute-start | bytes 196616 | tf_op jit(solution)/shard_map/ppermute | solution.py:282
  70.9 3.2 %collective-permute-done.13.dqx_ref = bf16[256,128]{1,0:T(8,128)(2,1)S(1)} collective-permute-done((bf16[256,128]{1,0:T(8,128)(2,1)S(1)}, bf16[256,128]{1,0:T(8,128)(2,1)S(1)}, u32[]{:S(2)}, u32[]{:S(2)}) %collective-permute-start.13) | collective-permute-done | bytes 65568 | tf_op jit(solution)/shard_map/ppermute | solution.py:282
  (27 shorter events, 8.4 us)
Async XLA Ops:
  2.5 11.9 %collective-permute-start.3 = (bf16[528,128]{1,0:T(8,128)(2,1)}, bf16[528,128]{1,0:T(8,128)(2,1)S(1)}, u32[]{:S(2)}, u32[]{:S(2)}) collective-permute-start(bf16[528,128]{1,0:T(8,128)(2,1)} %get-tuple-element.33), channel_id=1, source_target_pairs={{0,48},{8,24},{16,0},{24,40},{32,16},{40,56},{48,32},{56,8},{1,49}... | collective-permute-start | bytes 405512 | tf_op jit(solution)/shard_map/ppermute | solution.py:233
  8.8 10.8 %collective-permute-start.2 = (bf16[528,128]{1,0:T(8,128)(2,1)}, bf16[528,128]{1,0:T(8,128)(2,1)S(1)}, u32[]{:S(2)}, u32[]{:S(2)}) collective-permute-start(bf16[528,128]{1,0:T(8,128)(2,1)} %get-tuple-element.33), channel_id=1, source_target_pairs={{0,56},{8,0},{16,8},{24,16},{32,24},{40,32},{48,40},{56,48},{1,57}... | collective-permute-start | bytes 405512 | tf_op jit(solution)/shard_map/ppermute | solution.py:233
  8.8 10.8 %collective-permute-start.1 = (bf16[528,128]{1,0:T(8,128)(2,1)}, bf16[528,128]{1,0:T(8,128)(2,1)S(1)}, u32[]{:S(2)}, u32[]{:S(2)}) collective-permute-start(bf16[528,128]{1,0:T(8,128)(2,1)} %get-tuple-element.33), channel_id=1, source_target_pairs={{0,8},{8,16},{16,24},{24,32},{32,40},{40,48},{48,56},{56,0},{1,9},... | collective-permute-start | bytes 405512 | tf_op jit(solution)/shard_map/ppermute | solution.py:233
  10.9 14.2 %collective-permute-start.5 = (bf16[528,128]{1,0:T(8,128)(2,1)}, bf16[528,128]{1,0:T(8,128)(2,1)S(1)}, u32[]{:S(2)}, u32[]{:S(2)}) collective-permute-start(bf16[528,128]{1,0:T(8,128)(2,1)} %get-tuple-element.34), channel_id=1, source_target_pairs={{0,32},{8,40},{16,48},{24,56},{32,0},{40,8},{48,16},{56,24},{1,33}... | collective-permute-start | bytes 405512 | tf_op jit(solution)/shard_map/ppermute | solution.py:232
  19.7 11.9 %copy-start = (bf16[528,128]{1,0:T(8,128)(2,1)S(1)}, bf16[528,128]{1,0:T(8,128)(2,1)}, u32[]{:S(2)}) copy-start(bf16[528,128]{1,0:T(8,128)(2,1)} %get-tuple-element.33) | copy-start | bytes 405508
  19.7 22.3 %collective-permute-start.4 = (bf16[3,528,128]{2,1,0:T(8,128)(2,1)S(1)}, bf16[3,528,128]{2,1,0:T(8,128)(2,1)S(1)}, u32[]{:S(2)}, u32[]{:S(2)}) collective-permute-start(bf16[3,528,128]{2,1,0:T(8,128)(2,1)S(1)} %pad_maximum_fusion.refs_1_), channel_id=1, source_target_pairs={{0,4},{4,0},{1,5},{5,1},{2,6},{6,2},{3,7},{7,3},{8,12},{12,8},{9,1... | collective-permute-start | bytes 1216520 | tf_op jit(solution)/shard_map/ppermute | solution.py:237
  25.1 11.0 %collective-permute-start.6 = (bf16[2,528,128]{2,1,0:T(8,128)(2,1)S(1)}, bf16[2,528,128]{2,1,0:T(8,128)(2,1)S(1)}, u32[]{:S(2)}, u32[]{:S(2)}) collective-permute-start(bf16[2,528,128]{2,1,0:T(8,128)(2,1)S(1)} %bitcast_dynamic-update-slice_fusion.refs_2_), channel_id=1, source_target_pairs={{0,128},{64,192},{128,0},{192,64},{1,129},{65,193},{129,1},{193,65... | collective-permute-start | bytes 811016 | tf_op jit(solution)/shard_map/ppermute | solution.py:240
  28.4 12.5 %collective-permute-start.8 = (bf16[2,528,128]{2,1,0:T(8,128)(2,1)S(1)}, bf16[2,528,128]{2,1,0:T(8,128)(2,1)S(1)}, u32[]{:S(2)}, u32[]{:S(2)}) collective-permute-start(bf16[2,528,128]{2,1,0:T(8,128)(2,1)S(1)} %bitcast_dynamic-update-slice_fusion.refs_2_), channel_id=1, source_target_pairs={{0,64},{64,128},{128,192},{192,0},{1,65},{65,129},{129,193},{193,1... | collective-permute-start | bytes 811016 | tf_op jit(solution)/shard_map/ppermute | solution.py:240
  29.0 16.8 %collective-permute-start.7 = (bf16[2,528,128]{2,1,0:T(8,128)(2,1)S(1)}, bf16[2,528,128]{2,1,0:T(8,128)(2,1)S(1)}, u32[]{:S(2)}, u32[]{:S(2)}) collective-permute-start(bf16[2,528,128]{2,1,0:T(8,128)(2,1)S(1)} %bitcast_dynamic-update-slice_fusion.refs_2_), channel_id=1, source_target_pairs={{0,192},{64,0},{128,64},{192,128},{1,193},{65,1},{129,65},{193,129... | collective-permute-start | bytes 811016 | tf_op jit(solution)/shard_map/ppermute | solution.py:240
  31.6 10.4 %collective-permute-start = (bf16[528,128]{1,0:T(8,128)(2,1)S(1)}, bf16[528,128]{1,0:T(8,128)(2,1)S(1)}, u32[]{:S(2)}, u32[]{:S(2)}) collective-permute-start(bf16[528,128]{1,0:T(8,128)(2,1)S(1)} %copy-done), channel_id=1, source_target_pairs={{0,4},{4,0},{1,5},{5,1},{2,6},{6,2},{3,7},{7,3},{8,12},{12,8},{9,1... | collective-permute-start | bytes 405512 | tf_op jit(solution)/shard_map/ppermute | solution.py:237
  43.1 10.6 %collective-permute-start.9 = (bf16[2,512,128]{2,1,0:T(8,128)(2,1)S(1)}, bf16[2,512,128]{2,1,0:T(8,128)(2,1)S(1)}, u32[]{:S(2)}, u32[]{:S(2)}) collective-permute-start(bf16[2,512,128]{2,1,0:T(8,128)(2,1)S(1)} %get-tuple-element.47), channel_id=1, source_target_pairs={{0,128},{64,192},{128,0},{192,64},{1,129},{65,193},{129,1},{193,65... | collective-permute-start | bytes 786440 | tf_op jit(solution)/shard_map/ppermute | solution.py:259
  48.1 9.0 %collective-permute-start.14 = (bf16[2,512,128]{2,1,0:T(8,128)(2,1)S(1)}, bf16[2,512,128]{2,1,0:T(8,128)(2,1)S(1)}, u32[]{:S(2)}, u32[]{:S(2)}) collective-permute-start(bf16[2,512,128]{2,1,0:T(8,128)(2,1)S(1)} %get-tuple-element.59), channel_id=1, source_target_pairs={{0,192},{64,0},{128,64},{192,128},{1,193},{65,1},{129,65},{193,129... | collective-permute-start | bytes 786440 | tf_op jit(solution)/shard_map/ppermute | solution.py:259
  51.2 8.1 %collective-permute-start.15 = (bf16[2,512,128]{2,1,0:T(8,128)(2,1)S(1)}, bf16[2,512,128]{2,1,0:T(8,128)(2,1)S(1)}, u32[]{:S(2)}, u32[]{:S(2)}) collective-permute-start(bf16[2,512,128]{2,1,0:T(8,128)(2,1)S(1)} %get-tuple-element.60), channel_id=1, source_target_pairs={{0,64},{64,128},{128,192},{192,0},{1,65},{65,129},{129,193},{193,1... | collective-permute-start | bytes 786440 | tf_op jit(solution)/shard_map/ppermute | solution.py:259
  54.9 6.9 %collective-permute-start.10 = (bf16[2,256,128]{2,1,0:T(8,128)(2,1)S(1)}, bf16[2,256,128]{2,1,0:T(8,128)(2,1)S(1)}, u32[]{:S(2)}, u32[]{:S(2)}) collective-permute-start(bf16[2,256,128]{2,1,0:T(8,128)(2,1)S(1)} %get-tuple-element.52), channel_id=1, source_target_pairs={{0,56},{8,0},{16,8},{24,16},{32,24},{40,32},{48,40},{56,48},{1,57}... | collective-permute-start | bytes 393224 | tf_op jit(solution)/shard_map/ppermute | solution.py:274
  55.0 14.6 %collective-permute-start.11 = (bf16[2,256,128]{2,1,0:T(8,128)(2,1)S(1)}, bf16[2,256,128]{2,1,0:T(8,128)(2,1)S(1)}, u32[]{:S(2)}, u32[]{:S(2)}) collective-permute-start(bf16[2,256,128]{2,1,0:T(8,128)(2,1)S(1)} %get-tuple-element.53), channel_id=1, source_target_pairs={{0,8},{8,16},{16,24},{24,32},{32,40},{40,48},{48,56},{56,0},{1,9},... | collective-permute-start | bytes 393224 | tf_op jit(solution)/shard_map/ppermute | solution.py:274
  57.0 12.6 %collective-permute-start.12 = (bf16[2,256,128]{2,1,0:T(8,128)(2,1)S(1)}, bf16[2,256,128]{2,1,0:T(8,128)(2,1)S(1)}, u32[]{:S(2)}, u32[]{:S(2)}) collective-permute-start(bf16[2,256,128]{2,1,0:T(8,128)(2,1)S(1)} %get-tuple-element.54), channel_id=1, source_target_pairs={{48,0},{24,8},{0,16},{40,24},{16,32},{56,40},{32,48},{8,56},{49,1}... | collective-permute-start | bytes 393224 | tf_op jit(solution)/shard_map/ppermute | solution.py:274
  59.5 11.4 %collective-permute-start.16 = (bf16[512,128]{1,0:T(8,128)(2,1)S(1)}, bf16[512,128]{1,0:T(8,128)(2,1)S(1)}, u32[]{:S(2)}, u32[]{:S(2)}) collective-permute-start(bf16[512,128]{1,0:T(8,128)(2,1)S(1)} %get-tuple-element.62), channel_id=1, source_target_pairs={{0,32},{8,40},{16,48},{24,56},{32,0},{40,8},{48,16},{56,24},{1,33}... | collective-permute-start | bytes 393224 | tf_op jit(solution)/shard_map/ppermute | solution.py:280
  69.7 4.4 %collective-permute-start.13 = (bf16[256,128]{1,0:T(8,128)(2,1)S(1)}, bf16[256,128]{1,0:T(8,128)(2,1)S(1)}, u32[]{:S(2)}, u32[]{:S(2)}) collective-permute-start(bf16[256,128]{1,0:T(8,128)(2,1)S(1)} %get-tuple-element.56), channel_id=1, source_target_pairs={{0,4},{4,0},{1,5},{5,1},{2,6},{6,2},{3,7},{7,3},{8,12},{12,8},{9,1... | collective-permute-start | bytes 196616 | tf_op jit(solution)/shard_map/ppermute | solution.py:282

commit v14 on v12

--- a/solution.py
+++ b/solution.py
@@ -232,8 +232,8 @@
         both = lax.optimization_barrier(jnp.pad(mine[None], ((0, 1), (0, 0), (0, 0))))
         return lax.dynamic_update_slice(both, other[None], (1, 0, 0))
 
-    other_k = lax.ppermute(mine_k, "kx", X_SWAP)
-    q0 = beside(mine_q, lax.ppermute(mine_q, "kz", z_step(4)))
+    other_k = lax.ppermute(mine_k, "kz", z_step(4))
+    q0 = beside(mine_q, lax.ppermute(mine_q, "kx", X_SWAP))
     _, other_k = lax.optimization_barrier((q0, other_k))
     k0 = jnp.stack([mine_k, other_k])
     q_sets = [q0] + [lax.ppermute(q, "kz", p) for q, p in ((q0, z_step(1)), (q0, z_step(-1)), (q0, Z_PAIRS))]
@@ -264,10 +264,9 @@
 
     both = (0, 1)
     (dq1,), (own1,) = grad(0, both, (1,), (None,), (False,), F32)
-    (dq1,), (part,) = grad(1, both, (1,), (dq1,), (False,), F32)
-    q_pairs[0][1], part = lax.optimization_barrier((q_pairs[0][1], part))
+    k_sets[0], own1 = lax.optimization_barrier((k_sets[0], own1))
     (dq0,), (own0,) = grad(0, both, (0,), (None,), (False,), F32)
-    (dq0,), (part,) = grad(1, both, (0,), (dq0,), (False,), BF16, add=part)
+    (dq0, dq1), (part,) = grad(1, both, both, (dq0, dq1), (False, False), BF16)
     back = [send_back(1, part)]
     (dq0, dq1), (part,) = grad(2, both, both, (dq0, dq1), (False, False), BF16)
     back.append(send_back(2, part))
@@ -283,9 +282,9 @@
     dkv_keep, dkv_send = meet(
         [*own, *back], [both] * 5, (4 * BLK, DIM)
     )
-    dkv_last = lax.ppermute(dkv_send, "kx", X_SWAP)
+    dkv_last = lax.ppermute(dkv_send, "kz", z_step(4))
     dq_keep, dq_send = meet([dq_keep] + dq_back, [both] * 4, (2 * BLK, DIM))
-    dq_last = lax.ppermute(dq_send, "kz", z_step(4))
+    dq_last = lax.ppermute(dq_send, "kx", X_SWAP)
     operands = (q0, dq_keep, dq_last, dkv_keep, dkv_last)
     return tuple(call(last_kernel, [((2 * BLK, DIM), BF16)] * 3, operands))
 

time: 64.5 us -> 64.1 us (level)
  the two profiles are of different devices: /device:TPU:4 before, /device:TPU:64 now
where the time goes in v14:
time: 64.1 us; the launch traced here: 64 us
  starting transfers between devices  37.5 us (59%)
  waiting for transfers between devices  13.7 us (21%)
  Pallas kernels  11.1 us (17%)
  local copies, waits for them, and re-layouts  0.96 us (1%)
  between operations  0.75 us (1%)
    pallas_call x9, Pallas kernels, call(): pl.pallas_call(kernel, out_shape=[jax.ShapeDtypeStruct(s, t) for s, t in...  11.1 us
    ppermute x3, starting transfers between devices, body(): k_sets = [k0] + [lax.ppermute(k0, 'pb', y_step(-s)) for s in Y_FROM[1:]]  6.97 us
    ppermute x3, starting transfers between devices, send_back(): return lax.ppermute(part, 'pb', y_step(Y_FROM[turn]))  6.78 us
    ppermute x3, waiting for transfers between devices, body(): lax.ppermute(d, 'kz', p)  6.02 us
    ppermute x1, starting transfers between devices, body(): dkv_last = lax.ppermute(dkv_send, 'kz', z_step(4))  5.77 us
    ppermute x3, starting transfers between devices, body(): lax.ppermute(d, 'kz', p)  5.56 us
    ppermute x1, starting transfers between devices, body(): other_k = lax.ppermute(mine_k, 'kz', z_step(4))  5.39 us
    ppermute x3, starting transfers between devices, body(): lax.ppermute(q, 'kz', p)  4.77 us
  transfers between devices with their start and end apart: 16, of which 5 were waited for; matrix products, arithmetic and copies ran while one was open for 2% of the time, Pallas kernels for 13%

profile of v14, /device:TPU:64, one launch (start us, length us, event | category | flops | bytes accessed | tf_op | source)
XLA Modules:
  0.0 64.0 jit_solution(7864757868895162957)
XLA Ops:
  0.6 1.8 %shard_map.94 = (bf16[528,128]{1,0:T(8,128)(2,1)}, bf16[528,128]{1,0:T(8,128)(2,1)}) custom-call(s32[128]{0:T(128)} %refs_0_.1, bf16[256,128]{1,0:T(8,128)(2,1)} %refs_1_.1, bf16[256,128]{1,0:T(8,128)(2,1)} %refs_2_.1, bf16[1,256]{1,0:T(2,128)(2,1)} %bitcast.9, bf16[256,128]{1,0:T(8,128)(2,1)} %refs_4_.1, bf16[256,128]{1,0:T(8,128)(2,1)} %refs_5_.1, ...), custom_call_target="tpu_custom_call" | custom-call | tf_op jit(solution)/shard_map/pallas_call | solution.py:212
  2.5 1.6 %collective-permute-start = (bf16[528,128]{1,0:T(8,128)(2,1)}, bf16[528,128]{1,0:T(8,128)(2,1)S(1)}, u32[]{:S(2)}, u32[]{:S(2)}) collective-permute-start(bf16[528,128]{1,0:T(8,128)(2,1)} %get-tuple-element.29), channel_id=1, source_target_pairs={{0,4},{4,0},{1,5},{5,1},{2,6},{6,2},{3,7},{7,3},{8,12},{12,8},{9,1... | collective-permute-start | bytes 405512 | tf_op jit(solution)/shard_map/ppermute | solution.py:236
  4.0 5.4 %collective-permute-start.4 = (bf16[528,128]{1,0:T(8,128)(2,1)}, bf16[528,128]{1,0:T(8,128)(2,1)S(1)}, u32[]{:S(2)}, u32[]{:S(2)}) collective-permute-start(bf16[528,128]{1,0:T(8,128)(2,1)} %get-tuple-element.30), channel_id=1, source_target_pairs={{0,32},{8,40},{16,48},{24,56},{32,0},{40,8},{48,16},{56,24},{1,33}... | collective-permute-start | bytes 405512 | tf_op jit(solution)/shard_map/ppermute | solution.py:235
  9.4 0.9 %pad.4 = bf16[2,528,128]{2,1,0:T(8,128)(2,1)S(1)} pad(bf16[1,528,128]{2,1,0:T(8,128)(2,1)} %bitcast.6, bf16[]{:T(256)} %constant.1.clone.1), padding=0_1x0_0x0_0 | pad | bytes 405506 | tf_op jit(solution)/shard_map/jit(_pad)/pad | solution.py:232
  10.4 1.1 %collective-permute-start.2 = (bf16[2,528,128]{2,1,0:T(8,128)(2,1)S(1)}, bf16[2,528,128]{2,1,0:T(8,128)(2,1)S(1)}, u32[]{:S(2)}, u32[]{:S(2)}) collective-permute-start(bf16[2,528,128]{2,1,0:T(8,128)(2,1)S(1)} %bitcast_dynamic-update-slice_fusion.refs_0_.rows_ref), channel_id=1, source_target_pairs={{0,8},{8,16},{16,24},{24,32},{32,40},{40,48},{48,56},{56,0},{1,9},... | collective-permute-start | bytes 811016 | tf_op jit(solution)/shard_map/ppermute | solution.py:239
  11.5 1.0 %collective-permute-start.3 = (bf16[2,528,128]{2,1,0:T(8,128)(2,1)S(1)}, bf16[2,528,128]{2,1,0:T(8,128)(2,1)S(1)}, u32[]{:S(2)}, u32[]{:S(2)}) collective-permute-start(bf16[2,528,128]{2,1,0:T(8,128)(2,1)S(1)} %bitcast_dynamic-update-slice_fusion.refs_0_.rows_ref), channel_id=1, source_target_pairs={{0,56},{8,0},{16,8},{24,16},{32,24},{40,32},{48,40},{56,48},{1,57}... | collective-permute-start | bytes 811016 | tf_op jit(solution)/shard_map/ppermute | solution.py:239
  12.5 2.7 %collective-permute-start.1 = (bf16[2,528,128]{2,1,0:T(8,128)(2,1)S(1)}, bf16[2,528,128]{2,1,0:T(8,128)(2,1)S(1)}, u32[]{:S(2)}, u32[]{:S(2)}) collective-permute-start(bf16[2,528,128]{2,1,0:T(8,128)(2,1)S(1)} %bitcast_dynamic-update-slice_fusion.refs_0_.rows_ref), channel_id=1, source_target_pairs={{0,48},{8,24},{16,0},{24,40},{32,16},{40,56},{48,32},{56,8},{1,49}... | collective-permute-start | bytes 811016 | tf_op jit(solution)/shard_map/ppermute | solution.py:239
  15.2 1.7 %collective-permute-done.4 = bf16[528,128]{1,0:T(8,128)(2,1)S(1)} collective-permute-done((bf16[528,128]{1,0:T(8,128)(2,1)}, bf16[528,128]{1,0:T(8,128)(2,1)S(1)}, u32[]{:S(2)}, u32[]{:S(2)}) %collective-permute-start.4) | collective-permute-done | bytes 135200 | tf_op jit(solution)/shard_map/ppermute | solution.py:235
  16.9 3.3 %collective-permute-start.7 = (bf16[2,528,128]{2,1,0:T(8,128)(2,1)S(1)}, bf16[2,528,128]{2,1,0:T(8,128)(2,1)S(1)}, u32[]{:S(2)}, u32[]{:S(2)}) collective-permute-start(bf16[2,528,128]{2,1,0:T(8,128)(2,1)S(1)} %pad_maximum_fusion.refs_2_), channel_id=1, source_target_pairs={{0,128},{64,192},{128,0},{192,64},{1,129},{65,193},{129,1},{193,65... | collective-permute-start | bytes 811016 | tf_op jit(solution)/shard_map/ppermute | solution.py:240
  20.9 1.9 %collective-permute-done.2.refs_0_.refs_2_ = bf16[2,528,128]{2,1,0:T(8,128)(2,1)S(1)} collective-permute-done((bf16[2,528,128]{2,1,0:T(8,128)(2,1)S(1)}, bf16[2,528,128]{2,1,0:T(8,128)(2,1)S(1)}, u32[]{:S(2)}, u32[]{:S(2)}) %collective-permute-start.2) | collective-permute-done | bytes 270368 | tf_op jit(solution)/shard_map/ppermute | solution.py:239
  22.8 3.0 %collective-permute-start.5 = (bf16[2,528,128]{2,1,0:T(8,128)(2,1)S(1)}, bf16[2,528,128]{2,1,0:T(8,128)(2,1)S(1)}, u32[]{:S(2)}, u32[]{:S(2)}) collective-permute-start(bf16[2,528,128]{2,1,0:T(8,128)(2,1)S(1)} %pad_maximum_fusion.refs_2_), channel_id=1, source_target_pairs={{0,192},{64,0},{128,64},{192,128},{1,193},{65,1},{129,65},{193,129... | collective-permute-start | bytes 811016 | tf_op jit(solution)/shard_map/ppermute | solution.py:240
  25.8 1.1 %shard_map.95 = (f32[2,128,512]{2,1,0:T(8,128)S(1)}, f32[2,512,128]{2,1,0:T(8,128)S(1)}) custom-call(bf16[2,528,128]{2,1,0:T(8,128)(2,1)S(1)} %collective-permute-done.2.refs_0_.refs_2_, bf16[2,528,128]{2,1,0:T(8,128)(2,1)S(1)} %collective-permute-done.3.refs_1_.refs_3_, bf16[2,528,128]{2,1,0:T(8,128)(2,1)S(1)} %pad_maximum_fusion.refs_2_), custom_call_target="tpu_custom_call" | custom-call | flops 500000000 | bytes 1000000 | tf_op jit(solution)/shard_map/pallas_call | solution.py:212
  27.2 1.1 %shard_map.96 = (f32[2,128,512]{2,1,0:T(8,128)S(1)}, f32[2,512,128]{2,1,0:T(8,128)S(1)}) custom-call(bf16[2,528,128]{2,1,0:T(8,128)(2,1)S(1)} %bitcast_dynamic-update-slice_fusion.refs_0_.rows_ref, bf16[2,528,128]{2,1,0:T(8,128)(2,1)S(1)} %collective-permute-done.1.refs_1_, bf16[2,528,128]{2,1,0:T(8,128)(2,1)S(1)} %pad_maximum_fusion.refs_2_), custom_call_target="tpu_custom_call" | custom-call | flops 500000000 | bytes 1000000 | tf_op jit(solution)/shard_map/pallas_call | solution.py:212
  28.3 2.0 %shard_map.97 = (f32[2,128,512]{2,1,0:T(8,128)S(1)}, f32[2,128,512]{2,1,0:T(8,128)S(1)}, bf16[2,512,128]{2,1,0:T(8,128)(2,1)S(1)}) custom-call(bf16[2,528,128]{2,1,0:T(8,128)(2,1)S(1)} %bitcast_dynamic-update-slice_fusion.refs_0_.rows_ref, bf16[2,528,128]{2,1,0:T(8,128)(2,1)S(1)} %collective-permute-done.1.refs_1_, ...), custom_call_target="tpu_custom_call" | custom-call | flops 500000000 | bytes 1000000 | tf_op jit(solution)/shard_map/pallas_call | solution.py:212
  30.3 3.5 %collective-permute-start.8 = (bf16[2,512,128]{2,1,0:T(8,128)(2,1)S(1)}, bf16[2,512,128]{2,1,0:T(8,128)(2,1)S(1)}, u32[]{:S(2)}, u32[]{:S(2)}) collective-permute-start(bf16[2,512,128]{2,1,0:T(8,128)(2,1)S(1)} %get-tuple-element.42), channel_id=1, source_target_pairs={{0,128},{64,192},{128,0},{192,64},{1,129},{65,193},{129,1},{193,65... | collective-permute-start | bytes 786440 | tf_op jit(solution)/shard_map/ppermute | solution.py:263
  33.8 2.0 %shard_map.98 = (f32[2,128,512]{2,1,0:T(8,128)S(1)}, f32[2,128,512]{2,1,0:T(8,128)S(1)}, bf16[2,512,128]{2,1,0:T(8,128)(2,1)S(1)}) custom-call(bf16[2,528,128]{2,1,0:T(8,128)(2,1)S(1)} %bitcast_dynamic-update-slice_fusion.refs_0_.rows_ref, bf16[2,528,128]{2,1,0:T(8,128)(2,1)S(1)} %collective-permute-done.1.refs_1_, ...), custom_call_target="tpu_custom_call" | custom-call | flops 500000000 | bytes 1000000 | tf_op jit(solution)/shard_map/pallas_call | solution.py:212
  35.9 2.1 %shard_map.99 = (f32[2,256,128]{2,1,0:T(8,128)S(1)}, bf16[2,256,128]{2,1,0:T(8,128)(2,1)S(1)}, bf16[2,256,128]{2,1,0:T(8,128)(2,1)S(1)}, bf16[2,256,128]{2,1,0:T(8,128)(2,1)S(1)}, bf16[2,512,128]{2,1,0:T(8,128)(2,1)S(1)}) custom-call(bf16[2,528,128]{2,1,0:T(8,128)(2,1)S(1)} %bitcast_dynamic-update-slice_fusion.refs_0_.rows_ref, ...), custom_call_target="tpu_custom_call" | custom-call | flops 500000000 | bytes 1000000 | tf_op jit(solution)/shard_map/pallas_call | solution.py:212
  38.0 0.8 %collective-permute-start.14 = (bf16[2,512,128]{2,1,0:T(8,128)(2,1)S(1)}, bf16[2,512,128]{2,1,0:T(8,128)(2,1)S(1)}, u32[]{:S(2)}, u32[]{:S(2)}) collective-permute-start(bf16[2,512,128]{2,1,0:T(8,128)(2,1)S(1)} %get-tuple-element.52), channel_id=1, source_target_pairs={{0,64},{64,128},{128,192},{192,0},{1,65},{65,129},{129,193},{193,1... | collective-permute-start | bytes 786440 | tf_op jit(solution)/shard_map/ppermute | solution.py:263
  38.8 2.6 %collective-permute-start.13 = (bf16[2,512,128]{2,1,0:T(8,128)(2,1)S(1)}, bf16[2,512,128]{2,1,0:T(8,128)(2,1)S(1)}, u32[]{:S(2)}, u32[]{:S(2)}) collective-permute-start(bf16[2,512,128]{2,1,0:T(8,128)(2,1)S(1)} %get-tuple-element.51), channel_id=1, source_target_pairs={{0,192},{64,0},{128,64},{192,128},{1,193},{65,1},{129,65},{193,129... | collective-permute-start | bytes 786440 | tf_op jit(solution)/shard_map/ppermute | solution.py:263
  41.3 5.5 %collective-permute-start.10 = (bf16[2,256,128]{2,1,0:T(8,128)(2,1)S(1)}, bf16[2,256,128]{2,1,0:T(8,128)(2,1)S(1)}, u32[]{:S(2)}, u32[]{:S(2)}) collective-permute-start(bf16[2,256,128]{2,1,0:T(8,128)(2,1)S(1)} %get-tuple-element.44), channel_id=1, source_target_pairs={{0,56},{8,0},{16,8},{24,16},{32,24},{40,32},{48,40},{56,48},{1,57}... | collective-permute-start | bytes 393224 | tf_op jit(solution)/shard_map/ppermute | solution.py:277
  47.0 5.8 %collective-permute-start.15 = (bf16[512,128]{1,0:T(8,128)(2,1)S(1)}, bf16[512,128]{1,0:T(8,128)(2,1)S(1)}, u32[]{:S(2)}, u32[]{:S(2)}) collective-permute-start(bf16[512,128]{1,0:T(8,128)(2,1)S(1)} %get-tuple-element.54), channel_id=1, source_target_pairs={{0,32},{8,40},{16,48},{24,56},{32,0},{40,8},{48,16},{56,24},{1,33}... | collective-permute-start | bytes 393224 | tf_op jit(solution)/shard_map/ppermute | solution.py:285
  52.8 6.0 %collective-permute-done.11.refs_3_ = bf16[2,256,128]{2,1,0:T(8,128)(2,1)S(1)} collective-permute-done((bf16[2,256,128]{2,1,0:T(8,128)(2,1)S(1)}, bf16[2,256,128]{2,1,0:T(8,128)(2,1)S(1)}, u32[]{:S(2)}, u32[]{:S(2)}) %collective-permute-start.11) | collective-permute-done | bytes 131104 | tf_op jit(solution)/shard_map/ppermute | solution.py:277
  59.5 3.7 %collective-permute-done.12.dqx_ref = bf16[256,128]{1,0:T(8,128)(2,1)S(1)} collective-permute-done((bf16[256,128]{1,0:T(8,128)(2,1)S(1)}, bf16[256,128]{1,0:T(8,128)(2,1)S(1)}, u32[]{:S(2)}, u32[]{:S(2)}) %collective-permute-start.12) | collective-permute-done | bytes 65568 | tf_op jit(solution)/shard_map/ppermute | solution.py:287
  63.3 0.7 %shard_map.102 = (bf16[256,128]{1,0:T(8,128)(2,1)}, bf16[256,128]{1,0:T(8,128)(2,1)}, bf16[256,128]{1,0:T(8,128)(2,1)}) custom-call(bf16[2,528,128]{2,1,0:T(8,128)(2,1)S(1)} %bitcast_dynamic-update-slice_fusion.refs_0_.rows_ref, f32[256,128]{1,0:T(8,128)S(1)} %get-tuple-element.46.dq_ref, bf16[256,128]{1,0:T(8,128)(2,1)S(1)} %collective-permute-done.12.dqx_ref, ...), custom_call_target="tpu_custom_call" | custom-call | tf_op jit(solution)/shard_map/pallas_call | solution.py:212
  (22 shorter events, 1.9 us)
Async XLA Ops:
  2.5 7.9 %collective-permute-start = (bf16[528,128]{1,0:T(8,128)(2,1)}, bf16[528,128]{1,0:T(8,128)(2,1)S(1)}, u32[]{:S(2)}, u32[]{:S(2)}) collective-permute-start(bf16[528,128]{1,0:T(8,128)(2,1)} %get-tuple-element.29), channel_id=1, source_target_pairs={{0,4},{4,0},{1,5},{5,1},{2,6},{6,2},{3,7},{7,3},{8,12},{12,8},{9,1... | collective-permute-start | bytes 405512 | tf_op jit(solution)/shard_map/ppermute | solution.py:236
  4.0 12.8 %collective-permute-start.4 = (bf16[528,128]{1,0:T(8,128)(2,1)}, bf16[528,128]{1,0:T(8,128)(2,1)S(1)}, u32[]{:S(2)}, u32[]{:S(2)}) collective-permute-start(bf16[528,128]{1,0:T(8,128)(2,1)} %get-tuple-element.30), channel_id=1, source_target_pairs={{0,32},{8,40},{16,48},{24,56},{32,0},{40,8},{48,16},{56,24},{1,33}... | collective-permute-start | bytes 405512 | tf_op jit(solution)/shard_map/ppermute | solution.py:235
  10.4 6.5 %copy-start = (bf16[528,128]{1,0:T(8,128)(2,1)S(1)}, bf16[528,128]{1,0:T(8,128)(2,1)}, u32[]{:S(2)}) copy-start(bf16[528,128]{1,0:T(8,128)(2,1)} %get-tuple-element.30) | copy-start | bytes 405508
  10.4 12.3 %collective-permute-start.2 = (bf16[2,528,128]{2,1,0:T(8,128)(2,1)S(1)}, bf16[2,528,128]{2,1,0:T(8,128)(2,1)S(1)}, u32[]{:S(2)}, u32[]{:S(2)}) collective-permute-start(bf16[2,528,128]{2,1,0:T(8,128)(2,1)S(1)} %bitcast_dynamic-update-slice_fusion.refs_0_.rows_ref), channel_id=1, source_target_pairs={{0,8},{8,16},{16,24},{24,32},{32,40},{40,48},{48,56},{56,0},{1,9},... | collective-permute-start | bytes 811016 | tf_op jit(solution)/shard_map/ppermute | solution.py:239
  11.5 14.3 %collective-permute-start.3 = (bf16[2,528,128]{2,1,0:T(8,128)(2,1)S(1)}, bf16[2,528,128]{2,1,0:T(8,128)(2,1)S(1)}, u32[]{:S(2)}, u32[]{:S(2)}) collective-permute-start(bf16[2,528,128]{2,1,0:T(8,128)(2,1)S(1)} %bitcast_dynamic-update-slice_fusion.refs_0_.rows_ref), channel_id=1, source_target_pairs={{0,56},{8,0},{16,8},{24,16},{32,24},{40,32},{48,40},{56,48},{1,57}... | collective-permute-start | bytes 811016 | tf_op jit(solution)/shard_map/ppermute | solution.py:239
  12.5 14.7 %collective-permute-start.1 = (bf16[2,528,128]{2,1,0:T(8,128)(2,1)S(1)}, bf16[2,528,128]{2,1,0:T(8,128)(2,1)S(1)}, u32[]{:S(2)}, u32[]{:S(2)}) collective-permute-start(bf16[2,528,128]{2,1,0:T(8,128)(2,1)S(1)} %bitcast_dynamic-update-slice_fusion.refs_0_.rows_ref), channel_id=1, source_target_pairs={{0,48},{8,24},{16,0},{24,40},{32,16},{40,56},{48,32},{56,8},{1,49}... | collective-permute-start | bytes 811016 | tf_op jit(solution)/shard_map/ppermute | solution.py:239
  16.9 11.4 %collective-permute-start.7 = (bf16[2,528,128]{2,1,0:T(8,128)(2,1)S(1)}, bf16[2,528,128]{2,1,0:T(8,128)(2,1)S(1)}, u32[]{:S(2)}, u32[]{:S(2)}) collective-permute-start(bf16[2,528,128]{2,1,0:T(8,128)(2,1)S(1)} %pad_maximum_fusion.refs_2_), channel_id=1, source_target_pairs={{0,128},{64,192},{128,0},{192,64},{1,129},{65,193},{129,1},{193,65... | collective-permute-start | bytes 811016 | tf_op jit(solution)/shard_map/ppermute | solution.py:240
  20.2 13.6 %collective-permute-start.6 = (bf16[2,528,128]{2,1,0:T(8,128)(2,1)S(1)}, bf16[2,528,128]{2,1,0:T(8,128)(2,1)S(1)}, u32[]{:S(2)}, u32[]{:S(2)}) collective-permute-start(bf16[2,528,128]{2,1,0:T(8,128)(2,1)S(1)} %pad_maximum_fusion.refs_2_), channel_id=1, source_target_pairs={{0,64},{64,128},{128,192},{192,0},{1,65},{65,129},{129,193},{193,1... | collective-permute-start | bytes 811016 | tf_op jit(solution)/shard_map/ppermute | solution.py:240
  22.8 13.1 %collective-permute-start.5 = (bf16[2,528,128]{2,1,0:T(8,128)(2,1)S(1)}, bf16[2,528,128]{2,1,0:T(8,128)(2,1)S(1)}, u32[]{:S(2)}, u32[]{:S(2)}) collective-permute-start(bf16[2,528,128]{2,1,0:T(8,128)(2,1)S(1)} %pad_maximum_fusion.refs_2_), channel_id=1, source_target_pairs={{0,192},{64,0},{128,64},{192,128},{1,193},{65,1},{129,65},{193,129... | collective-permute-start | bytes 811016 | tf_op jit(solution)/shard_map/ppermute | solution.py:240
  30.3 16.5 %collective-permute-start.8 = (bf16[2,512,128]{2,1,0:T(8,128)(2,1)S(1)}, bf16[2,512,128]{2,1,0:T(8,128)(2,1)S(1)}, u32[]{:S(2)}, u32[]{:S(2)}) collective-permute-start(bf16[2,512,128]{2,1,0:T(8,128)(2,1)S(1)} %get-tuple-element.42), channel_id=1, source_target_pairs={{0,128},{64,192},{128,0},{192,64},{1,129},{65,193},{129,1},{193,65... | collective-permute-start | bytes 786440 | tf_op jit(solution)/shard_map/ppermute | solution.py:263
  38.0 8.9 %collective-permute-start.14 = (bf16[2,512,128]{2,1,0:T(8,128)(2,1)S(1)}, bf16[2,512,128]{2,1,0:T(8,128)(2,1)S(1)}, u32[]{:S(2)}, u32[]{:S(2)}) collective-permute-start(bf16[2,512,128]{2,1,0:T(8,128)(2,1)S(1)} %get-tuple-element.52), channel_id=1, source_target_pairs={{0,64},{64,128},{128,192},{192,0},{1,65},{65,129},{129,193},{193,1... | collective-permute-start | bytes 786440 | tf_op jit(solution)/shard_map/ppermute | solution.py:263
  38.8 8.1 %collective-permute-start.13 = (bf16[2,512,128]{2,1,0:T(8,128)(2,1)S(1)}, bf16[2,512,128]{2,1,0:T(8,128)(2,1)S(1)}, u32[]{:S(2)}, u32[]{:S(2)}) collective-permute-start(bf16[2,512,128]{2,1,0:T(8,128)(2,1)S(1)} %get-tuple-element.51), channel_id=1, source_target_pairs={{0,192},{64,0},{128,64},{192,128},{1,193},{65,1},{129,65},{193,129... | collective-permute-start | bytes 786440 | tf_op jit(solution)/shard_map/ppermute | solution.py:263
  41.3 11.5 %collective-permute-start.10 = (bf16[2,256,128]{2,1,0:T(8,128)(2,1)S(1)}, bf16[2,256,128]{2,1,0:T(8,128)(2,1)S(1)}, u32[]{:S(2)}, u32[]{:S(2)}) collective-permute-start(bf16[2,256,128]{2,1,0:T(8,128)(2,1)S(1)} %get-tuple-element.44), channel_id=1, source_target_pairs={{0,56},{8,0},{16,8},{24,16},{32,24},{40,32},{48,40},{56,48},{1,57}... | collective-permute-start | bytes 393224 | tf_op jit(solution)/shard_map/ppermute | solution.py:277
  46.8 12.0 %collective-permute-start.11 = (bf16[2,256,128]{2,1,0:T(8,128)(2,1)S(1)}, bf16[2,256,128]{2,1,0:T(8,128)(2,1)S(1)}, u32[]{:S(2)}, u32[]{:S(2)}) collective-permute-start(bf16[2,256,128]{2,1,0:T(8,128)(2,1)S(1)} %get-tuple-element.45), channel_id=1, source_target_pairs={{0,8},{8,16},{16,24},{24,32},{32,40},{40,48},{48,56},{56,0},{1,9},... | collective-permute-start | bytes 393224 | tf_op jit(solution)/shard_map/ppermute | solution.py:277
  46.9 12.0 %collective-permute-start.9 = (bf16[2,256,128]{2,1,0:T(8,128)(2,1)S(1)}, bf16[2,256,128]{2,1,0:T(8,128)(2,1)S(1)}, u32[]{:S(2)}, u32[]{:S(2)}) collective-permute-start(bf16[2,256,128]{2,1,0:T(8,128)(2,1)S(1)} %get-tuple-element.43), channel_id=1, source_target_pairs={{48,0},{24,8},{0,16},{40,24},{16,32},{56,40},{32,48},{8,56},{49,1}... | collective-permute-start | bytes 393224 | tf_op jit(solution)/shard_map/ppermute | solution.py:277
  47.0 12.5 %collective-permute-start.15 = (bf16[512,128]{1,0:T(8,128)(2,1)S(1)}, bf16[512,128]{1,0:T(8,128)(2,1)S(1)}, u32[]{:S(2)}, u32[]{:S(2)}) collective-permute-start(bf16[512,128]{1,0:T(8,128)(2,1)S(1)} %get-tuple-element.54), channel_id=1, source_target_pairs={{0,32},{8,40},{16,48},{24,56},{32,0},{40,8},{48,16},{56,24},{1,33}... | collective-permute-start | bytes 393224 | tf_op jit(solution)/shard_map/ppermute | solution.py:285
  58.9 4.4 %collective-permute-start.12 = (bf16[256,128]{1,0:T(8,128)(2,1)S(1)}, bf16[256,128]{1,0:T(8,128)(2,1)S(1)}, u32[]{:S(2)}, u32[]{:S(2)}) collective-permute-start(bf16[256,128]{1,0:T(8,128)(2,1)S(1)} %get-tuple-element.47), channel_id=1, source_target_pairs={{0,4},{4,0},{1,5},{5,1},{2,6},{6,2},{3,7},{7,3},{8,12},{12,8},{9,1... | collective-permute-start | bytes 196616 | tf_op jit(solution)/shard_map/ppermute | solution.py:287

commit v15 on v11

--- a/solution.py
+++ b/solution.py
@@ -93,7 +93,7 @@
     return dot(p.astype(BF16), g), dot(ds, q), dot(kt, ds)
 
 
-def grad_kernel(js, plan, own, add, split, *refs):
+def grad_kernel(js, groups, plan, own, add, *refs):
     refs = list(refs)
 
     def take(count):
@@ -101,12 +101,11 @@
         del refs[:count]
         return taken
 
-    q_refs, (y_ref,) = take(2 * len(plan)), take(1)
+    q_refs, (y_ref,) = [take(size) for size in groups], take(1)
     dqin_refs = [None if first else take(1)[0] for first, _ in plan]
     addin_ref = refs.pop(0) if add else None
-    dq_refs = [take(2 if last else 1) for _, last in plan]
-    dkv_refs = take(len(js)) if split else [refs.pop(0)]
-    dv_acc, dk_acc = refs
+    dq_refs = [take(size if last else 1) for size, (_, last) in zip(groups, plan)]
+    dkv_ref, dv_acc, dk_acc = refs
     count = len(js)
     half = count * BLK
 
@@ -116,11 +115,11 @@
 
     k, v = keys(0), keys(1)
     kt = k.T
-    low_j = [jnp.concatenate([y_ref[j, 4 * BLK :, :].astype(F32)[0:1, :]] * 4, 1) for j in js]
+    low_j = [y_ref[j, 4 * BLK :, :].astype(F32)[0:1, :] for j in js]
 
     for n, (first, last) in enumerate(plan):
-        pair = q_refs[2 * n : 2 * n + 2]
-        chunks = [(ref, a) for ref in pair for a in range(2)]
+        chunks = [(ref, a) for ref in q_refs[n] for a in range(2)]
+        lows = [jnp.concatenate([low] * len(chunks), 1) for low in low_j]
 
         def queries(array, b):
             at = (2 * array + b) * BLK
@@ -133,13 +132,13 @@
         lse_low, lse_high = lse_low * LOG2E, lse_high * LOG2E
         diagonal = own and n == 0
 
-        lses = [lse_high] * count + [lse_high + jnp.where(low_i <= low, 0.0, HIDE) for low in low_j]
+        lses = [lse_high] * count + [lse_high + jnp.where(low_i <= low, 0.0, HIDE) for low in lows]
         dv, dk, dq_high = tile(
             k, v, kt, queries(0, 1), queries(1, 1), lses, delta_high, count if diagonal else None
         )
         dv_acc[...] = dv if n == 0 else dv_acc[...] + dv
         dk_acc[...] = dk if n == 0 else dk_acc[...] + dk
-        lses = [lse_low + jnp.where(low <= low_i, 0.0, HIDE) for low in low_j]
+        lses = [lse_low + jnp.where(low <= low_i, 0.0, HIDE) for low in lows]
         dv, dk, dq_low = tile(
             k[:half], v[:half], kt[:, :half], queries(0, 0), queries(1, 0), lses, delta_low, 0 if diagonal else None
         )
@@ -151,7 +150,7 @@
             if not last:
                 dq_refs[n][0][b] = dq
             else:
-                for c in range(4):
+                for c in range(len(chunks)):
                     ref = dq_refs[n][c // 2]
                     ref[c % 2, b * BLK : (b + 1) * BLK, :] = dq[:, c * BLK : (c + 1) * BLK].T.astype(ref.dtype)
 
@@ -163,10 +162,7 @@
                 part = acc[source]
                 if add:
                     part = addin_ref[m, rows, :] + part
-                if split:
-                    dkv_refs[m][rows, :] = part.astype(BF16)
-                else:
-                    dkv_refs[0][m, rows, :] = part.astype(dkv_refs[0].dtype)
+                dkv_ref[m, rows, :] = part.astype(dkv_ref.dtype)
 
 
 def meet_kernel(parts, *refs):
@@ -238,46 +234,43 @@
     k0 = jnp.stack([mine_k, other_k])
     q_sets = [q0] + [lax.ppermute(q, "kz", p) for q, p in ((q0, z_step(1)), (q0, z_step(-1)), (late_q, Z_PAIRS))]
     k_sets = [k0] + [lax.ppermute(k0, "pb", y_step(-s)) for s in Y_FROM[1:]]
-    q_pairs = ([q_sets[0], q_sets[3]], [q_sets[1], q_sets[2]])
-
-    def grad(turn, js, pairs, dq_in, last, dkv_type, add=None, split=False):
-        plan = tuple((d is None, e) for d, e in zip(dq_in, last))
-        outs = []
-        for pair, end in zip(pairs, last):
-            if end:
-                outs += [((2, 2 * BLK, DIM), F32 if (pair, s) == (0, 0) else BF16) for s in range(2)]
-            else:
-                outs.append(((2, DIM, 4 * BLK), F32))
-        dkv_out = [((4 * BLK, DIM), BF16)] * len(js) if split else [((len(js), 4 * BLK, DIM), dkv_type)]
-        acc = pltpu.VMEM((2 * len(js) * BLK, DIM), F32)
-        results = call(
-            functools.partial(grad_kernel, js, plan, turn == 0 and pairs[0] == 0, add is not None, split),
-            outs + dkv_out,
-            [q for p in pairs for q in q_pairs[p]] + [k_sets[turn]] + [d for d in (*dq_in, add) if d is not None],
+    q_groups = [q_sets[:3], q_sets[3:]]
+
+    def grad(turn, group, dq_in, add, last, dkv_type):
+        sets = q_groups[group]
+        outs = [((2, DIM, 2 * len(sets) * BLK), F32)]
+        if last:
+            outs = [((2, 2 * BLK, DIM), F32 if (group, s) == (0, 0) else BF16) for s in range(len(sets))]
+        acc = pltpu.VMEM((4 * BLK, DIM), F32)
+        plan = ((dq_in is None, last),)
+        *dq, part = call(
+            functools.partial(grad_kernel, (0, 1), (len(sets),), plan, turn == 0 and group == 0, add is not None),
+            outs + [((2, 4 * BLK, DIM), dkv_type)],
+            [*sets, k_sets[turn]] + [d for d in (dq_in, add) if d is not None],
             [acc, acc],
             cost_estimate=COST,
         )
-        return results[: len(outs)], results[len(outs) :]
+        return (dq if last else dq[0]), part
 
     def send_back(turn, part):
         return lax.ppermute(part, "pb", y_step(Y_FROM[turn]))
 
     both = (0, 1)
     parts = []
-    dq1 = None
+    dq = None
     for turn in range(4):
-        dq1, (part,) = grad(turn, both, (1,), (dq1,), (turn == 3,), F32)
-        dq1 = dq1[0] if turn < 3 else dq1
+        dq, part = grad(turn, 0, dq, None, turn == 3, F32)
         parts.append(part)
-    dq_back = [lax.ppermute(d, "kz", p) for d, p in zip(dq1, (z_step(-1), z_step(1)))]
-    q_pairs[0][1], parts[3] = lax.optimization_barrier((q_pairs[0][1], parts[3]))
+    dq_keep, *dqs = dq
+    dq_back = [lax.ppermute(d, "kz", p) for d, p in zip(dqs, (z_step(-1), z_step(1)))]
+    q_groups[1][0], parts[3] = lax.optimization_barrier((q_groups[1][0], parts[3]))
     back = []
-    dq0 = None
+    dq = None
     for turn in (1, 2, 3):
-        (dq0,), (part,) = grad(turn, both, (0,), (dq0,), (False,), BF16, add=parts[turn])
+        dq, part = grad(turn, 1, dq, parts[turn], False, BF16)
         back.append(send_back(turn, part))
-    dq0, back[0] = lax.optimization_barrier((dq0, back[0]))
-    (dq_keep, dq_z2), (own,) = grad(0, both, (0,), (dq0,), (True,), F32, add=parts[0])
+    dq, back[0] = lax.optimization_barrier((dq, back[0]))
+    (dq_z2,), own = grad(0, 1, dq, parts[0], True, F32)
     dq_back.append(lax.ppermute(dq_z2, "kz", Z_BACK))
 
     def meet(operands, parts, shape):

time: 64 us -> 61.4 us (0.959)
  waiting for transfers between devices: 10.1 us -> 6.67 us
    ppermute x1, waiting for transfers between devices: 4.76 us -> 1.31 us  [body(): dq_back.append(lax.ppermute(dq_z2, 'kz', Z_BACK))]
    ppermute x1, waiting for transfers between devices: 3.44 us -> 1.24 us  [body(): dq_last = lax.ppermute(dq_send, 'kx', X_SWAP)]
    ppermute x1, waiting for transfers between devices: 0.01 us -> 2.18 us  [body(): dkv_last = lax.ppermute(dkv_send, 'kz', z_step(4))]
    ppermute x1, starting transfers between devices: 1.31 us -> 2.65 us  [body(): dq_back.append(lax.ppermute(dq_z2, 'kz', Z_BACK))]
    ppermute x3, starting transfers between devices: 4.26 us -> 3.41 us  [send_back(): return lax.ppermute(part, 'pb', y_step(Y_FROM[turn]))]
  transfers between devices with their start and end apart: 16 -> 16, of which waited for: 3 -> 4; matrix products, arithmetic and copies ran while one was open for 2% -> 2% of each run, Pallas kernels for 13% -> 14%
where the time goes in v15:
time: 61.4 us; the launch traced here: 61 us
  starting transfers between devices  40.6 us (66%)
  Pallas kernels  12 us (20%)
  waiting for transfers between devices  6.67 us (11%)
  local copies, waits for them, and re-layouts  0.96 us (2%)
  between operations  0.78 us (1%)
    pallas_call x12, Pallas kernels, call(): pl.pallas_call(kernel, out_shape=[jax.ShapeDtypeStruct(s, t) for s, t in...  12 us
    ppermute x3, starting transfers between devices, body(): lax.ppermute(q, 'kz', p)  9 us
    ppermute x1, starting transfers between devices, body(): other_k = lax.ppermute(mine_k, 'kz', z_step(4))  7.19 us
    ppermute x3, starting transfers between devices, body(): k_sets = [k0] + [lax.ppermute(k0, 'pb', y_step(-s)) for s in Y_FROM[1:]]  6.52 us
    ppermute x2, starting transfers between devices, body(): lax.ppermute(d, 'kz', p)  5.03 us
    ppermute x1, starting transfers between devices, body(): dkv_last = lax.ppermute(dkv_send, 'kz', z_step(4))  4.57 us
    ppermute x3, starting transfers between devices, send_back(): return lax.ppermute(part, 'pb', y_step(Y_FROM[turn]))  3.41 us
    ppermute x1, starting transfers between devices, body(): dq_back.append(lax.ppermute(dq_z2, 'kz', Z_BACK))  2.65 us
  transfers between devices with their start and end apart: 16, of which 4 were waited for; matrix products, arithmetic and copies ran while one was open for 2% of the time, Pallas kernels for 14%

profile of v15, /device:TPU:4, one launch (start us, length us, event | category | flops | bytes accessed | tf_op | source)
XLA Modules:
  0.0 61.0 jit_solution(1643739690154934027)
XLA Ops:
  0.6 1.8 %shard_map.94 = (bf16[528,128]{1,0:T(8,128)(2,1)}, bf16[528,128]{1,0:T(8,128)(2,1)}) custom-call(s32[128]{0:T(128)} %refs_0_.1, bf16[256,128]{1,0:T(8,128)(2,1)} %refs_1_.1, bf16[256,128]{1,0:T(8,128)(2,1)} %refs_2_.1, bf16[1,256]{1,0:T(2,128)(2,1)} %bitcast.9, bf16[256,128]{1,0:T(8,128)(2,1)} %refs_4_.1, bf16[256,128]{1,0:T(8,128)(2,1)} %refs_5_.1, ...), custom_call_target="tpu_custom_call" | custom-call | tf_op jit(solution)/shard_map/pallas_call | solution.py:208
  2.5 1.3 %collective-permute-start = (bf16[528,128]{1,0:T(8,128)(2,1)}, bf16[528,128]{1,0:T(8,128)(2,1)S(1)}, u32[]{:S(2)}, u32[]{:S(2)}) collective-permute-start(bf16[528,128]{1,0:T(8,128)(2,1)} %get-tuple-element.33), channel_id=1, source_target_pairs={{0,4},{4,0},{1,5},{5,1},{2,6},{6,2},{3,7},{7,3},{8,12},{12,8},{9,1... | collective-permute-start | bytes 405512 | tf_op jit(solution)/shard_map/ppermute | solution.py:232
  3.7 7.2 %collective-permute-start.3 = (bf16[528,128]{1,0:T(8,128)(2,1)}, bf16[528,128]{1,0:T(8,128)(2,1)S(1)}, u32[]{:S(2)}, u32[]{:S(2)}) collective-permute-start(bf16[528,128]{1,0:T(8,128)(2,1)} %get-tuple-element.34), channel_id=1, source_target_pairs={{0,32},{8,40},{16,48},{24,56},{32,0},{40,8},{48,16},{56,24},{1,33}... | collective-permute-start | bytes 405512 | tf_op jit(solution)/shard_map/ppermute | solution.py:231
  10.9 0.9 %pad.4 = bf16[2,528,128]{2,1,0:T(8,128)(2,1)S(1)} pad(bf16[1,528,128]{2,1,0:T(8,128)(2,1)} %bitcast.6, bf16[]{:T(256)} %constant.1.clone.1), padding=0_1x0_0x0_0 | pad | bytes 405506 | tf_op jit(solution)/shard_map/jit(_pad)/pad | solution.py:228
  11.9 1.1 %collective-permute-start.1 = (bf16[2,528,128]{2,1,0:T(8,128)(2,1)S(1)}, bf16[2,528,128]{2,1,0:T(8,128)(2,1)S(1)}, u32[]{:S(2)}, u32[]{:S(2)}) collective-permute-start(bf16[2,528,128]{2,1,0:T(8,128)(2,1)S(1)} %bitcast_dynamic-update-slice_fusion.refs_0_.rows_ref), channel_id=1, source_target_pairs={{0,8},{8,16},{16,24},{24,32},{32,40},{40,48},{48,56},{56,0},{1,9},... | collective-permute-start | bytes 811016 | tf_op jit(solution)/shard_map/ppermute | solution.py:235
  13.0 2.2 %collective-permute-start.2 = (bf16[2,528,128]{2,1,0:T(8,128)(2,1)S(1)}, bf16[2,528,128]{2,1,0:T(8,128)(2,1)S(1)}, u32[]{:S(2)}, u32[]{:S(2)}) collective-permute-start(bf16[2,528,128]{2,1,0:T(8,128)(2,1)S(1)} %bitcast_dynamic-update-slice_fusion.refs_0_.rows_ref), channel_id=1, source_target_pairs={{0,56},{8,0},{16,8},{24,16},{32,24},{40,32},{48,40},{56,48},{1,57}... | collective-permute-start | bytes 811016 | tf_op jit(solution)/shard_map/ppermute | solution.py:235
  15.2 1.9 %collective-permute-done.3 = bf16[528,128]{1,0:T(8,128)(2,1)S(1)} collective-permute-done((bf16[528,128]{1,0:T(8,128)(2,1)}, bf16[528,128]{1,0:T(8,128)(2,1)S(1)}, u32[]{:S(2)}, u32[]{:S(2)}) %collective-permute-start.3) | collective-permute-done | bytes 135200 | tf_op jit(solution)/shard_map/ppermute | solution.py:231
  17.2 3.3 %collective-permute-start.6 = (bf16[2,528,128]{2,1,0:T(8,128)(2,1)S(1)}, bf16[2,528,128]{2,1,0:T(8,128)(2,1)S(1)}, u32[]{:S(2)}, u32[]{:S(2)}) collective-permute-start(bf16[2,528,128]{2,1,0:T(8,128)(2,1)S(1)} %pad_maximum_fusion.refs_3_.refs_1_), channel_id=1, source_target_pairs={{0,128},{64,192},{128,0},{192,64},{1,129},{65,193},{129,1},{193,65... | collective-permute-start | bytes 811016 | tf_op jit(solution)/shard_map/ppermute | solution.py:236
  21.1 2.6 %collective-permute-start.4 = (bf16[2,528,128]{2,1,0:T(8,128)(2,1)S(1)}, bf16[2,528,128]{2,1,0:T(8,128)(2,1)S(1)}, u32[]{:S(2)}, u32[]{:S(2)}) collective-permute-start(bf16[2,528,128]{2,1,0:T(8,128)(2,1)S(1)} %pad_maximum_fusion.refs_3_.refs_1_), channel_id=1, source_target_pairs={{0,192},{64,0},{128,64},{192,128},{1,193},{65,1},{129,65},{193,129... | collective-permute-start | bytes 811016 | tf_op jit(solution)/shard_map/ppermute | solution.py:236
  23.7 5.7 %collective-permute-start.9 = (bf16[2,528,128]{2,1,0:T(8,128)(2,1)S(1)}, bf16[2,528,128]{2,1,0:T(8,128)(2,1)S(1)}, u32[]{:S(2)}, u32[]{:S(2)}) collective-permute-start(bf16[2,528,128]{2,1,0:T(8,128)(2,1)S(1)} %bitcast_dynamic-update-slice_fusion.refs_0_.rows_ref), channel_id=1, source_target_pairs={{0,48},{8,24},{16,0},{24,40},{32,16},{40,56},{48,32},{56,8},{1,49}... | collective-permute-start | bytes 811016 | tf_op jit(solution)/shard_map/ppermute | solution.py:235
  29.4 1.6 %shard_map.95 = (f32[2,128,768]{2,1,0:T(8,128)S(1)}, f32[2,512,128]{2,1,0:T(8,128)S(1)}) custom-call(bf16[2,528,128]{2,1,0:T(8,128)(2,1)S(1)} %bitcast_dynamic-update-slice_fusion.refs_0_.rows_ref, bf16[2,528,128]{2,1,0:T(8,128)(2,1)S(1)} %collective-permute-done.1.refs_1_, bf16[2,528,128]{2,1,0:T(8,128)(2,1)S(1)} %collective-permute-done.2.refs_2_, ...), custom_call_target="tpu_custom_call" | custom-call | flops 500000000 | bytes 1000000 | tf_op jit(solution)/shard_map/pallas_call | solution.py:208
  31.0 1.6 %shard_map.96 = (f32[2,128,768]{2,1,0:T(8,128)S(1)}, f32[2,512,128]{2,1,0:T(8,128)S(1)}) custom-call(bf16[2,528,128]{2,1,0:T(8,128)(2,1)S(1)} %bitcast_dynamic-update-slice_fusion.refs_0_.rows_ref, bf16[2,528,128]{2,1,0:T(8,128)(2,1)S(1)} %collective-permute-done.1.refs_1_, bf16[2,528,128]{2,1,0:T(8,128)(2,1)S(1)} %collective-permute-done.2.refs_2_, ...), custom_call_target="tpu_custom_call" | custom-call | flops 500000000 | bytes 1000000 | tf_op jit(solution)/shard_map/pallas_call | solution.py:208
  32.6 1.6 %shard_map.97 = (f32[2,128,768]{2,1,0:T(8,128)S(1)}, f32[2,512,128]{2,1,0:T(8,128)S(1)}) custom-call(bf16[2,528,128]{2,1,0:T(8,128)(2,1)S(1)} %bitcast_dynamic-update-slice_fusion.refs_0_.rows_ref, bf16[2,528,128]{2,1,0:T(8,128)(2,1)S(1)} %collective-permute-done.1.refs_1_, bf16[2,528,128]{2,1,0:T(8,128)(2,1)S(1)} %collective-permute-done.2.refs_2_, ...), custom_call_target="tpu_custom_call" | custom-call | flops 500000000 | bytes 1000000 | tf_op jit(solution)/shard_map/pallas_call | solution.py:208
  34.1 1.7 %shard_map.98 = (f32[2,256,128]{2,1,0:T(8,128)S(1)}, bf16[2,256,128]{2,1,0:T(8,128)(2,1)S(1)}, bf16[2,256,128]{2,1,0:T(8,128)(2,1)S(1)}, f32[2,512,128]{2,1,0:T(8,128)S(1)}) custom-call(bf16[2,528,128]{2,1,0:T(8,128)(2,1)S(1)} %bitcast_dynamic-update-slice_fusion.refs_0_.rows_ref, bf16[2,528,128]{2,1,0:T(8,128)(2,1)S(1)} %collective-permute-done.1.refs_1_, ...), custom_call_target="tpu_custom_call" | custom-call | flops 500000000 | bytes 1000000 | tf_op jit(solution)/shard_map/pallas_call | solution.py:208
  38.1 0.9 %collective-permute-start.14 = (bf16[2,512,128]{2,1,0:T(8,128)(2,1)S(1)}, bf16[2,512,128]{2,1,0:T(8,128)(2,1)S(1)}, u32[]{:S(2)}, u32[]{:S(2)}) collective-permute-start(bf16[2,512,128]{2,1,0:T(8,128)(2,1)S(1)} %get-tuple-element.60), channel_id=1, source_target_pairs={{0,64},{64,128},{128,192},{192,0},{1,65},{65,129},{129,193},{193,1... | collective-permute-start | bytes 786440 | tf_op jit(solution)/shard_map/ppermute | solution.py:256
  39.1 2.4 %collective-permute-start.13 = (bf16[2,512,128]{2,1,0:T(8,128)(2,1)S(1)}, bf16[2,512,128]{2,1,0:T(8,128)(2,1)S(1)}, u32[]{:S(2)}, u32[]{:S(2)}) collective-permute-start(bf16[2,512,128]{2,1,0:T(8,128)(2,1)S(1)} %get-tuple-element.59), channel_id=1, source_target_pairs={{0,192},{64,0},{128,64},{192,128},{1,193},{65,1},{129,65},{193,129... | collective-permute-start | bytes 786440 | tf_op jit(solution)/shard_map/ppermute | solution.py:256
  41.4 5.0 %collective-permute-start.7 = (bf16[2,256,128]{2,1,0:T(8,128)(2,1)S(1)}, bf16[2,256,128]{2,1,0:T(8,128)(2,1)S(1)}, u32[]{:S(2)}, u32[]{:S(2)}) collective-permute-start(bf16[2,256,128]{2,1,0:T(8,128)(2,1)S(1)} %get-tuple-element.40), channel_id=1, source_target_pairs={{0,56},{8,0},{16,8},{24,16},{32,24},{40,32},{48,40},{56,48},{1,57}... | collective-permute-start | bytes 393224 | tf_op jit(solution)/shard_map/ppermute | solution.py:265
  46.5 0.8 %shard_map.102 = (bf16[2,256,128]{2,1,0:T(8,128)(2,1)S(1)}, f32[2,512,128]{2,1,0:T(8,128)S(1)}) custom-call(bf16[2,528,128]{2,1,0:T(8,128)(2,1)S(1)} %collective-permute-done.9.refs_0_, bf16[2,528,128]{2,1,0:T(8,128)(2,1)S(1)} %pad_maximum_fusion.refs_3_.refs_1_, f32[2,128,256]{2,1,0:T(8,128)S(1)} %get-tuple-element.52.refs_2_, ...), custom_call_target="tpu_custom_call" | custom-call | flops 500000000 | bytes 1000000 | tf_op jit(solution)/shard_map/pallas_call | solution.py:208
  47.3 2.6 %collective-permute-start.11 = (bf16[2,256,128]{2,1,0:T(8,128)(2,1)S(1)}, bf16[2,256,128]{2,1,0:T(8,128)(2,1)S(1)}, u32[]{:S(2)}, u32[]{:S(2)}) collective-permute-start(bf16[2,256,128]{2,1,0:T(8,128)(2,1)S(1)} %get-tuple-element.54), channel_id=1, source_target_pairs={{48,0},{24,8},{0,16},{40,24},{16,32},{56,40},{32,48},{8,56},{49,1}... | collective-permute-start | bytes 393224 | tf_op jit(solution)/shard_map/ppermute | solution.py:274
  50.0 4.6 %collective-permute-start.15 = (bf16[512,128]{1,0:T(8,128)(2,1)S(1)}, bf16[512,128]{1,0:T(8,128)(2,1)S(1)}, u32[]{:S(2)}, u32[]{:S(2)}) collective-permute-start(bf16[512,128]{1,0:T(8,128)(2,1)S(1)} %get-tuple-element.62), channel_id=1, source_target_pairs={{0,32},{8,40},{16,48},{24,56},{32,0},{40,8},{48,16},{56,24},{1,33}... | collective-permute-start | bytes 393224 | tf_op jit(solution)/shard_map/ppermute | solution.py:282
  54.6 1.3 %collective-permute-done.11.refs_3_ = bf16[2,256,128]{2,1,0:T(8,128)(2,1)S(1)} collective-permute-done((bf16[2,256,128]{2,1,0:T(8,128)(2,1)S(1)}, bf16[2,256,128]{2,1,0:T(8,128)(2,1)S(1)}, u32[]{:S(2)}, u32[]{:S(2)}) %collective-permute-start.11) | collective-permute-done | bytes 131104 | tf_op jit(solution)/shard_map/ppermute | solution.py:274
  56.0 0.9 %collective-permute-start.12 = (bf16[256,128]{1,0:T(8,128)(2,1)S(1)}, bf16[256,128]{1,0:T(8,128)(2,1)S(1)}, u32[]{:S(2)}, u32[]{:S(2)}) collective-permute-start(bf16[256,128]{1,0:T(8,128)(2,1)S(1)} %get-tuple-element.56), channel_id=1, source_target_pairs={{0,4},{4,0},{1,5},{5,1},{2,6},{6,2},{3,7},{7,3},{8,12},{12,8},{9,1... | collective-permute-start | bytes 196616 | tf_op jit(solution)/shard_map/ppermute | solution.py:284
  56.9 2.2 %collective-permute-done.15.dkvz_ref = bf16[512,128]{1,0:T(8,128)(2,1)S(1)} collective-permute-done((bf16[512,128]{1,0:T(8,128)(2,1)S(1)}, bf16[512,128]{1,0:T(8,128)(2,1)S(1)}, u32[]{:S(2)}, u32[]{:S(2)}) %collective-permute-start.15) | collective-permute-done | bytes 131104 | tf_op jit(solution)/shard_map/ppermute | solution.py:282
  59.1 1.2 %collective-permute-done.12.dqx_ref = bf16[256,128]{1,0:T(8,128)(2,1)S(1)} collective-permute-done((bf16[256,128]{1,0:T(8,128)(2,1)S(1)}, bf16[256,128]{1,0:T(8,128)(2,1)S(1)}, u32[]{:S(2)}, u32[]{:S(2)}) %collective-permute-start.12) | collective-permute-done | bytes 65568 | tf_op jit(solution)/shard_map/ppermute | solution.py:284
  (25 shorter events, 3.9 us)
Async XLA Ops:
  2.5 9.4 %collective-permute-start = (bf16[528,128]{1,0:T(8,128)(2,1)}, bf16[528,128]{1,0:T(8,128)(2,1)S(1)}, u32[]{:S(2)}, u32[]{:S(2)}) collective-permute-start(bf16[528,128]{1,0:T(8,128)(2,1)} %get-tuple-element.33), channel_id=1, source_target_pairs={{0,4},{4,0},{1,5},{5,1},{2,6},{6,2},{3,7},{7,3},{8,12},{12,8},{9,1... | collective-permute-start | bytes 405512 | tf_op jit(solution)/shard_map/ppermute | solution.py:232
  3.7 13.4 %collective-permute-start.3 = (bf16[528,128]{1,0:T(8,128)(2,1)}, bf16[528,128]{1,0:T(8,128)(2,1)S(1)}, u32[]{:S(2)}, u32[]{:S(2)}) collective-permute-start(bf16[528,128]{1,0:T(8,128)(2,1)} %get-tuple-element.34), channel_id=1, source_target_pairs={{0,32},{8,40},{16,48},{24,56},{32,0},{40,8},{48,16},{56,24},{1,33}... | collective-permute-start | bytes 405512 | tf_op jit(solution)/shard_map/ppermute | solution.py:231
  11.9 5.3 %copy-start = (bf16[528,128]{1,0:T(8,128)(2,1)S(1)}, bf16[528,128]{1,0:T(8,128)(2,1)}, u32[]{:S(2)}) copy-start(bf16[528,128]{1,0:T(8,128)(2,1)} %get-tuple-element.34) | copy-start | bytes 405508
  11.9 11.8 %collective-permute-start.1 = (bf16[2,528,128]{2,1,0:T(8,128)(2,1)S(1)}, bf16[2,528,128]{2,1,0:T(8,128)(2,1)S(1)}, u32[]{:S(2)}, u32[]{:S(2)}) collective-permute-start(bf16[2,528,128]{2,1,0:T(8,128)(2,1)S(1)} %bitcast_dynamic-update-slice_fusion.refs_0_.rows_ref), channel_id=1, source_target_pairs={{0,8},{8,16},{16,24},{24,32},{32,40},{40,48},{48,56},{56,0},{1,9},... | collective-permute-start | bytes 811016 | tf_op jit(solution)/shard_map/ppermute | solution.py:235
  13.0 16.4 %collective-permute-start.2 = (bf16[2,528,128]{2,1,0:T(8,128)(2,1)S(1)}, bf16[2,528,128]{2,1,0:T(8,128)(2,1)S(1)}, u32[]{:S(2)}, u32[]{:S(2)}) collective-permute-start(bf16[2,528,128]{2,1,0:T(8,128)(2,1)S(1)} %bitcast_dynamic-update-slice_fusion.refs_0_.rows_ref), channel_id=1, source_target_pairs={{0,56},{8,0},{16,8},{24,16},{32,24},{40,32},{48,40},{56,48},{1,57}... | collective-permute-start | bytes 811016 | tf_op jit(solution)/shard_map/ppermute | solution.py:235
  17.2 13.8 %collective-permute-start.6 = (bf16[2,528,128]{2,1,0:T(8,128)(2,1)S(1)}, bf16[2,528,128]{2,1,0:T(8,128)(2,1)S(1)}, u32[]{:S(2)}, u32[]{:S(2)}) collective-permute-start(bf16[2,528,128]{2,1,0:T(8,128)(2,1)S(1)} %pad_maximum_fusion.refs_3_.refs_1_), channel_id=1, source_target_pairs={{0,128},{64,192},{128,0},{192,64},{1,129},{65,193},{129,1},{193,65... | collective-permute-start | bytes 811016 | tf_op jit(solution)/shard_map/ppermute | solution.py:236
  20.5 12.1 %collective-permute-start.5 = (bf16[2,528,128]{2,1,0:T(8,128)(2,1)S(1)}, bf16[2,528,128]{2,1,0:T(8,128)(2,1)S(1)}, u32[]{:S(2)}, u32[]{:S(2)}) collective-permute-start(bf16[2,528,128]{2,1,0:T(8,128)(2,1)S(1)} %pad_maximum_fusion.refs_3_.refs_1_), channel_id=1, source_target_pairs={{0,64},{64,128},{128,192},{192,0},{1,65},{65,129},{129,193},{193,1... | collective-permute-start | bytes 811016 | tf_op jit(solution)/shard_map/ppermute | solution.py:236
  21.1 13.0 %collective-permute-start.4 = (bf16[2,528,128]{2,1,0:T(8,128)(2,1)S(1)}, bf16[2,528,128]{2,1,0:T(8,128)(2,1)S(1)}, u32[]{:S(2)}, u32[]{:S(2)}) collective-permute-start(bf16[2,528,128]{2,1,0:T(8,128)(2,1)S(1)} %pad_maximum_fusion.refs_3_.refs_1_), channel_id=1, source_target_pairs={{0,192},{64,0},{128,64},{192,128},{1,193},{65,1},{129,65},{193,129... | collective-permute-start | bytes 811016 | tf_op jit(solution)/shard_map/ppermute | solution.py:236
  23.7 12.1 %collective-permute-start.9 = (bf16[2,528,128]{2,1,0:T(8,128)(2,1)S(1)}, bf16[2,528,128]{2,1,0:T(8,128)(2,1)S(1)}, u32[]{:S(2)}, u32[]{:S(2)}) collective-permute-start(bf16[2,528,128]{2,1,0:T(8,128)(2,1)S(1)} %bitcast_dynamic-update-slice_fusion.refs_0_.rows_ref), channel_id=1, source_target_pairs={{0,48},{8,24},{16,0},{24,40},{32,16},{40,56},{48,32},{56,8},{1,49}... | collective-permute-start | bytes 811016 | tf_op jit(solution)/shard_map/ppermute | solution.py:235
  36.6 9.9 %collective-permute-start.10 = (bf16[2,512,128]{2,1,0:T(8,128)(2,1)S(1)}, bf16[2,512,128]{2,1,0:T(8,128)(2,1)S(1)}, u32[]{:S(2)}, u32[]{:S(2)}) collective-permute-start(bf16[2,512,128]{2,1,0:T(8,128)(2,1)S(1)} %get-tuple-element.51), channel_id=1, source_target_pairs={{0,128},{64,192},{128,0},{192,64},{1,129},{65,193},{129,1},{193,65... | collective-permute-start | bytes 786440 | tf_op jit(solution)/shard_map/ppermute | solution.py:256
  38.1 11.8 %collective-permute-start.14 = (bf16[2,512,128]{2,1,0:T(8,128)(2,1)S(1)}, bf16[2,512,128]{2,1,0:T(8,128)(2,1)S(1)}, u32[]{:S(2)}, u32[]{:S(2)}) collective-permute-start(bf16[2,512,128]{2,1,0:T(8,128)(2,1)S(1)} %get-tuple-element.60), channel_id=1, source_target_pairs={{0,64},{64,128},{128,192},{192,0},{1,65},{65,129},{129,193},{193,1... | collective-permute-start | bytes 786440 | tf_op jit(solution)/shard_map/ppermute | solution.py:256
  39.1 10.9 %collective-permute-start.13 = (bf16[2,512,128]{2,1,0:T(8,128)(2,1)S(1)}, bf16[2,512,128]{2,1,0:T(8,128)(2,1)S(1)}, u32[]{:S(2)}, u32[]{:S(2)}) collective-permute-start(bf16[2,512,128]{2,1,0:T(8,128)(2,1)S(1)} %get-tuple-element.59), channel_id=1, source_target_pairs={{0,192},{64,0},{128,64},{192,128},{1,193},{65,1},{129,65},{193,129... | collective-permute-start | bytes 786440 | tf_op jit(solution)/shard_map/ppermute | solution.py:256
  41.4 13.2 %collective-permute-start.7 = (bf16[2,256,128]{2,1,0:T(8,128)(2,1)S(1)}, bf16[2,256,128]{2,1,0:T(8,128)(2,1)S(1)}, u32[]{:S(2)}, u32[]{:S(2)}) collective-permute-start(bf16[2,256,128]{2,1,0:T(8,128)(2,1)S(1)} %get-tuple-element.40), channel_id=1, source_target_pairs={{0,56},{8,0},{16,8},{24,16},{32,24},{40,32},{48,40},{56,48},{1,57}... | collective-permute-start | bytes 393224 | tf_op jit(solution)/shard_map/ppermute | solution.py:265
  46.5 8.1 %collective-permute-start.8 = (bf16[2,256,128]{2,1,0:T(8,128)(2,1)S(1)}, bf16[2,256,128]{2,1,0:T(8,128)(2,1)S(1)}, u32[]{:S(2)}, u32[]{:S(2)}) collective-permute-start(bf16[2,256,128]{2,1,0:T(8,128)(2,1)S(1)} %get-tuple-element.41), channel_id=1, source_target_pairs={{0,8},{8,16},{16,24},{24,32},{32,40},{40,48},{48,56},{56,0},{1,9},... | collective-permute-start | bytes 393224 | tf_op jit(solution)/shard_map/ppermute | solution.py:265
  47.3 8.6 %collective-permute-start.11 = (bf16[2,256,128]{2,1,0:T(8,128)(2,1)S(1)}, bf16[2,256,128]{2,1,0:T(8,128)(2,1)S(1)}, u32[]{:S(2)}, u32[]{:S(2)}) collective-permute-start(bf16[2,256,128]{2,1,0:T(8,128)(2,1)S(1)} %get-tuple-element.54), channel_id=1, source_target_pairs={{48,0},{24,8},{0,16},{40,24},{16,32},{56,40},{32,48},{8,56},{49,1}... | collective-permute-start | bytes 393224 | tf_op jit(solution)/shard_map/ppermute | solution.py:274
  50.0 9.1 %collective-permute-start.15 = (bf16[512,128]{1,0:T(8,128)(2,1)S(1)}, bf16[512,128]{1,0:T(8,128)(2,1)S(1)}, u32[]{:S(2)}, u32[]{:S(2)}) collective-permute-start(bf16[512,128]{1,0:T(8,128)(2,1)S(1)} %get-tuple-element.62), channel_id=1, source_target_pairs={{0,32},{8,40},{16,48},{24,56},{32,0},{40,8},{48,16},{56,24},{1,33}... | collective-permute-start | bytes 393224 | tf_op jit(solution)/shard_map/ppermute | solution.py:282
  56.0 4.4 %collective-permute-start.12 = (bf16[256,128]{1,0:T(8,128)(2,1)S(1)}, bf16[256,128]{1,0:T(8,128)(2,1)S(1)}, u32[]{:S(2)}, u32[]{:S(2)}) collective-permute-start(bf16[256,128]{1,0:T(8,128)(2,1)S(1)} %get-tuple-element.56), channel_id=1, source_target_pairs={{0,4},{4,0},{1,5},{5,1},{2,6},{6,2},{3,7},{7,3},{8,12},{12,8},{9,1... | collective-permute-start | bytes 196616 | tf_op jit(solution)/shard_map/ppermute | solution.py:284

commit v16 on v15

--- a/solution.py
+++ b/solution.py
@@ -232,7 +232,7 @@
     q0 = beside(mine_q, lax.ppermute(mine_q, "kx", X_SWAP))
     late_q, other_k = lax.optimization_barrier((q0, other_k))
     k0 = jnp.stack([mine_k, other_k])
-    q_sets = [q0] + [lax.ppermute(q, "kz", p) for q, p in ((q0, z_step(1)), (q0, z_step(-1)), (late_q, Z_PAIRS))]
+    q_sets = [q0] + [lax.ppermute(q, "kz", p) for q, p in ((q0, z_step(1)), (q0, Z_PAIRS), (late_q, z_step(-1)))]
     k_sets = [k0] + [lax.ppermute(k0, "pb", y_step(-s)) for s in Y_FROM[1:]]
     q_groups = [q_sets[:3], q_sets[3:]]
 
@@ -262,7 +262,7 @@
         dq, part = grad(turn, 0, dq, None, turn == 3, F32)
         parts.append(part)
     dq_keep, *dqs = dq
-    dq_back = [lax.ppermute(d, "kz", p) for d, p in zip(dqs, (z_step(-1), z_step(1)))]
+    dq_back = [lax.ppermute(d, "kz", p) for d, p in zip(dqs, (z_step(-1), Z_BACK))]
     q_groups[1][0], parts[3] = lax.optimization_barrier((q_groups[1][0], parts[3]))
     back = []
     dq = None
@@ -270,8 +270,8 @@
         dq, part = grad(turn, 1, dq, parts[turn], False, BF16)
         back.append(send_back(turn, part))
     dq, back[0] = lax.optimization_barrier((dq, back[0]))
-    (dq_z2,), own = grad(0, 1, dq, parts[0], True, F32)
-    dq_back.append(lax.ppermute(dq_z2, "kz", Z_BACK))
+    (dq_late,), own = grad(0, 1, dq, parts[0], True, F32)
+    dq_back.append(lax.ppermute(dq_late, "kz", z_step(1)))
 
     def meet(operands, parts, shape):
         return call(functools.partial(meet_kernel, parts), [(shape, F32), (shape, BF16)], operands)

time: 61.4 us -> 64.9 us (1.057)
  the two profiles are of different devices: /device:TPU:4 before, /device:TPU:8 now
where the time goes in v16:
time: 64.9 us; the launch traced here: 64.7 us
  starting transfers between devices  37.6 us (58%)
  waiting for transfers between devices  13.4 us (21%)
  Pallas kernels  12 us (18%)
  local copies, waits for them, and re-layouts  0.96 us (1%)
  between operations  0.76 us (1%)
    pallas_call x12, Pallas kernels, call(): pl.pallas_call(kernel, out_shape=[jax.ShapeDtypeStruct(s, t) for s, t in...  12 us
    ppermute x1, starting transfers between devices, body(): dkv_last = lax.ppermute(dkv_send, 'kz', z_step(4))  7.41 us
    ppermute x1, starting transfers between devices, body(): other_k = lax.ppermute(mine_k, 'kz', z_step(4))  7.19 us
    ppermute x1, waiting for transfers between devices, body(): dkv_last = lax.ppermute(dkv_send, 'kz', z_step(4))  6.44 us
    ppermute x3, starting transfers between devices, body(): lax.ppermute(q, 'kz', p)  4.68 us
    ppermute x3, starting transfers between devices, send_back(): return lax.ppermute(part, 'pb', y_step(Y_FROM[turn]))  4.48 us
    ppermute x3, starting transfers between devices, body(): k_sets = [k0] + [lax.ppermute(k0, 'pb', y_step(-s)) for s in Y_FROM[1:]]  4.41 us
    ppermute x1, starting transfers between devices, body(): dq_back.append(lax.ppermute(dq_late, 'kz', z_step(1)))  3.92 us
  transfers between devices with their start and end apart: 16, of which 6 were waited for; matrix products, arithmetic and copies ran while one was open for 2% of the time, Pallas kernels for 14%

profile of v16, /device:TPU:8, one launch (start us, length us, event | category | flops | bytes accessed | tf_op | source)
XLA Modules:
  0.0 64.7 jit_solution(4407547269795094801)
XLA Ops:
  0.6 1.8 %shard_map.94 = (bf16[528,128]{1,0:T(8,128)(2,1)}, bf16[528,128]{1,0:T(8,128)(2,1)}) custom-call(s32[128]{0:T(128)} %refs_0_.1, bf16[256,128]{1,0:T(8,128)(2,1)} %refs_1_.1, bf16[256,128]{1,0:T(8,128)(2,1)} %refs_2_.1, bf16[1,256]{1,0:T(2,128)(2,1)} %bitcast.9, bf16[256,128]{1,0:T(8,128)(2,1)} %refs_4_.1, bf16[256,128]{1,0:T(8,128)(2,1)} %refs_5_.1, ...), custom_call_target="tpu_custom_call" | custom-call | tf_op jit(solution)/shard_map/pallas_call | solution.py:208
  2.5 1.6 %collective-permute-start = (bf16[528,128]{1,0:T(8,128)(2,1)}, bf16[528,128]{1,0:T(8,128)(2,1)S(1)}, u32[]{:S(2)}, u32[]{:S(2)}) collective-permute-start(bf16[528,128]{1,0:T(8,128)(2,1)} %get-tuple-element.33), channel_id=1, source_target_pairs={{0,4},{4,0},{1,5},{5,1},{2,6},{6,2},{3,7},{7,3},{8,12},{12,8},{9,1... | collective-permute-start | bytes 405512 | tf_op jit(solution)/shard_map/ppermute | solution.py:232
  4.0 7.2 %collective-permute-start.3 = (bf16[528,128]{1,0:T(8,128)(2,1)}, bf16[528,128]{1,0:T(8,128)(2,1)S(1)}, u32[]{:S(2)}, u32[]{:S(2)}) collective-permute-start(bf16[528,128]{1,0:T(8,128)(2,1)} %get-tuple-element.34), channel_id=1, source_target_pairs={{0,32},{8,40},{16,48},{24,56},{32,0},{40,8},{48,16},{56,24},{1,33}... | collective-permute-start | bytes 405512 | tf_op jit(solution)/shard_map/ppermute | solution.py:231
  11.2 0.9 %pad.4 = bf16[2,528,128]{2,1,0:T(8,128)(2,1)S(1)} pad(bf16[1,528,128]{2,1,0:T(8,128)(2,1)} %bitcast.6, bf16[]{:T(256)} %constant.1.clone.1), padding=0_1x0_0x0_0 | pad | bytes 405506 | tf_op jit(solution)/shard_map/jit(_pad)/pad | solution.py:228
  12.2 1.1 %collective-permute-start.1 = (bf16[2,528,128]{2,1,0:T(8,128)(2,1)S(1)}, bf16[2,528,128]{2,1,0:T(8,128)(2,1)S(1)}, u32[]{:S(2)}, u32[]{:S(2)}) collective-permute-start(bf16[2,528,128]{2,1,0:T(8,128)(2,1)S(1)} %bitcast_dynamic-update-slice_fusion.refs_0_.rows_ref), channel_id=1, source_target_pairs={{0,8},{8,16},{16,24},{24,32},{32,40},{40,48},{48,56},{56,0},{1,9},... | collective-permute-start | bytes 811016 | tf_op jit(solution)/shard_map/ppermute | solution.py:235
  13.3 2.2 %collective-permute-start.2 = (bf16[2,528,128]{2,1,0:T(8,128)(2,1)S(1)}, bf16[2,528,128]{2,1,0:T(8,128)(2,1)S(1)}, u32[]{:S(2)}, u32[]{:S(2)}) collective-permute-start(bf16[2,528,128]{2,1,0:T(8,128)(2,1)S(1)} %bitcast_dynamic-update-slice_fusion.refs_0_.rows_ref), channel_id=1, source_target_pairs={{0,48},{8,24},{16,0},{24,40},{32,16},{40,56},{48,32},{56,8},{1,49}... | collective-permute-start | bytes 811016 | tf_op jit(solution)/shard_map/ppermute | solution.py:235
  15.5 1.9 %collective-permute-done.3 = bf16[528,128]{1,0:T(8,128)(2,1)S(1)} collective-permute-done((bf16[528,128]{1,0:T(8,128)(2,1)}, bf16[528,128]{1,0:T(8,128)(2,1)S(1)}, u32[]{:S(2)}, u32[]{:S(2)}) %collective-permute-start.3) | collective-permute-done | bytes 135200 | tf_op jit(solution)/shard_map/ppermute | solution.py:231
  17.5 2.4 %collective-permute-start.6 = (bf16[2,528,128]{2,1,0:T(8,128)(2,1)S(1)}, bf16[2,528,128]{2,1,0:T(8,128)(2,1)S(1)}, u32[]{:S(2)}, u32[]{:S(2)}) collective-permute-start(bf16[2,528,128]{2,1,0:T(8,128)(2,1)S(1)} %pad_maximum_fusion.refs_3_.refs_1_), channel_id=1, source_target_pairs={{0,128},{64,192},{128,0},{192,64},{1,129},{65,193},{129,1},{193,65... | collective-permute-start | bytes 811016 | tf_op jit(solution)/shard_map/ppermute | solution.py:236
  19.8 2.0 %collective-permute-start.4 = (bf16[2,528,128]{2,1,0:T(8,128)(2,1)S(1)}, bf16[2,528,128]{2,1,0:T(8,128)(2,1)S(1)}, u32[]{:S(2)}, u32[]{:S(2)}) collective-permute-start(bf16[2,528,128]{2,1,0:T(8,128)(2,1)S(1)} %pad_maximum_fusion.refs_3_.refs_1_), channel_id=1, source_target_pairs={{0,192},{64,0},{128,64},{192,128},{1,193},{65,1},{129,65},{193,129... | collective-permute-start | bytes 811016 | tf_op jit(solution)/shard_map/ppermute | solution.py:236
  21.9 1.4 %collective-permute-done.1.refs_1_ = bf16[2,528,128]{2,1,0:T(8,128)(2,1)S(1)} collective-permute-done((bf16[2,528,128]{2,1,0:T(8,128)(2,1)S(1)}, bf16[2,528,128]{2,1,0:T(8,128)(2,1)S(1)}, u32[]{:S(2)}, u32[]{:S(2)}) %collective-permute-start.1) | collective-permute-done | bytes 270368 | tf_op jit(solution)/shard_map/ppermute | solution.py:235
  23.3 1.4 %collective-permute-start.9 = (bf16[2,528,128]{2,1,0:T(8,128)(2,1)S(1)}, bf16[2,528,128]{2,1,0:T(8,128)(2,1)S(1)}, u32[]{:S(2)}, u32[]{:S(2)}) collective-permute-start(bf16[2,528,128]{2,1,0:T(8,128)(2,1)S(1)} %bitcast_dynamic-update-slice_fusion.refs_0_.rows_ref), channel_id=1, source_target_pairs={{0,56},{8,0},{16,8},{24,16},{32,24},{40,32},{48,40},{56,48},{1,57}... | collective-permute-start | bytes 811016 | tf_op jit(solution)/shard_map/ppermute | solution.py:235
  24.7 1.6 %shard_map.95 = (f32[2,128,768]{2,1,0:T(8,128)S(1)}, f32[2,512,128]{2,1,0:T(8,128)S(1)}) custom-call(bf16[2,528,128]{2,1,0:T(8,128)(2,1)S(1)} %bitcast_dynamic-update-slice_fusion.refs_0_.rows_ref, bf16[2,528,128]{2,1,0:T(8,128)(2,1)S(1)} %collective-permute-done.1.refs_1_, bf16[2,528,128]{2,1,0:T(8,128)(2,1)S(1)} %collective-permute-done.2.refs_2_, ...), custom_call_target="tpu_custom_call" | custom-call | flops 500000000 | bytes 1000000 | tf_op jit(solution)/shard_map/pallas_call | solution.py:208
  27.0 1.6 %shard_map.96 = (f32[2,128,768]{2,1,0:T(8,128)S(1)}, f32[2,512,128]{2,1,0:T(8,128)S(1)}) custom-call(bf16[2,528,128]{2,1,0:T(8,128)(2,1)S(1)} %bitcast_dynamic-update-slice_fusion.refs_0_.rows_ref, bf16[2,528,128]{2,1,0:T(8,128)(2,1)S(1)} %collective-permute-done.1.refs_1_, bf16[2,528,128]{2,1,0:T(8,128)(2,1)S(1)} %collective-permute-done.2.refs_2_, ...), custom_call_target="tpu_custom_call" | custom-call | flops 500000000 | bytes 1000000 | tf_op jit(solution)/shard_map/pallas_call | solution.py:208
  28.5 1.4 %collective-permute-done.5.refs_3_.refs_1_ = bf16[2,528,128]{2,1,0:T(8,128)(2,1)S(1)} collective-permute-done((bf16[2,528,128]{2,1,0:T(8,128)(2,1)S(1)}, bf16[2,528,128]{2,1,0:T(8,128)(2,1)S(1)}, u32[]{:S(2)}, u32[]{:S(2)}) %collective-permute-start.5) | collective-permute-done | bytes 270368 | tf_op jit(solution)/shard_map/ppermute | solution.py:236
  29.9 1.6 %shard_map.97 = (f32[2,128,768]{2,1,0:T(8,128)S(1)}, f32[2,512,128]{2,1,0:T(8,128)S(1)}) custom-call(bf16[2,528,128]{2,1,0:T(8,128)(2,1)S(1)} %bitcast_dynamic-update-slice_fusion.refs_0_.rows_ref, bf16[2,528,128]{2,1,0:T(8,128)(2,1)S(1)} %collective-permute-done.1.refs_1_, bf16[2,528,128]{2,1,0:T(8,128)(2,1)S(1)} %collective-permute-done.2.refs_2_, ...), custom_call_target="tpu_custom_call" | custom-call | flops 500000000 | bytes 1000000 | tf_op jit(solution)/shard_map/pallas_call | solution.py:208
  31.5 1.7 %shard_map.98 = (f32[2,256,128]{2,1,0:T(8,128)S(1)}, bf16[2,256,128]{2,1,0:T(8,128)(2,1)S(1)}, bf16[2,256,128]{2,1,0:T(8,128)(2,1)S(1)}, f32[2,512,128]{2,1,0:T(8,128)S(1)}) custom-call(bf16[2,528,128]{2,1,0:T(8,128)(2,1)S(1)} %bitcast_dynamic-update-slice_fusion.refs_0_.rows_ref, bf16[2,528,128]{2,1,0:T(8,128)(2,1)S(1)} %collective-permute-done.1.refs_1_, ...), custom_call_target="tpu_custom_call" | custom-call | flops 500000000 | bytes 1000000 | tf_op jit(solution)/shard_map/pallas_call | solution.py:208
  33.2 1.5 %collective-permute-done.9.refs_0_ = bf16[2,528,128]{2,1,0:T(8,128)(2,1)S(1)} collective-permute-done((bf16[2,528,128]{2,1,0:T(8,128)(2,1)S(1)}, bf16[2,528,128]{2,1,0:T(8,128)(2,1)S(1)}, u32[]{:S(2)}, u32[]{:S(2)}) %collective-permute-start.9) | collective-permute-done | bytes 270368 | tf_op jit(solution)/shard_map/ppermute | solution.py:235
  35.4 2.4 %collective-permute-start.10 = (bf16[2,512,128]{2,1,0:T(8,128)(2,1)S(1)}, bf16[2,512,128]{2,1,0:T(8,128)(2,1)S(1)}, u32[]{:S(2)}, u32[]{:S(2)}) collective-permute-start(bf16[2,512,128]{2,1,0:T(8,128)(2,1)S(1)} %get-tuple-element.51), channel_id=1, source_target_pairs={{0,128},{64,192},{128,0},{192,64},{1,129},{65,193},{129,1},{193,65... | collective-permute-start | bytes 786440 | tf_op jit(solution)/shard_map/ppermute | solution.py:256
  39.3 2.0 %collective-permute-start.13 = (bf16[2,512,128]{2,1,0:T(8,128)(2,1)S(1)}, bf16[2,512,128]{2,1,0:T(8,128)(2,1)S(1)}, u32[]{:S(2)}, u32[]{:S(2)}) collective-permute-start(bf16[2,512,128]{2,1,0:T(8,128)(2,1)S(1)} %get-tuple-element.59), channel_id=1, source_target_pairs={{0,192},{64,0},{128,64},{192,128},{1,193},{65,1},{129,65},{193,129... | collective-permute-start | bytes 786440 | tf_op jit(solution)/shard_map/ppermute | solution.py:256
  41.3 2.7 %collective-permute-start.7 = (bf16[2,256,128]{2,1,0:T(8,128)(2,1)S(1)}, bf16[2,256,128]{2,1,0:T(8,128)(2,1)S(1)}, u32[]{:S(2)}, u32[]{:S(2)}) collective-permute-start(bf16[2,256,128]{2,1,0:T(8,128)(2,1)S(1)} %get-tuple-element.40), channel_id=1, source_target_pairs={{0,56},{8,0},{16,8},{24,16},{32,24},{40,32},{48,40},{56,48},{1,57}... | collective-permute-start | bytes 393224 | tf_op jit(solution)/shard_map/ppermute | solution.py:265
  44.8 0.8 %shard_map.102 = (bf16[2,256,128]{2,1,0:T(8,128)(2,1)S(1)}, f32[2,512,128]{2,1,0:T(8,128)S(1)}) custom-call(bf16[2,528,128]{2,1,0:T(8,128)(2,1)S(1)} %collective-permute-done.9.refs_0_, bf16[2,528,128]{2,1,0:T(8,128)(2,1)S(1)} %pad_maximum_fusion.refs_3_.refs_1_, f32[2,128,256]{2,1,0:T(8,128)S(1)} %get-tuple-element.52.refs_2_, ...), custom_call_target="tpu_custom_call" | custom-call | flops 500000000 | bytes 1000000 | tf_op jit(solution)/shard_map/pallas_call | solution.py:208
  45.6 3.9 %collective-permute-start.11 = (bf16[2,256,128]{2,1,0:T(8,128)(2,1)S(1)}, bf16[2,256,128]{2,1,0:T(8,128)(2,1)S(1)}, u32[]{:S(2)}, u32[]{:S(2)}) collective-permute-start(bf16[2,256,128]{2,1,0:T(8,128)(2,1)S(1)} %get-tuple-element.54), channel_id=1, source_target_pairs={{0,8},{8,16},{16,24},{24,32},{32,40},{40,48},{48,56},{56,0},{1,9},... | collective-permute-start | bytes 393224 | tf_op jit(solution)/shard_map/ppermute | solution.py:274
  49.7 7.4 %collective-permute-start.15 = (bf16[512,128]{1,0:T(8,128)(2,1)S(1)}, bf16[512,128]{1,0:T(8,128)(2,1)S(1)}, u32[]{:S(2)}, u32[]{:S(2)}) collective-permute-start(bf16[512,128]{1,0:T(8,128)(2,1)S(1)} %get-tuple-element.62), channel_id=1, source_target_pairs={{0,32},{8,40},{16,48},{24,56},{32,0},{40,8},{48,16},{56,24},{1,33}... | collective-permute-start | bytes 393224 | tf_op jit(solution)/shard_map/ppermute | solution.py:282
  57.6 6.4 %collective-permute-done.15.dkvz_ref = bf16[512,128]{1,0:T(8,128)(2,1)S(1)} collective-permute-done((bf16[512,128]{1,0:T(8,128)(2,1)S(1)}, bf16[512,128]{1,0:T(8,128)(2,1)S(1)}, u32[]{:S(2)}, u32[]{:S(2)}) %collective-permute-start.15) | collective-permute-done | bytes 131104 | tf_op jit(solution)/shard_map/ppermute | solution.py:282
  (25 shorter events, 5.1 us)
Async XLA Ops:
  2.5 9.7 %collective-permute-start = (bf16[528,128]{1,0:T(8,128)(2,1)}, bf16[528,128]{1,0:T(8,128)(2,1)S(1)}, u32[]{:S(2)}, u32[]{:S(2)}) collective-permute-start(bf16[528,128]{1,0:T(8,128)(2,1)} %get-tuple-element.33), channel_id=1, source_target_pairs={{0,4},{4,0},{1,5},{5,1},{2,6},{6,2},{3,7},{7,3},{8,12},{12,8},{9,1... | collective-permute-start | bytes 405512 | tf_op jit(solution)/shard_map/ppermute | solution.py:232
  4.0 13.4 %collective-permute-start.3 = (bf16[528,128]{1,0:T(8,128)(2,1)}, bf16[528,128]{1,0:T(8,128)(2,1)S(1)}, u32[]{:S(2)}, u32[]{:S(2)}) collective-permute-start(bf16[528,128]{1,0:T(8,128)(2,1)} %get-tuple-element.34), channel_id=1, source_target_pairs={{0,32},{8,40},{16,48},{24,56},{32,0},{40,8},{48,16},{56,24},{1,33}... | collective-permute-start | bytes 405512 | tf_op jit(solution)/shard_map/ppermute | solution.py:231
  12.2 5.3 %copy-start = (bf16[528,128]{1,0:T(8,128)(2,1)S(1)}, bf16[528,128]{1,0:T(8,128)(2,1)}, u32[]{:S(2)}) copy-start(bf16[528,128]{1,0:T(8,128)(2,1)} %get-tuple-element.34) | copy-start | bytes 405508
  12.2 11.1 %collective-permute-start.1 = (bf16[2,528,128]{2,1,0:T(8,128)(2,1)S(1)}, bf16[2,528,128]{2,1,0:T(8,128)(2,1)S(1)}, u32[]{:S(2)}, u32[]{:S(2)}) collective-permute-start(bf16[2,528,128]{2,1,0:T(8,128)(2,1)S(1)} %bitcast_dynamic-update-slice_fusion.refs_0_.rows_ref), channel_id=1, source_target_pairs={{0,8},{8,16},{16,24},{24,32},{32,40},{40,48},{48,56},{56,0},{1,9},... | collective-permute-start | bytes 811016 | tf_op jit(solution)/shard_map/ppermute | solution.py:235
  13.3 11.4 %collective-permute-start.2 = (bf16[2,528,128]{2,1,0:T(8,128)(2,1)S(1)}, bf16[2,528,128]{2,1,0:T(8,128)(2,1)S(1)}, u32[]{:S(2)}, u32[]{:S(2)}) collective-permute-start(bf16[2,528,128]{2,1,0:T(8,128)(2,1)S(1)} %bitcast_dynamic-update-slice_fusion.refs_0_.rows_ref), channel_id=1, source_target_pairs={{0,48},{8,24},{16,0},{24,40},{32,16},{40,56},{48,32},{56,8},{1,49}... | collective-permute-start | bytes 811016 | tf_op jit(solution)/shard_map/ppermute | solution.py:235
  17.5 9.5 %collective-permute-start.6 = (bf16[2,528,128]{2,1,0:T(8,128)(2,1)S(1)}, bf16[2,528,128]{2,1,0:T(8,128)(2,1)S(1)}, u32[]{:S(2)}, u32[]{:S(2)}) collective-permute-start(bf16[2,528,128]{2,1,0:T(8,128)(2,1)S(1)} %pad_maximum_fusion.refs_3_.refs_1_), channel_id=1, source_target_pairs={{0,128},{64,192},{128,0},{192,64},{1,129},{65,193},{129,1},{193,65... | collective-permute-start | bytes 811016 | tf_op jit(solution)/shard_map/ppermute | solution.py:236
  19.8 10.1 %collective-permute-start.5 = (bf16[2,528,128]{2,1,0:T(8,128)(2,1)S(1)}, bf16[2,528,128]{2,1,0:T(8,128)(2,1)S(1)}, u32[]{:S(2)}, u32[]{:S(2)}) collective-permute-start(bf16[2,528,128]{2,1,0:T(8,128)(2,1)S(1)} %pad_maximum_fusion.refs_3_.refs_1_), channel_id=1, source_target_pairs={{0,64},{64,128},{128,192},{192,0},{1,65},{65,129},{129,193},{193,1... | collective-permute-start | bytes 811016 | tf_op jit(solution)/shard_map/ppermute | solution.py:236
  19.8 11.6 %collective-permute-start.4 = (bf16[2,528,128]{2,1,0:T(8,128)(2,1)S(1)}, bf16[2,528,128]{2,1,0:T(8,128)(2,1)S(1)}, u32[]{:S(2)}, u32[]{:S(2)}) collective-permute-start(bf16[2,528,128]{2,1,0:T(8,128)(2,1)S(1)} %pad_maximum_fusion.refs_3_.refs_1_), channel_id=1, source_target_pairs={{0,192},{64,0},{128,64},{192,128},{1,193},{65,1},{129,65},{193,129... | collective-permute-start | bytes 811016 | tf_op jit(solution)/shard_map/ppermute | solution.py:236
  23.3 11.4 %collective-permute-start.9 = (bf16[2,528,128]{2,1,0:T(8,128)(2,1)S(1)}, bf16[2,528,128]{2,1,0:T(8,128)(2,1)S(1)}, u32[]{:S(2)}, u32[]{:S(2)}) collective-permute-start(bf16[2,528,128]{2,1,0:T(8,128)(2,1)S(1)} %bitcast_dynamic-update-slice_fusion.refs_0_.rows_ref), channel_id=1, source_target_pairs={{0,56},{8,0},{16,8},{24,16},{32,24},{40,32},{48,40},{56,48},{1,57}... | collective-permute-start | bytes 811016 | tf_op jit(solution)/shard_map/ppermute | solution.py:235
  35.4 9.4 %collective-permute-start.10 = (bf16[2,512,128]{2,1,0:T(8,128)(2,1)S(1)}, bf16[2,512,128]{2,1,0:T(8,128)(2,1)S(1)}, u32[]{:S(2)}, u32[]{:S(2)}) collective-permute-start(bf16[2,512,128]{2,1,0:T(8,128)(2,1)S(1)} %get-tuple-element.51), channel_id=1, source_target_pairs={{0,128},{64,192},{128,0},{192,64},{1,129},{65,193},{129,1},{193,65... | collective-permute-start | bytes 786440 | tf_op jit(solution)/shard_map/ppermute | solution.py:256
  39.2 10.3 %collective-permute-start.14 = (bf16[2,512,128]{2,1,0:T(8,128)(2,1)S(1)}, bf16[2,512,128]{2,1,0:T(8,128)(2,1)S(1)}, u32[]{:S(2)}, u32[]{:S(2)}) collective-permute-start(bf16[2,512,128]{2,1,0:T(8,128)(2,1)S(1)} %get-tuple-element.60), channel_id=1, source_target_pairs={{0,64},{64,128},{128,192},{192,0},{1,65},{65,129},{129,193},{193,1... | collective-permute-start | bytes 786440 | tf_op jit(solution)/shard_map/ppermute | solution.py:256
  39.3 10.2 %collective-permute-start.13 = (bf16[2,512,128]{2,1,0:T(8,128)(2,1)S(1)}, bf16[2,512,128]{2,1,0:T(8,128)(2,1)S(1)}, u32[]{:S(2)}, u32[]{:S(2)}) collective-permute-start(bf16[2,512,128]{2,1,0:T(8,128)(2,1)S(1)} %get-tuple-element.59), channel_id=1, source_target_pairs={{0,192},{64,0},{128,64},{192,128},{1,193},{65,1},{129,65},{193,129... | collective-permute-start | bytes 786440 | tf_op jit(solution)/shard_map/ppermute | solution.py:256
  41.3 15.7 %collective-permute-start.7 = (bf16[2,256,128]{2,1,0:T(8,128)(2,1)S(1)}, bf16[2,256,128]{2,1,0:T(8,128)(2,1)S(1)}, u32[]{:S(2)}, u32[]{:S(2)}) collective-permute-start(bf16[2,256,128]{2,1,0:T(8,128)(2,1)S(1)} %get-tuple-element.40), channel_id=1, source_target_pairs={{0,56},{8,0},{16,8},{24,16},{32,24},{40,32},{48,40},{56,48},{1,57}... | collective-permute-start | bytes 393224 | tf_op jit(solution)/shard_map/ppermute | solution.py:265
  44.0 13.0 %collective-permute-start.8 = (bf16[2,256,128]{2,1,0:T(8,128)(2,1)S(1)}, bf16[2,256,128]{2,1,0:T(8,128)(2,1)S(1)}, u32[]{:S(2)}, u32[]{:S(2)}) collective-permute-start(bf16[2,256,128]{2,1,0:T(8,128)(2,1)S(1)} %get-tuple-element.41), channel_id=1, source_target_pairs={{48,0},{24,8},{0,16},{40,24},{16,32},{56,40},{32,48},{8,56},{49,1}... | collective-permute-start | bytes 393224 | tf_op jit(solution)/shard_map/ppermute | solution.py:265
  45.6 11.5 %collective-permute-start.11 = (bf16[2,256,128]{2,1,0:T(8,128)(2,1)S(1)}, bf16[2,256,128]{2,1,0:T(8,128)(2,1)S(1)}, u32[]{:S(2)}, u32[]{:S(2)}) collective-permute-start(bf16[2,256,128]{2,1,0:T(8,128)(2,1)S(1)} %get-tuple-element.54), channel_id=1, source_target_pairs={{0,8},{8,16},{16,24},{24,32},{32,40},{40,48},{48,56},{56,0},{1,9},... | collective-permute-start | bytes 393224 | tf_op jit(solution)/shard_map/ppermute | solution.py:274
  49.7 14.4 %collective-permute-start.15 = (bf16[512,128]{1,0:T(8,128)(2,1)S(1)}, bf16[512,128]{1,0:T(8,128)(2,1)S(1)}, u32[]{:S(2)}, u32[]{:S(2)}) collective-permute-start(bf16[512,128]{1,0:T(8,128)(2,1)S(1)} %get-tuple-element.62), channel_id=1, source_target_pairs={{0,32},{8,40},{16,48},{24,56},{32,0},{40,8},{48,16},{56,24},{1,33}... | collective-permute-start | bytes 393224 | tf_op jit(solution)/shard_map/ppermute | solution.py:282
  57.2 6.9 %collective-permute-start.12 = (bf16[256,128]{1,0:T(8,128)(2,1)S(1)}, bf16[256,128]{1,0:T(8,128)(2,1)S(1)}, u32[]{:S(2)}, u32[]{:S(2)}) collective-permute-start(bf16[256,128]{1,0:T(8,128)(2,1)S(1)} %get-tuple-element.56), channel_id=1, source_target_pairs={{0,4},{4,0},{1,5},{5,1},{2,6},{6,2},{3,7},{7,3},{8,12},{12,8},{9,1... | collective-permute-start | bytes 196616 | tf_op jit(solution)/shard_map/ppermute | solution.py:284

commit v17 on v15

--- a/solution.py
+++ b/solution.py
@@ -269,8 +269,8 @@
     for turn in (1, 2, 3):
         dq, part = grad(turn, 1, dq, parts[turn], False, BF16)
         back.append(send_back(turn, part))
-    dq, back[0] = lax.optimization_barrier((dq, back[0]))
     (dq_z2,), own = grad(0, 1, dq, parts[0], True, F32)
+    dq_z2, back[0] = lax.optimization_barrier((dq_z2, back[0]))
     dq_back.append(lax.ppermute(dq_z2, "kz", Z_BACK))
 
     def meet(operands, parts, shape):

time: 61.4 us -> 61.2 us (level)
  starting transfers between devices: 40.6 us -> 39.7 us
  waiting for transfers between devices: 6.67 us -> 7.47 us
    ppermute x1, starting transfers between devices: 2.65 us -> 1.77 us  [body(): dq_back.append(lax.ppermute(dq_z2, 'kz', Z_BACK))]
    ppermute x1, waiting for transfers between devices: 1.31 us -> 2.09 us  [body(): dq_back.append(lax.ppermute(dq_z2, 'kz', Z_BACK))]
    ppermute x1, waiting for transfers between devices: 1.24 us -> 2.02 us  [body(): dq_last = lax.ppermute(dq_send, 'kx', X_SWAP)]
    ppermute x1, waiting for transfers between devices: 2.18 us -> 1.41 us  [body(): dkv_last = lax.ppermute(dkv_send, 'kz', z_step(4))]
where the time goes in v17:
time: 61.2 us; the launch traced here: 61 us
  starting transfers between devices  39.7 us (65%)
  Pallas kernels  12 us (20%)
  waiting for transfers between devices  7.47 us (12%)
  local copies, waits for them, and re-layouts  0.96 us (2%)
  between operations  0.79 us (1%)
    pallas_call x12, Pallas kernels, call(): pl.pallas_call(kernel, out_shape=[jax.ShapeDtypeStruct(s, t) for s, t in...  12 us
    ppermute x3, starting transfers between devices, body(): lax.ppermute(q, 'kz', p)  9 us
    ppermute x1, starting transfers between devices, body(): other_k = lax.ppermute(mine_k, 'kz', z_step(4))  7.19 us
    ppermute x3, starting transfers between devices, body(): k_sets = [k0] + [lax.ppermute(k0, 'pb', y_step(-s)) for s in Y_FROM[1:]]  6.52 us
    ppermute x2, starting transfers between devices, body(): lax.ppermute(d, 'kz', p)  5.03 us
    ppermute x1, starting transfers between devices, body(): dkv_last = lax.ppermute(dkv_send, 'kz', z_step(4))  4.57 us
    ppermute x3, starting transfers between devices, send_back(): return lax.ppermute(part, 'pb', y_step(Y_FROM[turn]))  3.41 us
    ppermute x1, waiting for transfers between devices, body(): dq_back.append(lax.ppermute(dq_z2, 'kz', Z_BACK))  2.09 us
  transfers between devices with their start and end apart: 16, of which 4 were waited for; matrix products, arithmetic and copies ran while one was open for 2% of the time, Pallas kernels for 14%

profile of v17, /device:TPU:4, one launch (start us, length us, event | category | flops | bytes accessed | tf_op | source)
XLA Modules:
  0.0 61.0 jit_solution(11733015513013848217)
XLA Ops:
  0.6 1.8 %shard_map.94 = (bf16[528,128]{1,0:T(8,128)(2,1)}, bf16[528,128]{1,0:T(8,128)(2,1)}) custom-call(s32[128]{0:T(128)} %refs_0_.1, bf16[256,128]{1,0:T(8,128)(2,1)} %refs_1_.1, bf16[256,128]{1,0:T(8,128)(2,1)} %refs_2_.1, bf16[1,256]{1,0:T(2,128)(2,1)} %bitcast.9, bf16[256,128]{1,0:T(8,128)(2,1)} %refs_4_.1, bf16[256,128]{1,0:T(8,128)(2,1)} %refs_5_.1, ...), custom_call_target="tpu_custom_call" | custom-call | tf_op jit(solution)/shard_map/pallas_call | solution.py:208
  2.5 1.3 %collective-permute-start = (bf16[528,128]{1,0:T(8,128)(2,1)}, bf16[528,128]{1,0:T(8,128)(2,1)S(1)}, u32[]{:S(2)}, u32[]{:S(2)}) collective-permute-start(bf16[528,128]{1,0:T(8,128)(2,1)} %get-tuple-element.33), channel_id=1, source_target_pairs={{0,4},{4,0},{1,5},{5,1},{2,6},{6,2},{3,7},{7,3},{8,12},{12,8},{9,1... | collective-permute-start | bytes 405512 | tf_op jit(solution)/shard_map/ppermute | solution.py:232
  3.7 7.2 %collective-permute-start.3 = (bf16[528,128]{1,0:T(8,128)(2,1)}, bf16[528,128]{1,0:T(8,128)(2,1)S(1)}, u32[]{:S(2)}, u32[]{:S(2)}) collective-permute-start(bf16[528,128]{1,0:T(8,128)(2,1)} %get-tuple-element.34), channel_id=1, source_target_pairs={{0,32},{8,40},{16,48},{24,56},{32,0},{40,8},{48,16},{56,24},{1,33}... | collective-permute-start | bytes 405512 | tf_op jit(solution)/shard_map/ppermute | solution.py:231
  10.9 0.9 %pad.4 = bf16[2,528,128]{2,1,0:T(8,128)(2,1)S(1)} pad(bf16[1,528,128]{2,1,0:T(8,128)(2,1)} %bitcast.6, bf16[]{:T(256)} %constant.1.clone.1), padding=0_1x0_0x0_0 | pad | bytes 405506 | tf_op jit(solution)/shard_map/jit(_pad)/pad | solution.py:228
  11.9 1.1 %collective-permute-start.1 = (bf16[2,528,128]{2,1,0:T(8,128)(2,1)S(1)}, bf16[2,528,128]{2,1,0:T(8,128)(2,1)S(1)}, u32[]{:S(2)}, u32[]{:S(2)}) collective-permute-start(bf16[2,528,128]{2,1,0:T(8,128)(2,1)S(1)} %bitcast_dynamic-update-slice_fusion.refs_0_.rows_ref), channel_id=1, source_target_pairs={{0,8},{8,16},{16,24},{24,32},{32,40},{40,48},{48,56},{56,0},{1,9},... | collective-permute-start | bytes 811016 | tf_op jit(solution)/shard_map/ppermute | solution.py:235
  13.0 2.2 %collective-permute-start.2 = (bf16[2,528,128]{2,1,0:T(8,128)(2,1)S(1)}, bf16[2,528,128]{2,1,0:T(8,128)(2,1)S(1)}, u32[]{:S(2)}, u32[]{:S(2)}) collective-permute-start(bf16[2,528,128]{2,1,0:T(8,128)(2,1)S(1)} %bitcast_dynamic-update-slice_fusion.refs_0_.rows_ref), channel_id=1, source_target_pairs={{0,56},{8,0},{16,8},{24,16},{32,24},{40,32},{48,40},{56,48},{1,57}... | collective-permute-start | bytes 811016 | tf_op jit(solution)/shard_map/ppermute | solution.py:235
  15.2 1.9 %collective-permute-done.3 = bf16[528,128]{1,0:T(8,128)(2,1)S(1)} collective-permute-done((bf16[528,128]{1,0:T(8,128)(2,1)}, bf16[528,128]{1,0:T(8,128)(2,1)S(1)}, u32[]{:S(2)}, u32[]{:S(2)}) %collective-permute-start.3) | collective-permute-done | bytes 135200 | tf_op jit(solution)/shard_map/ppermute | solution.py:231
  17.2 3.3 %collective-permute-start.6 = (bf16[2,528,128]{2,1,0:T(8,128)(2,1)S(1)}, bf16[2,528,128]{2,1,0:T(8,128)(2,1)S(1)}, u32[]{:S(2)}, u32[]{:S(2)}) collective-permute-start(bf16[2,528,128]{2,1,0:T(8,128)(2,1)S(1)} %pad_maximum_fusion.refs_3_.refs_1_), channel_id=1, source_target_pairs={{0,128},{64,192},{128,0},{192,64},{1,129},{65,193},{129,1},{193,65... | collective-permute-start | bytes 811016 | tf_op jit(solution)/shard_map/ppermute | solution.py:236
  21.1 2.6 %collective-permute-start.4 = (bf16[2,528,128]{2,1,0:T(8,128)(2,1)S(1)}, bf16[2,528,128]{2,1,0:T(8,128)(2,1)S(1)}, u32[]{:S(2)}, u32[]{:S(2)}) collective-permute-start(bf16[2,528,128]{2,1,0:T(8,128)(2,1)S(1)} %pad_maximum_fusion.refs_3_.refs_1_), channel_id=1, source_target_pairs={{0,192},{64,0},{128,64},{192,128},{1,193},{65,1},{129,65},{193,129... | collective-permute-start | bytes 811016 | tf_op jit(solution)/shard_map/ppermute | solution.py:236
  23.7 5.7 %collective-permute-start.9 = (bf16[2,528,128]{2,1,0:T(8,128)(2,1)S(1)}, bf16[2,528,128]{2,1,0:T(8,128)(2,1)S(1)}, u32[]{:S(2)}, u32[]{:S(2)}) collective-permute-start(bf16[2,528,128]{2,1,0:T(8,128)(2,1)S(1)} %bitcast_dynamic-update-slice_fusion.refs_0_.rows_ref), channel_id=1, source_target_pairs={{0,48},{8,24},{16,0},{24,40},{32,16},{40,56},{48,32},{56,8},{1,49}... | collective-permute-start | bytes 811016 | tf_op jit(solution)/shard_map/ppermute | solution.py:235
  29.4 1.6 %shard_map.95 = (f32[2,128,768]{2,1,0:T(8,128)S(1)}, f32[2,512,128]{2,1,0:T(8,128)S(1)}) custom-call(bf16[2,528,128]{2,1,0:T(8,128)(2,1)S(1)} %bitcast_dynamic-update-slice_fusion.refs_0_.rows_ref, bf16[2,528,128]{2,1,0:T(8,128)(2,1)S(1)} %collective-permute-done.1.refs_1_, bf16[2,528,128]{2,1,0:T(8,128)(2,1)S(1)} %collective-permute-done.2.refs_2_, ...), custom_call_target="tpu_custom_call" | custom-call | flops 500000000 | bytes 1000000 | tf_op jit(solution)/shard_map/pallas_call | solution.py:208
  31.0 1.6 %shard_map.96 = (f32[2,128,768]{2,1,0:T(8,128)S(1)}, f32[2,512,128]{2,1,0:T(8,128)S(1)}) custom-call(bf16[2,528,128]{2,1,0:T(8,128)(2,1)S(1)} %bitcast_dynamic-update-slice_fusion.refs_0_.rows_ref, bf16[2,528,128]{2,1,0:T(8,128)(2,1)S(1)} %collective-permute-done.1.refs_1_, bf16[2,528,128]{2,1,0:T(8,128)(2,1)S(1)} %collective-permute-done.2.refs_2_, ...), custom_call_target="tpu_custom_call" | custom-call | flops 500000000 | bytes 1000000 | tf_op jit(solution)/shard_map/pallas_call | solution.py:208
  32.6 1.6 %shard_map.97 = (f32[2,128,768]{2,1,0:T(8,128)S(1)}, f32[2,512,128]{2,1,0:T(8,128)S(1)}) custom-call(bf16[2,528,128]{2,1,0:T(8,128)(2,1)S(1)} %bitcast_dynamic-update-slice_fusion.refs_0_.rows_ref, bf16[2,528,128]{2,1,0:T(8,128)(2,1)S(1)} %collective-permute-done.1.refs_1_, bf16[2,528,128]{2,1,0:T(8,128)(2,1)S(1)} %collective-permute-done.2.refs_2_, ...), custom_call_target="tpu_custom_call" | custom-call | flops 500000000 | bytes 1000000 | tf_op jit(solution)/shard_map/pallas_call | solution.py:208
  34.1 1.7 %shard_map.98 = (f32[2,256,128]{2,1,0:T(8,128)S(1)}, bf16[2,256,128]{2,1,0:T(8,128)(2,1)S(1)}, bf16[2,256,128]{2,1,0:T(8,128)(2,1)S(1)}, f32[2,512,128]{2,1,0:T(8,128)S(1)}) custom-call(bf16[2,528,128]{2,1,0:T(8,128)(2,1)S(1)} %bitcast_dynamic-update-slice_fusion.refs_0_.rows_ref, bf16[2,528,128]{2,1,0:T(8,128)(2,1)S(1)} %collective-permute-done.1.refs_1_, ...), custom_call_target="tpu_custom_call" | custom-call | flops 500000000 | bytes 1000000 | tf_op jit(solution)/shard_map/pallas_call | solution.py:208
  38.1 0.9 %collective-permute-start.14 = (bf16[2,512,128]{2,1,0:T(8,128)(2,1)S(1)}, bf16[2,512,128]{2,1,0:T(8,128)(2,1)S(1)}, u32[]{:S(2)}, u32[]{:S(2)}) collective-permute-start(bf16[2,512,128]{2,1,0:T(8,128)(2,1)S(1)} %get-tuple-element.60), channel_id=1, source_target_pairs={{0,64},{64,128},{128,192},{192,0},{1,65},{65,129},{129,193},{193,1... | collective-permute-start | bytes 786440 | tf_op jit(solution)/shard_map/ppermute | solution.py:256
  39.1 2.4 %collective-permute-start.13 = (bf16[2,512,128]{2,1,0:T(8,128)(2,1)S(1)}, bf16[2,512,128]{2,1,0:T(8,128)(2,1)S(1)}, u32[]{:S(2)}, u32[]{:S(2)}) collective-permute-start(bf16[2,512,128]{2,1,0:T(8,128)(2,1)S(1)} %get-tuple-element.59), channel_id=1, source_target_pairs={{0,192},{64,0},{128,64},{192,128},{1,193},{65,1},{129,65},{193,129... | collective-permute-start | bytes 786440 | tf_op jit(solution)/shard_map/ppermute | solution.py:256
  41.4 5.0 %collective-permute-start.7 = (bf16[2,256,128]{2,1,0:T(8,128)(2,1)S(1)}, bf16[2,256,128]{2,1,0:T(8,128)(2,1)S(1)}, u32[]{:S(2)}, u32[]{:S(2)}) collective-permute-start(bf16[2,256,128]{2,1,0:T(8,128)(2,1)S(1)} %get-tuple-element.40), channel_id=1, source_target_pairs={{0,56},{8,0},{16,8},{24,16},{32,24},{40,32},{48,40},{56,48},{1,57}... | collective-permute-start | bytes 393224 | tf_op jit(solution)/shard_map/ppermute | solution.py:265
  46.5 0.8 %shard_map.102 = (bf16[2,256,128]{2,1,0:T(8,128)(2,1)S(1)}, f32[2,512,128]{2,1,0:T(8,128)S(1)}) custom-call(bf16[2,528,128]{2,1,0:T(8,128)(2,1)S(1)} %collective-permute-done.9.refs_0_, bf16[2,528,128]{2,1,0:T(8,128)(2,1)S(1)} %pad_maximum_fusion.refs_3_.refs_1_, f32[2,128,256]{2,1,0:T(8,128)S(1)} %get-tuple-element.50.refs_2_, ...), custom_call_target="tpu_custom_call" | custom-call | flops 500000000 | bytes 1000000 | tf_op jit(solution)/shard_map/pallas_call | solution.py:208
  47.3 1.8 %collective-permute-start.11 = (bf16[2,256,128]{2,1,0:T(8,128)(2,1)S(1)}, bf16[2,256,128]{2,1,0:T(8,128)(2,1)S(1)}, u32[]{:S(2)}, u32[]{:S(2)}) collective-permute-start(bf16[2,256,128]{2,1,0:T(8,128)(2,1)S(1)} %get-tuple-element.54), channel_id=1, source_target_pairs={{48,0},{24,8},{0,16},{40,24},{16,32},{56,40},{32,48},{8,56},{49,1}... | collective-permute-start | bytes 393224 | tf_op jit(solution)/shard_map/ppermute | solution.py:274
  49.2 4.6 %collective-permute-start.15 = (bf16[512,128]{1,0:T(8,128)(2,1)S(1)}, bf16[512,128]{1,0:T(8,128)(2,1)S(1)}, u32[]{:S(2)}, u32[]{:S(2)}) collective-permute-start(bf16[512,128]{1,0:T(8,128)(2,1)S(1)} %get-tuple-element.62), channel_id=1, source_target_pairs={{0,32},{8,40},{16,48},{24,56},{32,0},{40,8},{48,16},{56,24},{1,33}... | collective-permute-start | bytes 393224 | tf_op jit(solution)/shard_map/ppermute | solution.py:282
  53.7 2.1 %collective-permute-done.11.refs_3_ = bf16[2,256,128]{2,1,0:T(8,128)(2,1)S(1)} collective-permute-done((bf16[2,256,128]{2,1,0:T(8,128)(2,1)S(1)}, bf16[2,256,128]{2,1,0:T(8,128)(2,1)S(1)}, u32[]{:S(2)}, u32[]{:S(2)}) %collective-permute-start.11) | collective-permute-done | bytes 131104 | tf_op jit(solution)/shard_map/ppermute | solution.py:274
  55.9 0.9 %collective-permute-start.12 = (bf16[256,128]{1,0:T(8,128)(2,1)S(1)}, bf16[256,128]{1,0:T(8,128)(2,1)S(1)}, u32[]{:S(2)}, u32[]{:S(2)}) collective-permute-start(bf16[256,128]{1,0:T(8,128)(2,1)S(1)} %get-tuple-element.56), channel_id=1, source_target_pairs={{0,4},{4,0},{1,5},{5,1},{2,6},{6,2},{3,7},{7,3},{8,12},{12,8},{9,1... | collective-permute-start | bytes 196616 | tf_op jit(solution)/shard_map/ppermute | solution.py:284
  56.8 1.4 %collective-permute-done.15.dkvz_ref = bf16[512,128]{1,0:T(8,128)(2,1)S(1)} collective-permute-done((bf16[512,128]{1,0:T(8,128)(2,1)S(1)}, bf16[512,128]{1,0:T(8,128)(2,1)S(1)}, u32[]{:S(2)}, u32[]{:S(2)}) %collective-permute-start.15) | collective-permute-done | bytes 131104 | tf_op jit(solution)/shard_map/ppermute | solution.py:282
  58.2 2.0 %collective-permute-done.12.dqx_ref = bf16[256,128]{1,0:T(8,128)(2,1)S(1)} collective-permute-done((bf16[256,128]{1,0:T(8,128)(2,1)S(1)}, bf16[256,128]{1,0:T(8,128)(2,1)S(1)}, u32[]{:S(2)}, u32[]{:S(2)}) %collective-permute-start.12) | collective-permute-done | bytes 65568 | tf_op jit(solution)/shard_map/ppermute | solution.py:284
  (25 shorter events, 3.9 us)
Async XLA Ops:
  2.5 9.4 %collective-permute-start = (bf16[528,128]{1,0:T(8,128)(2,1)}, bf16[528,128]{1,0:T(8,128)(2,1)S(1)}, u32[]{:S(2)}, u32[]{:S(2)}) collective-permute-start(bf16[528,128]{1,0:T(8,128)(2,1)} %get-tuple-element.33), channel_id=1, source_target_pairs={{0,4},{4,0},{1,5},{5,1},{2,6},{6,2},{3,7},{7,3},{8,12},{12,8},{9,1... | collective-permute-start | bytes 405512 | tf_op jit(solution)/shard_map/ppermute | solution.py:232
  3.7 13.4 %collective-permute-start.3 = (bf16[528,128]{1,0:T(8,128)(2,1)}, bf16[528,128]{1,0:T(8,128)(2,1)S(1)}, u32[]{:S(2)}, u32[]{:S(2)}) collective-permute-start(bf16[528,128]{1,0:T(8,128)(2,1)} %get-tuple-element.34), channel_id=1, source_target_pairs={{0,32},{8,40},{16,48},{24,56},{32,0},{40,8},{48,16},{56,24},{1,33}... | collective-permute-start | bytes 405512 | tf_op jit(solution)/shard_map/ppermute | solution.py:231
  11.9 5.3 %copy-start = (bf16[528,128]{1,0:T(8,128)(2,1)S(1)}, bf16[528,128]{1,0:T(8,128)(2,1)}, u32[]{:S(2)}) copy-start(bf16[528,128]{1,0:T(8,128)(2,1)} %get-tuple-element.34) | copy-start | bytes 405508
  11.9 11.8 %collective-permute-start.1 = (bf16[2,528,128]{2,1,0:T(8,128)(2,1)S(1)}, bf16[2,528,128]{2,1,0:T(8,128)(2,1)S(1)}, u32[]{:S(2)}, u32[]{:S(2)}) collective-permute-start(bf16[2,528,128]{2,1,0:T(8,128)(2,1)S(1)} %bitcast_dynamic-update-slice_fusion.refs_0_.rows_ref), channel_id=1, source_target_pairs={{0,8},{8,16},{16,24},{24,32},{32,40},{40,48},{48,56},{56,0},{1,9},... | collective-permute-start | bytes 811016 | tf_op jit(solution)/shard_map/ppermute | solution.py:235
  13.0 16.4 %collective-permute-start.2 = (bf16[2,528,128]{2,1,0:T(8,128)(2,1)S(1)}, bf16[2,528,128]{2,1,0:T(8,128)(2,1)S(1)}, u32[]{:S(2)}, u32[]{:S(2)}) collective-permute-start(bf16[2,528,128]{2,1,0:T(8,128)(2,1)S(1)} %bitcast_dynamic-update-slice_fusion.refs_0_.rows_ref), channel_id=1, source_target_pairs={{0,56},{8,0},{16,8},{24,16},{32,24},{40,32},{48,40},{56,48},{1,57}... | collective-permute-start | bytes 811016 | tf_op jit(solution)/shard_map/ppermute | solution.py:235
  17.2 13.8 %collective-permute-start.6 = (bf16[2,528,128]{2,1,0:T(8,128)(2,1)S(1)}, bf16[2,528,128]{2,1,0:T(8,128)(2,1)S(1)}, u32[]{:S(2)}, u32[]{:S(2)}) collective-permute-start(bf16[2,528,128]{2,1,0:T(8,128)(2,1)S(1)} %pad_maximum_fusion.refs_3_.refs_1_), channel_id=1, source_target_pairs={{0,128},{64,192},{128,0},{192,64},{1,129},{65,193},{129,1},{193,65... | collective-permute-start | bytes 811016 | tf_op jit(solution)/shard_map/ppermute | solution.py:236
  20.5 12.1 %collective-permute-start.5 = (bf16[2,528,128]{2,1,0:T(8,128)(2,1)S(1)}, bf16[2,528,128]{2,1,0:T(8,128)(2,1)S(1)}, u32[]{:S(2)}, u32[]{:S(2)}) collective-permute-start(bf16[2,528,128]{2,1,0:T(8,128)(2,1)S(1)} %pad_maximum_fusion.refs_3_.refs_1_), channel_id=1, source_target_pairs={{0,64},{64,128},{128,192},{192,0},{1,65},{65,129},{129,193},{193,1... | collective-permute-start | bytes 811016 | tf_op jit(solution)/shard_map/ppermute | solution.py:236
  21.1 13.0 %collective-permute-start.4 = (bf16[2,528,128]{2,1,0:T(8,128)(2,1)S(1)}, bf16[2,528,128]{2,1,0:T(8,128)(2,1)S(1)}, u32[]{:S(2)}, u32[]{:S(2)}) collective-permute-start(bf16[2,528,128]{2,1,0:T(8,128)(2,1)S(1)} %pad_maximum_fusion.refs_3_.refs_1_), channel_id=1, source_target_pairs={{0,192},{64,0},{128,64},{192,128},{1,193},{65,1},{129,65},{193,129... | collective-permute-start | bytes 811016 | tf_op jit(solution)/shard_map/ppermute | solution.py:236
  23.7 12.1 %collective-permute-start.9 = (bf16[2,528,128]{2,1,0:T(8,128)(2,1)S(1)}, bf16[2,528,128]{2,1,0:T(8,128)(2,1)S(1)}, u32[]{:S(2)}, u32[]{:S(2)}) collective-permute-start(bf16[2,528,128]{2,1,0:T(8,128)(2,1)S(1)} %bitcast_dynamic-update-slice_fusion.refs_0_.rows_ref), channel_id=1, source_target_pairs={{0,48},{8,24},{16,0},{24,40},{32,16},{40,56},{48,32},{56,8},{1,49}... | collective-permute-start | bytes 811016 | tf_op jit(solution)/shard_map/ppermute | solution.py:235
  36.6 10.7 %collective-permute-start.10 = (bf16[2,512,128]{2,1,0:T(8,128)(2,1)S(1)}, bf16[2,512,128]{2,1,0:T(8,128)(2,1)S(1)}, u32[]{:S(2)}, u32[]{:S(2)}) collective-permute-start(bf16[2,512,128]{2,1,0:T(8,128)(2,1)S(1)} %get-tuple-element.53), channel_id=1, source_target_pairs={{0,128},{64,192},{128,0},{192,64},{1,129},{65,193},{129,1},{193,65... | collective-permute-start | bytes 786440 | tf_op jit(solution)/shard_map/ppermute | solution.py:256
  38.1 10.9 %collective-permute-start.14 = (bf16[2,512,128]{2,1,0:T(8,128)(2,1)S(1)}, bf16[2,512,128]{2,1,0:T(8,128)(2,1)S(1)}, u32[]{:S(2)}, u32[]{:S(2)}) collective-permute-start(bf16[2,512,128]{2,1,0:T(8,128)(2,1)S(1)} %get-tuple-element.60), channel_id=1, source_target_pairs={{0,64},{64,128},{128,192},{192,0},{1,65},{65,129},{129,193},{193,1... | collective-permute-start | bytes 786440 | tf_op jit(solution)/shard_map/ppermute | solution.py:256
  39.1 10.0 %collective-permute-start.13 = (bf16[2,512,128]{2,1,0:T(8,128)(2,1)S(1)}, bf16[2,512,128]{2,1,0:T(8,128)(2,1)S(1)}, u32[]{:S(2)}, u32[]{:S(2)}) collective-permute-start(bf16[2,512,128]{2,1,0:T(8,128)(2,1)S(1)} %get-tuple-element.59), channel_id=1, source_target_pairs={{0,192},{64,0},{128,64},{192,128},{1,193},{65,1},{129,65},{193,129... | collective-permute-start | bytes 786440 | tf_op jit(solution)/shard_map/ppermute | solution.py:256
  41.4 12.3 %collective-permute-start.7 = (bf16[2,256,128]{2,1,0:T(8,128)(2,1)S(1)}, bf16[2,256,128]{2,1,0:T(8,128)(2,1)S(1)}, u32[]{:S(2)}, u32[]{:S(2)}) collective-permute-start(bf16[2,256,128]{2,1,0:T(8,128)(2,1)S(1)} %get-tuple-element.40), channel_id=1, source_target_pairs={{0,56},{8,0},{16,8},{24,16},{32,24},{40,32},{48,40},{56,48},{1,57}... | collective-permute-start | bytes 393224 | tf_op jit(solution)/shard_map/ppermute | solution.py:265
  46.5 7.3 %collective-permute-start.8 = (bf16[2,256,128]{2,1,0:T(8,128)(2,1)S(1)}, bf16[2,256,128]{2,1,0:T(8,128)(2,1)S(1)}, u32[]{:S(2)}, u32[]{:S(2)}) collective-permute-start(bf16[2,256,128]{2,1,0:T(8,128)(2,1)S(1)} %get-tuple-element.41), channel_id=1, source_target_pairs={{0,8},{8,16},{16,24},{24,32},{32,40},{40,48},{48,56},{56,0},{1,9},... | collective-permute-start | bytes 393224 | tf_op jit(solution)/shard_map/ppermute | solution.py:265
  47.3 8.6 %collective-permute-start.11 = (bf16[2,256,128]{2,1,0:T(8,128)(2,1)S(1)}, bf16[2,256,128]{2,1,0:T(8,128)(2,1)S(1)}, u32[]{:S(2)}, u32[]{:S(2)}) collective-permute-start(bf16[2,256,128]{2,1,0:T(8,128)(2,1)S(1)} %get-tuple-element.54), channel_id=1, source_target_pairs={{48,0},{24,8},{0,16},{40,24},{16,32},{56,40},{32,48},{8,56},{49,1}... | collective-permute-start | bytes 393224 | tf_op jit(solution)/shard_map/ppermute | solution.py:274
  49.2 9.1 %collective-permute-start.15 = (bf16[512,128]{1,0:T(8,128)(2,1)S(1)}, bf16[512,128]{1,0:T(8,128)(2,1)S(1)}, u32[]{:S(2)}, u32[]{:S(2)}) collective-permute-start(bf16[512,128]{1,0:T(8,128)(2,1)S(1)} %get-tuple-element.62), channel_id=1, source_target_pairs={{0,32},{8,40},{16,48},{24,56},{32,0},{40,8},{48,16},{56,24},{1,33}... | collective-permute-start | bytes 393224 | tf_op jit(solution)/shard_map/ppermute | solution.py:282
  55.9 4.4 %collective-permute-start.12 = (bf16[256,128]{1,0:T(8,128)(2,1)S(1)}, bf16[256,128]{1,0:T(8,128)(2,1)S(1)}, u32[]{:S(2)}, u32[]{:S(2)}) collective-permute-start(bf16[256,128]{1,0:T(8,128)(2,1)S(1)} %get-tuple-element.56), channel_id=1, source_target_pairs={{0,4},{4,0},{1,5},{5,1},{2,6},{6,2},{3,7},{7,3},{8,12},{12,8},{9,1... | collective-permute-start | bytes 196616 | tf_op jit(solution)/shard_map/ppermute | solution.py:284

commit v18 on v17

--- a/solution.py
+++ b/solution.py
@@ -59,6 +59,9 @@
     krows_buf[...] = jnp.full(krows_buf.shape, low, F32).astype(BF16)
     store(krows_buf, kout_ref.at[4 * BLK :])
     store_blocks(1, qout_ref, 2 * BLK)
+    store_blocks(6, qout_ref, 0)
+    store_blocks(4, kout_ref, 0)
+    store_blocks(5, kout_ref, 2 * BLK)
     loads[2].wait()
     loads[3].wait()
     lse = lse_buf[...].astype(F32)
@@ -70,9 +73,6 @@
     rows.append(jnp.full((1, DIM), jnp.where(swapped, 1.0, 0.0), F32))
     qrows_buf[...] = jnp.concatenate(rows + [jnp.zeros((10, DIM), F32)], axis=0).astype(BF16)
     store(qrows_buf, qout_ref.at[4 * BLK :])
-    store_blocks(6, qout_ref, 0)
-    store_blocks(4, kout_ref, 0)
-    store_blocks(5, kout_ref, 2 * BLK)
     for copy in stores:
         copy.wait()
 

time: 61.2 us -> 61.2 us (level)
  no operation moved by 1% of the time
where the time goes in v18:
time: 61.2 us; the launch traced here: 61 us
  starting transfers between devices  39.7 us (65%)
  Pallas kernels  12.1 us (20%)
  waiting for transfers between devices  7.47 us (12%)
  local copies, waits for them, and re-layouts  0.96 us (2%)
  between operations  0.79 us (1%)
    pallas_call x12, Pallas kernels, call(): pl.pallas_call(kernel, out_shape=[jax.ShapeDtypeStruct(s, t) for s, t in...  12.1 us
    ppermute x3, starting transfers between devices, body(): lax.ppermute(q, 'kz', p)  9 us
    ppermute x1, starting transfers between devices, body(): other_k = lax.ppermute(mine_k, 'kz', z_step(4))  7.19 us
    ppermute x3, starting transfers between devices, body(): k_sets = [k0] + [lax.ppermute(k0, 'pb', y_step(-s)) for s in Y_FROM[1:]]  6.52 us
    ppermute x2, starting transfers between devices, body(): lax.ppermute(d, 'kz', p)  5.03 us
    ppermute x1, starting transfers between devices, body(): dkv_last = lax.ppermute(dkv_send, 'kz', z_step(4))  4.57 us
    ppermute x3, starting transfers between devices, send_back(): return lax.ppermute(part, 'pb', y_step(Y_FROM[turn]))  3.41 us
    ppermute x1, waiting for transfers between devices, body(): dq_back.append(lax.ppermute(dq_z2, 'kz', Z_BACK))  2.09 us
  transfers between devices with their start and end apart: 16, of which 4 were waited for; matrix products, arithmetic and copies ran while one was open for 2% of the time, Pallas kernels for 14%

profile of v18, /device:TPU:4, one launch (start us, length us, event | category | flops | bytes accessed | tf_op | source)
XLA Modules:
  0.0 61.0 jit_solution(6887187916323253835)
XLA Ops:
  0.6 1.9 %shard_map.94 = (bf16[528,128]{1,0:T(8,128)(2,1)}, bf16[528,128]{1,0:T(8,128)(2,1)}) custom-call(s32[128]{0:T(128)} %refs_0_.1, bf16[256,128]{1,0:T(8,128)(2,1)} %refs_1_.1, bf16[256,128]{1,0:T(8,128)(2,1)} %refs_2_.1, bf16[1,256]{1,0:T(2,128)(2,1)} %bitcast.9, bf16[256,128]{1,0:T(8,128)(2,1)} %refs_4_.1, bf16[256,128]{1,0:T(8,128)(2,1)} %refs_5_.1, ...), custom_call_target="tpu_custom_call" | custom-call | tf_op jit(solution)/shard_map/pallas_call | solution.py:208
  2.5 1.3 %collective-permute-start = (bf16[528,128]{1,0:T(8,128)(2,1)}, bf16[528,128]{1,0:T(8,128)(2,1)S(1)}, u32[]{:S(2)}, u32[]{:S(2)}) collective-permute-start(bf16[528,128]{1,0:T(8,128)(2,1)} %get-tuple-element.33), channel_id=1, source_target_pairs={{0,4},{4,0},{1,5},{5,1},{2,6},{6,2},{3,7},{7,3},{8,12},{12,8},{9,1... | collective-permute-start | bytes 405512 | tf_op jit(solution)/shard_map/ppermute | solution.py:232
  3.8 7.2 %collective-permute-start.3 = (bf16[528,128]{1,0:T(8,128)(2,1)}, bf16[528,128]{1,0:T(8,128)(2,1)S(1)}, u32[]{:S(2)}, u32[]{:S(2)}) collective-permute-start(bf16[528,128]{1,0:T(8,128)(2,1)} %get-tuple-element.34), channel_id=1, source_target_pairs={{0,32},{8,40},{16,48},{24,56},{32,0},{40,8},{48,16},{56,24},{1,33}... | collective-permute-start | bytes 405512 | tf_op jit(solution)/shard_map/ppermute | solution.py:231
  11.0 0.9 %pad.4 = bf16[2,528,128]{2,1,0:T(8,128)(2,1)S(1)} pad(bf16[1,528,128]{2,1,0:T(8,128)(2,1)} %bitcast.6, bf16[]{:T(256)} %constant.1.clone.1), padding=0_1x0_0x0_0 | pad | bytes 405506 | tf_op jit(solution)/shard_map/jit(_pad)/pad | solution.py:228
  11.9 1.1 %collective-permute-start.1 = (bf16[2,528,128]{2,1,0:T(8,128)(2,1)S(1)}, bf16[2,528,128]{2,1,0:T(8,128)(2,1)S(1)}, u32[]{:S(2)}, u32[]{:S(2)}) collective-permute-start(bf16[2,528,128]{2,1,0:T(8,128)(2,1)S(1)} %bitcast_dynamic-update-slice_fusion.refs_0_.rows_ref), channel_id=1, source_target_pairs={{0,8},{8,16},{16,24},{24,32},{32,40},{40,48},{48,56},{56,0},{1,9},... | collective-permute-start | bytes 811016 | tf_op jit(solution)/shard_map/ppermute | solution.py:235
  13.0 2.2 %collective-permute-start.2 = (bf16[2,528,128]{2,1,0:T(8,128)(2,1)S(1)}, bf16[2,528,128]{2,1,0:T(8,128)(2,1)S(1)}, u32[]{:S(2)}, u32[]{:S(2)}) collective-permute-start(bf16[2,528,128]{2,1,0:T(8,128)(2,1)S(1)} %bitcast_dynamic-update-slice_fusion.refs_0_.rows_ref), channel_id=1, source_target_pairs={{0,56},{8,0},{16,8},{24,16},{32,24},{40,32},{48,40},{56,48},{1,57}... | collective-permute-start | bytes 811016 | tf_op jit(solution)/shard_map/ppermute | solution.py:235
  15.3 1.9 %collective-permute-done.3 = bf16[528,128]{1,0:T(8,128)(2,1)S(1)} collective-permute-done((bf16[528,128]{1,0:T(8,128)(2,1)}, bf16[528,128]{1,0:T(8,128)(2,1)S(1)}, u32[]{:S(2)}, u32[]{:S(2)}) %collective-permute-start.3) | collective-permute-done | bytes 135200 | tf_op jit(solution)/shard_map/ppermute | solution.py:231
  17.2 3.3 %collective-permute-start.6 = (bf16[2,528,128]{2,1,0:T(8,128)(2,1)S(1)}, bf16[2,528,128]{2,1,0:T(8,128)(2,1)S(1)}, u32[]{:S(2)}, u32[]{:S(2)}) collective-permute-start(bf16[2,528,128]{2,1,0:T(8,128)(2,1)S(1)} %pad_maximum_fusion.refs_3_.refs_1_), channel_id=1, source_target_pairs={{0,128},{64,192},{128,0},{192,64},{1,129},{65,193},{129,1},{193,65... | collective-permute-start | bytes 811016 | tf_op jit(solution)/shard_map/ppermute | solution.py:236
  21.2 2.6 %collective-permute-start.4 = (bf16[2,528,128]{2,1,0:T(8,128)(2,1)S(1)}, bf16[2,528,128]{2,1,0:T(8,128)(2,1)S(1)}, u32[]{:S(2)}, u32[]{:S(2)}) collective-permute-start(bf16[2,528,128]{2,1,0:T(8,128)(2,1)S(1)} %pad_maximum_fusion.refs_3_.refs_1_), channel_id=1, source_target_pairs={{0,192},{64,0},{128,64},{192,128},{1,193},{65,1},{129,65},{193,129... | collective-permute-start | bytes 811016 | tf_op jit(solution)/shard_map/ppermute | solution.py:236
  23.7 5.7 %collective-permute-start.9 = (bf16[2,528,128]{2,1,0:T(8,128)(2,1)S(1)}, bf16[2,528,128]{2,1,0:T(8,128)(2,1)S(1)}, u32[]{:S(2)}, u32[]{:S(2)}) collective-permute-start(bf16[2,528,128]{2,1,0:T(8,128)(2,1)S(1)} %bitcast_dynamic-update-slice_fusion.refs_0_.rows_ref), channel_id=1, source_target_pairs={{0,48},{8,24},{16,0},{24,40},{32,16},{40,56},{48,32},{56,8},{1,49}... | collective-permute-start | bytes 811016 | tf_op jit(solution)/shard_map/ppermute | solution.py:235
  29.4 1.6 %shard_map.95 = (f32[2,128,768]{2,1,0:T(8,128)S(1)}, f32[2,512,128]{2,1,0:T(8,128)S(1)}) custom-call(bf16[2,528,128]{2,1,0:T(8,128)(2,1)S(1)} %bitcast_dynamic-update-slice_fusion.refs_0_.rows_ref, bf16[2,528,128]{2,1,0:T(8,128)(2,1)S(1)} %collective-permute-done.1.refs_1_, bf16[2,528,128]{2,1,0:T(8,128)(2,1)S(1)} %collective-permute-done.2.refs_2_, ...), custom_call_target="tpu_custom_call" | custom-call | flops 500000000 | bytes 1000000 | tf_op jit(solution)/shard_map/pallas_call | solution.py:208
  31.0 1.6 %shard_map.96 = (f32[2,128,768]{2,1,0:T(8,128)S(1)}, f32[2,512,128]{2,1,0:T(8,128)S(1)}) custom-call(bf16[2,528,128]{2,1,0:T(8,128)(2,1)S(1)} %bitcast_dynamic-update-slice_fusion.refs_0_.rows_ref, bf16[2,528,128]{2,1,0:T(8,128)(2,1)S(1)} %collective-permute-done.1.refs_1_, bf16[2,528,128]{2,1,0:T(8,128)(2,1)S(1)} %collective-permute-done.2.refs_2_, ...), custom_call_target="tpu_custom_call" | custom-call | flops 500000000 | bytes 1000000 | tf_op jit(solution)/shard_map/pallas_call | solution.py:208
  32.6 1.6 %shard_map.97 = (f32[2,128,768]{2,1,0:T(8,128)S(1)}, f32[2,512,128]{2,1,0:T(8,128)S(1)}) custom-call(bf16[2,528,128]{2,1,0:T(8,128)(2,1)S(1)} %bitcast_dynamic-update-slice_fusion.refs_0_.rows_ref, bf16[2,528,128]{2,1,0:T(8,128)(2,1)S(1)} %collective-permute-done.1.refs_1_, bf16[2,528,128]{2,1,0:T(8,128)(2,1)S(1)} %collective-permute-done.2.refs_2_, ...), custom_call_target="tpu_custom_call" | custom-call | flops 500000000 | bytes 1000000 | tf_op jit(solution)/shard_map/pallas_call | solution.py:208
  34.2 1.7 %shard_map.98 = (f32[2,256,128]{2,1,0:T(8,128)S(1)}, bf16[2,256,128]{2,1,0:T(8,128)(2,1)S(1)}, bf16[2,256,128]{2,1,0:T(8,128)(2,1)S(1)}, f32[2,512,128]{2,1,0:T(8,128)S(1)}) custom-call(bf16[2,528,128]{2,1,0:T(8,128)(2,1)S(1)} %bitcast_dynamic-update-slice_fusion.refs_0_.rows_ref, bf16[2,528,128]{2,1,0:T(8,128)(2,1)S(1)} %collective-permute-done.1.refs_1_, ...), custom_call_target="tpu_custom_call" | custom-call | flops 500000000 | bytes 1000000 | tf_op jit(solution)/shard_map/pallas_call | solution.py:208
  38.2 0.9 %collective-permute-start.14 = (bf16[2,512,128]{2,1,0:T(8,128)(2,1)S(1)}, bf16[2,512,128]{2,1,0:T(8,128)(2,1)S(1)}, u32[]{:S(2)}, u32[]{:S(2)}) collective-permute-start(bf16[2,512,128]{2,1,0:T(8,128)(2,1)S(1)} %get-tuple-element.60), channel_id=1, source_target_pairs={{0,64},{64,128},{128,192},{192,0},{1,65},{65,129},{129,193},{193,1... | collective-permute-start | bytes 786440 | tf_op jit(solution)/shard_map/ppermute | solution.py:256
  39.1 2.4 %collective-permute-start.13 = (bf16[2,512,128]{2,1,0:T(8,128)(2,1)S(1)}, bf16[2,512,128]{2,1,0:T(8,128)(2,1)S(1)}, u32[]{:S(2)}, u32[]{:S(2)}) collective-permute-start(bf16[2,512,128]{2,1,0:T(8,128)(2,1)S(1)} %get-tuple-element.59), channel_id=1, source_target_pairs={{0,192},{64,0},{128,64},{192,128},{1,193},{65,1},{129,65},{193,129... | collective-permute-start | bytes 786440 | tf_op jit(solution)/shard_map/ppermute | solution.py:256
  41.5 5.0 %collective-permute-start.7 = (bf16[2,256,128]{2,1,0:T(8,128)(2,1)S(1)}, bf16[2,256,128]{2,1,0:T(8,128)(2,1)S(1)}, u32[]{:S(2)}, u32[]{:S(2)}) collective-permute-start(bf16[2,256,128]{2,1,0:T(8,128)(2,1)S(1)} %get-tuple-element.40), channel_id=1, source_target_pairs={{0,56},{8,0},{16,8},{24,16},{32,24},{40,32},{48,40},{56,48},{1,57}... | collective-permute-start | bytes 393224 | tf_op jit(solution)/shard_map/ppermute | solution.py:265
  46.5 0.8 %shard_map.102 = (bf16[2,256,128]{2,1,0:T(8,128)(2,1)S(1)}, f32[2,512,128]{2,1,0:T(8,128)S(1)}) custom-call(bf16[2,528,128]{2,1,0:T(8,128)(2,1)S(1)} %collective-permute-done.9.refs_0_, bf16[2,528,128]{2,1,0:T(8,128)(2,1)S(1)} %pad_maximum_fusion.refs_3_.refs_1_, f32[2,128,256]{2,1,0:T(8,128)S(1)} %get-tuple-element.50.refs_2_, ...), custom_call_target="tpu_custom_call" | custom-call | flops 500000000 | bytes 1000000 | tf_op jit(solution)/shard_map/pallas_call | solution.py:208
  47.3 1.8 %collective-permute-start.11 = (bf16[2,256,128]{2,1,0:T(8,128)(2,1)S(1)}, bf16[2,256,128]{2,1,0:T(8,128)(2,1)S(1)}, u32[]{:S(2)}, u32[]{:S(2)}) collective-permute-start(bf16[2,256,128]{2,1,0:T(8,128)(2,1)S(1)} %get-tuple-element.54), channel_id=1, source_target_pairs={{48,0},{24,8},{0,16},{40,24},{16,32},{56,40},{32,48},{8,56},{49,1}... | collective-permute-start | bytes 393224 | tf_op jit(solution)/shard_map/ppermute | solution.py:274
  49.2 4.6 %collective-permute-start.15 = (bf16[512,128]{1,0:T(8,128)(2,1)S(1)}, bf16[512,128]{1,0:T(8,128)(2,1)S(1)}, u32[]{:S(2)}, u32[]{:S(2)}) collective-permute-start(bf16[512,128]{1,0:T(8,128)(2,1)S(1)} %get-tuple-element.62), channel_id=1, source_target_pairs={{0,32},{8,40},{16,48},{24,56},{32,0},{40,8},{48,16},{56,24},{1,33}... | collective-permute-start | bytes 393224 | tf_op jit(solution)/shard_map/ppermute | solution.py:282
  53.8 2.1 %collective-permute-done.11.refs_3_ = bf16[2,256,128]{2,1,0:T(8,128)(2,1)S(1)} collective-permute-done((bf16[2,256,128]{2,1,0:T(8,128)(2,1)S(1)}, bf16[2,256,128]{2,1,0:T(8,128)(2,1)S(1)}, u32[]{:S(2)}, u32[]{:S(2)}) %collective-permute-start.11) | collective-permute-done | bytes 131104 | tf_op jit(solution)/shard_map/ppermute | solution.py:274
  55.9 0.9 %collective-permute-start.12 = (bf16[256,128]{1,0:T(8,128)(2,1)S(1)}, bf16[256,128]{1,0:T(8,128)(2,1)S(1)}, u32[]{:S(2)}, u32[]{:S(2)}) collective-permute-start(bf16[256,128]{1,0:T(8,128)(2,1)S(1)} %get-tuple-element.56), channel_id=1, source_target_pairs={{0,4},{4,0},{1,5},{5,1},{2,6},{6,2},{3,7},{7,3},{8,12},{12,8},{9,1... | collective-permute-start | bytes 196616 | tf_op jit(solution)/shard_map/ppermute | solution.py:284
  56.9 1.4 %collective-permute-done.15.dkvz_ref = bf16[512,128]{1,0:T(8,128)(2,1)S(1)} collective-permute-done((bf16[512,128]{1,0:T(8,128)(2,1)S(1)}, bf16[512,128]{1,0:T(8,128)(2,1)S(1)}, u32[]{:S(2)}, u32[]{:S(2)}) %collective-permute-start.15) | collective-permute-done | bytes 131104 | tf_op jit(solution)/shard_map/ppermute | solution.py:282
  58.3 2.0 %collective-permute-done.12.dqx_ref = bf16[256,128]{1,0:T(8,128)(2,1)S(1)} collective-permute-done((bf16[256,128]{1,0:T(8,128)(2,1)S(1)}, bf16[256,128]{1,0:T(8,128)(2,1)S(1)}, u32[]{:S(2)}, u32[]{:S(2)}) %collective-permute-start.12) | collective-permute-done | bytes 65568 | tf_op jit(solution)/shard_map/ppermute | solution.py:284
  (25 shorter events, 3.9 us)
Async XLA Ops:
  2.5 9.4 %collective-permute-start = (bf16[528,128]{1,0:T(8,128)(2,1)}, bf16[528,128]{1,0:T(8,128)(2,1)S(1)}, u32[]{:S(2)}, u32[]{:S(2)}) collective-permute-start(bf16[528,128]{1,0:T(8,128)(2,1)} %get-tuple-element.33), channel_id=1, source_target_pairs={{0,4},{4,0},{1,5},{5,1},{2,6},{6,2},{3,7},{7,3},{8,12},{12,8},{9,1... | collective-permute-start | bytes 405512 | tf_op jit(solution)/shard_map/ppermute | solution.py:232
  3.8 13.4 %collective-permute-start.3 = (bf16[528,128]{1,0:T(8,128)(2,1)}, bf16[528,128]{1,0:T(8,128)(2,1)S(1)}, u32[]{:S(2)}, u32[]{:S(2)}) collective-permute-start(bf16[528,128]{1,0:T(8,128)(2,1)} %get-tuple-element.34), channel_id=1, source_target_pairs={{0,32},{8,40},{16,48},{24,56},{32,0},{40,8},{48,16},{56,24},{1,33}... | collective-permute-start | bytes 405512 | tf_op jit(solution)/shard_map/ppermute | solution.py:231
  11.9 5.3 %copy-start = (bf16[528,128]{1,0:T(8,128)(2,1)S(1)}, bf16[528,128]{1,0:T(8,128)(2,1)}, u32[]{:S(2)}) copy-start(bf16[528,128]{1,0:T(8,128)(2,1)} %get-tuple-element.34) | copy-start | bytes 405508
  11.9 11.8 %collective-permute-start.1 = (bf16[2,528,128]{2,1,0:T(8,128)(2,1)S(1)}, bf16[2,528,128]{2,1,0:T(8,128)(2,1)S(1)}, u32[]{:S(2)}, u32[]{:S(2)}) collective-permute-start(bf16[2,528,128]{2,1,0:T(8,128)(2,1)S(1)} %bitcast_dynamic-update-slice_fusion.refs_0_.rows_ref), channel_id=1, source_target_pairs={{0,8},{8,16},{16,24},{24,32},{32,40},{40,48},{48,56},{56,0},{1,9},... | collective-permute-start | bytes 811016 | tf_op jit(solution)/shard_map/ppermute | solution.py:235
  13.0 16.4 %collective-permute-start.2 = (bf16[2,528,128]{2,1,0:T(8,128)(2,1)S(1)}, bf16[2,528,128]{2,1,0:T(8,128)(2,1)S(1)}, u32[]{:S(2)}, u32[]{:S(2)}) collective-permute-start(bf16[2,528,128]{2,1,0:T(8,128)(2,1)S(1)} %bitcast_dynamic-update-slice_fusion.refs_0_.rows_ref), channel_id=1, source_target_pairs={{0,56},{8,0},{16,8},{24,16},{32,24},{40,32},{48,40},{56,48},{1,57}... | collective-permute-start | bytes 811016 | tf_op jit(solution)/shard_map/ppermute | solution.py:235
  17.2 13.8 %collective-permute-start.6 = (bf16[2,528,128]{2,1,0:T(8,128)(2,1)S(1)}, bf16[2,528,128]{2,1,0:T(8,128)(2,1)S(1)}, u32[]{:S(2)}, u32[]{:S(2)}) collective-permute-start(bf16[2,528,128]{2,1,0:T(8,128)(2,1)S(1)} %pad_maximum_fusion.refs_3_.refs_1_), channel_id=1, source_target_pairs={{0,128},{64,192},{128,0},{192,64},{1,129},{65,193},{129,1},{193,65... | collective-permute-start | bytes 811016 | tf_op jit(solution)/shard_map/ppermute | solution.py:236
  20.5 12.1 %collective-permute-start.5 = (bf16[2,528,128]{2,1,0:T(8,128)(2,1)S(1)}, bf16[2,528,128]{2,1,0:T(8,128)(2,1)S(1)}, u32[]{:S(2)}, u32[]{:S(2)}) collective-permute-start(bf16[2,528,128]{2,1,0:T(8,128)(2,1)S(1)} %pad_maximum_fusion.refs_3_.refs_1_), channel_id=1, source_target_pairs={{0,64},{64,128},{128,192},{192,0},{1,65},{65,129},{129,193},{193,1... | collective-permute-start | bytes 811016 | tf_op jit(solution)/shard_map/ppermute | solution.py:236
  21.2 13.0 %collective-permute-start.4 = (bf16[2,528,128]{2,1,0:T(8,128)(2,1)S(1)}, bf16[2,528,128]{2,1,0:T(8,128)(2,1)S(1)}, u32[]{:S(2)}, u32[]{:S(2)}) collective-permute-start(bf16[2,528,128]{2,1,0:T(8,128)(2,1)S(1)} %pad_maximum_fusion.refs_3_.refs_1_), channel_id=1, source_target_pairs={{0,192},{64,0},{128,64},{192,128},{1,193},{65,1},{129,65},{193,129... | collective-permute-start | bytes 811016 | tf_op jit(solution)/shard_map/ppermute | solution.py:236
  23.7 12.1 %collective-permute-start.9 = (bf16[2,528,128]{2,1,0:T(8,128)(2,1)S(1)}, bf16[2,528,128]{2,1,0:T(8,128)(2,1)S(1)}, u32[]{:S(2)}, u32[]{:S(2)}) collective-permute-start(bf16[2,528,128]{2,1,0:T(8,128)(2,1)S(1)} %bitcast_dynamic-update-slice_fusion.refs_0_.rows_ref), channel_id=1, source_target_pairs={{0,48},{8,24},{16,0},{24,40},{32,16},{40,56},{48,32},{56,8},{1,49}... | collective-permute-start | bytes 811016 | tf_op jit(solution)/shard_map/ppermute | solution.py:235
  36.6 10.7 %collective-permute-start.10 = (bf16[2,512,128]{2,1,0:T(8,128)(2,1)S(1)}, bf16[2,512,128]{2,1,0:T(8,128)(2,1)S(1)}, u32[]{:S(2)}, u32[]{:S(2)}) collective-permute-start(bf16[2,512,128]{2,1,0:T(8,128)(2,1)S(1)} %get-tuple-element.53), channel_id=1, source_target_pairs={{0,128},{64,192},{128,0},{192,64},{1,129},{65,193},{129,1},{193,65... | collective-permute-start | bytes 786440 | tf_op jit(solution)/shard_map/ppermute | solution.py:256
  38.2 10.9 %collective-permute-start.14 = (bf16[2,512,128]{2,1,0:T(8,128)(2,1)S(1)}, bf16[2,512,128]{2,1,0:T(8,128)(2,1)S(1)}, u32[]{:S(2)}, u32[]{:S(2)}) collective-permute-start(bf16[2,512,128]{2,1,0:T(8,128)(2,1)S(1)} %get-tuple-element.60), channel_id=1, source_target_pairs={{0,64},{64,128},{128,192},{192,0},{1,65},{65,129},{129,193},{193,1... | collective-permute-start | bytes 786440 | tf_op jit(solution)/shard_map/ppermute | solution.py:256
  39.1 10.0 %collective-permute-start.13 = (bf16[2,512,128]{2,1,0:T(8,128)(2,1)S(1)}, bf16[2,512,128]{2,1,0:T(8,128)(2,1)S(1)}, u32[]{:S(2)}, u32[]{:S(2)}) collective-permute-start(bf16[2,512,128]{2,1,0:T(8,128)(2,1)S(1)} %get-tuple-element.59), channel_id=1, source_target_pairs={{0,192},{64,0},{128,64},{192,128},{1,193},{65,1},{129,65},{193,129... | collective-permute-start | bytes 786440 | tf_op jit(solution)/shard_map/ppermute | solution.py:256
  41.5 12.3 %collective-permute-start.7 = (bf16[2,256,128]{2,1,0:T(8,128)(2,1)S(1)}, bf16[2,256,128]{2,1,0:T(8,128)(2,1)S(1)}, u32[]{:S(2)}, u32[]{:S(2)}) collective-permute-start(bf16[2,256,128]{2,1,0:T(8,128)(2,1)S(1)} %get-tuple-element.40), channel_id=1, source_target_pairs={{0,56},{8,0},{16,8},{24,16},{32,24},{40,32},{48,40},{56,48},{1,57}... | collective-permute-start | bytes 393224 | tf_op jit(solution)/shard_map/ppermute | solution.py:265
  46.5 7.3 %collective-permute-start.8 = (bf16[2,256,128]{2,1,0:T(8,128)(2,1)S(1)}, bf16[2,256,128]{2,1,0:T(8,128)(2,1)S(1)}, u32[]{:S(2)}, u32[]{:S(2)}) collective-permute-start(bf16[2,256,128]{2,1,0:T(8,128)(2,1)S(1)} %get-tuple-element.41), channel_id=1, source_target_pairs={{0,8},{8,16},{16,24},{24,32},{32,40},{40,48},{48,56},{56,0},{1,9},... | collective-permute-start | bytes 393224 | tf_op jit(solution)/shard_map/ppermute | solution.py:265
  47.3 8.6 %collective-permute-start.11 = (bf16[2,256,128]{2,1,0:T(8,128)(2,1)S(1)}, bf16[2,256,128]{2,1,0:T(8,128)(2,1)S(1)}, u32[]{:S(2)}, u32[]{:S(2)}) collective-permute-start(bf16[2,256,128]{2,1,0:T(8,128)(2,1)S(1)} %get-tuple-element.54), channel_id=1, source_target_pairs={{48,0},{24,8},{0,16},{40,24},{16,32},{56,40},{32,48},{8,56},{49,1}... | collective-permute-start | bytes 393224 | tf_op jit(solution)/shard_map/ppermute | solution.py:274
  49.2 9.1 %collective-permute-start.15 = (bf16[512,128]{1,0:T(8,128)(2,1)S(1)}, bf16[512,128]{1,0:T(8,128)(2,1)S(1)}, u32[]{:S(2)}, u32[]{:S(2)}) collective-permute-start(bf16[512,128]{1,0:T(8,128)(2,1)S(1)} %get-tuple-element.62), channel_id=1, source_target_pairs={{0,32},{8,40},{16,48},{24,56},{32,0},{40,8},{48,16},{56,24},{1,33}... | collective-permute-start | bytes 393224 | tf_op jit(solution)/shard_map/ppermute | solution.py:282
  55.9 4.4 %collective-permute-start.12 = (bf16[256,128]{1,0:T(8,128)(2,1)S(1)}, bf16[256,128]{1,0:T(8,128)(2,1)S(1)}, u32[]{:S(2)}, u32[]{:S(2)}) collective-permute-start(bf16[256,128]{1,0:T(8,128)(2,1)S(1)} %get-tuple-element.56), channel_id=1, source_target_pairs={{0,4},{4,0},{1,5},{5,1},{2,6},{6,2},{3,7},{7,3},{8,12},{12,8},{9,1... | collective-permute-start | bytes 196616 | tf_op jit(solution)/shard_map/ppermute | solution.py:284
